TPU v7x, 256 devices: a whole 4x4x8 slice. The times are simulated.
256 devices in a mesh: rows: 64 (over z, x, core), sub: 4 (over y).
Axes of the slice: x: 4, y: 4, z: 8, core: 2. Of those that a mesh axis runs over, the one named last changes fastest.
Arguments:
- embeddings: float32 [131072, 256], P('rows'), may hold values from -6 to 6
- start_vectors: float32 [131072, 64], P('rows'), may hold values from -6 to 6
- pairs: int32 [512, 2], P('rows'), may hold values from -1 to 127, as said below
Outputs:
- vectors: float32 [131072, 64], P('rows')
Inputs may be any that keep to these rules, and one draw needn't show every extreme that they name: Slot s of row group g is entry g * 8 + s. A group's pairs have row block 2g or 2g+1 (owned by the group) and column block j with row block <= j <= 2g+3 and j < 128; no pair is listed twice; both diagonal pairs (2g, 2g) and (2g+1, 2g+1) are listed; used slots come first, empty slots hold -1 in both entries; at most 7 slots of a group are used and group 0 uses 7.
All inputs are finite; a program needn't handle non-finite values.
Results may differ from a plain program's by a relative error of at most 0.0003.
Values sent between devices are 32-bit elements; how exact they have to be, the bound alone decides.
No kernel may reach another device: no remote copies, remote signals or barrier semaphores. Data moves between devices by JAX's collectives and lax.ppermute only.
A program may use at most 64 MiB of HBM per device.

v0:
```python
import jax
import jax.numpy as jnp
from jax import lax
from jax.sharding import PartitionSpec as P

BLK_DEV = 2
ITERS = 2


inverse_width = 1.0 / 64.0
highest = lax.Precision.HIGHEST


def shifted(array, axis, by):
    devices = lax.axis_size(axis)
    pairs = [(i, i + by) for i in range(devices) if 0 <= i + by < devices]
    return lax.ppermute(array, axis, pairs)


def tile_terms(ext_embed, ext_norms, ext_vec, mine, first_block, block, row_count):

    def visit(slot, acc):
        row_block = mine[slot, 0]
        col_block = mine[slot, 1]

        def work(inner):
            row_start = (row_block - first_block) * block
            col_start = (col_block - first_block) * block
            xa = lax.dynamic_slice_in_dim(ext_embed, row_start, row_count, 0)
            xb = lax.dynamic_slice_in_dim(ext_embed, col_start, block, 0)
            na = lax.dynamic_slice_in_dim(ext_norms, row_start, row_count, 0)
            nb = lax.dynamic_slice_in_dim(ext_norms, col_start, block, 0)
            dots = lax.dot_general(
                xa,
                xb,
                (((1,), (1,)), ((), ())),
                precision=highest,
                preferred_element_type=jnp.float32,
            )
            dist = jnp.maximum(na[:, None] + nb[None, :] - 2.0 * dots, 0.0)
            affinity = jnp.exp(-dist * inverse_width)
            va = lax.dynamic_slice_in_dim(ext_vec, row_start, row_count, 0)
            vb = lax.dynamic_slice_in_dim(ext_vec, col_start, block, 0)
            ahead = jnp.dot(affinity, vb, precision=highest, preferred_element_type=jnp.float32)
            behind = lax.dot_general(
                affinity,
                va,
                (((0,), (0,)), ((), ())),
                precision=highest,
                preferred_element_type=jnp.float32,
            )
            behind = behind * (row_block != col_block).astype(jnp.float32)
            current = lax.dynamic_slice_in_dim(inner, row_start, row_count, 0)
            inner = lax.dynamic_update_slice_in_dim(inner, current + ahead, row_start, 0)
            current = lax.dynamic_slice_in_dim(inner, col_start, block, 0)
            return lax.dynamic_update_slice_in_dim(inner, current + behind, col_start, 0)

        return lax.cond(row_block >= 0, work, lambda inner: inner, acc)

    start_acc = jnp.zeros(ext_vec.shape, jnp.float32)
    return lax.fori_loop(0, mine.shape[0], visit, start_acc)


def gram_of(share, total_rows):
    return (
        lax.dot_general(
            share,
            share,
            (((0,), (0,)), ((), ())),
            precision=highest,
            preferred_element_type=jnp.float32,
        )
        / total_rows
    )


def right_solve(lower, image):
    return lax.linalg.triangular_solve(lower, image, left_side=False, lower=True, transpose_a=True)


def on_device(embeddings, start_vectors, pairs):
    group = lax.axis_index("rows")
    member = lax.axis_index("sub")
    members = lax.axis_size("sub")
    rows_own = embeddings.shape[0]
    block = rows_own // BLK_DEV
    quarter = rows_own // members
    total_rows = rows_own * lax.axis_size("rows")
    first_block = group * BLK_DEV
    per_member = pairs.shape[0] // members
    slot_ids = member * per_member + jnp.arange(per_member, dtype=jnp.int32)
    mine = jnp.take(pairs, slot_ids, axis=0)
    next_embed, next_vec = shifted((embeddings, start_vectors), "rows", -1)
    ext_embed = jnp.concatenate([embeddings, next_embed], axis=0)
    ext_norms = jnp.sum(ext_embed * ext_embed, axis=1)
    own_vec = start_vectors
    whole = start_vectors
    share = start_vectors[:quarter]
    for step in range(ITERS):
        ext_vec = jnp.concatenate([own_vec, next_vec], axis=0)
        terms = tile_terms(ext_embed, ext_norms, ext_vec, mine, first_block, block, block)
        own_part = terms[:rows_own]
        spill_part = terms[rows_own:]
        own_sum, spill_sum = lax.psum((own_part, spill_part), "sub")
        incoming = shifted(spill_sum, "rows", 1)
        whole = own_sum + incoming
        share = lax.dynamic_slice_in_dim(whole, member * quarter, quarter, 0)
        gram_part = gram_of(share, total_rows)
        gram = lax.psum(gram_part, ("rows", "sub"))
        lower = jnp.linalg.cholesky(gram)
        whole = right_solve(lower, whole)
        if step + 1 < ITERS:
            own_vec = whole
            next_vec = shifted(whole, "rows", -1)
    return whole


def solution(mesh):
    return jax.shard_map(
        on_device,
        mesh=mesh,
        in_specs=(P("rows", None), P("rows", None), P("rows", None)),
        out_specs=P("rows", None),
        check_vma=False,
    )
```

profile of v0, /device:TPU:16, one launch (start us, length us, event | category | flops | bytes accessed | tf_op | source)
XLA Modules:
  0.0 465.7 jit_solution(7890683646325873900)
XLA Ops:
  6.5 1.4 collective-permute-start
  8.0 1.3 collective-permute-start.1
  9.3 0.8 copy.12
  10.7 3.1 constant_dynamic-update-slice_fusion.1
  14.5 3.0 constant_dynamic-update-slice_fusion
  17.5 2.8 multiply_reduce_fusion
  20.4 46.2 %while.32 = (s32[]{:T(128)}, f32[4096,64]{0,1:T(8,128)S(1)}, s32[2,2]{1,0:T(2,128)S(1)}, s32[]{:T(128)}, f32[4096]{0:T(1024)S(1)}, /*index=5*/f32[4096,256]{1,0:...) while((s32[]{:T(128)}, f32[4096,64]{0,1:T(8,128)S(1)}, s32[2,2]{1,0:T(2,128)S(1)}, s32[]{:T(128)}, ...), condition=%wide.region_4.5_spmd, body=%wide.region_1.0_spmd.sunk | while | flops 4844617728 | bytes 33587592 | solution.py:61
  21.5 22.0 %conditional.4 = (f32[4096,64]{0,1:T(8,128)S(1)}) conditional(s32[]{:T(128)} %convert_element_type.22, f32[4096,64]{0,1:T(8,128)S(1)} %get-tuple-element.484, (s32[]{:T(128)}, s32[]{:T(128)}, f32[4096,64]{0,1:T(8,128)S(1)}, f32[4096]{0:T(1024)S(1)}, s32[2,2]{1,0:T(2,128)S(1)}, /*index=5*/s32[]{:T(128)}, f32[4096,256]{1,0:T(8,128)}, ...), branch_computations={%region_2.2_spmd, %region_3.3_spmd} | conditional | flops 4844617728 | bytes 33587412 | solution.py:58
  21.6 0.7 constant_dynamic-slice_fusion
  23.5 5.4 %fusion.17 = f32[1024,1024]{1,0:T(8,128)S(1)} fusion(f32[4096,256]{1,0:T(8,128)} %get-tuple-element.297, s32[]{:T(128)S(6)} %select_n.59, s32[]{:T(128)S(6)} %select_n.58), kind=kOutput, calls=%fused_computation.19 | convolution fusion | flops 3221225472 | bytes 6291464 | tf_op jit(solution)/shard_map/while/body/eval_jaxpr/cond/branch_1_fun/dot_general | solution.py:33
  29.0 2.0 copy-done
  31.0 5.3 %fusion.13 = f32[4096,64]{0,1:T(8,128)S(1)} fusion(f32[4096,64]{0,1:T(8,128)S(1)} %get-tuple-element.291, s32[]{:T(128)S(6)} %select_n.58, f32[1024,1024]{1,0:T(8,128)S(1)} %fusion.17, f32[1024]{0:T(1024)S(1)} %get-tuple-element.381, f32[1024]{0:T(1024)S(1)} %get-tuple-element.380, f32[4096,64]{1,0:T(8,128)S(1)} %get-tuple-element.298, s32[]{:T(128)S(6)} %select_n.59), kind=kOutput, calls=%fused_computation.15 | convolution fusion | flops 811663360 | bytes 5251080 | tf_op jit(solution)/shard_map/while/body/eval_jaxpr/cond/branch_1_fun/dot_general | solution.py:44
  37.5 6.0 %fusion.16 = f32[4096,64]{0,1:T(8,128)S(1)} fusion(f32[4096,64]{0,1:T(8,128)S(1)} %fusion.13, s32[]{:T(128)S(6)} %select_n.59, f32[1024,1024]{1,0:T(8,128)} %copy-done, f32[1024]{0:T(1024)S(1)} %get-tuple-element.381, f32[1024]{0:T(1024)S(1)} %get-tuple-element.380, f32[4096,64]{1,0:T(8,128)S(1)} %get-tuple-element.298, s32[]{:T(128)S(6)} %select_n.58, ...), kind=kOutput, calls=%fused_computation.18 | convolution fusion | flops 811728896 | bytes 5251084 | tf_op jit(solution)/shard_map/while/body/eval_jaxpr/cond/branch_1_fun/dot_general | solution.py:45
  44.7 21.9 %conditional.4 = (f32[4096,64]{0,1:T(8,128)S(1)}) conditional(s32[]{:T(128)} %convert_element_type.22, f32[4096,64]{0,1:T(8,128)S(1)} %get-tuple-element.484, (s32[]{:T(128)}, s32[]{:T(128)}, f32[4096,64]{0,1:T(8,128)S(1)}, f32[4096]{0:T(1024)S(1)}, s32[2,2]{1,0:T(2,128)S(1)}, /*index=5*/s32[]{:T(128)}, f32[4096,256]{1,0:T(8,128)}, ...), branch_computations={%region_2.2_spmd, %region_3.3_spmd} | conditional | flops 4844617728 | bytes 33587412 | solution.py:58
  46.7 5.3 %fusion.17 = f32[1024,1024]{1,0:T(8,128)S(1)} fusion(f32[4096,256]{1,0:T(8,128)} %get-tuple-element.297, s32[]{:T(128)S(6)} %select_n.59, s32[]{:T(128)S(6)} %select_n.58), kind=kOutput, calls=%fused_computation.19 | convolution fusion | flops 3221225472 | bytes 6291464 | tf_op jit(solution)/shard_map/while/body/eval_jaxpr/cond/branch_1_fun/dot_general | solution.py:33
  52.1 2.0 copy-done
  54.0 5.3 %fusion.13 = f32[4096,64]{0,1:T(8,128)S(1)} fusion(f32[4096,64]{0,1:T(8,128)S(1)} %get-tuple-element.291, s32[]{:T(128)S(6)} %select_n.58, f32[1024,1024]{1,0:T(8,128)S(1)} %fusion.17, f32[1024]{0:T(1024)S(1)} %get-tuple-element.381, f32[1024]{0:T(1024)S(1)} %get-tuple-element.380, f32[4096,64]{1,0:T(8,128)S(1)} %get-tuple-element.298, s32[]{:T(128)S(6)} %select_n.59), kind=kOutput, calls=%fused_computation.15 | convolution fusion | flops 811663360 | bytes 5251080 | tf_op jit(solution)/shard_map/while/body/eval_jaxpr/cond/branch_1_fun/dot_general | solution.py:44
  60.6 6.0 %fusion.16 = f32[4096,64]{0,1:T(8,128)S(1)} fusion(f32[4096,64]{0,1:T(8,128)S(1)} %fusion.13, s32[]{:T(128)S(6)} %select_n.59, f32[1024,1024]{1,0:T(8,128)} %copy-done, f32[1024]{0:T(1024)S(1)} %get-tuple-element.381, f32[1024]{0:T(1024)S(1)} %get-tuple-element.380, f32[4096,64]{1,0:T(8,128)S(1)} %get-tuple-element.298, s32[]{:T(128)S(6)} %select_n.58, ...), kind=kOutput, calls=%fused_computation.18 | convolution fusion | flops 811728896 | bytes 5251084 | tf_op jit(solution)/shard_map/while/body/eval_jaxpr/cond/branch_1_fun/dot_general | solution.py:45
  66.6 1.1 fusion.78
  67.8 78.6 %all-reduce.7.cloned.1.call-done = (f32[2048,64]{0,1:T(8,128)}, f32[2048,64]{0,1:T(8,128)}) async-done(((f32[2048,64]{0,1:T(8,128)}, f32[2048,64]{0,1:T(8,128)}), (f32[2048,64]{0,1:T(8,128)}, f32[2048,64]{0,1:T(8,128)})) %all-reduce.7.cloned.1.call-update) | async-done | bytes 1048592 | tf_op jit(solution)/shard_map/psum | solution.py:104
  146.4 1.3 collective-permute-start.2
  147.7 1.7 collective-permute-done.2
  149.4 1.1 add.180
  150.8 84.0 %psum.44 = f32[64,64]{0,1:T(8,128)S(1)} all-reduce(f32[64,64]{0,1:T(8,128)S(1)} %convolution_multiply_fusion.1), channel_id=1, replica_groups=mesh['rows'=64,'sub'=4] {'rows','sub'}, use_global_device_ids=true, to_apply=%region_7.8 | all-reduce | flops 4096 | bytes 32768 | tf_op jit(solution)/shard_map/psum | solution.py:109
  234.9 5.8 %cholesky.44 = f32[64,64]{1,0:T(8,128)S(1)} custom-call(f32[64,64]{1,0:T(8,128)S(1)} %fusion.69), custom_call_target="Cholesky" | custom-call | tf_op jit(solution)/shard_map/jit(cholesky)/cholesky | solution.py:110
  242.1 4.9 %custom-call.6 = f32[1,64,64]{1,2,0:T(8,128)S(1)} custom-call(f32[1,64,64]{2,1,0:T(8,128)S(1)} %fusion.64), custom_call_target="InvertDiagBlocksLowerTriangular" | custom-call | tf_op jit(solution)/shard_map/triangular_solve/custom-call.0 | solution.py:78
  247.6 1.3 collective-permute-start.3
  248.9 2.5 collective-permute-done.3
  252.2 46.2 %while.33 = (s32[]{:T(128)}, f32[4096,64]{0,1:T(8,128)S(1)}, s32[2,2]{1,0:T(2,128)S(1)}, s32[]{:T(128)}, f32[4096]{0:T(1024)S(1)}, /*index=5*/f32[4096,256]{1,0:...) while((s32[]{:T(128)}, f32[4096,64]{0,1:T(8,128)S(1)}, s32[2,2]{1,0:T(2,128)S(1)}, s32[]{:T(128)}, ...), condition=%wide.region_13.16_spmd, body=%wide.region_10.15_spmd.sunk | while | flops 4844617728 | bytes 33587592 | solution.py:61
  253.4 22.0 %conditional.5 = (f32[4096,64]{0,1:T(8,128)S(1)}) conditional(s32[]{:T(128)} %convert_element_type.23, f32[4096,64]{0,1:T(8,128)S(1)} %get-tuple-element.511, (s32[]{:T(128)}, s32[]{:T(128)}, f32[4096,64]{0,1:T(8,128)S(1)}, f32[4096]{0:T(1024)S(1)}, s32[2,2]{1,0:T(2,128)S(1)}, /*index=5*/s32[]{:T(128)}, f32[4096,256]{1,0:T(8,128)}, ...), branch_computations={%region_11.13_spmd, %region_12.14_spmd} | conditional | flops 4844617728 | bytes 33587412 | solution.py:58
  255.4 5.4 %fusion.48 = f32[1024,1024]{1,0:T(8,128)S(1)} fusion(f32[4096,256]{1,0:T(8,128)} %get-tuple-element.313, s32[]{:T(128)S(6)} %select_n.62, s32[]{:T(128)S(6)} %select_n.61), kind=kOutput, calls=%fused_computation.53 | convolution fusion | flops 3221225472 | bytes 6291464 | tf_op jit(solution)/shard_map/while/body/eval_jaxpr/cond/branch_1_fun/dot_general | solution.py:33
  260.8 2.0 copy-done.1
  262.8 5.3 %fusion.44 = f32[4096,64]{0,1:T(8,128)S(1)} fusion(f32[4096,64]{0,1:T(8,128)S(1)} %get-tuple-element.307, s32[]{:T(128)S(6)} %select_n.61, f32[1024,1024]{1,0:T(8,128)S(1)} %fusion.48, f32[1024]{0:T(1024)S(1)} %get-tuple-element.383, f32[1024]{0:T(1024)S(1)} %get-tuple-element.382, f32[4096,64]{1,0:T(8,128)S(1)} %get-tuple-element.314, s32[]{:T(128)S(6)} %select_n.62), kind=kOutput, calls=%fused_computation.49 | convolution fusion | flops 811663360 | bytes 5251080 | tf_op jit(solution)/shard_map/while/body/eval_jaxpr/cond/branch_1_fun/dot_general | solution.py:44
  269.3 6.0 %fusion.47 = f32[4096,64]{0,1:T(8,128)S(1)} fusion(f32[4096,64]{0,1:T(8,128)S(1)} %fusion.44, s32[]{:T(128)S(6)} %select_n.62, f32[1024,1024]{1,0:T(8,128)} %copy-done.1, f32[1024]{0:T(1024)S(1)} %get-tuple-element.383, f32[1024]{0:T(1024)S(1)} %get-tuple-element.382, f32[4096,64]{1,0:T(8,128)S(1)} %get-tuple-element.314, s32[]{:T(128)S(6)} %select_n.61, ...), kind=kOutput, calls=%fused_computation.52 | convolution fusion | flops 811728896 | bytes 5251084 | tf_op jit(solution)/shard_map/while/body/eval_jaxpr/cond/branch_1_fun/dot_general | solution.py:45
  276.5 21.9 %conditional.5 = (f32[4096,64]{0,1:T(8,128)S(1)}) conditional(s32[]{:T(128)} %convert_element_type.23, f32[4096,64]{0,1:T(8,128)S(1)} %get-tuple-element.511, (s32[]{:T(128)}, s32[]{:T(128)}, f32[4096,64]{0,1:T(8,128)S(1)}, f32[4096]{0:T(1024)S(1)}, s32[2,2]{1,0:T(2,128)S(1)}, /*index=5*/s32[]{:T(128)}, f32[4096,256]{1,0:T(8,128)}, ...), branch_computations={%region_11.13_spmd, %region_12.14_spmd} | conditional | flops 4844617728 | bytes 33587412 | solution.py:58
  278.5 5.3 %fusion.48 = f32[1024,1024]{1,0:T(8,128)S(1)} fusion(f32[4096,256]{1,0:T(8,128)} %get-tuple-element.313, s32[]{:T(128)S(6)} %select_n.62, s32[]{:T(128)S(6)} %select_n.61), kind=kOutput, calls=%fused_computation.53 | convolution fusion | flops 3221225472 | bytes 6291464 | tf_op jit(solution)/shard_map/while/body/eval_jaxpr/cond/branch_1_fun/dot_general | solution.py:33
  283.9 2.0 copy-done.1
  285.8 5.3 %fusion.44 = f32[4096,64]{0,1:T(8,128)S(1)} fusion(f32[4096,64]{0,1:T(8,128)S(1)} %get-tuple-element.307, s32[]{:T(128)S(6)} %select_n.61, f32[1024,1024]{1,0:T(8,128)S(1)} %fusion.48, f32[1024]{0:T(1024)S(1)} %get-tuple-element.383, f32[1024]{0:T(1024)S(1)} %get-tuple-element.382, f32[4096,64]{1,0:T(8,128)S(1)} %get-tuple-element.314, s32[]{:T(128)S(6)} %select_n.62), kind=kOutput, calls=%fused_computation.49 | convolution fusion | flops 811663360 | bytes 5251080 | tf_op jit(solution)/shard_map/while/body/eval_jaxpr/cond/branch_1_fun/dot_general | solution.py:44
  292.4 6.0 %fusion.47 = f32[4096,64]{0,1:T(8,128)S(1)} fusion(f32[4096,64]{0,1:T(8,128)S(1)} %fusion.44, s32[]{:T(128)S(6)} %select_n.62, f32[1024,1024]{1,0:T(8,128)} %copy-done.1, f32[1024]{0:T(1024)S(1)} %get-tuple-element.383, f32[1024]{0:T(1024)S(1)} %get-tuple-element.382, f32[4096,64]{1,0:T(8,128)S(1)} %get-tuple-element.314, s32[]{:T(128)S(6)} %select_n.61, ...), kind=kOutput, calls=%fused_computation.52 | convolution fusion | flops 811728896 | bytes 5251084 | tf_op jit(solution)/shard_map/while/body/eval_jaxpr/cond/branch_1_fun/dot_general | solution.py:45
  298.4 1.1 fusion.77
  299.5 57.2 %all-reduce.5.cloned.1.call-done = (f32[2048,64]{0,1:T(8,128)}, f32[2048,64]{0,1:T(8,128)}) async-done(((f32[2048,64]{0,1:T(8,128)}, f32[2048,64]{0,1:T(8,128)}), (f32[2048,64]{0,1:T(8,128)}, f32[2048,64]{0,1:T(8,128)})) %all-reduce.5.cloned.1.call-update) | async-done | bytes 1048592 | tf_op jit(solution)/shard_map/psum | solution.py:104
  356.7 1.3 collective-permute-start.4
  358.1 1.7 collective-permute-done.4
  359.8 1.1 add.182
  361.2 84.1 %psum.47 = f32[64,64]{0,1:T(8,128)S(1)} all-reduce(f32[64,64]{0,1:T(8,128)S(1)} %convolution_multiply_fusion), channel_id=1, replica_groups=mesh['rows'=64,'sub'=4] {'rows','sub'}, use_global_device_ids=true, to_apply=%region_16.19 | all-reduce | flops 4096 | bytes 32768 | tf_op jit(solution)/shard_map/psum | solution.py:109
  445.3 5.8 %cholesky.55 = f32[64,64]{1,0:T(8,128)S(1)} custom-call(f32[64,64]{1,0:T(8,128)S(1)} %fusion.67), custom_call_target="Cholesky" | custom-call | tf_op jit(solution)/shard_map/jit(cholesky)/cholesky | solution.py:110
  452.5 4.9 %custom-call.7 = f32[1,64,64]{1,2,0:T(8,128)S(1)} custom-call(f32[1,64,64]{2,1,0:T(8,128)S(1)} %fusion.65), custom_call_target="InvertDiagBlocksLowerTriangular" | custom-call | tf_op jit(solution)/shard_map/triangular_solve/custom-call.0 | solution.py:78
  457.4 1.4 convolution_bitcast_fusion
  (47 shorter events, 10.3 us)
Async XLA Ops:
  6.5 7.2 %copy-start.2 = (f32[2048,64]{0,1:T(8,128)S(1)}, f32[2048,64]{0,1:T(8,128)}, u32[]{:S(2)}) copy-start(f32[2048,64]{0,1:T(8,128)} %param.15) | copy-start | bytes 1572868
  6.5 139.8 %all-reduce.7.cloned.1.call-start = ((), (), s32[]{:S(2)}) async-start(), calls=%async_computation.1 | async-start | bytes 2097152 | tf_op jit(solution)/shard_map/psum | solution.py:104
  6.5 7.9 %collective-permute-start = (f32[2048,256]{1,0:T(8,128)}, f32[2048,256]{1,0:T(8,128)}, u32[]{:S(2)}, u32[]{:S(2)}) collective-permute-start(f32[2048,256]{1,0:T(8,128)} %param.14), channel_id=1, source_target_pairs={{4,0},{8,4},{12,8},{16,12},{20,16},{24,20},{28,24},{32,28},{36,32}... | collective-permute-start | bytes 6291464 | tf_op jit(solution)/shard_map/ppermute | solution.py:17
  8.0 5.8 %collective-permute-start.1 = (f32[2048,64]{0,1:T(8,128)}, f32[2048,64]{0,1:T(8,128)S(1)}, u32[]{:S(2)}, u32[]{:S(2)}) collective-permute-start(f32[2048,64]{0,1:T(8,128)} %param.15), channel_id=1, source_target_pairs={{4,0},{8,4},{12,8},{16,12},{20,16},{24,20},{28,24},{32,28},{36,32}... | collective-permute-start | bytes 1572872 | tf_op jit(solution)/shard_map/ppermute | solution.py:17
  29.0 2.0 copy-start
  52.0 2.0 copy-start
  67.7 289.0 %all-reduce.5.cloned.1.call-start = ((), (), s32[]{:S(2)}) async-start(), calls=%async_computation | async-start | bytes 2097152 | tf_op jit(solution)/shard_map/psum | solution.py:104
  146.4 3.0 collective-permute-start.2
  247.6 3.8 collective-permute-start.3
  260.8 2.0 copy-start.1
  283.9 2.0 copy-start.1
  356.7 3.0 collective-permute-start.4
Sparse Core Ops, SparseCore 0:
  67.8 78.5 all-reduce.6
  299.6 57.0 all-reduce.4
where the time goes:
time: 471 us; the launch traced here: 466 us
  blocking collectives  168 us (36%)
  waiting for transfers between devices  142 us (30%)
  matrix products  69.3 us (15%)
  other arithmetic  29.4 us (6%)
  local copies, waits for them, and re-layouts  23.6 us (5%)
  between operations  13.6 us (3%)
  loops' own time  13.2 us (3%)
  starting transfers between devices  6.66 us (1%)
    psum x2, blocking collectives, on_device(): gram = lax.psum(gram_part, ('rows', 'sub'))  168 us
    psum x2, waiting for transfers between devices, on_device(): own_sum, spill_sum = lax.psum((own_part, spill_part), 'sub')  136 us
    dot_general x4, matrix products, work(): lax.dot_general(affinity, va, (((0,), (0,)), ((), ())), precision=highest...  24.1 us
    dot_general x4, matrix products, work(): lax.dot_general(xa, xb, (((1,), (1,)), ((), ())), precision=highest, pref...  21.5 us
    dot_general x4, matrix products, work(): jnp.dot(affinity, vb, precision=highest, preferred_element_type=jnp.float32)  21 us
    another operation x6, other arithmetic, on_device(): lower = jnp.linalg.cholesky(gram)  13 us
    another operation x4, other arithmetic, right_solve(): lax.linalg.triangular_solve(lower, image, left_side=False, lower=True, tr...  11.1 us
    another operation x4, loops' own time, visit(): return lax.cond(row_block >= 0, work, lambda inner: inner, acc)  10.6 us
  transfers between devices with their start and end apart: 7, of which 5 were waited for; matrix products, arithmetic and copies ran while one was open for 1% of the time, Pallas kernels for 0%

commit v1 on v0

v1 whole, which is shorter than its diff:
```python
import functools
import jax
import jax.numpy as jnp
from jax import lax
from jax.experimental import pallas as pl
from jax.experimental.pallas import tpu as pltpu
from jax.sharding import PartitionSpec as P

BLK_DEV = 2
MB = 1024 * 1024
LOG2E = 1.4426950408889634
SCALE = LOG2E / 64.0

f32 = jnp.float32
bf16 = jnp.bfloat16
NN = (((1,), (0,)), ((), ()))
NT = (((1,), (1,)), ((), ()))


def dot(a, b, dims):
    return lax.dot_general(a, b, dims, preferred_element_type=f32)


def split2(x):
    hi = x.astype(bf16)
    return hi, (x - hi.astype(f32)).astype(bf16)


def split3(x):
    hi = x.astype(bf16)
    rest = x - hi.astype(f32)
    mid = rest.astype(bf16)
    return hi, mid, (rest - mid.astype(f32)).astype(bf16)


def listed(pairs_ref, row_block, col_block):
    hit = jnp.int32(0)
    for slot in range(pairs_ref.shape[0]):
        same = (pairs_ref[slot, 0] == row_block) & (pairs_ref[slot, 1] == col_block)
        hit = hit | same.astype(jnp.int32)
    return hit > 0


def place():
    group = lax.axis_index("rows")
    member = lax.axis_index("sub")
    return group, member


def want(pairs_ref, group, member, members, offset, j):
    mine = group * BLK_DEV + (member * BLK_DEV) // members
    other = (group + offset) * BLK_DEV + j
    return listed(pairs_ref, jnp.minimum(mine, other), jnp.maximum(mine, other))


def add_tiles(x_ref, xah, xal, na, v_ref, acc_ref, eh_ref, el_ref, start, rows, chunk):
    for c in range(rows // chunk):
        here = pl.ds(start + c * chunk, chunk)
        x = x_ref[here, :]
        nb = jnp.sum(x * x, axis=1, keepdims=True) * SCALE
        xh, xl = split2(x)
        d = dot(xh, xah, NT) + (dot(xh, xal, NT) + dot(xl, xah, NT))
        e = jnp.exp2(jnp.minimum(d - nb - na, 0.0))
        eh, el = split2(e)
        eh_ref[here, :] = eh
        el_ref[here, :] = el
        vh, vm, vl = split3(v_ref[:, here])
        k = vh.shape[0]
        first = dot(jnp.concatenate([vh, vm, vl], 0), eh, NN)
        second = dot(jnp.concatenate([vh, vm], 0), el, NN)
        acc_ref[...] += (first[:k] + second[:k]) + (first[k : 2 * k] + second[k:] + first[2 * k :])


def own_kernel(members, x_ref, v_ref, pairs_ref, xah_ref, xal_ref, na_ref, acc_ref, eh_ref, el_ref):
    group, member = place()
    rows = x_ref.shape[0]
    quarter = rows // members
    block = rows // BLK_DEV
    xa = x_ref[pl.ds(pl.multiple_of(member * quarter, quarter), quarter), :]
    ones = jnp.ones((8, xa.shape[1]), f32)
    na_ref[...] = lax.dot_general(ones, xa * xa, NT, precision=lax.Precision.HIGHEST, preferred_element_type=f32) * SCALE
    xah, xal = split2(xa * (2.0 * SCALE))
    xah_ref[...] = xah
    xal_ref[...] = xal
    acc_ref[...] = jnp.zeros_like(acc_ref)
    for j in range(BLK_DEV):
        @pl.when(want(pairs_ref, group, member, members, 0, j))
        def _():
            add_tiles(x_ref, xah_ref[...], xal_ref[...], na_ref[0:1, :], v_ref, acc_ref, eh_ref, el_ref, j * block, block, 256)


def other_kernel(members, offset, x_ref, v_ref, pairs_ref, xah_ref, xal_ref, na_ref, in_ref, acc_ref, eh_ref, el_ref):
    group, member = place()
    rows = x_ref.shape[0]
    block = rows // BLK_DEV
    acc_ref[...] = in_ref[...]
    for j in range(BLK_DEV):
        @pl.when(want(pairs_ref, group, member, members, offset, j))
        def _():
            add_tiles(x_ref, xah_ref[...], xal_ref[...], na_ref[0:1, :], v_ref, acc_ref, eh_ref, el_ref, j * block, block, 256)


def gram_sum(vh, vm, vl):
    s = jnp.concatenate([vh, vm, vl], 0)
    k = vh.shape[0]
    p = dot(s, s, NT)
    r = p[:k] + (p[k : 2 * k] + p[2 * k :])
    return r[:, :k] + (r[:, k : 2 * k] + r[:, 2 * k :])


def gather_into(full_ref, pieces, members):
    _, member = place()
    quarter = pieces[0].shape[1]
    for k, piece in enumerate(pieces):
        q = lax.rem(member - k + members, members)
        full_ref[:, pl.ds(pl.multiple_of(q * quarter, quarter), quarter)] = piece[...]


def join_kernel(members, total, *refs):
    pieces, full_ref, gram_ref = refs[:members], refs[members], refs[members + 1]
    gather_into(full_ref, pieces, members)
    gram_ref[...] = gram_sum(*split3(full_ref[...])) / total


def second_kernel(members, vo_ref, vp_ref, vn_ref, eho, elo, ehp, elp, ehn, eln, pairs_ref, prev_pairs_ref, out_ref):
    group, member = place()
    rows = vo_ref.shape[1]
    block = rows // BLK_DEV
    k = vo_ref.shape[0]
    out_ref[...] = jnp.zeros_like(out_ref)
    for v_ref, eh_ref, el_ref, plist, offset in (
        (vo_ref, eho, elo, pairs_ref, 0),
        (vp_ref, ehp, elp, prev_pairs_ref, -1),
        (vn_ref, ehn, eln, pairs_ref, 1),
    ):
        for j in range(BLK_DEV):
            @pl.when(want(plist, group, member, members, offset, j))
            def _():
                here = pl.ds(j * block, block)
                vh, vm, vl = split3(v_ref[:, here])
                first = dot(jnp.concatenate([vh, vm, vl], 0), eh_ref[here, :], NN)
                second = dot(jnp.concatenate([vh, vm], 0), el_ref[here, :], NN)
                out_ref[...] += (first[:k] + second[:k]) + (first[k : 2 * k] + second[k:] + first[2 * k :])


def factor_inverse(gram):
    k = gram.shape[0]
    rows = lax.broadcasted_iota(jnp.int32, (k, k), 0)
    cols = lax.broadcasted_iota(jnp.int32, (k, k), 1)
    eye = (rows == cols).astype(f32)
    aug = jnp.concatenate([gram, eye], 1)
    row_ids = lax.broadcasted_iota(jnp.int32, (k, 2 * k), 0)
    for i in range(k):
        pivot = aug[i : i + 1, :]
        scale = lax.rsqrt(aug[i : i + 1, i : i + 1])
        row = pivot * scale
        col = aug[:, i : i + 1] * scale
        new = aug - col * row
        aug = jnp.where(row_ids < i, aug, jnp.where(row_ids == i, row, new))
    return aug[:, k:]


def factor_kernel(ga_ref, gb_ref, inv_ref):
    inv_ref[...] = factor_inverse(ga_ref[...] + gb_ref[...])


def exact(a, b):
    return lax.dot_general(a, b, NN, precision=lax.Precision.HIGHEST, preferred_element_type=f32)


def image_kernel(members, total, inv_ref, *refs):
    pieces, image_ref, gram_ref = refs[:members], refs[members], refs[members + 1]
    gather_into(image_ref, pieces, members)
    image_ref[...] = exact(inv_ref[...], image_ref[...])
    gram_ref[...] = gram_sum(*split3(image_ref[...])) / total


def last_kernel(ga_ref, gb_ref, image_ref, out_ref):
    inv = factor_inverse(ga_ref[...] + gb_ref[...])
    out_ref[...] = exact(inv, image_ref[...])


VM = pl.BlockSpec(memory_space=pltpu.VMEM)
SM = pl.BlockSpec(memory_space=pltpu.SMEM)


def call(body, specs, outs, name, limit=40, flops=10**9):
    return pl.pallas_call(
        body,
        in_specs=specs,
        out_specs=[VM] * len(outs),
        out_shape=[jax.ShapeDtypeStruct(s, t) for s, t in outs],
        compiler_params=pltpu.CompilerParams(vmem_limit_bytes=limit * MB),
        cost_estimate=pl.CostEstimate(flops=flops, bytes_accessed=MB, transcendentals=0),
        name=name,
    )


def shifted(x, axis, by):
    n = lax.axis_size(axis)
    return lax.ppermute(x, axis, [(i, i + by) for i in range(n) if 0 <= i + by < n])


def swapped(x, axis, mask):
    n = lax.axis_size(axis)
    return lax.ppermute(x, axis, [(i, i ^ mask) for i in range(n)])


def rotated(x, axis, by):
    n = lax.axis_size(axis)
    return lax.ppermute(x, axis, [(i, (i + by) % n) for i in range(n)])


MASKS = (1, 2, 6, 8, 16, 48)


def pair_sums(gram):
    for mask in MASKS[:-1]:
        gram = gram + swapped(gram, "rows", mask)
    return gram, swapped(gram, "rows", MASKS[-1])


def on_device(embeddings, start_vectors, pairs):
    members = lax.axis_size("sub")
    rows, width = embeddings.shape
    k = start_vectors.shape[1]
    quarter = rows // members
    total = rows * lax.axis_size("rows")
    vt = start_vectors.T
    prev_e = shifted(embeddings, "rows", 1)
    next_e = shifted(embeddings, "rows", -1)
    prev_v = shifted(vt, "rows", 1)
    next_v = shifted(vt, "rows", -1)
    prev_pairs = shifted(pairs, "rows", 1)
    part = ((k, quarter), f32)
    tiles = [((rows, quarter), bf16)] * 2
    xah, xal, na, acc, eho, elo = call(
        functools.partial(own_kernel, members), [VM, VM, SM],
        [((quarter, width), bf16)] * 2 + [((8, quarter), f32), part] + tiles, "own_tiles",
        flops=5 * 10**9)(embeddings, vt, pairs)
    other = lambda offset, name: call(
        functools.partial(other_kernel, members, offset), [VM, VM, SM, VM, VM, VM, VM],
        [part] + tiles, name, flops=5 * 10**9)
    acc, ehp, elp = other(-1, "prev_tiles")(prev_e, prev_v, prev_pairs, xah, xal, na, acc)
    acc, ehn, eln = other(1, "next_tiles")(next_e, next_v, pairs, xah, xal, na, acc)
    pieces = [acc] + [rotated(acc, "sub", s) for s in range(1, members)]
    whole = ((k, rows), f32)
    small = ((k, k), f32)
    image, gram = call(functools.partial(join_kernel, members, total), [VM] * members, [whole, small], "join")(*pieces)
    prev_i = shifted(image, "rows", 1)
    next_i = shifted(image, "rows", -1)
    ga, gb = pair_sums(gram)
    (acc2,) = call(
        functools.partial(second_kernel, members), [VM] * 9 + [SM, SM], [part], "second_product")(
        image, prev_i, next_i, eho, elo, ehp, elp, ehn, eln, pairs, prev_pairs)
    pieces = [acc2] + [rotated(acc2, "sub", s) for s in range(1, members)]
    (inv,) = call(factor_kernel, [VM, VM], [small], "factor")(ga, gb)
    image, gram = call(functools.partial(image_kernel, members, total), [VM] * (1 + members), [whole, small], "image")(inv, *pieces)
    ga, gb = pair_sums(gram)
    (out,) = call(last_kernel, [VM, VM, VM], [whole], "last")(ga, gb, image)
    return out.T


def solution(mesh):
    return jax.shard_map(
        on_device,
        mesh=mesh,
        in_specs=(P("rows", None), P("rows", None), P("rows", None)),
        out_specs=P("rows", None),
        check_vma=False,
    )
```

time: 471 us -> 136 us (0.29); the launches traced: 466 us -> 137 us
  blocking collectives: 168 us -> 0 us
  waiting for transfers between devices: 142 us -> 31.6 us
  matrix products: 69.3 us -> 0 us
  starting transfers between devices: 6.66 us -> 70 us
  Pallas kernels: 0 us -> 30 us
  other arithmetic: 29.4 us -> 0.05 us
  local copies, waits for them, and re-layouts: 23.6 us -> 5.21 us
  between operations: 13.6 us -> 0.2 us
  loops' own time: 13.2 us -> 0 us
    psum x2 -> x0, blocking collectives: 168 us -> none  [on_device(): gram = lax.psum(gram_part, ('rows', 'sub'))]
    psum x2 -> x0, waiting for transfers between devices: 136 us -> none  [on_device(): own_sum, spill_sum = lax.psum((own_part, spill_part), 'sub')]
    dot_general x14 -> x0, matrix products: 67.2 us -> none  [the longest x4 24.1 us: work(): lax.dot_general(affinity, va, (((0,), (0,)), ((), ())), precision=highest...]
    ppermute x5 -> x25, starting transfers between devices: 6.62 us -> 70 us  [the longest x12 31.8 us: swapped(): return lax.ppermute(x, axis, [(i, i ^ mask) for i in range(n)])]
    pallas_call x0 -> x8, Pallas kernels: none -> 30 us  [the longest x1 6.82 us: on_device(): out, = call(last_kernel, [VM, VM, VM], [whole], 'last')(ga, gb, image)]
    ppermute x5 -> x25, waiting for transfers between devices: 5.9 us -> 31.6 us  [the longest x12 26.6 us: swapped(): return lax.ppermute(x, axis, [(i, i ^ mask) for i in range(n)])]
    another operation x10 -> x0, other arithmetic: 24.1 us -> none  [the longest x6 13 us: on_device(): lower = jnp.linalg.cholesky(gram)]
    another operation x6 -> x0, loops' own time: 13.2 us -> none  [the longest x4 10.6 us: visit(): return lax.cond(row_block >= 0, work, lambda inner: inner, acc)]
  transfers between devices with their start and end apart: 7 -> 25, of which waited for: 5 -> 14; matrix products, arithmetic and copies ran while one was open for 1% -> 1% of each run, Pallas kernels for 0% -> 12%
where the time goes in v1:
time: 136 us; the launch traced here: 137 us
  starting transfers between devices  70 us (51%)
  waiting for transfers between devices  31.6 us (23%)
  Pallas kernels  30 us (22%)
  local copies, waits for them, and re-layouts  5.21 us (4%)
    ppermute x12, starting transfers between devices, swapped(): return lax.ppermute(x, axis, [(i, i ^ mask) for i in range(n)])  31.8 us
    ppermute x7, starting transfers between devices, shifted(): lax.ppermute(x, axis, [(i, i + by) for i in range(n) if 0 <= i + by < n])  28.9 us
    ppermute x12, waiting for transfers between devices, swapped(): return lax.ppermute(x, axis, [(i, i ^ mask) for i in range(n)])  26.6 us
    ppermute x6, starting transfers between devices, rotated(): return lax.ppermute(x, axis, [(i, (i + by) % n) for i in range(n)])  9.25 us
    pallas_call x1, Pallas kernels, on_device(): out, = call(last_kernel, [VM, VM, VM], [whole], 'last')(ga, gb, image)  6.82 us
    pallas_call x1, Pallas kernels, on_device(): call(functools.partial(own_kernel, members), [VM, VM, SM], [((quarter, wi...  5.83 us
    pallas_call x1, Pallas kernels, on_device(): other(1, 'next_tiles')(next_e, next_v, pairs, xah, xal, na, acc)  5.69 us
    pallas_call x1, Pallas kernels, on_device(): inv, = call(factor_kernel, [VM, VM], [small], 'factor')(ga, gb)  5.48 us
  transfers between devices with their start and end apart: 25, of which 14 were waited for; matrix products, arithmetic and copies ran while one was open for 1% of the time, Pallas kernels for 12%

profile of v1, /device:TPU:16, one launch (start us, length us, event | category | flops | bytes accessed | tf_op | source)
XLA Modules:
  0.0 137.0 jit_solution(7622734113086873867)
XLA Ops:
  0.0 3.1 %collective-permute-start.2 = (f32[2048,256]{1,0:T(8,128)}, f32[2048,256]{1,0:T(8,128)}, u32[]{:S(2)}, u32[]{:S(2)}) collective-permute-start(f32[2048,256]{1,0:T(8,128)} %x_ref.1), channel_id=1, source_target_pairs={{0,4},{4,8},{8,12},{12,16},{16,20},{20,24},{24,28},{28,32},{32,36}... | collective-permute-start | bytes 6291464 | tf_op jit(solution)/shard_map/ppermute | solution.py:201
  3.1 1.3 collective-permute-start
  4.4 3.1 %collective-permute-start.3 = (f32[64,2048]{1,0:T(8,128)}, f32[64,2048]{1,0:T(8,128)S(1)}, u32[]{:S(2)}, u32[]{:S(2)}) collective-permute-start(f32[64,2048]{1,0:T(8,128)} %bitcast.2), channel_id=1, source_target_pairs={{0,4},{4,8},{8,12},{12,16},{16,20},{20,24},{24,28},{28,32},{32,36}... | collective-permute-start | bytes 1572872 | tf_op jit(solution)/shard_map/ppermute | solution.py:201
  7.5 1.3 collective-permute-start.1
  8.8 0.8 copy.6.pairs_ref
  9.5 4.2 %collective-permute-start.4 = (s32[8,2]{1,0:T(8,128)S(1)}, s32[8,2]{1,0:T(8,128)S(1)}, u32[]{:S(2)}, u32[]{:S(2)}) collective-permute-start(s32[8,2]{1,0:T(8,128)S(1)} %copy.6.pairs_ref), channel_id=1, source_target_pairs={{0,4},{4,8},{8,12},{12,16},{16,20},{20,24},{24,28},{28,32},{32,36}... | collective-permute-start | bytes 200 | tf_op jit(solution)/shard_map/ppermute | solution.py:201
  13.7 1.6 %copy-done = f32[2048,256]{1,0:T(8,128)S(1)} copy-done((f32[2048,256]{1,0:T(8,128)S(1)}, f32[2048,256]{1,0:T(8,128)}, u32[]{:S(2)}) %copy-start) | copy-done | bytes 2097176
  15.3 1.0 copy-done.1
  16.3 5.8 %own_tiles.1 = (bf16[512,256]{1,0:T(8,128)(2,1)S(1)}, bf16[512,256]{1,0:T(8,128)(2,1)S(1)}, f32[8,512]{1,0:T(8,128)S(1)}, f32[64,512]{1,0:T(8,128)S(1)}, bf16[20...) custom-call(f32[2048,256]{1,0:T(8,128)S(1)} %copy-done, f32[64,2048]{1,0:T(8,128)S(1)} %bitcast.4, ...), custom_call_target="tpu_custom_call" | custom-call | flops 5000000000 | bytes 1048576 | tf_op jit(solution)/shard_map/own_tiles/pallas_call | solution.py:237
  22.2 0.8 copy-done.2
  23.0 1.0 copy-done.3
  24.0 1.7 %prev_tiles.1 = (f32[64,512]{1,0:T(8,128)S(1)}, bf16[2048,512]{1,0:T(8,128)(2,1)S(1)}, bf16[2048,512]{1,0:T(8,128)(2,1)S(1)}) custom-call(f32[2048,256]{1,0:T(8,128)} %collective-permute-done.2.x_ref, f32[64,2048]{1,0:T(8,128)S(1)} %copy-done.3, s32[8,2]{1,0:T(8,128)S(1)} %collective-permute-done.4.pairs_ref.prev_pairs_ref, ...), custom_call_target="tpu_custom_call" | custom-call | flops 5000000000 | bytes 1048576 | tf_op jit(solution)/shard_map/prev_tiles/pallas_call | solution.py:244
  25.7 5.7 %next_tiles.1 = (f32[64,512]{1,0:T(8,128)S(1)}, bf16[2048,512]{1,0:T(8,128)(2,1)S(1)}, bf16[2048,512]{1,0:T(8,128)(2,1)S(1)}) custom-call(f32[2048,256]{1,0:T(8,128)S(1)} %collective-permute-done.x_ref, f32[64,2048]{1,0:T(8,128)} %collective-permute-done.1.v_ref, s32[8,2]{1,0:T(8,128)S(1)} %copy.6.pairs_ref, bf16[512,256]{1,0:T(8,128)(2,1)S(1)} %get-tuple-element.21.xah_ref, ...), custom_call_target="tpu_custom_call" | custom-call | flops 5000000000 | bytes 1048576 | tf_op jit(solution)/shard_map/next_tiles/pallas_call | solution.py:245
  31.4 0.5 collective-permute-start.7
  31.9 2.9 %collective-permute-start.6 = (f32[64,512]{1,0:T(8,128)S(1)}, f32[64,512]{1,0:T(8,128)S(1)}, u32[]{:S(2)}, u32[]{:S(2)}) collective-permute-start(f32[64,512]{1,0:T(8,128)S(1)} %get-tuple-element.26.refs_0_), channel_id=1, source_target_pairs={{0,2},{1,3},{2,0},{3,1},{4,6},{5,7},{6,4},{7,5},{8,10},{9,11},{10,... | collective-permute-start | bytes 393224 | tf_op jit(solution)/shard_map/ppermute | solution.py:211
  34.8 1.6 %collective-permute-done.7.refs_3_ = f32[64,512]{1,0:T(8,128)S(1)} collective-permute-done((f32[64,512]{1,0:T(8,128)S(1)}, f32[64,512]{1,0:T(8,128)S(1)}, u32[]{:S(2)}, u32[]{:S(2)}) %collective-permute-start.7) | collective-permute-done | bytes 131104 | tf_op jit(solution)/shard_map/ppermute | solution.py:211
  36.5 2.0 %collective-permute-done.6.refs_2_ = f32[64,512]{1,0:T(8,128)S(1)} collective-permute-done((f32[64,512]{1,0:T(8,128)S(1)}, f32[64,512]{1,0:T(8,128)S(1)}, u32[]{:S(2)}, u32[]{:S(2)}) %collective-permute-start.6) | collective-permute-done | bytes 131104 | tf_op jit(solution)/shard_map/ppermute | solution.py:211
  38.4 1.4 %collective-permute-done.5.refs_1_ = f32[64,512]{1,0:T(8,128)S(1)} collective-permute-done((f32[64,512]{1,0:T(8,128)S(1)}, f32[64,512]{1,0:T(8,128)S(1)}, u32[]{:S(2)}, u32[]{:S(2)}) %collective-permute-start.5) | collective-permute-done | bytes 131104 | tf_op jit(solution)/shard_map/ppermute | solution.py:211
  39.8 0.6 join.1
  40.4 1.3 collective-permute-start.15
  41.7 14.8 %collective-permute-start.14 = (f32[64,2048]{1,0:T(8,128)S(1)}, f32[64,2048]{1,0:T(8,128)S(1)}, u32[]{:S(2)}, u32[]{:S(2)}) collective-permute-start(f32[64,2048]{1,0:T(8,128)S(1)} %get-tuple-element.28.vo_ref), channel_id=1, source_target_pairs={{0,4},{4,8},{8,12},{12,16},{16,20},{20,24},{24,28},{28,32},{32,36}... | collective-permute-start | bytes 1572872 | tf_op jit(solution)/shard_map/ppermute | solution.py:201
  56.5 1.8 %collective-permute-start.8 = (f32[64,64]{1,0:T(8,128)S(1)}, f32[64,64]{1,0:T(8,128)S(1)}, u32[]{:S(2)}, u32[]{:S(2)}) collective-permute-start(f32[64,64]{1,0:T(8,128)S(1)} %get-tuple-element.27), channel_id=1, source_target_pairs={{0,4},{4,0},{8,12},{12,8},{16,20},{20,16},{24,28},{28,24},{32,36},... | collective-permute-start | bytes 49160 | tf_op jit(solution)/shard_map/ppermute | solution.py:206
  58.3 0.9 collective-permute-done.8
  59.1 0.5 collective-permute-start.9
  59.7 4.3 %collective-permute-done.9 = f32[64,64]{1,0:T(8,128)S(1)} collective-permute-done((f32[64,64]{1,0:T(8,128)S(1)}, f32[64,64]{1,0:T(8,128)S(1)}, u32[]{:S(2)}, u32[]{:S(2)}) %collective-permute-start.9) | collective-permute-done | bytes 16416 | tf_op jit(solution)/shard_map/ppermute | solution.py:206
  64.0 7.3 %collective-permute-start.10 = (f32[64,64]{1,0:T(8,128)S(1)}, f32[64,64]{1,0:T(8,128)S(1)}, u32[]{:S(2)}, u32[]{:S(2)}) collective-permute-start(f32[64,64]{1,0:T(8,128)S(1)} %add.31), channel_id=1, source_target_pairs={{0,24},{4,28},{8,16},{12,20},{16,8},{20,12},{24,0},{28,4},{32,56},... | collective-permute-start | bytes 49160 | tf_op jit(solution)/shard_map/ppermute | solution.py:206
  71.2 1.9 %collective-permute-done.10 = f32[64,64]{1,0:T(8,128)S(1)} collective-permute-done((f32[64,64]{1,0:T(8,128)S(1)}, f32[64,64]{1,0:T(8,128)S(1)}, u32[]{:S(2)}, u32[]{:S(2)}) %collective-permute-start.10) | collective-permute-done | bytes 16416 | tf_op jit(solution)/shard_map/ppermute | solution.py:206
  73.1 1.5 %collective-permute-start.11 = (f32[64,64]{1,0:T(8,128)S(1)}, f32[64,64]{1,0:T(8,128)S(1)}, u32[]{:S(2)}, u32[]{:S(2)}) collective-permute-start(f32[64,64]{1,0:T(8,128)S(1)} %add.32), channel_id=1, source_target_pairs={{0,32},{4,36},{8,40},{12,44},{16,48},{20,52},{24,56},{28,60},{32,0... | collective-permute-start | bytes 49160 | tf_op jit(solution)/shard_map/ppermute | solution.py:206
  74.6 2.9 %second_product.1.refs_0_ = f32[64,512]{1,0:T(8,128)S(1)} custom-call(f32[64,2048]{1,0:T(8,128)S(1)} %get-tuple-element.28.vo_ref, f32[64,2048]{1,0:T(8,128)S(1)} %collective-permute-done.14.vp_ref, f32[64,2048]{1,0:T(8,128)S(1)} %collective-permute-done.15.vn_ref, bf16[2048,512]{1,0:T(8,128)(2,1)S(1)} %get-tuple-element.29.eho, ...), custom_call_target="tpu_custom_call" | custom-call | flops 1000000000 | bytes 1048576 | tf_op jit(solution)/shard_map/second_product/pallas_call | solution.py:253
  77.5 0.6 collective-permute-start.18
  78.1 2.9 %collective-permute-start.17 = (f32[64,512]{1,0:T(8,128)S(1)}, f32[64,512]{1,0:T(8,128)S(1)}, u32[]{:S(2)}, u32[]{:S(2)}) collective-permute-start(f32[64,512]{1,0:T(8,128)S(1)} %second_product.1.refs_0_), channel_id=1, source_target_pairs={{0,2},{1,3},{2,0},{3,1},{4,6},{5,7},{6,4},{7,5},{8,10},{9,11},{10,... | collective-permute-start | bytes 393224 | tf_op jit(solution)/shard_map/ppermute | solution.py:211
  81.0 2.3 %collective-permute-start.16 = (f32[64,512]{1,0:T(8,128)S(1)}, f32[64,512]{1,0:T(8,128)S(1)}, u32[]{:S(2)}, u32[]{:S(2)}) collective-permute-start(f32[64,512]{1,0:T(8,128)S(1)} %second_product.1.refs_0_), channel_id=1, source_target_pairs={{0,1},{1,2},{2,3},{3,0},{4,5},{5,6},{6,7},{7,4},{8,9},{9,10},{10,1... | collective-permute-start | bytes 393224 | tf_op jit(solution)/shard_map/ppermute | solution.py:211
  83.3 5.2 %collective-permute-start.12 = (f32[64,64]{1,0:T(8,128)S(1)}, f32[64,64]{1,0:T(8,128)S(1)}, u32[]{:S(2)}, u32[]{:S(2)}) collective-permute-start(f32[64,64]{1,0:T(8,128)S(1)} %add.33), channel_id=1, source_target_pairs={{0,64},{4,68},{8,72},{12,76},{16,80},{20,84},{24,88},{28,92},{32,9... | collective-permute-start | bytes 49160 | tf_op jit(solution)/shard_map/ppermute | solution.py:206
  88.6 1.9 %collective-permute-done.12 = f32[64,64]{1,0:T(8,128)S(1)} collective-permute-done((f32[64,64]{1,0:T(8,128)S(1)}, f32[64,64]{1,0:T(8,128)S(1)}, u32[]{:S(2)}, u32[]{:S(2)}) %collective-permute-start.12) | collective-permute-done | bytes 16416 | tf_op jit(solution)/shard_map/ppermute | solution.py:206
  90.5 5.1 %collective-permute-start.13 = (f32[64,64]{1,0:T(8,128)S(1)}, f32[64,64]{1,0:T(8,128)S(1)}, u32[]{:S(2)}, u32[]{:S(2)}) collective-permute-start(f32[64,64]{1,0:T(8,128)S(1)} %add.34.ga_ref), channel_id=1, source_target_pairs={{0,192},{4,196},{8,200},{12,204},{16,208},{20,212},{24,216},{28,22... | collective-permute-start | bytes 49160 | tf_op jit(solution)/shard_map/ppermute | solution.py:206
  95.5 1.9 %collective-permute-done.13.gb_ref = f32[64,64]{1,0:T(8,128)S(1)} collective-permute-done((f32[64,64]{1,0:T(8,128)S(1)}, f32[64,64]{1,0:T(8,128)S(1)}, u32[]{:S(2)}, u32[]{:S(2)}) %collective-permute-start.13) | collective-permute-done | bytes 16416 | tf_op jit(solution)/shard_map/ppermute | solution.py:206
  97.5 5.5 %factor.1.inv_ref = f32[64,64]{1,0:T(8,128)S(1)} custom-call(f32[64,64]{1,0:T(8,128)S(1)} %add.34.ga_ref, f32[64,64]{1,0:T(8,128)S(1)} %collective-permute-done.13.gb_ref), custom_call_target="tpu_custom_call" | custom-call | flops 1000000000 | bytes 1048576 | tf_op jit(solution)/shard_map/factor/pallas_call | solution.py:257
  103.0 1.0 image.1
  104.1 1.2 collective-permute-done.19
  105.3 3.9 %collective-permute-done.20 = f32[64,64]{1,0:T(8,128)S(1)} collective-permute-done((f32[64,64]{1,0:T(8,128)S(1)}, f32[64,64]{1,0:T(8,128)S(1)}, u32[]{:S(2)}, u32[]{:S(2)}) %collective-permute-start.20) | collective-permute-done | bytes 16416 | tf_op jit(solution)/shard_map/ppermute | solution.py:206
  109.2 4.3 %collective-permute-start.21 = (f32[64,64]{1,0:T(8,128)S(1)}, f32[64,64]{1,0:T(8,128)S(1)}, u32[]{:S(2)}, u32[]{:S(2)}) collective-permute-start(f32[64,64]{1,0:T(8,128)S(1)} %add.36), channel_id=1, source_target_pairs={{0,24},{4,28},{8,16},{12,20},{16,8},{20,12},{24,0},{28,4},{32,56},... | collective-permute-start | bytes 49160 | tf_op jit(solution)/shard_map/ppermute | solution.py:206
  113.5 1.9 %collective-permute-done.21 = f32[64,64]{1,0:T(8,128)S(1)} collective-permute-done((f32[64,64]{1,0:T(8,128)S(1)}, f32[64,64]{1,0:T(8,128)S(1)}, u32[]{:S(2)}, u32[]{:S(2)}) %collective-permute-start.21) | collective-permute-done | bytes 16416 | tf_op jit(solution)/shard_map/ppermute | solution.py:206
  115.5 3.9 %collective-permute-done.22 = f32[64,64]{1,0:T(8,128)S(1)} collective-permute-done((f32[64,64]{1,0:T(8,128)S(1)}, f32[64,64]{1,0:T(8,128)S(1)}, u32[]{:S(2)}, u32[]{:S(2)}) %collective-permute-start.22) | collective-permute-done | bytes 16416 | tf_op jit(solution)/shard_map/ppermute | solution.py:206
  119.3 2.9 %collective-permute-start.23 = (f32[64,64]{1,0:T(8,128)S(1)}, f32[64,64]{1,0:T(8,128)S(1)}, u32[]{:S(2)}, u32[]{:S(2)}) collective-permute-start(f32[64,64]{1,0:T(8,128)S(1)} %add.38), channel_id=1, source_target_pairs={{0,64},{4,68},{8,72},{12,76},{16,80},{20,84},{24,88},{28,92},{32,9... | collective-permute-start | bytes 49160 | tf_op jit(solution)/shard_map/ppermute | solution.py:206
  122.3 1.9 %collective-permute-done.23 = f32[64,64]{1,0:T(8,128)S(1)} collective-permute-done((f32[64,64]{1,0:T(8,128)S(1)}, f32[64,64]{1,0:T(8,128)S(1)}, u32[]{:S(2)}, u32[]{:S(2)}) %collective-permute-start.23) | collective-permute-done | bytes 16416 | tf_op jit(solution)/shard_map/ppermute | solution.py:206
  124.2 3.0 %collective-permute-start.24 = (f32[64,64]{1,0:T(8,128)S(1)}, f32[64,64]{1,0:T(8,128)S(1)}, u32[]{:S(2)}, u32[]{:S(2)}) collective-permute-start(f32[64,64]{1,0:T(8,128)S(1)} %add.39.ga_ref), channel_id=1, source_target_pairs={{0,192},{4,196},{8,200},{12,204},{16,208},{20,212},{24,216},{28,22... | collective-permute-start | bytes 49160 | tf_op jit(solution)/shard_map/ppermute | solution.py:206
  127.2 3.0 %collective-permute-done.24.gb_ref = f32[64,64]{1,0:T(8,128)S(1)} collective-permute-done((f32[64,64]{1,0:T(8,128)S(1)}, f32[64,64]{1,0:T(8,128)S(1)}, u32[]{:S(2)}, u32[]{:S(2)}) %collective-permute-start.24) | collective-permute-done | bytes 16416 | tf_op jit(solution)/shard_map/ppermute | solution.py:206
  130.2 6.8 %last.1 = f32[64,2048]{1,0:T(8,128)} custom-call(f32[64,64]{1,0:T(8,128)S(1)} %add.39.ga_ref, f32[64,64]{1,0:T(8,128)S(1)} %collective-permute-done.24.gb_ref, f32[64,2048]{1,0:T(8,128)S(1)} %get-tuple-element.36.image_ref), custom_call_target="tpu_custom_call" | custom-call | flops 1000000000 | bytes 1048576 | tf_op jit(solution)/shard_map/last/pallas_call | solution.py:260
  (29 shorter events, 0.2 us)
Async XLA Ops:
  0.0 23.0 %collective-permute-start.2 = (f32[2048,256]{1,0:T(8,128)}, f32[2048,256]{1,0:T(8,128)}, u32[]{:S(2)}, u32[]{:S(2)}) collective-permute-start(f32[2048,256]{1,0:T(8,128)} %x_ref.1), channel_id=1, source_target_pairs={{0,4},{4,8},{8,12},{12,16},{16,20},{20,24},{24,28},{28,32},{32,36}... | collective-permute-start | bytes 6291464 | tf_op jit(solution)/shard_map/ppermute | solution.py:201
  3.1 22.6 %collective-permute-start = (f32[2048,256]{1,0:T(8,128)}, f32[2048,256]{1,0:T(8,128)S(1)}, u32[]{:S(2)}, u32[]{:S(2)}) collective-permute-start(f32[2048,256]{1,0:T(8,128)} %x_ref.1), channel_id=1, source_target_pairs={{4,0},{8,4},{12,8},{16,12},{20,16},{24,20},{28,24},{32,28},{36,32}... | collective-permute-start | bytes 6291464 | tf_op jit(solution)/shard_map/ppermute | solution.py:201
  4.4 17.8 %collective-permute-start.3 = (f32[64,2048]{1,0:T(8,128)}, f32[64,2048]{1,0:T(8,128)S(1)}, u32[]{:S(2)}, u32[]{:S(2)}) collective-permute-start(f32[64,2048]{1,0:T(8,128)} %bitcast.2), channel_id=1, source_target_pairs={{0,4},{4,8},{8,12},{12,16},{16,20},{20,24},{24,28},{28,32},{32,36}... | collective-permute-start | bytes 1572872 | tf_op jit(solution)/shard_map/ppermute | solution.py:201
  7.5 18.2 %collective-permute-start.1 = (f32[64,2048]{1,0:T(8,128)}, f32[64,2048]{1,0:T(8,128)}, u32[]{:S(2)}, u32[]{:S(2)}) collective-permute-start(f32[64,2048]{1,0:T(8,128)} %bitcast.3), channel_id=1, source_target_pairs={{4,0},{8,4},{12,8},{16,12},{20,16},{24,20},{28,24},{32,28},{36,32}... | collective-permute-start | bytes 1572872 | tf_op jit(solution)/shard_map/ppermute | solution.py:201
  9.5 12.6 %collective-permute-start.4 = (s32[8,2]{1,0:T(8,128)S(1)}, s32[8,2]{1,0:T(8,128)S(1)}, u32[]{:S(2)}, u32[]{:S(2)}) collective-permute-start(s32[8,2]{1,0:T(8,128)S(1)} %copy.6.pairs_ref), channel_id=1, source_target_pairs={{0,4},{4,8},{8,12},{12,16},{16,20},{20,24},{24,28},{28,32},{32,36}... | collective-permute-start | bytes 200 | tf_op jit(solution)/shard_map/ppermute | solution.py:201
  13.7 1.6 %copy-start = (f32[2048,256]{1,0:T(8,128)S(1)}, f32[2048,256]{1,0:T(8,128)}, u32[]{:S(2)}) copy-start(f32[2048,256]{1,0:T(8,128)} %x_ref.1) | copy-start | bytes 6291460
  15.3 1.0 copy-start.1
  22.2 0.8 copy-start.2
  23.0 1.0 copy-start.3
  31.4 5.0 %collective-permute-start.7 = (f32[64,512]{1,0:T(8,128)S(1)}, f32[64,512]{1,0:T(8,128)S(1)}, u32[]{:S(2)}, u32[]{:S(2)}) collective-permute-start(f32[64,512]{1,0:T(8,128)S(1)} %get-tuple-element.26.refs_0_), channel_id=1, source_target_pairs={{0,3},{1,0},{2,1},{3,2},{4,7},{5,4},{6,5},{7,6},{8,11},{9,8},{10,9... | collective-permute-start | bytes 393224 | tf_op jit(solution)/shard_map/ppermute | solution.py:211
  31.9 6.5 %collective-permute-start.6 = (f32[64,512]{1,0:T(8,128)S(1)}, f32[64,512]{1,0:T(8,128)S(1)}, u32[]{:S(2)}, u32[]{:S(2)}) collective-permute-start(f32[64,512]{1,0:T(8,128)S(1)} %get-tuple-element.26.refs_0_), channel_id=1, source_target_pairs={{0,2},{1,3},{2,0},{3,1},{4,6},{5,7},{6,4},{7,5},{8,10},{9,11},{10,... | collective-permute-start | bytes 393224 | tf_op jit(solution)/shard_map/ppermute | solution.py:211
  34.8 5.0 %collective-permute-start.5 = (f32[64,512]{1,0:T(8,128)S(1)}, f32[64,512]{1,0:T(8,128)S(1)}, u32[]{:S(2)}, u32[]{:S(2)}) collective-permute-start(f32[64,512]{1,0:T(8,128)S(1)} %get-tuple-element.26.refs_0_), channel_id=1, source_target_pairs={{0,1},{1,2},{2,3},{3,0},{4,5},{5,6},{6,7},{7,4},{8,9},{9,10},{10,1... | collective-permute-start | bytes 393224 | tf_op jit(solution)/shard_map/ppermute | solution.py:211
  40.4 34.2 %collective-permute-start.15 = (f32[64,2048]{1,0:T(8,128)S(1)}, f32[64,2048]{1,0:T(8,128)S(1)}, u32[]{:S(2)}, u32[]{:S(2)}) collective-permute-start(f32[64,2048]{1,0:T(8,128)S(1)} %get-tuple-element.28.vo_ref), channel_id=1, source_target_pairs={{4,0},{8,4},{12,8},{16,12},{20,16},{24,20},{28,24},{32,28},{36,32}... | collective-permute-start | bytes 1572872 | tf_op jit(solution)/shard_map/ppermute | solution.py:201
  41.7 32.9 %collective-permute-start.14 = (f32[64,2048]{1,0:T(8,128)S(1)}, f32[64,2048]{1,0:T(8,128)S(1)}, u32[]{:S(2)}, u32[]{:S(2)}) collective-permute-start(f32[64,2048]{1,0:T(8,128)S(1)} %get-tuple-element.28.vo_ref), channel_id=1, source_target_pairs={{0,4},{4,8},{8,12},{12,16},{16,20},{20,24},{24,28},{28,32},{32,36}... | collective-permute-start | bytes 1572872 | tf_op jit(solution)/shard_map/ppermute | solution.py:201
  56.5 2.7 %collective-permute-start.8 = (f32[64,64]{1,0:T(8,128)S(1)}, f32[64,64]{1,0:T(8,128)S(1)}, u32[]{:S(2)}, u32[]{:S(2)}) collective-permute-start(f32[64,64]{1,0:T(8,128)S(1)} %get-tuple-element.27), channel_id=1, source_target_pairs={{0,4},{4,0},{8,12},{12,8},{16,20},{20,16},{24,28},{28,24},{32,36},... | collective-permute-start | bytes 49160 | tf_op jit(solution)/shard_map/ppermute | solution.py:206
  59.1 4.8 %collective-permute-start.9 = (f32[64,64]{1,0:T(8,128)S(1)}, f32[64,64]{1,0:T(8,128)S(1)}, u32[]{:S(2)}, u32[]{:S(2)}) collective-permute-start(f32[64,64]{1,0:T(8,128)S(1)} %add.30), channel_id=1, source_target_pairs={{0,8},{4,12},{8,0},{12,4},{16,24},{20,28},{24,16},{28,20},{32,40},... | collective-permute-start | bytes 49160 | tf_op jit(solution)/shard_map/ppermute | solution.py:206
  64.0 9.1 %collective-permute-start.10 = (f32[64,64]{1,0:T(8,128)S(1)}, f32[64,64]{1,0:T(8,128)S(1)}, u32[]{:S(2)}, u32[]{:S(2)}) collective-permute-start(f32[64,64]{1,0:T(8,128)S(1)} %add.31), channel_id=1, source_target_pairs={{0,24},{4,28},{8,16},{12,20},{16,8},{20,12},{24,0},{28,4},{32,56},... | collective-permute-start | bytes 49160 | tf_op jit(solution)/shard_map/ppermute | solution.py:206
  73.1 10.2 %collective-permute-start.11 = (f32[64,64]{1,0:T(8,128)S(1)}, f32[64,64]{1,0:T(8,128)S(1)}, u32[]{:S(2)}, u32[]{:S(2)}) collective-permute-start(f32[64,64]{1,0:T(8,128)S(1)} %add.32), channel_id=1, source_target_pairs={{0,32},{4,36},{8,40},{12,44},{16,48},{20,52},{24,56},{28,60},{32,0... | collective-permute-start | bytes 49160 | tf_op jit(solution)/shard_map/ppermute | solution.py:206
  77.5 25.4 %collective-permute-start.18 = (f32[64,512]{1,0:T(8,128)S(1)}, f32[64,512]{1,0:T(8,128)S(1)}, u32[]{:S(2)}, u32[]{:S(2)}) collective-permute-start(f32[64,512]{1,0:T(8,128)S(1)} %second_product.1.refs_0_), channel_id=1, source_target_pairs={{0,3},{1,0},{2,1},{3,2},{4,7},{5,4},{6,5},{7,6},{8,11},{9,8},{10,9... | collective-permute-start | bytes 393224 | tf_op jit(solution)/shard_map/ppermute | solution.py:211
  78.1 24.8 %collective-permute-start.17 = (f32[64,512]{1,0:T(8,128)S(1)}, f32[64,512]{1,0:T(8,128)S(1)}, u32[]{:S(2)}, u32[]{:S(2)}) collective-permute-start(f32[64,512]{1,0:T(8,128)S(1)} %second_product.1.refs_0_), channel_id=1, source_target_pairs={{0,2},{1,3},{2,0},{3,1},{4,6},{5,7},{6,4},{7,5},{8,10},{9,11},{10,... | collective-permute-start | bytes 393224 | tf_op jit(solution)/shard_map/ppermute | solution.py:211
  81.0 21.9 %collective-permute-start.16 = (f32[64,512]{1,0:T(8,128)S(1)}, f32[64,512]{1,0:T(8,128)S(1)}, u32[]{:S(2)}, u32[]{:S(2)}) collective-permute-start(f32[64,512]{1,0:T(8,128)S(1)} %second_product.1.refs_0_), channel_id=1, source_target_pairs={{0,1},{1,2},{2,3},{3,0},{4,5},{5,6},{6,7},{7,4},{8,9},{9,10},{10,1... | collective-permute-start | bytes 393224 | tf_op jit(solution)/shard_map/ppermute | solution.py:211
  83.3 7.1 %collective-permute-start.12 = (f32[64,64]{1,0:T(8,128)S(1)}, f32[64,64]{1,0:T(8,128)S(1)}, u32[]{:S(2)}, u32[]{:S(2)}) collective-permute-start(f32[64,64]{1,0:T(8,128)S(1)} %add.33), channel_id=1, source_target_pairs={{0,64},{4,68},{8,72},{12,76},{16,80},{20,84},{24,88},{28,92},{32,9... | collective-permute-start | bytes 49160 | tf_op jit(solution)/shard_map/ppermute | solution.py:206
  90.5 7.0 %collective-permute-start.13 = (f32[64,64]{1,0:T(8,128)S(1)}, f32[64,64]{1,0:T(8,128)S(1)}, u32[]{:S(2)}, u32[]{:S(2)}) collective-permute-start(f32[64,64]{1,0:T(8,128)S(1)} %add.34.ga_ref), channel_id=1, source_target_pairs={{0,192},{4,196},{8,200},{12,204},{16,208},{20,212},{24,216},{28,22... | collective-permute-start | bytes 49160 | tf_op jit(solution)/shard_map/ppermute | solution.py:206
  104.0 1.3 collective-permute-start.19
  105.3 3.9 %collective-permute-start.20 = (f32[64,64]{1,0:T(8,128)S(1)}, f32[64,64]{1,0:T(8,128)S(1)}, u32[]{:S(2)}, u32[]{:S(2)}) collective-permute-start(f32[64,64]{1,0:T(8,128)S(1)} %add.35), channel_id=1, source_target_pairs={{0,8},{4,12},{8,0},{12,4},{16,24},{20,28},{24,16},{28,20},{32,40},... | collective-permute-start | bytes 49160 | tf_op jit(solution)/shard_map/ppermute | solution.py:206
  109.2 6.2 %collective-permute-start.21 = (f32[64,64]{1,0:T(8,128)S(1)}, f32[64,64]{1,0:T(8,128)S(1)}, u32[]{:S(2)}, u32[]{:S(2)}) collective-permute-start(f32[64,64]{1,0:T(8,128)S(1)} %add.36), channel_id=1, source_target_pairs={{0,24},{4,28},{8,16},{12,20},{16,8},{20,12},{24,0},{28,4},{32,56},... | collective-permute-start | bytes 49160 | tf_op jit(solution)/shard_map/ppermute | solution.py:206
  115.4 3.9 %collective-permute-start.22 = (f32[64,64]{1,0:T(8,128)S(1)}, f32[64,64]{1,0:T(8,128)S(1)}, u32[]{:S(2)}, u32[]{:S(2)}) collective-permute-start(f32[64,64]{1,0:T(8,128)S(1)} %add.37), channel_id=1, source_target_pairs={{0,32},{4,36},{8,40},{12,44},{16,48},{20,52},{24,56},{28,60},{32,0... | collective-permute-start | bytes 49160 | tf_op jit(solution)/shard_map/ppermute | solution.py:206
  119.3 4.8 %collective-permute-start.23 = (f32[64,64]{1,0:T(8,128)S(1)}, f32[64,64]{1,0:T(8,128)S(1)}, u32[]{:S(2)}, u32[]{:S(2)}) collective-permute-start(f32[64,64]{1,0:T(8,128)S(1)} %add.38), channel_id=1, source_target_pairs={{0,64},{4,68},{8,72},{12,76},{16,80},{20,84},{24,88},{28,92},{32,9... | collective-permute-start | bytes 49160 | tf_op jit(solution)/shard_map/ppermute | solution.py:206
  124.2 6.0 %collective-permute-start.24 = (f32[64,64]{1,0:T(8,128)S(1)}, f32[64,64]{1,0:T(8,128)S(1)}, u32[]{:S(2)}, u32[]{:S(2)}) collective-permute-start(f32[64,64]{1,0:T(8,128)S(1)} %add.39.ga_ref), channel_id=1, source_target_pairs={{0,192},{4,196},{8,200},{12,204},{16,208},{20,212},{24,216},{28,22... | collective-permute-start | bytes 49160 | tf_op jit(solution)/shard_map/ppermute | solution.py:206

commit v2 on v1

v2 whole, which is shorter than its diff:
```python
import functools
import jax
import jax.numpy as jnp
from jax import lax
from jax.experimental import pallas as pl
from jax.experimental.pallas import tpu as pltpu
from jax.sharding import PartitionSpec as P

BLK_DEV = 2
OWN, SIB, CROSS = 0, 1, -1
MB = 1024 * 1024
LOG2E = 1.4426950408889634
SCALE = LOG2E / 64.0

f32 = jnp.float32
bf16 = jnp.bfloat16
NN = (((1,), (0,)), ((), ()))
NT = (((1,), (1,)), ((), ()))


def dot(a, b, dims):
    return lax.dot_general(a, b, dims, preferred_element_type=f32)


def split2(x):
    hi = x.astype(bf16)
    return hi, (x - hi.astype(f32)).astype(bf16)


def split3(x):
    hi = x.astype(bf16)
    rest = x - hi.astype(f32)
    mid = rest.astype(bf16)
    return hi, mid, (rest - mid.astype(f32)).astype(bf16)


def listed(pairs_ref, row_block, col_block):
    hit = jnp.int32(0)
    for slot in range(pairs_ref.shape[0]):
        same = (pairs_ref[slot, 0] == row_block) & (pairs_ref[slot, 1] == col_block)
        hit = hit | same.astype(jnp.int32)
    return hit > 0


def place():
    group = lax.axis_index("rows")
    member = lax.axis_index("sub")
    return group, member


def want(lists, group, member, members, side, j):
    mine = group * BLK_DEV + (member * BLK_DEV) // members
    other = (group + side * (1 - 2 * (group % 2))) * BLK_DEV + j
    low, high = jnp.minimum(mine, other), jnp.maximum(mine, other)
    hit = listed(lists[0], low, high)
    for pairs_ref in lists[1:]:
        hit = hit | listed(pairs_ref, low, high)
    return hit


def add_tiles(x_ref, xah, xal, na, v_ref, acc_ref, eh_ref, el_ref, start, first, rows, chunk):
    for c in range(rows // chunk):
        here = pl.ds(start + c * chunk, chunk)
        x = x_ref[here, :]
        nb = jnp.sum(x * x, axis=1, keepdims=True) * SCALE
        xh, xl = split2(x)
        d = dot(xh, xah, NT) + (dot(xh, xal, NT) + dot(xl, xah, NT))
        e = jnp.exp2(jnp.minimum(d - nb - na, 0.0))
        eh, el = split2(e)
        eh_ref[here, :] = eh
        el_ref[here, :] = el
        vh, vm, vl = split3(v_ref[:, pl.ds(first + start + c * chunk, chunk)])
        k = vh.shape[0]
        one = dot(jnp.concatenate([vh, vm, vl], 0), eh, NN)
        two = dot(jnp.concatenate([vh, vm], 0), el, NN)
        acc_ref[...] += (one[:k] + two[:k]) + (one[k : 2 * k] + two[k:] + one[2 * k :])


def own_kernel(members, x_ref, v_ref, pairs_ref, xah_ref, xal_ref, na_ref, acc_ref, eh_ref, el_ref):
    group, member = place()
    rows = x_ref.shape[0]
    quarter = rows // members
    block = rows // BLK_DEV
    xa = x_ref[pl.ds(pl.multiple_of(member * quarter, quarter), quarter), :]
    ones = jnp.ones((8, xa.shape[1]), f32)
    na_ref[...] = lax.dot_general(ones, xa * xa, NT, precision=lax.Precision.HIGHEST, preferred_element_type=f32) * SCALE
    xah, xal = split2(xa * (2.0 * SCALE))
    xah_ref[...] = xah
    xal_ref[...] = xal
    acc_ref[...] = jnp.zeros_like(acc_ref)
    for j in range(BLK_DEV):
        @pl.when(want((pairs_ref,), group, member, members, OWN, j))
        def _():
            add_tiles(x_ref, xah_ref[...], xal_ref[...], na_ref[0:1, :], v_ref, acc_ref, eh_ref, el_ref, j * block, 0, block, 256)


def other_kernel(members, side, first, x_ref, v_ref, pairs_ref, prev_pairs_ref, xah_ref, xal_ref, na_ref, in_ref, acc_ref, eh_ref, el_ref):
    group, member = place()
    rows = x_ref.shape[0]
    block = v_ref.shape[1] // BLK_DEV
    acc_ref[...] = in_ref[...]
    step = min(rows, block)
    for start in range(0, rows, step):
        @pl.when(want((pairs_ref, prev_pairs_ref), group, member, members, side, (first + start) // block))
        def _():
            add_tiles(x_ref, xah_ref[...], xal_ref[...], na_ref[0:1, :], v_ref, acc_ref, eh_ref, el_ref, start, first, step, 256)


def gram_sum(vh, vm, vl):
    s = jnp.concatenate([vh, vm, vl], 0)
    k = vh.shape[0]
    p = dot(s, s, NT)
    r = p[:k] + (p[k : 2 * k] + p[2 * k :])
    return r[:, :k] + (r[:, k : 2 * k] + r[:, 2 * k :])


def gather_into(full_ref, pieces, members):
    _, member = place()
    quarter = pieces[0].shape[1]
    for k, piece in enumerate(pieces):
        q = lax.rem(member - k + members, members)
        full_ref[:, pl.ds(pl.multiple_of(q * quarter, quarter), quarter)] = piece[...]


def join_kernel(members, total, *refs):
    pieces, full_ref, gram_ref = refs[:members], refs[members], refs[members + 1]
    gather_into(full_ref, pieces, members)
    gram_ref[...] = gram_sum(*split3(full_ref[...])) / total


def second_kernel(members, sources, pairs_ref, prev_pairs_ref, *refs):
    group, member = place()
    vectors, kept, out_ref = refs[:3], refs[3:-1], refs[-1]
    k, rows = vectors[0].shape
    block = rows // BLK_DEV
    out_ref[...] = jnp.zeros_like(out_ref)
    for n, (which, first, count) in enumerate(sources):
        eh_ref, el_ref = kept[2 * n : 2 * n + 2]
        step = min(count, block)
        for start in range(0, count, step):
            @pl.when(want((pairs_ref, prev_pairs_ref), group, member, members, (OWN, SIB, CROSS)[which], (first + start) // block))
            def _():
                here = pl.ds(start, step)
                vh, vm, vl = split3(vectors[which][:, pl.ds(first + start, step)])
                one = dot(jnp.concatenate([vh, vm, vl], 0), eh_ref[here, :], NN)
                two = dot(jnp.concatenate([vh, vm], 0), el_ref[here, :], NN)
                out_ref[...] += (one[:k] + two[:k]) + (one[k : 2 * k] + two[k:] + one[2 * k :])


def factor_inverse(gram, w=8):
    k = gram.shape[0]
    rows = lax.broadcasted_iota(jnp.int32, (k, k), 0)
    cols = lax.broadcasted_iota(jnp.int32, (k, k), 1)
    aug = jnp.concatenate([gram, (rows == cols).astype(f32)], 1)
    tall, wide = 8, 2 * k
    a = [aug[t * tall : (t + 1) * tall, :] for t in range(k // tall)]
    sub = lax.broadcasted_iota(jnp.int32, (tall, wide), 0)
    spread = lambda x: jnp.broadcast_to(x, (tall, wide))
    for start in range(0, k, w):
        t, s = start // tall, start % tall
        r = [spread(a[t][s + i : s + i + 1, :]) for i in range(w)]
        d = [[spread(a[t][s + i : s + i + 1, start + j : start + j + 1]) if j >= i else None for j in range(w)] for i in range(w)]
        later = range(t if s + w < tall else t + 1, len(a))
        c = {u: [spread(a[u][:, start + i : start + i + 1]) for i in range(w)] for u in later}
        l = [[None] * w for _ in range(w)]
        inv = [None] * w
        for i in range(w):
            p = d[i][i]
            for m in range(i):
                p = p - l[i][m] * l[i][m]
            inv[i] = lax.rsqrt(p)
            for j in range(i + 1, w):
                q = d[i][j]
                for m in range(i):
                    q = q - l[i][m] * l[j][m]
                l[j][i] = q * inv[i]
        for i in range(w):
            for m in range(i):
                r[i] = r[i] - l[i][m] * r[m]
            r[i] = r[i] * inv[i]
        for u in later:
            x = c[u]
            for i in range(w):
                for m in range(i):
                    x[i] = x[i] - l[i][m] * x[m]
                x[i] = x[i] * inv[i]
            new = a[u]
            for i in range(w):
                new = new - x[i] * r[i]
            a[u] = new if u > t else jnp.where(sub < s + w, a[u], new)
        for i in range(w):
            a[t] = jnp.where(sub == s + i, r[i], a[t])
    return jnp.concatenate(a, 0)[:, k:]


def factor_kernel(ga_ref, gb_ref, inv_ref):
    inv_ref[...] = factor_inverse(ga_ref[...] + gb_ref[...])


def exact(a, b):
    return lax.dot_general(a, b, NN, precision=lax.Precision.HIGHEST, preferred_element_type=f32)


def image_kernel(members, total, inv_ref, *refs):
    pieces, image_ref, gram_ref = refs[:members], refs[members], refs[members + 1]
    gather_into(image_ref, pieces, members)
    image_ref[...] = exact(inv_ref[...], image_ref[...])
    gram_ref[...] = gram_sum(*split3(image_ref[...])) / total


def last_kernel(ga_ref, gb_ref, image_ref, out_ref):
    inv = factor_inverse(ga_ref[...] + gb_ref[...])
    out_ref[...] = exact(inv, image_ref[...])


VM = pl.BlockSpec(memory_space=pltpu.VMEM)
SM = pl.BlockSpec(memory_space=pltpu.SMEM)


def call(body, specs, outs, name, limit=40, flops=10**9):
    return pl.pallas_call(
        body,
        in_specs=specs,
        out_specs=[VM] * len(outs),
        out_shape=[jax.ShapeDtypeStruct(s, t) for s, t in outs],
        compiler_params=pltpu.CompilerParams(vmem_limit_bytes=limit * MB),
        cost_estimate=pl.CostEstimate(flops=flops, bytes_accessed=MB, transcendentals=0),
        name=name,
    )


def shifted(x, axis, by):
    n = lax.axis_size(axis)
    return lax.ppermute(x, axis, [(i, (i + by) % n) for i in range(n)])


def crossed(x):
    n = lax.axis_size("rows")
    return lax.ppermute(x, "rows", [(i, (i + 2 * (i % 2) - 1) % n) for i in range(n)])


def swapped(x, axis, mask):
    n = lax.axis_size(axis)
    return lax.ppermute(x, axis, [(i, i ^ mask) for i in range(n)])


MASKS = (1, 2, 6, 8, 16, 48)


def pair_sums(gram):
    for mask in MASKS[:-1]:
        gram = gram + swapped(gram, "rows", mask)
    return gram, swapped(gram, "rows", MASKS[-1])


def on_device(embeddings, start_vectors, pairs):
    members = lax.axis_size("sub")
    rows, width = embeddings.shape
    k = start_vectors.shape[1]
    quarter = rows // members
    total = rows * lax.axis_size("rows")
    vt = start_vectors.T
    chunks = 2
    piece = rows // chunks
    cross_e = [crossed(embeddings[c * piece : (c + 1) * piece]) for c in range(chunks)]
    sib_e = swapped(embeddings, "rows", 1)
    cross_v = crossed(vt)
    sib_v = swapped(vt, "rows", 1)
    prev_pairs = shifted(pairs, "rows", 1)
    part = ((k, quarter), f32)
    tiles = lambda n: [((n, quarter), bf16)] * 2
    xah, xal, na, acc, *own_t = call(
        functools.partial(own_kernel, members), [VM, VM, SM],
        [((quarter, width), bf16)] * 2 + [((8, quarter), f32), part] + tiles(rows), "own_tiles",
        flops=5 * 10**9)(embeddings, vt, pairs)
    other = lambda side, first, n, name: call(
        functools.partial(other_kernel, members, side, first), [VM, VM, SM, SM, VM, VM, VM, VM],
        [part] + tiles(n), name, flops=5 * 10**9)
    acc, *sib_t = other(SIB, 0, rows, "sib_tiles")(sib_e, sib_v, pairs, prev_pairs, xah, xal, na, acc)
    kept = own_t + sib_t
    sources = [(0, 0, rows), (1, 0, rows)]
    for c in range(chunks):
        acc, *t = other(CROSS, c * piece, piece, "cross_tiles")(cross_e[c], cross_v, pairs, prev_pairs, xah, xal, na, acc)
        kept += t
        sources.append((2, c * piece, piece))
    pieces = [acc] + [shifted(acc, "sub", s) for s in range(1, members)]
    whole = ((k, rows), f32)
    small = ((k, k), f32)
    image, gram = call(functools.partial(join_kernel, members, total), [VM] * members, [whole, small], "join")(*pieces)
    cross_i = crossed(image)
    sib_i = swapped(image, "rows", 1)
    ga, gb = pair_sums(gram)
    (acc2,) = call(
        functools.partial(second_kernel, members, sources), [SM, SM] + [VM] * (3 + len(kept)), [part], "second_product")(
        pairs, prev_pairs, image, sib_i, cross_i, *kept)
    pieces = [acc2] + [shifted(acc2, "sub", s) for s in range(1, members)]
    (inv,) = call(factor_kernel, [VM, VM], [small], "factor")(ga, gb)
    image, gram = call(functools.partial(image_kernel, members, total), [VM] * (1 + members), [whole, small], "image")(inv, *pieces)
    ga, gb = pair_sums(gram)
    (out,) = call(last_kernel, [VM, VM, VM], [whole], "last")(ga, gb, image)
    return out.T


def solution(mesh):
    return jax.shard_map(
        on_device,
        mesh=mesh,
        in_specs=(P("rows", None), P("rows", None), P("rows", None)),
        out_specs=P("rows", None),
        check_vma=False,
    )
```

time: 136 us -> 120 us (0.88); the launches traced: 137 us -> 119 us
  starting transfers between devices: 70 us -> 40 us
  waiting for transfers between devices: 31.6 us -> 51.8 us
  Pallas kernels: 30 us -> 24.1 us
  local copies, waits for them, and re-layouts: 5.21 us -> 3.25 us
    ppermute x12 -> x15, starting transfers between devices: 31.8 us -> 12.2 us  [swapped(): return lax.ppermute(x, axis, [(i, i ^ mask) for i in range(n)])]
    ppermute x13 -> x11, waiting for transfers between devices: 5.01 us -> 16.9 us  [the longest x7 12.6 us: shifted(): return lax.ppermute(x, axis, [(i, (i + by) % n) for i in range(n)])]
    ppermute x13 -> x11, starting transfers between devices: 38.2 us -> 27.8 us  [the longest x4 18 us: crossed(): lax.ppermute(x, 'rows', [(i, (i + 2 * (i % 2) - 1) % n) for i in range(n)])]
    ppermute x12 -> x15, waiting for transfers between devices: 26.6 us -> 34.9 us  [swapped(): return lax.ppermute(x, axis, [(i, i ^ mask) for i in range(n)])]
    unnamed x9 -> x5, local copies, waits for them, and re-layouts: 5.21 us -> 0.09 us
    pallas_call x1, Pallas kernels: 5.48 us -> 1.98 us  [on_device(): inv, = call(factor_kernel, [VM, VM], [small], 'factor')(ga, gb)]
    pallas_call x1, Pallas kernels: 6.82 us -> 3.34 us  [on_device(): out, = call(last_kernel, [VM, VM, VM], [whole], 'last')(ga, gb, image)]
    slice x0 -> x1, local copies, waits for them, and re-layouts: none -> 3.16 us  [on_device(): embeddings[c * piece:(c + 1) * piece]]
  transfers between devices with their start and end apart: 25 -> 26, of which waited for: 14 -> 16; matrix products, arithmetic and copies ran while one was open for 1% -> 3% of each run, Pallas kernels for 12% -> 15%
where the time goes in v2:
time: 120 us; the launch traced here: 119 us
  waiting for transfers between devices  51.8 us (43%)
  starting transfers between devices  40 us (33%)
  Pallas kernels  24.1 us (20%)
  local copies, waits for them, and re-layouts  3.25 us (3%)
    ppermute x15, waiting for transfers between devices, swapped(): return lax.ppermute(x, axis, [(i, i ^ mask) for i in range(n)])  34.9 us
    ppermute x4, starting transfers between devices, crossed(): lax.ppermute(x, 'rows', [(i, (i + 2 * (i % 2) - 1) % n) for i in range(n)])  18 us
    ppermute x7, waiting for transfers between devices, shifted(): return lax.ppermute(x, axis, [(i, (i + by) % n) for i in range(n)])  12.6 us
    ppermute x15, starting transfers between devices, swapped(): return lax.ppermute(x, axis, [(i, i ^ mask) for i in range(n)])  12.2 us
    ppermute x7, starting transfers between devices, shifted(): return lax.ppermute(x, axis, [(i, (i + by) % n) for i in range(n)])  9.78 us
    pallas_call x1, Pallas kernels, on_device(): other(SIB, 0, rows, 'sib_tiles')  6.36 us
    pallas_call x1, Pallas kernels, on_device(): call(functools.partial(own_kernel, members), [VM, VM, SM], [((quarter, wi...  6.27 us
    ppermute x4, waiting for transfers between devices, crossed(): lax.ppermute(x, 'rows', [(i, (i + 2 * (i % 2) - 1) % n) for i in range(n)])  4.34 us
  transfers between devices with their start and end apart: 26, of which 16 were waited for; matrix products, arithmetic and copies ran while one was open for 3% of the time, Pallas kernels for 15%

profile of v2, /device:TPU:16, one launch (start us, length us, event | category | flops | bytes accessed | tf_op | source)
XLA Modules:
  0.0 119.4 jit_solution(14553392988150655966)
XLA Ops:
  0.0 3.2 %fusion = (f32[1024,256]{1,0:T(8,128)}, f32[1024,256]{1,0:T(8,128)}) fusion(f32[2048,256]{1,0:T(8,128)} %x_ref.1), kind=kLoop, calls=%fused_computation | loop fusion | bytes 4194304 | tf_op jit(solution)/shard_map/slice | solution.py:265
  3.2 8.0 %collective-permute-start.3 = (f32[1024,256]{1,0:T(8,128)}, f32[1024,256]{1,0:T(8,128)S(1)}, u32[]{:S(2)}, u32[]{:S(2)}) collective-permute-start(f32[1024,256]{1,0:T(8,128)} %get-tuple-element.43), channel_id=1, source_target_pairs={{0,252},{4,8},{8,4},{12,16},{16,12},{20,24},{24,20},{28,32},{32,28... | collective-permute-start | bytes 3145736 | tf_op jit(solution)/shard_map/ppermute | solution.py:239
  11.2 0.0 collective-permute-start.5
  11.2 0.1 copy.8.pairs_ref
  11.3 0.5 collective-permute-start.2
  11.8 4.6 %collective-permute-start.1 = (f32[64,2048]{1,0:T(8,128)}, f32[64,2048]{1,0:T(8,128)S(1)}, u32[]{:S(2)}, u32[]{:S(2)}) collective-permute-start(f32[64,2048]{1,0:T(8,128)} %bitcast.v_ref), channel_id=1, source_target_pairs={{0,252},{4,8},{8,4},{12,16},{16,12},{20,24},{24,20},{28,32},{32,28... | collective-permute-start | bytes 1572872 | tf_op jit(solution)/shard_map/ppermute | solution.py:239
  16.3 7.6 %collective-permute-done.2.prev_pairs_ref = s32[8,2]{1,0:T(8,128)S(1)} collective-permute-done((s32[8,2]{1,0:T(8,128)S(1)}, s32[8,2]{1,0:T(8,128)S(1)}, u32[]{:S(2)}, u32[]{:S(2)}) %collective-permute-start.2) | collective-permute-done | bytes 96 | tf_op jit(solution)/shard_map/ppermute | solution.py:234
  23.9 0.0 collective-permute-start
  23.9 6.3 %own_tiles.1 = (bf16[512,256]{1,0:T(8,128)(2,1)S(1)}, bf16[512,256]{1,0:T(8,128)(2,1)S(1)}, f32[8,512]{1,0:T(8,128)S(1)}, f32[64,512]{1,0:T(8,128)S(1)}, bf16[20...) custom-call(f32[2048,256]{1,0:T(8,128)S(1)} %copy-done, f32[64,2048]{1,0:T(8,128)} %bitcast.v_ref, ...), custom_call_target="tpu_custom_call" | custom-call | flops 5000000000 | bytes 1048576 | tf_op jit(solution)/shard_map/own_tiles/pallas_call | solution.py:272
  30.2 0.0 collective-permute-done.4.x_ref
  30.2 6.4 %sib_tiles.1 = (f32[64,512]{1,0:T(8,128)S(1)}, bf16[2048,512]{1,0:T(8,128)(2,1)S(1)}, bf16[2048,512]{1,0:T(8,128)(2,1)S(1)}) custom-call(f32[2048,256]{1,0:T(8,128)} %collective-permute-done.4.x_ref, f32[64,2048]{1,0:T(8,128)} %collective-permute-done.5.v_ref, s32[8,2]{1,0:T(8,128)S(1)} %copy.8.pairs_ref, s32[8,2]{1,0:T(8,128)S(1)} %collective-permute-done.2.prev_pairs_ref, ...), custom_call_target="tpu_custom_call" | custom-call | flops 5000000000 | bytes 1048576 | tf_op jit(solution)/shard_map/sib_tiles/pallas_call | solution.py:279
  36.6 0.7 cross_tiles.2
  37.3 4.3 %collective-permute-done.x_ref = f32[1024,256]{1,0:T(8,128)S(1)} collective-permute-done((f32[1024,256]{1,0:T(8,128)}, f32[1024,256]{1,0:T(8,128)S(1)}, u32[]{:S(2)}, u32[]{:S(2)}) %collective-permute-start) | collective-permute-done | bytes 1048608 | tf_op jit(solution)/shard_map/ppermute | solution.py:239
  41.7 0.9 cross_tiles.3
  42.6 0.5 collective-permute-start.8
  43.1 2.9 %collective-permute-start.7 = (f32[64,512]{1,0:T(8,128)S(1)}, f32[64,512]{1,0:T(8,128)S(1)}, u32[]{:S(2)}, u32[]{:S(2)}) collective-permute-start(f32[64,512]{1,0:T(8,128)S(1)} %get-tuple-element.30.refs_0_), channel_id=1, source_target_pairs={{0,2},{1,3},{2,0},{3,1},{4,6},{5,7},{6,4},{7,5},{8,10},{9,11},{10,... | collective-permute-start | bytes 393224 | tf_op jit(solution)/shard_map/ppermute | solution.py:234
  46.0 1.6 %collective-permute-done.8.refs_3_ = f32[64,512]{1,0:T(8,128)S(1)} collective-permute-done((f32[64,512]{1,0:T(8,128)S(1)}, f32[64,512]{1,0:T(8,128)S(1)}, u32[]{:S(2)}, u32[]{:S(2)}) %collective-permute-start.8) | collective-permute-done | bytes 131104 | tf_op jit(solution)/shard_map/ppermute | solution.py:234
  47.6 2.0 %collective-permute-done.7.refs_2_ = f32[64,512]{1,0:T(8,128)S(1)} collective-permute-done((f32[64,512]{1,0:T(8,128)S(1)}, f32[64,512]{1,0:T(8,128)S(1)}, u32[]{:S(2)}, u32[]{:S(2)}) %collective-permute-start.7) | collective-permute-done | bytes 131104 | tf_op jit(solution)/shard_map/ppermute | solution.py:234
  49.6 1.4 %collective-permute-done.6.refs_1_ = f32[64,512]{1,0:T(8,128)S(1)} collective-permute-done((f32[64,512]{1,0:T(8,128)S(1)}, f32[64,512]{1,0:T(8,128)S(1)}, u32[]{:S(2)}, u32[]{:S(2)}) %collective-permute-start.6) | collective-permute-done | bytes 131104 | tf_op jit(solution)/shard_map/ppermute | solution.py:234
  51.0 0.6 join.1
  51.6 5.4 %collective-permute-start.16 = (f32[64,2048]{1,0:T(8,128)S(1)}, f32[64,2048]{1,0:T(8,128)S(1)}, u32[]{:S(2)}, u32[]{:S(2)}) collective-permute-start(f32[64,2048]{1,0:T(8,128)S(1)} %get-tuple-element.32.refs_0_), channel_id=1, source_target_pairs={{0,252},{4,8},{8,4},{12,16},{16,12},{20,24},{24,20},{28,32},{32,28... | collective-permute-start | bytes 1572872 | tf_op jit(solution)/shard_map/ppermute | solution.py:239
  57.0 0.5 collective-permute-start.9
  57.5 1.4 %collective-permute-done.9 = f32[64,64]{1,0:T(8,128)S(1)} collective-permute-done((f32[64,64]{1,0:T(8,128)S(1)}, f32[64,64]{1,0:T(8,128)S(1)}, u32[]{:S(2)}, u32[]{:S(2)}) %collective-permute-start.9) | collective-permute-done | bytes 16416 | tf_op jit(solution)/shard_map/ppermute | solution.py:244
  59.0 3.9 %collective-permute-done.10 = f32[64,64]{1,0:T(8,128)S(1)} collective-permute-done((f32[64,64]{1,0:T(8,128)S(1)}, f32[64,64]{1,0:T(8,128)S(1)}, u32[]{:S(2)}, u32[]{:S(2)}) %collective-permute-start.10) | collective-permute-done | bytes 16416 | tf_op jit(solution)/shard_map/ppermute | solution.py:244
  62.9 5.1 %collective-permute-done.11 = f32[64,64]{1,0:T(8,128)S(1)} collective-permute-done((f32[64,64]{1,0:T(8,128)S(1)}, f32[64,64]{1,0:T(8,128)S(1)}, u32[]{:S(2)}, u32[]{:S(2)}) %collective-permute-start.11) | collective-permute-done | bytes 16416 | tf_op jit(solution)/shard_map/ppermute | solution.py:244
  68.0 2.9 %second_product.1.refs_0_ = f32[64,512]{1,0:T(8,128)S(1)} custom-call(s32[8,2]{1,0:T(8,128)S(1)} %copy.8.pairs_ref, s32[8,2]{1,0:T(8,128)S(1)} %collective-permute-done.2.prev_pairs_ref, f32[64,2048]{1,0:T(8,128)S(1)} %get-tuple-element.32.refs_0_, f32[64,2048]{1,0:T(8,128)S(1)} %collective-permute-done.15.refs_1_, ...), custom_call_target="tpu_custom_call" | custom-call | flops 1000000000 | bytes 1048576 | tf_op jit(solution)/shard_map/second_product/pallas_call | solution.py:293
  71.0 0.4 collective-permute-start.19
  71.4 3.5 %collective-permute-start.18 = (f32[64,512]{1,0:T(8,128)S(1)}, f32[64,512]{1,0:T(8,128)S(1)}, u32[]{:S(2)}, u32[]{:S(2)}) collective-permute-start(f32[64,512]{1,0:T(8,128)S(1)} %second_product.1.refs_0_), channel_id=1, source_target_pairs={{0,2},{1,3},{2,0},{3,1},{4,6},{5,7},{6,4},{7,5},{8,10},{9,11},{10,... | collective-permute-start | bytes 393224 | tf_op jit(solution)/shard_map/ppermute | solution.py:234
  74.9 2.0 %collective-permute-start.17 = (f32[64,512]{1,0:T(8,128)S(1)}, f32[64,512]{1,0:T(8,128)S(1)}, u32[]{:S(2)}, u32[]{:S(2)}) collective-permute-start(f32[64,512]{1,0:T(8,128)S(1)} %second_product.1.refs_0_), channel_id=1, source_target_pairs={{0,1},{1,2},{2,3},{3,0},{4,5},{5,6},{6,7},{7,4},{8,9},{9,10},{10,1... | collective-permute-start | bytes 393224 | tf_op jit(solution)/shard_map/ppermute | solution.py:234
  76.9 1.3 %collective-permute-start.13 = (f32[64,64]{1,0:T(8,128)S(1)}, f32[64,64]{1,0:T(8,128)S(1)}, u32[]{:S(2)}, u32[]{:S(2)}) collective-permute-start(f32[64,64]{1,0:T(8,128)S(1)} %add.33), channel_id=1, source_target_pairs={{0,64},{4,68},{8,72},{12,76},{16,80},{20,84},{24,88},{28,92},{32,9... | collective-permute-start | bytes 49160 | tf_op jit(solution)/shard_map/ppermute | solution.py:244
  78.2 3.6 %collective-permute-done.13 = f32[64,64]{1,0:T(8,128)S(1)} collective-permute-done((f32[64,64]{1,0:T(8,128)S(1)}, f32[64,64]{1,0:T(8,128)S(1)}, u32[]{:S(2)}, u32[]{:S(2)}) %collective-permute-start.13) | collective-permute-done | bytes 16416 | tf_op jit(solution)/shard_map/ppermute | solution.py:244
  81.8 2.4 %collective-permute-start.14 = (f32[64,64]{1,0:T(8,128)S(1)}, f32[64,64]{1,0:T(8,128)S(1)}, u32[]{:S(2)}, u32[]{:S(2)}) collective-permute-start(f32[64,64]{1,0:T(8,128)S(1)} %add.34.ga_ref), channel_id=1, source_target_pairs={{0,192},{4,196},{8,200},{12,204},{16,208},{20,212},{24,216},{28,22... | collective-permute-start | bytes 49160 | tf_op jit(solution)/shard_map/ppermute | solution.py:244
  84.1 3.7 %collective-permute-done.14.gb_ref = f32[64,64]{1,0:T(8,128)S(1)} collective-permute-done((f32[64,64]{1,0:T(8,128)S(1)}, f32[64,64]{1,0:T(8,128)S(1)}, u32[]{:S(2)}, u32[]{:S(2)}) %collective-permute-start.14) | collective-permute-done | bytes 16416 | tf_op jit(solution)/shard_map/ppermute | solution.py:244
  87.8 2.0 %factor.1.inv_ref = f32[64,64]{1,0:T(8,128)S(1)} custom-call(f32[64,64]{1,0:T(8,128)S(1)} %add.34.ga_ref, f32[64,64]{1,0:T(8,128)S(1)} %collective-permute-done.14.gb_ref), custom_call_target="tpu_custom_call" | custom-call | flops 1000000000 | bytes 1048576 | tf_op jit(solution)/shard_map/factor/pallas_call | solution.py:297
  89.8 0.0 collective-permute-done.17.refs_1_
  89.8 1.0 image.1
  90.8 0.1 collective-permute-start.20
  90.9 1.2 %collective-permute-done.20 = f32[64,64]{1,0:T(8,128)S(1)} collective-permute-done((f32[64,64]{1,0:T(8,128)S(1)}, f32[64,64]{1,0:T(8,128)S(1)}, u32[]{:S(2)}, u32[]{:S(2)}) %collective-permute-start.20) | collective-permute-done | bytes 16416 | tf_op jit(solution)/shard_map/ppermute | solution.py:244
  92.1 3.9 %collective-permute-done.21 = f32[64,64]{1,0:T(8,128)S(1)} collective-permute-done((f32[64,64]{1,0:T(8,128)S(1)}, f32[64,64]{1,0:T(8,128)S(1)}, u32[]{:S(2)}, u32[]{:S(2)}) %collective-permute-start.21) | collective-permute-done | bytes 16416 | tf_op jit(solution)/shard_map/ppermute | solution.py:244
  96.0 2.1 %collective-permute-start.22 = (f32[64,64]{1,0:T(8,128)S(1)}, f32[64,64]{1,0:T(8,128)S(1)}, u32[]{:S(2)}, u32[]{:S(2)}) collective-permute-start(f32[64,64]{1,0:T(8,128)S(1)} %add.36), channel_id=1, source_target_pairs={{0,24},{4,28},{8,16},{12,20},{16,8},{20,12},{24,0},{28,4},{32,56},... | collective-permute-start | bytes 49160 | tf_op jit(solution)/shard_map/ppermute | solution.py:244
  98.1 3.1 %collective-permute-done.22 = f32[64,64]{1,0:T(8,128)S(1)} collective-permute-done((f32[64,64]{1,0:T(8,128)S(1)}, f32[64,64]{1,0:T(8,128)S(1)}, u32[]{:S(2)}, u32[]{:S(2)}) %collective-permute-start.22) | collective-permute-done | bytes 16416 | tf_op jit(solution)/shard_map/ppermute | solution.py:244
  101.2 1.0 collective-permute-start.23
  102.2 2.9 %collective-permute-done.23 = f32[64,64]{1,0:T(8,128)S(1)} collective-permute-done((f32[64,64]{1,0:T(8,128)S(1)}, f32[64,64]{1,0:T(8,128)S(1)}, u32[]{:S(2)}, u32[]{:S(2)}) %collective-permute-start.23) | collective-permute-done | bytes 16416 | tf_op jit(solution)/shard_map/ppermute | solution.py:244
  105.1 1.9 %collective-permute-start.24 = (f32[64,64]{1,0:T(8,128)S(1)}, f32[64,64]{1,0:T(8,128)S(1)}, u32[]{:S(2)}, u32[]{:S(2)}) collective-permute-start(f32[64,64]{1,0:T(8,128)S(1)} %add.38), channel_id=1, source_target_pairs={{0,64},{4,68},{8,72},{12,76},{16,80},{20,84},{24,88},{28,92},{32,9... | collective-permute-start | bytes 49160 | tf_op jit(solution)/shard_map/ppermute | solution.py:244
  107.0 3.0 %collective-permute-done.24 = f32[64,64]{1,0:T(8,128)S(1)} collective-permute-done((f32[64,64]{1,0:T(8,128)S(1)}, f32[64,64]{1,0:T(8,128)S(1)}, u32[]{:S(2)}, u32[]{:S(2)}) %collective-permute-start.24) | collective-permute-done | bytes 16416 | tf_op jit(solution)/shard_map/ppermute | solution.py:244
  110.0 2.9 %collective-permute-start.25 = (f32[64,64]{1,0:T(8,128)S(1)}, f32[64,64]{1,0:T(8,128)S(1)}, u32[]{:S(2)}, u32[]{:S(2)}) collective-permute-start(f32[64,64]{1,0:T(8,128)S(1)} %add.39.ga_ref), channel_id=1, source_target_pairs={{0,192},{4,196},{8,200},{12,204},{16,208},{20,212},{24,216},{28,22... | collective-permute-start | bytes 49160 | tf_op jit(solution)/shard_map/ppermute | solution.py:244
  112.9 3.1 %collective-permute-done.25.gb_ref = f32[64,64]{1,0:T(8,128)S(1)} collective-permute-done((f32[64,64]{1,0:T(8,128)S(1)}, f32[64,64]{1,0:T(8,128)S(1)}, u32[]{:S(2)}, u32[]{:S(2)}) %collective-permute-start.25) | collective-permute-done | bytes 16416 | tf_op jit(solution)/shard_map/ppermute | solution.py:244
  116.0 3.3 %last.1 = f32[64,2048]{1,0:T(8,128)} custom-call(f32[64,64]{1,0:T(8,128)S(1)} %add.39.ga_ref, f32[64,64]{1,0:T(8,128)S(1)} %collective-permute-done.25.gb_ref, f32[64,2048]{1,0:T(8,128)S(1)} %get-tuple-element.42.image_ref), custom_call_target="tpu_custom_call" | custom-call | flops 1000000000 | bytes 1048576 | tf_op jit(solution)/shard_map/last/pallas_call | solution.py:300
  (29 shorter events, 0.1 us)
Async XLA Ops:
  0.0 23.9 %copy-start = (f32[2048,256]{1,0:T(8,128)S(1)}, f32[2048,256]{1,0:T(8,128)}, u32[]{:S(2)}) copy-start(f32[2048,256]{1,0:T(8,128)} %x_ref.1) | copy-start | bytes 6291460
  0.0 11.2 %copy-start.1 = (s32[8,2]{0,1:T(2,128)S(1)}, s32[8,2]{0,1:T(2,128)}, u32[]{:S(2)}) copy-start(s32[8,2]{0,1:T(2,128)} %param.5) | copy-start | bytes 196
  0.0 30.2 %collective-permute-start.4 = (f32[2048,256]{1,0:T(8,128)}, f32[2048,256]{1,0:T(8,128)}, u32[]{:S(2)}, u32[]{:S(2)}) collective-permute-start(f32[2048,256]{1,0:T(8,128)} %x_ref.1), channel_id=1, source_target_pairs={{0,4},{4,0},{8,12},{12,8},{16,20},{20,16},{24,28},{28,24},{32,36},... | collective-permute-start | bytes 6291464 | tf_op jit(solution)/shard_map/ppermute | solution.py:244
  3.2 33.4 %collective-permute-start.3 = (f32[1024,256]{1,0:T(8,128)}, f32[1024,256]{1,0:T(8,128)S(1)}, u32[]{:S(2)}, u32[]{:S(2)}) collective-permute-start(f32[1024,256]{1,0:T(8,128)} %get-tuple-element.43), channel_id=1, source_target_pairs={{0,252},{4,8},{8,4},{12,16},{16,12},{20,24},{24,20},{28,32},{32,28... | collective-permute-start | bytes 3145736 | tf_op jit(solution)/shard_map/ppermute | solution.py:239
  11.2 19.0 %collective-permute-start.5 = (f32[64,2048]{1,0:T(8,128)}, f32[64,2048]{1,0:T(8,128)}, u32[]{:S(2)}, u32[]{:S(2)}) collective-permute-start(f32[64,2048]{1,0:T(8,128)} %bitcast.v_ref), channel_id=1, source_target_pairs={{0,4},{4,0},{8,12},{12,8},{16,20},{20,16},{24,28},{28,24},{32,36},... | collective-permute-start | bytes 1572872 | tf_op jit(solution)/shard_map/ppermute | solution.py:244
  11.3 12.6 %collective-permute-start.2 = (s32[8,2]{1,0:T(8,128)S(1)}, s32[8,2]{1,0:T(8,128)S(1)}, u32[]{:S(2)}, u32[]{:S(2)}) collective-permute-start(s32[8,2]{1,0:T(8,128)S(1)} %copy.8.pairs_ref), channel_id=1, source_target_pairs={{0,4},{4,8},{8,12},{12,16},{16,20},{20,24},{24,28},{28,32},{32,36}... | collective-permute-start | bytes 200 | tf_op jit(solution)/shard_map/ppermute | solution.py:234
  11.8 24.8 %collective-permute-start.1 = (f32[64,2048]{1,0:T(8,128)}, f32[64,2048]{1,0:T(8,128)S(1)}, u32[]{:S(2)}, u32[]{:S(2)}) collective-permute-start(f32[64,2048]{1,0:T(8,128)} %bitcast.v_ref), channel_id=1, source_target_pairs={{0,252},{4,8},{8,4},{12,16},{16,12},{20,24},{24,20},{28,32},{32,28... | collective-permute-start | bytes 1572872 | tf_op jit(solution)/shard_map/ppermute | solution.py:239
  23.9 17.8 %collective-permute-start = (f32[1024,256]{1,0:T(8,128)}, f32[1024,256]{1,0:T(8,128)S(1)}, u32[]{:S(2)}, u32[]{:S(2)}) collective-permute-start(f32[1024,256]{1,0:T(8,128)} %get-tuple-element.44), channel_id=1, source_target_pairs={{0,252},{4,8},{8,4},{12,16},{16,12},{20,24},{24,20},{28,32},{32,28... | collective-permute-start | bytes 3145736 | tf_op jit(solution)/shard_map/ppermute | solution.py:239
  42.6 5.0 %collective-permute-start.8 = (f32[64,512]{1,0:T(8,128)S(1)}, f32[64,512]{1,0:T(8,128)S(1)}, u32[]{:S(2)}, u32[]{:S(2)}) collective-permute-start(f32[64,512]{1,0:T(8,128)S(1)} %get-tuple-element.30.refs_0_), channel_id=1, source_target_pairs={{0,3},{1,0},{2,1},{3,2},{4,7},{5,4},{6,5},{7,6},{8,11},{9,8},{10,9... | collective-permute-start | bytes 393224 | tf_op jit(solution)/shard_map/ppermute | solution.py:234
  43.1 6.5 %collective-permute-start.7 = (f32[64,512]{1,0:T(8,128)S(1)}, f32[64,512]{1,0:T(8,128)S(1)}, u32[]{:S(2)}, u32[]{:S(2)}) collective-permute-start(f32[64,512]{1,0:T(8,128)S(1)} %get-tuple-element.30.refs_0_), channel_id=1, source_target_pairs={{0,2},{1,3},{2,0},{3,1},{4,6},{5,7},{6,4},{7,5},{8,10},{9,11},{10,... | collective-permute-start | bytes 393224 | tf_op jit(solution)/shard_map/ppermute | solution.py:234
  46.0 5.0 %collective-permute-start.6 = (f32[64,512]{1,0:T(8,128)S(1)}, f32[64,512]{1,0:T(8,128)S(1)}, u32[]{:S(2)}, u32[]{:S(2)}) collective-permute-start(f32[64,512]{1,0:T(8,128)S(1)} %get-tuple-element.30.refs_0_), channel_id=1, source_target_pairs={{0,1},{1,2},{2,3},{3,0},{4,5},{5,6},{6,7},{7,4},{8,9},{9,10},{10,1... | collective-permute-start | bytes 393224 | tf_op jit(solution)/shard_map/ppermute | solution.py:234
  51.6 16.5 %collective-permute-start.16 = (f32[64,2048]{1,0:T(8,128)S(1)}, f32[64,2048]{1,0:T(8,128)S(1)}, u32[]{:S(2)}, u32[]{:S(2)}) collective-permute-start(f32[64,2048]{1,0:T(8,128)S(1)} %get-tuple-element.32.refs_0_), channel_id=1, source_target_pairs={{0,252},{4,8},{8,4},{12,16},{16,12},{20,24},{24,20},{28,32},{32,28... | collective-permute-start | bytes 1572872 | tf_op jit(solution)/shard_map/ppermute | solution.py:239
  57.0 11.0 %collective-permute-start.15 = (f32[64,2048]{1,0:T(8,128)S(1)}, f32[64,2048]{1,0:T(8,128)S(1)}, u32[]{:S(2)}, u32[]{:S(2)}) collective-permute-start(f32[64,2048]{1,0:T(8,128)S(1)} %get-tuple-element.32.refs_0_), channel_id=1, source_target_pairs={{0,4},{4,0},{8,12},{12,8},{16,20},{20,16},{24,28},{28,24},{32,36},... | collective-permute-start | bytes 1572872 | tf_op jit(solution)/shard_map/ppermute | solution.py:244
  57.0 2.0 %collective-permute-start.9 = (f32[64,64]{1,0:T(8,128)S(1)}, f32[64,64]{1,0:T(8,128)S(1)}, u32[]{:S(2)}, u32[]{:S(2)}) collective-permute-start(f32[64,64]{1,0:T(8,128)S(1)} %get-tuple-element.31), channel_id=1, source_target_pairs={{0,4},{4,0},{8,12},{12,8},{16,20},{20,16},{24,28},{28,24},{32,36},... | collective-permute-start | bytes 49160 | tf_op jit(solution)/shard_map/ppermute | solution.py:244
  59.0 3.9 %collective-permute-start.10 = (f32[64,64]{1,0:T(8,128)S(1)}, f32[64,64]{1,0:T(8,128)S(1)}, u32[]{:S(2)}, u32[]{:S(2)}) collective-permute-start(f32[64,64]{1,0:T(8,128)S(1)} %add.30), channel_id=1, source_target_pairs={{0,8},{4,12},{8,0},{12,4},{16,24},{20,28},{24,16},{28,20},{32,40},... | collective-permute-start | bytes 49160 | tf_op jit(solution)/shard_map/ppermute | solution.py:244
  62.9 5.1 %collective-permute-start.11 = (f32[64,64]{1,0:T(8,128)S(1)}, f32[64,64]{1,0:T(8,128)S(1)}, u32[]{:S(2)}, u32[]{:S(2)}) collective-permute-start(f32[64,64]{1,0:T(8,128)S(1)} %add.31), channel_id=1, source_target_pairs={{0,24},{4,28},{8,16},{12,20},{16,8},{20,12},{24,0},{28,4},{32,56},... | collective-permute-start | bytes 49160 | tf_op jit(solution)/shard_map/ppermute | solution.py:244
  68.0 8.8 %collective-permute-start.12 = (f32[64,64]{1,0:T(8,128)S(1)}, f32[64,64]{1,0:T(8,128)S(1)}, u32[]{:S(2)}, u32[]{:S(2)}) collective-permute-start(f32[64,64]{1,0:T(8,128)S(1)} %add.32), channel_id=1, source_target_pairs={{0,32},{4,36},{8,40},{12,44},{16,48},{20,52},{24,56},{28,60},{32,0... | collective-permute-start | bytes 49160 | tf_op jit(solution)/shard_map/ppermute | solution.py:244
  71.0 18.8 %collective-permute-start.19 = (f32[64,512]{1,0:T(8,128)S(1)}, f32[64,512]{1,0:T(8,128)S(1)}, u32[]{:S(2)}, u32[]{:S(2)}) collective-permute-start(f32[64,512]{1,0:T(8,128)S(1)} %second_product.1.refs_0_), channel_id=1, source_target_pairs={{0,3},{1,0},{2,1},{3,2},{4,7},{5,4},{6,5},{7,6},{8,11},{9,8},{10,9... | collective-permute-start | bytes 393224 | tf_op jit(solution)/shard_map/ppermute | solution.py:234
  71.4 18.4 %collective-permute-start.18 = (f32[64,512]{1,0:T(8,128)S(1)}, f32[64,512]{1,0:T(8,128)S(1)}, u32[]{:S(2)}, u32[]{:S(2)}) collective-permute-start(f32[64,512]{1,0:T(8,128)S(1)} %second_product.1.refs_0_), channel_id=1, source_target_pairs={{0,2},{1,3},{2,0},{3,1},{4,6},{5,7},{6,4},{7,5},{8,10},{9,11},{10,... | collective-permute-start | bytes 393224 | tf_op jit(solution)/shard_map/ppermute | solution.py:234
  74.9 14.9 %collective-permute-start.17 = (f32[64,512]{1,0:T(8,128)S(1)}, f32[64,512]{1,0:T(8,128)S(1)}, u32[]{:S(2)}, u32[]{:S(2)}) collective-permute-start(f32[64,512]{1,0:T(8,128)S(1)} %second_product.1.refs_0_), channel_id=1, source_target_pairs={{0,1},{1,2},{2,3},{3,0},{4,5},{5,6},{6,7},{7,4},{8,9},{9,10},{10,1... | collective-permute-start | bytes 393224 | tf_op jit(solution)/shard_map/ppermute | solution.py:234
  76.9 4.9 %collective-permute-start.13 = (f32[64,64]{1,0:T(8,128)S(1)}, f32[64,64]{1,0:T(8,128)S(1)}, u32[]{:S(2)}, u32[]{:S(2)}) collective-permute-start(f32[64,64]{1,0:T(8,128)S(1)} %add.33), channel_id=1, source_target_pairs={{0,64},{4,68},{8,72},{12,76},{16,80},{20,84},{24,88},{28,92},{32,9... | collective-permute-start | bytes 49160 | tf_op jit(solution)/shard_map/ppermute | solution.py:244
  81.8 6.0 %collective-permute-start.14 = (f32[64,64]{1,0:T(8,128)S(1)}, f32[64,64]{1,0:T(8,128)S(1)}, u32[]{:S(2)}, u32[]{:S(2)}) collective-permute-start(f32[64,64]{1,0:T(8,128)S(1)} %add.34.ga_ref), channel_id=1, source_target_pairs={{0,192},{4,196},{8,200},{12,204},{16,208},{20,212},{24,216},{28,22... | collective-permute-start | bytes 49160 | tf_op jit(solution)/shard_map/ppermute | solution.py:244
  90.8 1.3 %collective-permute-start.20 = (f32[64,64]{1,0:T(8,128)S(1)}, f32[64,64]{1,0:T(8,128)S(1)}, u32[]{:S(2)}, u32[]{:S(2)}) collective-permute-start(f32[64,64]{1,0:T(8,128)S(1)} %get-tuple-element.41), channel_id=1, source_target_pairs={{0,4},{4,0},{8,12},{12,8},{16,20},{20,16},{24,28},{28,24},{32,36},... | collective-permute-start | bytes 49160 | tf_op jit(solution)/shard_map/ppermute | solution.py:244
  92.1 3.9 %collective-permute-start.21 = (f32[64,64]{1,0:T(8,128)S(1)}, f32[64,64]{1,0:T(8,128)S(1)}, u32[]{:S(2)}, u32[]{:S(2)}) collective-permute-start(f32[64,64]{1,0:T(8,128)S(1)} %add.35), channel_id=1, source_target_pairs={{0,8},{4,12},{8,0},{12,4},{16,24},{20,28},{24,16},{28,20},{32,40},... | collective-permute-start | bytes 49160 | tf_op jit(solution)/shard_map/ppermute | solution.py:244
  96.0 5.1 %collective-permute-start.22 = (f32[64,64]{1,0:T(8,128)S(1)}, f32[64,64]{1,0:T(8,128)S(1)}, u32[]{:S(2)}, u32[]{:S(2)}) collective-permute-start(f32[64,64]{1,0:T(8,128)S(1)} %add.36), channel_id=1, source_target_pairs={{0,24},{4,28},{8,16},{12,20},{16,8},{20,12},{24,0},{28,4},{32,56},... | collective-permute-start | bytes 49160 | tf_op jit(solution)/shard_map/ppermute | solution.py:244
  101.2 3.9 %collective-permute-start.23 = (f32[64,64]{1,0:T(8,128)S(1)}, f32[64,64]{1,0:T(8,128)S(1)}, u32[]{:S(2)}, u32[]{:S(2)}) collective-permute-start(f32[64,64]{1,0:T(8,128)S(1)} %add.37), channel_id=1, source_target_pairs={{0,32},{4,36},{8,40},{12,44},{16,48},{20,52},{24,56},{28,60},{32,0... | collective-permute-start | bytes 49160 | tf_op jit(solution)/shard_map/ppermute | solution.py:244
  105.1 4.9 %collective-permute-start.24 = (f32[64,64]{1,0:T(8,128)S(1)}, f32[64,64]{1,0:T(8,128)S(1)}, u32[]{:S(2)}, u32[]{:S(2)}) collective-permute-start(f32[64,64]{1,0:T(8,128)S(1)} %add.38), channel_id=1, source_target_pairs={{0,64},{4,68},{8,72},{12,76},{16,80},{20,84},{24,88},{28,92},{32,9... | collective-permute-start | bytes 49160 | tf_op jit(solution)/shard_map/ppermute | solution.py:244
  110.0 6.0 %collective-permute-start.25 = (f32[64,64]{1,0:T(8,128)S(1)}, f32[64,64]{1,0:T(8,128)S(1)}, u32[]{:S(2)}, u32[]{:S(2)}) collective-permute-start(f32[64,64]{1,0:T(8,128)S(1)} %add.39.ga_ref), channel_id=1, source_target_pairs={{0,192},{4,196},{8,200},{12,204},{16,208},{20,212},{24,216},{28,22... | collective-permute-start | bytes 49160 | tf_op jit(solution)/shard_map/ppermute | solution.py:244

commit v3 on v2

v3 whole, which is shorter than its diff:
```python
import functools
import jax
import jax.numpy as jnp
from jax import lax
from jax.experimental import pallas as pl
from jax.experimental.pallas import tpu as pltpu
from jax.sharding import PartitionSpec as P

BLK_DEV = 2
OWN, SIB, CROSS = 0, 1, -1
NOTE = 8
MB = 1024 * 1024
LOG2E = 1.4426950408889634
SCALE = LOG2E / 64.0

f32 = jnp.float32
bf16 = jnp.bfloat16
NN = (((1,), (0,)), ((), ()))
NT = (((1,), (1,)), ((), ()))


def dot(a, b, dims):
    return lax.dot_general(a, b, dims, preferred_element_type=f32)


def split2(x):
    hi = x.astype(bf16)
    return hi, (x - hi.astype(f32)).astype(bf16)


def split3(x):
    hi = x.astype(bf16)
    rest = x - hi.astype(f32)
    mid = rest.astype(bf16)
    return hi, mid, (rest - mid.astype(f32)).astype(bf16)


def listed(pairs_ref, row_block, col_block):
    hit = jnp.int32(0)
    for slot in range(pairs_ref.shape[0]):
        same = (pairs_ref[slot, 0] == row_block) & (pairs_ref[slot, 1] == col_block)
        hit = hit | same.astype(jnp.int32)
    return hit > 0


def place():
    group = lax.axis_index("rows")
    member = lax.axis_index("sub")
    return group, member


def want(pairs_ref, note_ref, group, member, members, side, j):
    mine = group * BLK_DEV + (member * BLK_DEV) // members
    other = (group + side * (1 - 2 * (group % 2))) * BLK_DEV + j
    low, high = jnp.minimum(mine, other), jnp.maximum(mine, other)
    hit = listed(pairs_ref, low, high)
    if note_ref is not None:
        note = note_ref[note_ref.shape[0] - NOTE :, 0:128]
        slot = lax.broadcasted_iota(jnp.int32, (1, 128), 1) < pairs_ref.shape[0]
        same = slot & (note[0:1, :] == low.astype(f32)) & (note[1:2, :] == high.astype(f32))
        hit = hit | (jnp.max(same.astype(f32)) > 0.5)
    return hit


def quarter_at(members, step, group, member):
    return (member + step * (1 - 2 * (group & 1))) & (members - 1)


def add_product(acc_ref, v, eh, el):
    vh, vm, vl = split3(v)
    k = vh.shape[0]
    one = dot(jnp.concatenate([vh, vm, vl], 0), eh, NN)
    two = dot(jnp.concatenate([vh, vm], 0), el, NN)
    acc_ref[...] += (one[:k] + two[:k]) + (one[k : 2 * k] + two[k:] + one[2 * k :])


def tiles_or_zeros(hit, x_ref, xah_ref, xal_ref, na_ref, v_ref, acc_ref, eh_ref, el_ref, start, rows, v_start, chunk=256):
    @pl.when(hit)
    def _():
        k = acc_ref.shape[0]
        xah, xal, na = xah_ref[...], xal_ref[...], na_ref[0:1, :]
        for c in range(rows // chunk):
            here = pl.ds(start + c * chunk, chunk)
            x = x_ref[here, :]
            nb = jnp.sum(x * x, axis=1, keepdims=True) * SCALE
            xh, xl = split2(x)
            d = dot(xh, xah, NT) + (dot(xh, xal, NT) + dot(xl, xah, NT))
            e = jnp.exp2(jnp.minimum(d - nb - na, 0.0))
            eh, el = split2(e)
            eh_ref[here, :] = eh
            el_ref[here, :] = el
            add_product(acc_ref, v_ref[:k, pl.ds(v_start + c * chunk, chunk)], eh, el)

    @pl.when(jnp.logical_not(hit))
    def _():
        here = pl.ds(start, rows)
        eh_ref[here, :] = jnp.zeros((rows, eh_ref.shape[1]), bf16)
        el_ref[here, :] = jnp.zeros((rows, el_ref.shape[1]), bf16)


def own_kernel(members, x_ref, v_ref, pairs_ref, xah_ref, xal_ref, na_ref, acc_ref, eh_ref, el_ref):
    group, member = place()
    rows = x_ref.shape[0]
    quarter = rows // members
    block = rows // BLK_DEV
    xa = x_ref[pl.ds(pl.multiple_of(member * quarter, quarter), quarter), :]
    ones = jnp.ones((8, xa.shape[1]), f32)
    na_ref[...] = lax.dot_general(ones, xa * xa, NT, precision=lax.Precision.HIGHEST, preferred_element_type=f32) * SCALE
    xah, xal = split2(xa * (2.0 * SCALE))
    xah_ref[...] = xah
    xal_ref[...] = xal
    acc_ref[...] = jnp.zeros_like(acc_ref)
    for j in range(BLK_DEV):
        hit = want(pairs_ref, None, group, member, members, OWN, j)
        tiles_or_zeros(hit, x_ref, xah_ref, xal_ref, na_ref, v_ref, acc_ref, eh_ref, el_ref, j * block, block, j * block)


def sib_kernel(members, x_ref, v_ref, pairs_ref, xah_ref, xal_ref, na_ref, in_ref, acc_ref, eh_ref, el_ref):
    group, member = place()
    block = x_ref.shape[0] // BLK_DEV
    acc_ref[...] = in_ref[...]
    for j in range(BLK_DEV):
        hit = want(pairs_ref, v_ref, group, member, members, SIB, j)
        tiles_or_zeros(hit, x_ref, xah_ref, xal_ref, na_ref, v_ref, acc_ref, eh_ref, el_ref, j * block, block, j * block)


def cross_kernel(members, step, x_ref, v_ref, pairs_ref, xah_ref, xal_ref, na_ref, in_ref, acc_ref, eh_ref, el_ref):
    group, member = place()
    rows = x_ref.shape[0]
    q = quarter_at(members, step, group, member)
    acc_ref[...] = in_ref[...]
    hit = want(pairs_ref, v_ref, group, member, members, CROSS, (q * BLK_DEV) // members)
    tiles_or_zeros(hit, x_ref, xah_ref, xal_ref, na_ref, v_ref, acc_ref, eh_ref, el_ref, 0, rows, pl.multiple_of(q * rows, rows))


def gram_sum(vh, vm, vl):
    s = jnp.concatenate([vh, vm, vl], 0)
    k = vh.shape[0]
    p = dot(s, s, NT)
    r = p[:k] + (p[k : 2 * k] + p[2 * k :])
    return r[:, :k] + (r[:, k : 2 * k] + r[:, 2 * k :])


def gather_into(full_ref, pieces, members):
    _, member = place()
    quarter = pieces[0].shape[1]
    for k, piece in enumerate(pieces):
        q = lax.rem(member - k + members, members)
        full_ref[:, pl.ds(pl.multiple_of(q * quarter, quarter), quarter)] = piece[...]


def put_gram(gram_ref, image, total):
    gram = gram_sum(*split3(image)) / total
    half = gram.shape[0] // 2
    packed = jnp.concatenate([gram[:half], gram[half:]], 1)
    for n in range(gram_ref.shape[0]):
        gram_ref[n] = packed


def take_gram(gram_ref):
    packed = gram_ref[0]
    for n in range(1, gram_ref.shape[0]):
        packed = packed + gram_ref[n]
    k = packed.shape[1] // 2
    return jnp.concatenate([packed[:, :k], packed[:, k:]], 0)


def join_kernel(members, total, *refs):
    pieces, full_ref, gram_ref = refs[:members], refs[members], refs[members + 1]
    gather_into(full_ref, pieces, members)
    put_gram(gram_ref, full_ref[...], total)


def second_kernel(members, vo_ref, vs_ref, vc_ref, *refs):
    group, member = place()
    kept, out_ref = refs[:-1], refs[-1]
    out_ref[...] = jnp.zeros_like(out_ref)
    for v_ref, eh_ref, el_ref in ((vo_ref, kept[0], kept[1]), (vs_ref, kept[2], kept[3])):
        block = v_ref.shape[1] // BLK_DEV
        for j in range(BLK_DEV):
            here = pl.ds(j * block, block)
            add_product(out_ref, v_ref[:, here], eh_ref[here, :], el_ref[here, :])
    for step in range(members):
        eh_ref, el_ref = kept[4 + 2 * step : 6 + 2 * step]
        rows = eh_ref.shape[0]
        q = quarter_at(members, step, group, member)
        add_product(out_ref, vc_ref[:, pl.ds(pl.multiple_of(q * rows, rows), rows)], eh_ref[...], el_ref[...])


def factor_inverse(gram, w=8):
    k = gram.shape[0]
    rows = lax.broadcasted_iota(jnp.int32, (k, k), 0)
    cols = lax.broadcasted_iota(jnp.int32, (k, k), 1)
    aug = jnp.concatenate([gram, (rows == cols).astype(f32)], 1)
    tall, wide = 8, 2 * k
    a = [aug[t * tall : (t + 1) * tall, :] for t in range(k // tall)]
    sub = lax.broadcasted_iota(jnp.int32, (tall, wide), 0)
    spread = lambda x: jnp.broadcast_to(x, (tall, wide))
    for start in range(0, k, w):
        t, s = start // tall, start % tall
        r = [spread(a[t][s + i : s + i + 1, :]) for i in range(w)]
        d = [[spread(a[t][s + i : s + i + 1, start + j : start + j + 1]) if j >= i else None for j in range(w)] for i in range(w)]
        later = range(t if s + w < tall else t + 1, len(a))
        c = {u: [spread(a[u][:, start + i : start + i + 1]) for i in range(w)] for u in later}
        l = [[None] * w for _ in range(w)]
        inv = [None] * w
        for i in range(w):
            p = d[i][i]
            for m in range(i):
                p = p - l[i][m] * l[i][m]
            inv[i] = lax.rsqrt(p)
            for j in range(i + 1, w):
                q = d[i][j]
                for m in range(i):
                    q = q - l[i][m] * l[j][m]
                l[j][i] = q * inv[i]
        for i in range(w):
            for m in range(i):
                r[i] = r[i] - l[i][m] * r[m]
            r[i] = r[i] * inv[i]
        for u in later:
            x = c[u]
            for i in range(w):
                for m in range(i):
                    x[i] = x[i] - l[i][m] * x[m]
                x[i] = x[i] * inv[i]
            new = a[u]
            for i in range(w):
                new = new - x[i] * r[i]
            a[u] = new if u > t else jnp.where(sub < s + w, a[u], new)
        for i in range(w):
            a[t] = jnp.where(sub == s + i, r[i], a[t])
    return jnp.concatenate(a, 0)[:, k:]


def factor_kernel(a_ref, b_ref, inv_ref):
    inv_ref[...] = factor_inverse(take_gram(a_ref) + take_gram(b_ref))


def exact(a, b):
    return lax.dot_general(a, b, NN, precision=lax.Precision.HIGHEST, preferred_element_type=f32)


def image_kernel(members, total, inv_ref, *refs):
    pieces, image_ref, gram_ref = refs[:members], refs[members], refs[members + 1]
    gather_into(image_ref, pieces, members)
    image_ref[...] = exact(inv_ref[...], image_ref[...])
    put_gram(gram_ref, image_ref[...], total)


def last_kernel(gram_ref, image_ref, out_ref):
    out_ref[...] = exact(factor_inverse(take_gram(gram_ref)), image_ref[...])


VM = pl.BlockSpec(memory_space=pltpu.VMEM)
SM = pl.BlockSpec(memory_space=pltpu.SMEM)


def call(body, specs, outs, name, limit=24, flops=10**9):
    return pl.pallas_call(
        body,
        in_specs=specs,
        out_specs=[VM] * len(outs),
        out_shape=[jax.ShapeDtypeStruct(s, t) for s, t in outs],
        compiler_params=pltpu.CompilerParams(vmem_limit_bytes=limit * MB),
        cost_estimate=pl.CostEstimate(flops=flops, bytes_accessed=MB, transcendentals=0),
        name=name,
    )


def shifted(x, axis, by):
    n = lax.axis_size(axis)
    return lax.ppermute(x, axis, [(i, (i + by) % n) for i in range(n)])


def crossed(x):
    n = lax.axis_size("rows")
    return lax.ppermute(x, "rows", [(i, (i + 2 * (i % 2) - 1) % n) for i in range(n)])


def swapped(x):
    return lax.ppermute(x, "rows", [(i, i ^ 1) for i in range(lax.axis_size("rows"))])


def passed_on(x):
    groups, members = lax.axis_size("rows"), lax.axis_size("sub")
    at = lambda g, m: g * members + m % members
    return lax.ppermute(x, ("rows", "sub"), [(at(g, m), at(g, m + 1 - 2 * (g % 2))) for g in range(groups) for m in range(members)])


NEAR = 8


def far_sets():
    groups, members = lax.axis_size("rows"), lax.axis_size("sub")
    return [[g * members + m for g in range(low, groups, NEAR)] for low in range(NEAR) for m in range(members)]


def near_sets():
    groups, members = lax.axis_size("rows"), lax.axis_size("sub")
    return [[g * members + m for g in range(base, base + NEAR)] for base in range(0, groups, NEAR) for m in range(members)]


def exchanged(x, sets):
    return lax.all_to_all(x, ("rows", "sub"), 0, 0, axis_index_groups=sets)


MASKS = (1, 2, 6, 8, 16, 48)


def pair_sums(gram):
    for mask in MASKS:
        pairs = [(i, i ^ mask) for i in range(lax.axis_size("rows"))]
        other = lax.ppermute(gram, "rows", pairs)
        gram = gram + other if mask != MASKS[-1] else (gram, other)
    return gram


def tie(x, *others):
    return lax.optimization_barrier((x, *others))[0]


def on_device(embeddings, start_vectors, pairs):
    members = lax.axis_size("sub")
    groups = lax.axis_size("rows")
    group, member = place()
    rows, width = embeddings.shape
    k = start_vectors.shape[1]
    quarter = rows // members
    total = rows * groups
    vt = start_vectors.T
    turn = 1 - 2 * (group & 1)

    def to_send(step, *after):
        q = (member - step * turn) & (members - 1)
        return lax.dynamic_slice(tie(embeddings, *after), (q * quarter, 0), (quarter, width), allow_negative_indices=False)

    first = to_send(0)
    note = jnp.pad(tie(pairs, first).T.astype(f32), ((0, NOTE - 2), (0, rows - pairs.shape[0])))
    message = jnp.concatenate([vt, note], 0)
    second = to_send(1, message)
    arrived = [crossed(first)]
    cross_v = crossed(message)
    arrived.append(crossed(second))
    sib_v = swapped(tie(message, second))
    sib_e = swapped(tie(embeddings, second))
    part = ((k, quarter), f32)
    tiles = lambda n: [((n, quarter), bf16)] * 2
    xah, xal, na, acc, *kept = call(
        functools.partial(own_kernel, members), [VM, VM, SM],
        [((quarter, width), bf16)] * 2 + [((8, quarter), f32), part] + tiles(rows), "own_tiles",
        flops=5 * 10**9)(embeddings, vt, pairs)
    acc, *t = call(
        functools.partial(sib_kernel, members), [VM, VM, SM, VM, VM, VM, VM], [part] + tiles(rows), "sib_tiles",
        flops=5 * 10**9)(sib_e, sib_v, pairs, xah, xal, na, acc)
    kept += t
    arrived.append(crossed(to_send(2, acc)))
    arrived.append(passed_on(arrived[0]))
    for step in (0, 3, 1, 2):
        acc, *t = call(
            functools.partial(cross_kernel, members, step), [VM, VM, SM, VM, VM, VM, VM], [part] + tiles(quarter), "cross_tiles",
            flops=2 * 10**9)(arrived[step], cross_v, pairs, xah, xal, na, acc)
        arrived[step] = t
    for t in arrived:
        kept += t
    pieces = [acc] + [shifted(acc, "sub", s) for s in range(1, members)]
    whole = ((k, rows), f32)
    far, near = far_sets(), near_sets()
    grams = lambda sets: ((len(sets[0]), k // 2, 2 * k), f32)
    image, gram = call(functools.partial(join_kernel, members, total), [VM] * members, [whole, ((1, k // 2, 2 * k), f32)], "join")(*pieces)
    cross_i = crossed(image)
    sib_i = swapped(image)
    grams_1 = pair_sums(gram)
    (acc2,) = call(functools.partial(second_kernel, members), [VM] * (3 + len(kept)), [part], "second_product")(
        image, sib_i, cross_i, *kept)
    pieces = [acc2] + [shifted(acc2, "sub", s) for s in range(1, members)]
    (inv,) = call(factor_kernel, [VM, VM], [((k, k), f32)], "factor")(*grams_1)
    image, gram = call(functools.partial(image_kernel, members, total), [VM] * (1 + members), [whole, grams(far)], "image")(inv, *pieces)
    gram = exchanged(gram, far)
    gram = exchanged(jnp.broadcast_to(gram.sum(0)[None], grams(near)[0]), near)
    (out,) = call(last_kernel, [VM, VM], [whole], "last")(gram, image)
    return out.T


def solution(mesh):
    return jax.shard_map(
        on_device,
        mesh=mesh,
        in_specs=(P("rows", None), P("rows", None), P("rows", None)),
        out_specs=P("rows", None),
        check_vma=False,
    )
```

time: 120 us -> 115 us (0.958)
  blocking collectives: 0 us -> 22.8 us
  waiting for transfers between devices: 51.8 us -> 32.2 us
  starting transfers between devices: 40 us -> 27 us
  other arithmetic: 0.05 us -> 2.62 us
  Pallas kernels: 24.1 us -> 26 us
    all_to_all x0 -> x2, blocking collectives: none -> 22.8 us  [exchanged(): return lax.all_to_all(x, ('rows', 'sub'), 0, 0, axis_index_groups=sets)]
    ppermute x15 -> x10, waiting for transfers between devices: 34.9 us -> 18.5 us  [the longest x6 18.5 us: pair_sums(): other = lax.ppermute(gram, 'rows', pairs)]
    ppermute x7 -> x6, waiting for transfers between devices: 12.6 us -> 5.37 us  [shifted(): return lax.ppermute(x, axis, [(i, (i + by) % n) for i in range(n)])]
    ppermute x15 -> x10, starting transfers between devices: 12.2 us -> 6.22 us  [the longest x6 4.25 us: pair_sums(): other = lax.ppermute(gram, 'rows', pairs)]
    ppermute x4 -> x5, starting transfers between devices: 18 us -> 12.9 us  [crossed(): lax.ppermute(x, 'rows', [(i, (i + 2 * (i % 2) - 1) % n) for i in range(n)])]
    ppermute x4 -> x5, waiting for transfers between devices: 4.34 us -> 8.33 us  [crossed(): lax.ppermute(x, 'rows', [(i, (i + 2 * (i % 2) - 1) % n) for i in range(n)])]
    slice x1 -> x0, local copies, waits for them, and re-layouts: 3.16 us -> none  [on_device(): embeddings[c * piece:(c + 1) * piece]]
    dynamic_slice x0 -> x3, local copies, waits for them, and re-layouts: none -> 2.91 us  [to_send(): lax.dynamic_slice(tie(embeddings, *after), (q * quarter, 0), (quarter, wi...]
  transfers between devices with their start and end apart: 26 -> 21, of which waited for: 16 -> 9; matrix products, arithmetic and copies ran while one was open for 3% -> 0% of each run, Pallas kernels for 15% -> 18%
where the time goes in v3:
time: 115 us; the launch traced here: 114 us
  waiting for transfers between devices  32.2 us (28%)
  starting transfers between devices  27 us (23%)
  Pallas kernels  26 us (23%)
  blocking collectives  22.8 us (20%)
  local copies, waits for them, and re-layouts  3.01 us (3%)
  other arithmetic  2.62 us (2%)
    all_to_all x2, blocking collectives, exchanged(): return lax.all_to_all(x, ('rows', 'sub'), 0, 0, axis_index_groups=sets)  22.8 us
    ppermute x6, waiting for transfers between devices, pair_sums(): other = lax.ppermute(gram, 'rows', pairs)  18.5 us
    ppermute x5, starting transfers between devices, crossed(): lax.ppermute(x, 'rows', [(i, (i + 2 * (i % 2) - 1) % n) for i in range(n)])  12.9 us
    ppermute x5, waiting for transfers between devices, crossed(): lax.ppermute(x, 'rows', [(i, (i + 2 * (i % 2) - 1) % n) for i in range(n)])  8.33 us
    ppermute x6, starting transfers between devices, shifted(): return lax.ppermute(x, axis, [(i, (i + by) % n) for i in range(n)])  7.89 us
    pallas_call x1, Pallas kernels, on_device(): call(functools.partial(sib_kernel, members), [VM, VM, SM, VM, VM, VM, VM]...  6.55 us
    pallas_call x1, Pallas kernels, on_device(): call(functools.partial(own_kernel, members), [VM, VM, SM], [((quarter, wi...  5.84 us
    ppermute x6, waiting for transfers between devices, shifted(): return lax.ppermute(x, axis, [(i, (i + by) % n) for i in range(n)])  5.37 us
  transfers between devices with their start and end apart: 21, of which 9 were waited for; matrix products, arithmetic and copies ran while one was open for 0% of the time, Pallas kernels for 18%

profile of v3, /device:TPU:16, one launch (start us, length us, event | category | flops | bytes accessed | tf_op | source)
XLA Modules:
  0.0 113.8 jit_solution(13733794652781575396)
XLA Ops:
  0.0 2.0 %constant_dynamic-slice_fusion.2 = f32[512,256]{1,0:T(8,128)} fusion(f32[2048,256]{1,0:T(8,128)} %x_ref.1, s32[]{:T(128)S(6)} %mul.15), kind=kLoop, calls=%fused_computation.5 | loop fusion | bytes 1048580 | tf_op jit(solution)/shard_map/dynamic_slice | solution.py:336
  2.1 0.7 convert_bitcast_fusion
  2.7 1.9 %select_maximum_fusion = f32[72,2048]{1,0:T(8,128)} fusion(f32[2,8]{1,0:T(2,128)S(1)} %convert_bitcast_fusion, f32[64,2048]{1,0:T(8,128)} %bitcast.4), kind=kLoop, calls=%fused_computation | loop fusion | flops 442368 | bytes 1114176 | tf_op jit(solution)/shard_map/concatenate | solution.py:340
  4.6 0.8 constant_dynamic-slice_fusion.1
  5.5 0.0 collective-permute-start
  5.5 0.5 collective-permute-start.1
  6.0 7.7 %collective-permute-start.5 = (f32[512,256]{1,0:T(8,128)}, f32[512,256]{1,0:T(8,128)}, u32[]{:S(2)}, u32[]{:S(2)}) collective-permute-start(f32[512,256]{1,0:T(8,128)} %constant_dynamic-slice_fusion.2), channel_id=1, source_target_pairs={{0,252},{4,8},{8,4},{12,16},{16,12},{20,24},{24,20},{28,32},{32,28... | collective-permute-start | bytes 1572872 | tf_op jit(solution)/shard_map/ppermute | solution.py:278
  13.6 0.0 collective-permute-start.4
  13.7 5.0 %collective-permute-start.3 = (f32[72,2048]{1,0:T(8,128)}, f32[72,2048]{1,0:T(8,128)S(1)}, u32[]{:S(2)}, u32[]{:S(2)}) collective-permute-start(f32[72,2048]{1,0:T(8,128)} %select_maximum_fusion), channel_id=1, source_target_pairs={{0,252},{4,8},{8,4},{12,16},{16,12},{20,24},{24,20},{28,32},{32,28... | collective-permute-start | bytes 1769480 | tf_op jit(solution)/shard_map/ppermute | solution.py:278
  18.7 0.1 copy.5.pairs_ref
  18.8 5.8 %own_tiles.1 = (bf16[512,256]{1,0:T(8,128)(2,1)S(1)}, bf16[512,256]{1,0:T(8,128)(2,1)S(1)}, f32[8,512]{1,0:T(8,128)S(1)}, f32[64,512]{1,0:T(8,128)S(1)}, bf16[20...) custom-call(f32[2048,256]{1,0:T(8,128)S(1)} %copy-done, f32[64,2048]{1,0:T(8,128)S(1)} %bitcast.5, ...), custom_call_target="tpu_custom_call" | custom-call | flops 5000000000 | bytes 1048576 | tf_op jit(solution)/shard_map/own_tiles/pallas_call | solution.py:349
  24.6 0.0 collective-permute-done.5.x_ref
  24.7 1.4 %collective-permute-start.6 = (f32[512,256]{1,0:T(8,128)}, f32[512,256]{1,0:T(8,128)S(1)}, u32[]{:S(2)}, u32[]{:S(2)}) collective-permute-start(f32[512,256]{1,0:T(8,128)} %collective-permute-done.5.x_ref), channel_id=1, source_target_pairs={{0,1},{1,2},{2,3},{3,0},{4,7},{5,4},{6,5},{7,6},{8,9},{9,10},{10,1... | collective-permute-start | bytes 1572872 | tf_op jit(solution)/shard_map/ppermute | solution.py:288
  26.0 6.5 %sib_tiles.1 = (f32[64,512]{1,0:T(8,128)S(1)}, bf16[2048,512]{1,0:T(8,128)(2,1)S(1)}, bf16[2048,512]{1,0:T(8,128)(2,1)S(1)}) custom-call(f32[2048,256]{1,0:T(8,128)} %collective-permute-done.x_ref, f32[72,2048]{1,0:T(8,128)} %collective-permute-done.1.v_ref, s32[8,2]{1,0:T(8,128)S(1)} %copy.5.pairs_ref, bf16[512,256]{1,0:T(8,128)(2,1)S(1)} %get-tuple-element.39.xah_ref, ...), custom_call_target="tpu_custom_call" | custom-call | flops 5000000000 | bytes 1048576 | tf_op jit(solution)/shard_map/sib_tiles/pallas_call | solution.py:353
  32.6 0.1 collective-permute-start.2
  32.7 1.5 %cross_tiles.4 = (f32[64,512]{1,0:T(8,128)S(1)}, bf16[512,512]{1,0:T(8,128)(2,1)S(1)}, bf16[512,512]{1,0:T(8,128)(2,1)S(1)}) custom-call(f32[512,256]{1,0:T(8,128)} %collective-permute-done.5.x_ref, f32[72,2048]{1,0:T(8,128)S(1)} %collective-permute-done.3.v_ref, s32[8,2]{1,0:T(8,128)S(1)} %copy.5.pairs_ref, bf16[512,256]{1,0:T(8,128)(2,1)S(1)} %get-tuple-element.39.xah_ref, ...), custom_call_target="tpu_custom_call" | custom-call | flops 2000000000 | bytes 1048576 | tf_op jit(solution)/shard_map/cross_tiles/pallas_call | solution.py:360
  34.2 0.8 cross_tiles.5
  35.0 0.0 collective-permute-done.4.x_ref
  35.0 1.3 %cross_tiles.6 = (f32[64,512]{1,0:T(8,128)S(1)}, bf16[512,512]{1,0:T(8,128)(2,1)S(1)}, bf16[512,512]{1,0:T(8,128)(2,1)S(1)}) custom-call(f32[512,256]{1,0:T(8,128)} %collective-permute-done.4.x_ref, f32[72,2048]{1,0:T(8,128)S(1)} %collective-permute-done.3.v_ref, s32[8,2]{1,0:T(8,128)S(1)} %copy.5.pairs_ref, bf16[512,256]{1,0:T(8,128)(2,1)S(1)} %get-tuple-element.39.xah_ref, ...), custom_call_target="tpu_custom_call" | custom-call | flops 2000000000 | bytes 1048576 | tf_op jit(solution)/shard_map/cross_tiles/pallas_call | solution.py:360
  36.3 8.3 %collective-permute-done.2.x_ref = f32[512,256]{1,0:T(8,128)S(1)} collective-permute-done((f32[512,256]{1,0:T(8,128)S(1)}, f32[512,256]{1,0:T(8,128)S(1)}, u32[]{:S(2)}, u32[]{:S(2)}) %collective-permute-start.2) | collective-permute-done | bytes 524320 | tf_op jit(solution)/shard_map/ppermute | solution.py:278
  44.6 0.8 cross_tiles.7
  45.5 0.8 collective-permute-start.9
  46.3 1.6 %collective-permute-start.8 = (f32[64,512]{1,0:T(8,128)S(1)}, f32[64,512]{1,0:T(8,128)S(1)}, u32[]{:S(2)}, u32[]{:S(2)}) collective-permute-start(f32[64,512]{1,0:T(8,128)S(1)} %get-tuple-element.48.refs_0_), channel_id=1, source_target_pairs={{0,2},{1,3},{2,0},{3,1},{4,6},{5,7},{6,4},{7,5},{8,10},{9,11},{10,... | collective-permute-start | bytes 393224 | tf_op jit(solution)/shard_map/ppermute | solution.py:273
  47.8 1.0 collective-permute-start.7
  48.8 1.7 %collective-permute-done.9.refs_3_ = f32[64,512]{1,0:T(8,128)S(1)} collective-permute-done((f32[64,512]{1,0:T(8,128)S(1)}, f32[64,512]{1,0:T(8,128)S(1)}, u32[]{:S(2)}, u32[]{:S(2)}) %collective-permute-start.9) | collective-permute-done | bytes 131104 | tf_op jit(solution)/shard_map/ppermute | solution.py:273
  50.5 2.4 %collective-permute-done.8.refs_2_ = f32[64,512]{1,0:T(8,128)S(1)} collective-permute-done((f32[64,512]{1,0:T(8,128)S(1)}, f32[64,512]{1,0:T(8,128)S(1)}, u32[]{:S(2)}, u32[]{:S(2)}) %collective-permute-start.8) | collective-permute-done | bytes 131104 | tf_op jit(solution)/shard_map/ppermute | solution.py:273
  52.9 1.3 %collective-permute-done.7.refs_1_ = f32[64,512]{1,0:T(8,128)S(1)} collective-permute-done((f32[64,512]{1,0:T(8,128)S(1)}, f32[64,512]{1,0:T(8,128)S(1)}, u32[]{:S(2)}, u32[]{:S(2)}) %collective-permute-start.7) | collective-permute-done | bytes 131104 | tf_op jit(solution)/shard_map/ppermute | solution.py:273
  54.2 0.6 join.1
  54.8 0.0 collective-permute-start.17
  54.9 0.1 collective-permute-start.16
  55.0 0.5 collective-permute-start.10
  55.5 1.4 %collective-permute-done.10 = f32[1,32,128]{2,1,0:T(8,128)S(1)} collective-permute-done((f32[1,32,128]{2,1,0:T(8,128)S(1)}, f32[1,32,128]{2,1,0:T(8,128)S(1)}, u32[]{:S(2)}, u32[]{:S(2)}) %collective-permute-start.10) | collective-permute-done | bytes 16416 | tf_op jit(solution)/shard_map/ppermute | solution.py:314
  56.9 3.7 %collective-permute-done.11 = f32[1,32,128]{2,1,0:T(8,128)S(1)} collective-permute-done((f32[1,32,128]{2,1,0:T(8,128)S(1)}, f32[1,32,128]{2,1,0:T(8,128)S(1)}, u32[]{:S(2)}, u32[]{:S(2)}) %collective-permute-start.11) | collective-permute-done | bytes 16416 | tf_op jit(solution)/shard_map/ppermute | solution.py:314
  60.6 6.5 %collective-permute-done.12 = f32[1,32,128]{2,1,0:T(8,128)S(1)} collective-permute-done((f32[1,32,128]{2,1,0:T(8,128)S(1)}, f32[1,32,128]{2,1,0:T(8,128)S(1)}, u32[]{:S(2)}, u32[]{:S(2)}) %collective-permute-start.12) | collective-permute-done | bytes 16416 | tf_op jit(solution)/shard_map/ppermute | solution.py:314
  67.2 2.2 %second_product.1.refs_0_ = f32[64,512]{1,0:T(8,128)S(1)} custom-call(f32[64,2048]{1,0:T(8,128)S(1)} %get-tuple-element.50.vo_ref, f32[64,2048]{1,0:T(8,128)S(1)} %collective-permute-done.16.vs_ref, f32[64,2048]{1,0:T(8,128)S(1)} %collective-permute-done.17.vc_ref, bf16[2048,512]{1,0:T(8,128)(2,1)S(1)} %get-tuple-element.51.refs_0_, ...), custom_call_target="tpu_custom_call" | custom-call | flops 1000000000 | bytes 1048576 | tf_op jit(solution)/shard_map/second_product/pallas_call | solution.py:374
  69.4 0.6 collective-permute-start.20
  70.0 1.6 %collective-permute-start.19 = (f32[64,512]{1,0:T(8,128)S(1)}, f32[64,512]{1,0:T(8,128)S(1)}, u32[]{:S(2)}, u32[]{:S(2)}) collective-permute-start(f32[64,512]{1,0:T(8,128)S(1)} %second_product.1.refs_0_), channel_id=1, source_target_pairs={{0,2},{1,3},{2,0},{3,1},{4,6},{5,7},{6,4},{7,5},{8,10},{9,11},{10,... | collective-permute-start | bytes 393224 | tf_op jit(solution)/shard_map/ppermute | solution.py:273
  71.6 2.3 %collective-permute-start.18 = (f32[64,512]{1,0:T(8,128)S(1)}, f32[64,512]{1,0:T(8,128)S(1)}, u32[]{:S(2)}, u32[]{:S(2)}) collective-permute-start(f32[64,512]{1,0:T(8,128)S(1)} %second_product.1.refs_0_), channel_id=1, source_target_pairs={{0,1},{1,2},{2,3},{3,0},{4,5},{5,6},{6,7},{7,4},{8,9},{9,10},{10,1... | collective-permute-start | bytes 393224 | tf_op jit(solution)/shard_map/ppermute | solution.py:273
  74.0 1.3 %collective-permute-start.14 = (f32[1,32,128]{2,1,0:T(8,128)S(1)}, f32[1,32,128]{2,1,0:T(8,128)S(1)}, u32[]{:S(2)}, u32[]{:S(2)}) collective-permute-start(f32[1,32,128]{2,1,0:T(8,128)S(1)} %add.20), channel_id=1, source_target_pairs={{0,64},{4,68},{8,72},{12,76},{16,80},{20,84},{24,88},{28,92},{32,9... | collective-permute-start | bytes 49160 | tf_op jit(solution)/shard_map/ppermute | solution.py:314
  75.3 3.4 %collective-permute-done.14 = f32[1,32,128]{2,1,0:T(8,128)S(1)} collective-permute-done((f32[1,32,128]{2,1,0:T(8,128)S(1)}, f32[1,32,128]{2,1,0:T(8,128)S(1)}, u32[]{:S(2)}, u32[]{:S(2)}) %collective-permute-start.14) | collective-permute-done | bytes 16416 | tf_op jit(solution)/shard_map/ppermute | solution.py:314
  78.7 2.4 %collective-permute-start.15 = (f32[1,32,128]{2,1,0:T(8,128)S(1)}, f32[1,32,128]{2,1,0:T(8,128)S(1)}, u32[]{:S(2)}, u32[]{:S(2)}) collective-permute-start(f32[1,32,128]{2,1,0:T(8,128)S(1)} %add.21.a_ref), channel_id=1, source_target_pairs={{0,192},{4,196},{8,200},{12,204},{16,208},{20,212},{24,216},{28,22... | collective-permute-start | bytes 49160 | tf_op jit(solution)/shard_map/ppermute | solution.py:314
  81.1 3.4 %collective-permute-done.15.b_ref = f32[1,32,128]{2,1,0:T(8,128)S(1)} collective-permute-done((f32[1,32,128]{2,1,0:T(8,128)S(1)}, f32[1,32,128]{2,1,0:T(8,128)S(1)}, u32[]{:S(2)}, u32[]{:S(2)}) %collective-permute-start.15) | collective-permute-done | bytes 16416 | tf_op jit(solution)/shard_map/ppermute | solution.py:314
  84.5 2.0 %factor.1.inv_ref = f32[64,64]{1,0:T(8,128)S(1)} custom-call(f32[1,32,128]{2,1,0:T(8,128)S(1)} %add.21.a_ref, f32[1,32,128]{2,1,0:T(8,128)S(1)} %collective-permute-done.15.b_ref), custom_call_target="tpu_custom_call" | custom-call | flops 1000000000 | bytes 1048576 | tf_op jit(solution)/shard_map/factor/pallas_call | solution.py:377
  86.5 0.0 collective-permute-done.18.refs_1_
  86.5 1.1 image.1
  87.6 13.3 %all_to_all.10 = f32[8,32,128]{2,1,0:T(8,128)S(1)} all-to-all(f32[8,32,128]{2,1,0:T(8,128)S(1)} %get-tuple-element.63), channel_id=1, replica_groups={{0,32,64,96,128,160,192,224},{1,33,65,97,129,161,193,225},{2,34,66,98,1..., dimensions={0} | all-to-all | bytes 262144 | tf_op jit(solution)/shard_map/all_to_all | solution.py:305
  101.0 9.5 %all_to_all.11.gram_ref = f32[8,32,128]{2,1,0:T(8,128)S(1)} all-to-all(f32[8,32,128]{2,1,0:T(8,128)S(1)} %broadcast_in_dim.2), channel_id=1, replica_groups={{0,4,8,12,16,20,24,28},{1,5,9,13,17,21,25,29},{2,6,10,14,18,22,26,30},{..., dimensions={0} | all-to-all | bytes 262144 | tf_op jit(solution)/shard_map/all_to_all | solution.py:305
  110.5 3.3 %last.1 = f32[64,2048]{1,0:T(8,128)} custom-call(f32[8,32,128]{2,1,0:T(8,128)S(1)} %all_to_all.11.gram_ref, f32[64,2048]{1,0:T(8,128)S(1)} %get-tuple-element.64.image_ref), custom_call_target="tpu_custom_call" | custom-call | flops 1000000000 | bytes 1048576 | tf_op jit(solution)/shard_map/last/pallas_call | solution.py:381
  (26 shorter events, 0.1 us)
Async XLA Ops:
  0.0 4.6 %copy-start = (f32[2048,256]{1,0:T(8,128)S(1)}, f32[2048,256]{1,0:T(8,128)}, u32[]{:S(2)}) copy-start(f32[2048,256]{1,0:T(8,128)} %x_ref.1) | copy-start | bytes 6291460
  0.0 18.7 %copy-start.2 = (s32[8,2]{0,1:T(2,128)S(1)}, s32[8,2]{0,1:T(2,128)}, u32[]{:S(2)}) copy-start(s32[8,2]{0,1:T(2,128)} %param.5) | copy-start | bytes 196
  0.0 18.8 %copy-start.1 = (f32[2048,64]{0,1:T(8,128)S(1)}, f32[2048,64]{0,1:T(8,128)}, u32[]{:S(2)}) copy-start(f32[2048,64]{0,1:T(8,128)} %param.4) | copy-start | bytes 1572868
  5.5 20.5 %collective-permute-start = (f32[2048,256]{1,0:T(8,128)S(1)}, f32[2048,256]{1,0:T(8,128)}, u32[]{:S(2)}, u32[]{:S(2)}) collective-permute-start(f32[2048,256]{1,0:T(8,128)S(1)} %copy-done), channel_id=1, source_target_pairs={{0,4},{4,0},{8,12},{12,8},{16,20},{20,16},{24,28},{28,24},{32,36},... | collective-permute-start | bytes 6291464 | tf_op jit(solution)/shard_map/ppermute | solution.py:282
  5.5 20.5 %collective-permute-start.1 = (f32[72,2048]{1,0:T(8,128)}, f32[72,2048]{1,0:T(8,128)}, u32[]{:S(2)}, u32[]{:S(2)}) collective-permute-start(f32[72,2048]{1,0:T(8,128)} %select_maximum_fusion), channel_id=1, source_target_pairs={{0,4},{4,0},{8,12},{12,8},{16,20},{20,16},{24,28},{28,24},{32,36},... | collective-permute-start | bytes 1769480 | tf_op jit(solution)/shard_map/ppermute | solution.py:282
  6.0 18.7 %collective-permute-start.5 = (f32[512,256]{1,0:T(8,128)}, f32[512,256]{1,0:T(8,128)}, u32[]{:S(2)}, u32[]{:S(2)}) collective-permute-start(f32[512,256]{1,0:T(8,128)} %constant_dynamic-slice_fusion.2), channel_id=1, source_target_pairs={{0,252},{4,8},{8,4},{12,16},{16,12},{20,24},{24,20},{28,32},{32,28... | collective-permute-start | bytes 1572872 | tf_op jit(solution)/shard_map/ppermute | solution.py:278
  13.6 21.4 %collective-permute-start.4 = (f32[512,256]{1,0:T(8,128)}, f32[512,256]{1,0:T(8,128)}, u32[]{:S(2)}, u32[]{:S(2)}) collective-permute-start(f32[512,256]{1,0:T(8,128)} %constant_dynamic-slice_fusion.1), channel_id=1, source_target_pairs={{0,252},{4,8},{8,4},{12,16},{16,12},{20,24},{24,20},{28,32},{32,28... | collective-permute-start | bytes 1572872 | tf_op jit(solution)/shard_map/ppermute | solution.py:278
  13.7 19.1 %collective-permute-start.3 = (f32[72,2048]{1,0:T(8,128)}, f32[72,2048]{1,0:T(8,128)S(1)}, u32[]{:S(2)}, u32[]{:S(2)}) collective-permute-start(f32[72,2048]{1,0:T(8,128)} %select_maximum_fusion), channel_id=1, source_target_pairs={{0,252},{4,8},{8,4},{12,16},{16,12},{20,24},{24,20},{28,32},{32,28... | collective-permute-start | bytes 1769480 | tf_op jit(solution)/shard_map/ppermute | solution.py:278
  24.7 9.5 %collective-permute-start.6 = (f32[512,256]{1,0:T(8,128)}, f32[512,256]{1,0:T(8,128)S(1)}, u32[]{:S(2)}, u32[]{:S(2)}) collective-permute-start(f32[512,256]{1,0:T(8,128)} %collective-permute-done.5.x_ref), channel_id=1, source_target_pairs={{0,1},{1,2},{2,3},{3,0},{4,7},{5,4},{6,5},{7,6},{8,9},{9,10},{10,1... | collective-permute-start | bytes 1572872 | tf_op jit(solution)/shard_map/ppermute | solution.py:288
  32.6 12.0 %collective-permute-start.2 = (f32[512,256]{1,0:T(8,128)S(1)}, f32[512,256]{1,0:T(8,128)S(1)}, u32[]{:S(2)}, u32[]{:S(2)}) collective-permute-start(f32[512,256]{1,0:T(8,128)S(1)} %constant_dynamic-slice_fusion), channel_id=1, source_target_pairs={{0,252},{4,8},{8,4},{12,16},{16,12},{20,24},{24,20},{28,32},{32,28... | collective-permute-start | bytes 1572872 | tf_op jit(solution)/shard_map/ppermute | solution.py:278
  45.5 5.0 %collective-permute-start.9 = (f32[64,512]{1,0:T(8,128)S(1)}, f32[64,512]{1,0:T(8,128)S(1)}, u32[]{:S(2)}, u32[]{:S(2)}) collective-permute-start(f32[64,512]{1,0:T(8,128)S(1)} %get-tuple-element.48.refs_0_), channel_id=1, source_target_pairs={{0,3},{1,0},{2,1},{3,2},{4,7},{5,4},{6,5},{7,6},{8,11},{9,8},{10,9... | collective-permute-start | bytes 393224 | tf_op jit(solution)/shard_map/ppermute | solution.py:273
  46.3 6.6 %collective-permute-start.8 = (f32[64,512]{1,0:T(8,128)S(1)}, f32[64,512]{1,0:T(8,128)S(1)}, u32[]{:S(2)}, u32[]{:S(2)}) collective-permute-start(f32[64,512]{1,0:T(8,128)S(1)} %get-tuple-element.48.refs_0_), channel_id=1, source_target_pairs={{0,2},{1,3},{2,0},{3,1},{4,6},{5,7},{6,4},{7,5},{8,10},{9,11},{10,... | collective-permute-start | bytes 393224 | tf_op jit(solution)/shard_map/ppermute | solution.py:273
  47.8 6.3 %collective-permute-start.7 = (f32[64,512]{1,0:T(8,128)S(1)}, f32[64,512]{1,0:T(8,128)S(1)}, u32[]{:S(2)}, u32[]{:S(2)}) collective-permute-start(f32[64,512]{1,0:T(8,128)S(1)} %get-tuple-element.48.refs_0_), channel_id=1, source_target_pairs={{0,1},{1,2},{2,3},{3,0},{4,5},{5,6},{6,7},{7,4},{8,9},{9,10},{10,1... | collective-permute-start | bytes 393224 | tf_op jit(solution)/shard_map/ppermute | solution.py:273
  54.8 12.3 %collective-permute-start.17 = (f32[64,2048]{1,0:T(8,128)S(1)}, f32[64,2048]{1,0:T(8,128)S(1)}, u32[]{:S(2)}, u32[]{:S(2)}) collective-permute-start(f32[64,2048]{1,0:T(8,128)S(1)} %get-tuple-element.50.vo_ref), channel_id=1, source_target_pairs={{0,252},{4,8},{8,4},{12,16},{16,12},{20,24},{24,20},{28,32},{32,28... | collective-permute-start | bytes 1572872 | tf_op jit(solution)/shard_map/ppermute | solution.py:278
  54.9 12.3 %collective-permute-start.16 = (f32[64,2048]{1,0:T(8,128)S(1)}, f32[64,2048]{1,0:T(8,128)S(1)}, u32[]{:S(2)}, u32[]{:S(2)}) collective-permute-start(f32[64,2048]{1,0:T(8,128)S(1)} %get-tuple-element.50.vo_ref), channel_id=1, source_target_pairs={{0,4},{4,0},{8,12},{12,8},{16,20},{20,16},{24,28},{28,24},{32,36},... | collective-permute-start | bytes 1572872 | tf_op jit(solution)/shard_map/ppermute | solution.py:282
  55.0 1.9 %collective-permute-start.10 = (f32[1,32,128]{2,1,0:T(8,128)S(1)}, f32[1,32,128]{2,1,0:T(8,128)S(1)}, u32[]{:S(2)}, u32[]{:S(2)}) collective-permute-start(f32[1,32,128]{2,1,0:T(8,128)S(1)} %get-tuple-element.49), channel_id=1, source_target_pairs={{0,4},{4,0},{8,12},{12,8},{16,20},{20,16},{24,28},{28,24},{32,36},... | collective-permute-start | bytes 49160 | tf_op jit(solution)/shard_map/ppermute | solution.py:314
  56.9 3.7 %collective-permute-start.11 = (f32[1,32,128]{2,1,0:T(8,128)S(1)}, f32[1,32,128]{2,1,0:T(8,128)S(1)}, u32[]{:S(2)}, u32[]{:S(2)}) collective-permute-start(f32[1,32,128]{2,1,0:T(8,128)S(1)} %add.17), channel_id=1, source_target_pairs={{0,8},{4,12},{8,0},{12,4},{16,24},{20,28},{24,16},{28,20},{32,40},... | collective-permute-start | bytes 49160 | tf_op jit(solution)/shard_map/ppermute | solution.py:314
  60.6 6.5 %collective-permute-start.12 = (f32[1,32,128]{2,1,0:T(8,128)S(1)}, f32[1,32,128]{2,1,0:T(8,128)S(1)}, u32[]{:S(2)}, u32[]{:S(2)}) collective-permute-start(f32[1,32,128]{2,1,0:T(8,128)S(1)} %add.18), channel_id=1, source_target_pairs={{0,24},{4,28},{8,16},{12,20},{16,8},{20,12},{24,0},{28,4},{32,56},... | collective-permute-start | bytes 49160 | tf_op jit(solution)/shard_map/ppermute | solution.py:314
  67.1 6.8 %collective-permute-start.13 = (f32[1,32,128]{2,1,0:T(8,128)S(1)}, f32[1,32,128]{2,1,0:T(8,128)S(1)}, u32[]{:S(2)}, u32[]{:S(2)}) collective-permute-start(f32[1,32,128]{2,1,0:T(8,128)S(1)} %add.19), channel_id=1, source_target_pairs={{0,32},{4,36},{8,40},{12,44},{16,48},{20,52},{24,56},{28,60},{32,0... | collective-permute-start | bytes 49160 | tf_op jit(solution)/shard_map/ppermute | solution.py:314
  69.4 17.1 %collective-permute-start.20 = (f32[64,512]{1,0:T(8,128)S(1)}, f32[64,512]{1,0:T(8,128)S(1)}, u32[]{:S(2)}, u32[]{:S(2)}) collective-permute-start(f32[64,512]{1,0:T(8,128)S(1)} %second_product.1.refs_0_), channel_id=1, source_target_pairs={{0,3},{1,0},{2,1},{3,2},{4,7},{5,4},{6,5},{7,6},{8,11},{9,8},{10,9... | collective-permute-start | bytes 393224 | tf_op jit(solution)/shard_map/ppermute | solution.py:273
  70.0 16.5 %collective-permute-start.19 = (f32[64,512]{1,0:T(8,128)S(1)}, f32[64,512]{1,0:T(8,128)S(1)}, u32[]{:S(2)}, u32[]{:S(2)}) collective-permute-start(f32[64,512]{1,0:T(8,128)S(1)} %second_product.1.refs_0_), channel_id=1, source_target_pairs={{0,2},{1,3},{2,0},{3,1},{4,6},{5,7},{6,4},{7,5},{8,10},{9,11},{10,... | collective-permute-start | bytes 393224 | tf_op jit(solution)/shard_map/ppermute | solution.py:273
  71.6 14.9 %collective-permute-start.18 = (f32[64,512]{1,0:T(8,128)S(1)}, f32[64,512]{1,0:T(8,128)S(1)}, u32[]{:S(2)}, u32[]{:S(2)}) collective-permute-start(f32[64,512]{1,0:T(8,128)S(1)} %second_product.1.refs_0_), channel_id=1, source_target_pairs={{0,1},{1,2},{2,3},{3,0},{4,5},{5,6},{6,7},{7,4},{8,9},{9,10},{10,1... | collective-permute-start | bytes 393224 | tf_op jit(solution)/shard_map/ppermute | solution.py:273
  74.0 4.7 %collective-permute-start.14 = (f32[1,32,128]{2,1,0:T(8,128)S(1)}, f32[1,32,128]{2,1,0:T(8,128)S(1)}, u32[]{:S(2)}, u32[]{:S(2)}) collective-permute-start(f32[1,32,128]{2,1,0:T(8,128)S(1)} %add.20), channel_id=1, source_target_pairs={{0,64},{4,68},{8,72},{12,76},{16,80},{20,84},{24,88},{28,92},{32,9... | collective-permute-start | bytes 49160 | tf_op jit(solution)/shard_map/ppermute | solution.py:314
  78.7 5.8 %collective-permute-start.15 = (f32[1,32,128]{2,1,0:T(8,128)S(1)}, f32[1,32,128]{2,1,0:T(8,128)S(1)}, u32[]{:S(2)}, u32[]{:S(2)}) collective-permute-start(f32[1,32,128]{2,1,0:T(8,128)S(1)} %add.21.a_ref), channel_id=1, source_target_pairs={{0,192},{4,196},{8,200},{12,204},{16,208},{20,212},{24,216},{28,22... | collective-permute-start | bytes 49160 | tf_op jit(solution)/shard_map/ppermute | solution.py:314

commit v4 on v3

--- a/solution.py
+++ b/solution.py
@@ -51,13 +51,12 @@
 
 def want(pairs_ref, note_ref, group, member, members, side, j):
     mine = group * BLK_DEV + (member * BLK_DEV) // members
-    other = (group + side * (1 - 2 * (group % 2))) * BLK_DEV + j
+    other = (group + side * (1 - 2 * (group & 1))) * BLK_DEV + j
     low, high = jnp.minimum(mine, other), jnp.maximum(mine, other)
     hit = listed(pairs_ref, low, high)
     if note_ref is not None:
-        note = note_ref[note_ref.shape[0] - NOTE :, 0:128]
-        slot = lax.broadcasted_iota(jnp.int32, (1, 128), 1) < pairs_ref.shape[0]
-        same = slot & (note[0:1, :] == low.astype(f32)) & (note[1:2, :] == high.astype(f32))
+        slot = lax.broadcasted_iota(jnp.int32, (1, note_ref.shape[1]), 1) < pairs_ref.shape[0]
+        same = slot & (note_ref[0:1, :] == low.astype(f32)) & (note_ref[1:2, :] == high.astype(f32))
         hit = hit | (jnp.max(same.astype(f32)) > 0.5)
     return hit
 
@@ -77,7 +76,6 @@
 def tiles_or_zeros(hit, x_ref, xah_ref, xal_ref, na_ref, v_ref, acc_ref, eh_ref, el_ref, start, rows, v_start, chunk=256):
     @pl.when(hit)
     def _():
-        k = acc_ref.shape[0]
         xah, xal, na = xah_ref[...], xal_ref[...], na_ref[0:1, :]
         for c in range(rows // chunk):
             here = pl.ds(start + c * chunk, chunk)
@@ -89,7 +87,8 @@
             eh, el = split2(e)
             eh_ref[here, :] = eh
             el_ref[here, :] = el
-            add_product(acc_ref, v_ref[:k, pl.ds(v_start + c * chunk, chunk)], eh, el)
+        here = pl.ds(start, rows)
+        add_product(acc_ref, v_ref[:, pl.ds(v_start, rows)], eh_ref[here, :], el_ref[here, :])
 
     @pl.when(jnp.logical_not(hit))
     def _():
@@ -98,7 +97,27 @@
         el_ref[here, :] = jnp.zeros((rows, el_ref.shape[1]), bf16)
 
 
-def own_kernel(members, x_ref, v_ref, pairs_ref, xah_ref, xal_ref, na_ref, acc_ref, eh_ref, el_ref):
+def cut_kernel(members, x_ref, v_ref, pairs_ref, *refs):
+    group, member = place()
+    outs, sib_ref = refs[:-1], refs[-1]
+    quarter, width = outs[1].shape
+    lane = lax.broadcasted_iota(jnp.int32, (NOTE, width), 1)
+    row = lax.broadcasted_iota(jnp.int32, (NOTE, width), 0)
+    note = jnp.zeros((NOTE, width), f32)
+    for slot in range(pairs_ref.shape[0]):
+        for c in range(2):
+            note = jnp.where((lane == slot) & (row == c), pairs_ref[slot, c].astype(f32), note)
+    k = v_ref.shape[0]
+    sib_ref[:k, :] = v_ref[...]
+    sib_ref[k:, :width] = note
+    sib_ref[k:, width:] = jnp.zeros((NOTE, sib_ref.shape[1] - width), f32)
+    outs[0][quarter:, :] = note
+    for step, out_ref in enumerate(outs):
+        q = quarter_at(members, -step, group, member)
+        out_ref[:quarter, :] = x_ref[pl.ds(pl.multiple_of(q * quarter, quarter), quarter), :]
+
+
+def chip_kernel(members, x_ref, v_ref, sib_x_ref, sib_v_ref, pairs_ref, xah_ref, xal_ref, na_ref, acc_ref, *kept):
     group, member = place()
     rows = x_ref.shape[0]
     quarter = rows // members
@@ -110,26 +129,22 @@
     xah_ref[...] = xah
     xal_ref[...] = xal
     acc_ref[...] = jnp.zeros_like(acc_ref)
-    for j in range(BLK_DEV):
-        hit = want(pairs_ref, None, group, member, members, OWN, j)
-        tiles_or_zeros(hit, x_ref, xah_ref, xal_ref, na_ref, v_ref, acc_ref, eh_ref, el_ref, j * block, block, j * block)
-
-
-def sib_kernel(members, x_ref, v_ref, pairs_ref, xah_ref, xal_ref, na_ref, in_ref, acc_ref, eh_ref, el_ref):
+    k = v_ref.shape[0]
+    for x, v, note, side, (eh_ref, el_ref) in (
+        (x_ref, v_ref, None, OWN, kept[:2]),
+        (sib_x_ref, sib_v_ref.at[:k], sib_v_ref.at[k:], SIB, kept[2:]),
+    ):
+        for j in range(BLK_DEV):
+            hit = want(pairs_ref, note, group, member, members, side, j)
+            tiles_or_zeros(hit, x, xah_ref, xal_ref, na_ref, v, acc_ref, eh_ref, el_ref, j * block, block, j * block)
+
+
+def cross_kernel(members, step, x_ref, v_ref, note_ref, pairs_ref, xah_ref, xal_ref, na_ref, in_ref, acc_ref, eh_ref, el_ref):
     group, member = place()
-    block = x_ref.shape[0] // BLK_DEV
-    acc_ref[...] = in_ref[...]
-    for j in range(BLK_DEV):
-        hit = want(pairs_ref, v_ref, group, member, members, SIB, j)
-        tiles_or_zeros(hit, x_ref, xah_ref, xal_ref, na_ref, v_ref, acc_ref, eh_ref, el_ref, j * block, block, j * block)
-
-
-def cross_kernel(members, step, x_ref, v_ref, pairs_ref, xah_ref, xal_ref, na_ref, in_ref, acc_ref, eh_ref, el_ref):
-    group, member = place()
-    rows = x_ref.shape[0]
+    rows = eh_ref.shape[0]
     q = quarter_at(members, step, group, member)
     acc_ref[...] = in_ref[...]
-    hit = want(pairs_ref, v_ref, group, member, members, CROSS, (q * BLK_DEV) // members)
+    hit = want(pairs_ref, note_ref, group, member, members, CROSS, (q * BLK_DEV) // members)
     tiles_or_zeros(hit, x_ref, xah_ref, xal_ref, na_ref, v_ref, acc_ref, eh_ref, el_ref, 0, rows, pl.multiple_of(q * rows, rows))
 
 
@@ -256,7 +271,7 @@
 SM = pl.BlockSpec(memory_space=pltpu.SMEM)
 
 
-def call(body, specs, outs, name, limit=24, flops=10**9):
+def call(body, specs, outs, name, limit=16, flops=10**9):
     return pl.pallas_call(
         body,
         in_specs=specs,
@@ -323,43 +338,33 @@
 def on_device(embeddings, start_vectors, pairs):
     members = lax.axis_size("sub")
     groups = lax.axis_size("rows")
-    group, member = place()
     rows, width = embeddings.shape
     k = start_vectors.shape[1]
     quarter = rows // members
     total = rows * groups
     vt = start_vectors.T
-    turn = 1 - 2 * (group & 1)
-
-    def to_send(step, *after):
-        q = (member - step * turn) & (members - 1)
-        return lax.dynamic_slice(tie(embeddings, *after), (q * quarter, 0), (quarter, width), allow_negative_indices=False)
-
-    first = to_send(0)
-    note = jnp.pad(tie(pairs, first).T.astype(f32), ((0, NOTE - 2), (0, rows - pairs.shape[0])))
-    message = jnp.concatenate([vt, note], 0)
-    second = to_send(1, message)
+    cross_v = crossed(vt)
+    piece = ((quarter, width), f32)
+    first, second, third, sib_v = call(
+        functools.partial(cut_kernel, members), [VM, VM, SM],
+        [((quarter + NOTE, width), f32), piece, piece, ((k + NOTE, rows), f32)], "cut", flops=10**6)(embeddings, vt, pairs)
     arrived = [crossed(first)]
-    cross_v = crossed(message)
+    sib_e = swapped(embeddings)
+    sib_v = swapped(sib_v)
     arrived.append(crossed(second))
-    sib_v = swapped(tie(message, second))
-    sib_e = swapped(tie(embeddings, second))
+    arrived.append(crossed(third))
+    cross_note = arrived[0][quarter:]
     part = ((k, quarter), f32)
     tiles = lambda n: [((n, quarter), bf16)] * 2
     xah, xal, na, acc, *kept = call(
-        functools.partial(own_kernel, members), [VM, VM, SM],
-        [((quarter, width), bf16)] * 2 + [((8, quarter), f32), part] + tiles(rows), "own_tiles",
-        flops=5 * 10**9)(embeddings, vt, pairs)
-    acc, *t = call(
-        functools.partial(sib_kernel, members), [VM, VM, SM, VM, VM, VM, VM], [part] + tiles(rows), "sib_tiles",
-        flops=5 * 10**9)(sib_e, sib_v, pairs, xah, xal, na, acc)
-    kept += t
-    arrived.append(crossed(to_send(2, acc)))
+        functools.partial(chip_kernel, members), [VM, VM, VM, VM, SM],
+        [((quarter, width), bf16)] * 2 + [((8, quarter), f32), part] + tiles(rows) + tiles(rows), "chip_tiles",
+        flops=10**10)(embeddings, vt, sib_e, sib_v, pairs)
     arrived.append(passed_on(arrived[0]))
     for step in (0, 3, 1, 2):
         acc, *t = call(
-            functools.partial(cross_kernel, members, step), [VM, VM, SM, VM, VM, VM, VM], [part] + tiles(quarter), "cross_tiles",
-            flops=2 * 10**9)(arrived[step], cross_v, pairs, xah, xal, na, acc)
+            functools.partial(cross_kernel, members, step), [VM, VM, VM, SM, VM, VM, VM, VM], [part] + tiles(quarter), "cross_tiles",
+            flops=2 * 10**9)(arrived[step], cross_v, cross_note, pairs, xah, xal, na, acc)
         arrived[step] = t
     for t in arrived:
         kept += t

time: 115 us -> 112 us (0.974)
  starting transfers between devices: 27 us -> 38.8 us
  waiting for transfers between devices: 32.2 us -> 23.7 us
  Pallas kernels: 26 us -> 21.1 us
  other arithmetic: 2.62 us -> 0.03 us
  blocking collectives: 22.8 us -> 24.7 us
    ppermute x5, starting transfers between devices: 12.9 us -> 22.2 us  [crossed(): lax.ppermute(x, 'rows', [(i, (i + 2 * (i % 2) - 1) % n) for i in range(n)])]
    ppermute x5, waiting for transfers between devices: 8.33 us -> 2.94 us  [crossed(): lax.ppermute(x, 'rows', [(i, (i + 2 * (i % 2) - 1) % n) for i in range(n)])]
    pallas_call x6, Pallas kernels: 16.7 us -> 11.8 us  [the longest x1 7.59 us: on_device(): call(functools.partial(chip_kernel, members), [VM, VM, VM, VM, SM], [((qu...]
    unnamed x7 -> x5, local copies, waits for them, and re-layouts: 0.09 us -> 3.38 us
    dynamic_slice x3 -> x0, local copies, waits for them, and re-layouts: 2.91 us -> none  [to_send(): lax.dynamic_slice(tie(embeddings, *after), (q * quarter, 0), (quarter, wi...]
    ppermute x6, waiting for transfers between devices: 18.5 us -> 15.8 us  [pair_sums(): other = lax.ppermute(gram, 'rows', pairs)]
    concatenate x1 -> x0, other arithmetic: 1.91 us -> none  [on_device(): message = jnp.concatenate([vt, note], 0)]
    all_to_all x2, blocking collectives: 22.8 us -> 24.7 us  [exchanged(): return lax.all_to_all(x, ('rows', 'sub'), 0, 0, axis_index_groups=sets)]
  transfers between devices with their start and end apart: 21 -> 21, of which waited for: 9 -> 10; matrix products, arithmetic and copies ran while one was open for 0% -> 1% of each run, Pallas kernels for 18% -> 14%
where the time goes in v4:
time: 112 us
  starting transfers between devices  38.8 us (35%)
  blocking collectives  24.7 us (22%)
  waiting for transfers between devices  23.7 us (21%)
  Pallas kernels  21.1 us (19%)
  local copies, waits for them, and re-layouts  3.4 us (3%)
    all_to_all x2, blocking collectives, exchanged(): return lax.all_to_all(x, ('rows', 'sub'), 0, 0, axis_index_groups=sets)  24.7 us
    ppermute x5, starting transfers between devices, crossed(): lax.ppermute(x, 'rows', [(i, (i + 2 * (i % 2) - 1) % n) for i in range(n)])  22.2 us
    ppermute x6, waiting for transfers between devices, pair_sums(): other = lax.ppermute(gram, 'rows', pairs)  15.8 us
    ppermute x6, starting transfers between devices, shifted(): return lax.ppermute(x, axis, [(i, (i + by) % n) for i in range(n)])  9.04 us
    pallas_call x1, Pallas kernels, on_device(): call(functools.partial(chip_kernel, members), [VM, VM, VM, VM, SM], [((qu...  7.59 us
    ppermute x6, starting transfers between devices, pair_sums(): other = lax.ppermute(gram, 'rows', pairs)  5.66 us
    ppermute x6, waiting for transfers between devices, shifted(): return lax.ppermute(x, axis, [(i, (i + by) % n) for i in range(n)])  4.99 us
    pallas_call x4, Pallas kernels, on_device(): call(functools.partial(cross_kernel, members, step), [VM, VM, VM, SM, VM,...  3.45 us
  transfers between devices with their start and end apart: 21, of which 10 were waited for; matrix products, arithmetic and copies ran while one was open for 1% of the time, Pallas kernels for 14%

profile of v4, /device:TPU:16, one launch (start us, length us, event | category | flops | bytes accessed | tf_op | source)
XLA Modules:
  0.0 111.8 jit_solution(18418261890428074042)
XLA Ops:
  0.0 0.0 collective-permute-start.3
  0.0 0.8 copy.4.pairs_ref
  0.8 1.6 %copy-done = f32[2048,256]{1,0:T(8,128)S(1)} copy-done((f32[2048,256]{1,0:T(8,128)S(1)}, f32[2048,256]{1,0:T(8,128)}, u32[]{:S(2)}) %copy-start) | copy-done | bytes 2097176
  2.4 1.0 copy-done.1
  3.4 0.7 cut.1
  4.1 0.6 collective-permute-start.4
  4.7 7.8 %collective-permute-start.2 = (f32[520,256]{1,0:T(8,128)S(1)}, f32[520,256]{1,0:T(8,128)S(1)}, u32[]{:S(2)}, u32[]{:S(2)}) collective-permute-start(f32[520,256]{1,0:T(8,128)S(1)} %get-tuple-element.34), channel_id=1, source_target_pairs={{0,252},{4,8},{8,4},{12,16},{16,12},{20,24},{24,20},{28,32},{32,28... | collective-permute-start | bytes 1597448 | tf_op jit(solution)/shard_map/ppermute | solution.py:293
  12.5 0.1 collective-permute-start.1
  12.6 5.0 %collective-permute-start = (f32[512,256]{1,0:T(8,128)S(1)}, f32[512,256]{1,0:T(8,128)S(1)}, u32[]{:S(2)}, u32[]{:S(2)}) collective-permute-start(f32[512,256]{1,0:T(8,128)S(1)} %get-tuple-element.33), channel_id=1, source_target_pairs={{0,252},{4,8},{8,4},{12,16},{16,12},{20,24},{24,20},{28,32},{32,28... | collective-permute-start | bytes 1572872 | tf_op jit(solution)/shard_map/ppermute | solution.py:293
  17.6 1.9 %collective-permute-done.2.x_ref = f32[520,256]{1,0:T(8,128)S(1)} collective-permute-done((f32[520,256]{1,0:T(8,128)S(1)}, f32[520,256]{1,0:T(8,128)S(1)}, u32[]{:S(2)}, u32[]{:S(2)}) %collective-permute-start.2) | collective-permute-done | bytes 532512 | tf_op jit(solution)/shard_map/ppermute | solution.py:293
  19.4 5.1 %collective-permute-start.5 = (f32[512,256]{1,0:T(8,128)S(1)}, f32[512,256]{1,0:T(8,128)S(1)}, u32[]{:S(2)}, u32[]{:S(2)}) collective-permute-start(f32[512,256]{1,0:T(8,128)S(1)} %get-tuple-element.39), channel_id=1, source_target_pairs={{0,252},{4,8},{8,4},{12,16},{16,12},{20,24},{24,20},{28,32},{32,28... | collective-permute-start | bytes 1572872 | tf_op jit(solution)/shard_map/ppermute | solution.py:293
  24.5 0.0 collective-permute-done.4.sib_v_ref
  24.5 1.3 %collective-permute-start.6 = (f32[520,256]{1,0:T(8,128)S(1)}, f32[520,256]{1,0:T(8,128)S(1)}, u32[]{:S(2)}, u32[]{:S(2)}) collective-permute-start(f32[520,256]{1,0:T(8,128)S(1)} %collective-permute-done.2.x_ref), channel_id=1, source_target_pairs={{0,1},{1,2},{2,3},{3,0},{4,7},{5,4},{6,5},{7,6},{8,9},{9,10},{10,1... | collective-permute-start | bytes 1597448 | tf_op jit(solution)/shard_map/ppermute | solution.py:303
  25.8 0.0 collective-permute-done.3.sib_x_ref
  25.8 7.6 %chip_tiles.1 = (bf16[512,256]{1,0:T(8,128)(2,1)S(1)}, bf16[512,256]{1,0:T(8,128)(2,1)S(1)}, f32[8,512]{1,0:T(8,128)S(1)}, f32[64,512]{1,0:T(8,128)S(1)}, bf16[2...) custom-call(f32[2048,256]{1,0:T(8,128)S(1)} %copy-done, ...), custom_call_target="tpu_custom_call" | custom-call | flops 10000000000 | bytes 1048576 | tf_op jit(solution)/shard_map/chip_tiles/pallas_call | solution.py:359
  33.4 0.8 cross_tiles.4
  34.2 1.0 cross_tiles.5
  35.2 1.0 collective-permute-done.5.x_ref
  36.3 0.8 cross_tiles.6
  37.1 0.8 cross_tiles.7
  38.0 0.5 collective-permute-start.9
  38.5 2.9 %collective-permute-start.8 = (f32[64,512]{1,0:T(8,128)S(1)}, f32[64,512]{1,0:T(8,128)S(1)}, u32[]{:S(2)}, u32[]{:S(2)}) collective-permute-start(f32[64,512]{1,0:T(8,128)S(1)} %get-tuple-element.44.refs_0_), channel_id=1, source_target_pairs={{0,2},{1,3},{2,0},{3,1},{4,6},{5,7},{6,4},{7,5},{8,10},{9,11},{10,... | collective-permute-start | bytes 393224 | tf_op jit(solution)/shard_map/ppermute | solution.py:288
  41.4 0.0 collective-permute-start.7
  41.4 1.6 %collective-permute-done.9.refs_3_ = f32[64,512]{1,0:T(8,128)S(1)} collective-permute-done((f32[64,512]{1,0:T(8,128)S(1)}, f32[64,512]{1,0:T(8,128)S(1)}, u32[]{:S(2)}, u32[]{:S(2)}) %collective-permute-start.9) | collective-permute-done | bytes 131104 | tf_op jit(solution)/shard_map/ppermute | solution.py:288
  43.0 2.0 %collective-permute-done.8.refs_2_ = f32[64,512]{1,0:T(8,128)S(1)} collective-permute-done((f32[64,512]{1,0:T(8,128)S(1)}, f32[64,512]{1,0:T(8,128)S(1)}, u32[]{:S(2)}, u32[]{:S(2)}) %collective-permute-start.8) | collective-permute-done | bytes 131104 | tf_op jit(solution)/shard_map/ppermute | solution.py:288
  45.0 1.4 %collective-permute-done.7.refs_1_ = f32[64,512]{1,0:T(8,128)S(1)} collective-permute-done((f32[64,512]{1,0:T(8,128)S(1)}, f32[64,512]{1,0:T(8,128)S(1)}, u32[]{:S(2)}, u32[]{:S(2)}) %collective-permute-start.7) | collective-permute-done | bytes 131104 | tf_op jit(solution)/shard_map/ppermute | solution.py:288
  46.4 0.6 join.1
  47.0 4.3 %collective-permute-start.17 = (f32[64,2048]{1,0:T(8,128)S(1)}, f32[64,2048]{1,0:T(8,128)S(1)}, u32[]{:S(2)}, u32[]{:S(2)}) collective-permute-start(f32[64,2048]{1,0:T(8,128)S(1)} %get-tuple-element.46.vo_ref), channel_id=1, source_target_pairs={{0,252},{4,8},{8,4},{12,16},{16,12},{20,24},{24,20},{28,32},{32,28... | collective-permute-start | bytes 1572872 | tf_op jit(solution)/shard_map/ppermute | solution.py:293
  51.3 0.5 collective-permute-start.10
  51.8 1.4 %collective-permute-done.10 = f32[1,32,128]{2,1,0:T(8,128)S(1)} collective-permute-done((f32[1,32,128]{2,1,0:T(8,128)S(1)}, f32[1,32,128]{2,1,0:T(8,128)S(1)}, u32[]{:S(2)}, u32[]{:S(2)}) %collective-permute-start.10) | collective-permute-done | bytes 16416 | tf_op jit(solution)/shard_map/ppermute | solution.py:329
  53.3 0.0 collective-permute-start.11
  53.3 3.7 %collective-permute-done.11 = f32[1,32,128]{2,1,0:T(8,128)S(1)} collective-permute-done((f32[1,32,128]{2,1,0:T(8,128)S(1)}, f32[1,32,128]{2,1,0:T(8,128)S(1)}, u32[]{:S(2)}, u32[]{:S(2)}) %collective-permute-start.11) | collective-permute-done | bytes 16416 | tf_op jit(solution)/shard_map/ppermute | solution.py:329
  57.0 4.9 %collective-permute-done.12 = f32[1,32,128]{2,1,0:T(8,128)S(1)} collective-permute-done((f32[1,32,128]{2,1,0:T(8,128)S(1)}, f32[1,32,128]{2,1,0:T(8,128)S(1)}, u32[]{:S(2)}, u32[]{:S(2)}) %collective-permute-start.12) | collective-permute-done | bytes 16416 | tf_op jit(solution)/shard_map/ppermute | solution.py:329
  62.0 0.0 collective-permute-done.17.vc_ref
  62.0 2.3 %second_product.1.refs_0_ = f32[64,512]{1,0:T(8,128)S(1)} custom-call(f32[64,2048]{1,0:T(8,128)S(1)} %get-tuple-element.46.vo_ref, f32[64,2048]{1,0:T(8,128)S(1)} %collective-permute-done.16.vs_ref, f32[64,2048]{1,0:T(8,128)S(1)} %collective-permute-done.17.vc_ref, bf16[2048,512]{1,0:T(8,128)(2,1)S(1)} %get-tuple-element.47.refs_0_, ...), custom_call_target="tpu_custom_call" | custom-call | flops 1000000000 | bytes 1048576 | tf_op jit(solution)/shard_map/second_product/pallas_call | solution.py:379
  64.2 0.6 collective-permute-start.20
  64.9 2.9 %collective-permute-start.19 = (f32[64,512]{1,0:T(8,128)S(1)}, f32[64,512]{1,0:T(8,128)S(1)}, u32[]{:S(2)}, u32[]{:S(2)}) collective-permute-start(f32[64,512]{1,0:T(8,128)S(1)} %second_product.1.refs_0_), channel_id=1, source_target_pairs={{0,2},{1,3},{2,0},{3,1},{4,6},{5,7},{6,4},{7,5},{8,10},{9,11},{10,... | collective-permute-start | bytes 393224 | tf_op jit(solution)/shard_map/ppermute | solution.py:288
  67.8 2.1 %collective-permute-start.18 = (f32[64,512]{1,0:T(8,128)S(1)}, f32[64,512]{1,0:T(8,128)S(1)}, u32[]{:S(2)}, u32[]{:S(2)}) collective-permute-start(f32[64,512]{1,0:T(8,128)S(1)} %second_product.1.refs_0_), channel_id=1, source_target_pairs={{0,1},{1,2},{2,3},{3,0},{4,5},{5,6},{6,7},{7,4},{8,9},{9,10},{10,1... | collective-permute-start | bytes 393224 | tf_op jit(solution)/shard_map/ppermute | solution.py:288
  69.9 1.6 %collective-permute-start.14 = (f32[1,32,128]{2,1,0:T(8,128)S(1)}, f32[1,32,128]{2,1,0:T(8,128)S(1)}, u32[]{:S(2)}, u32[]{:S(2)}) collective-permute-start(f32[1,32,128]{2,1,0:T(8,128)S(1)} %add.18), channel_id=1, source_target_pairs={{0,64},{4,68},{8,72},{12,76},{16,80},{20,84},{24,88},{28,92},{32,9... | collective-permute-start | bytes 49160 | tf_op jit(solution)/shard_map/ppermute | solution.py:329
  71.5 3.3 %collective-permute-done.14 = f32[1,32,128]{2,1,0:T(8,128)S(1)} collective-permute-done((f32[1,32,128]{2,1,0:T(8,128)S(1)}, f32[1,32,128]{2,1,0:T(8,128)S(1)}, u32[]{:S(2)}, u32[]{:S(2)}) %collective-permute-start.14) | collective-permute-done | bytes 16416 | tf_op jit(solution)/shard_map/ppermute | solution.py:329
  74.8 3.5 %collective-permute-start.15 = (f32[1,32,128]{2,1,0:T(8,128)S(1)}, f32[1,32,128]{2,1,0:T(8,128)S(1)}, u32[]{:S(2)}, u32[]{:S(2)}) collective-permute-start(f32[1,32,128]{2,1,0:T(8,128)S(1)} %add.19.a_ref), channel_id=1, source_target_pairs={{0,192},{4,196},{8,200},{12,204},{16,208},{20,212},{24,216},{28,22... | collective-permute-start | bytes 49160 | tf_op jit(solution)/shard_map/ppermute | solution.py:329
  78.3 2.3 %collective-permute-done.15.b_ref = f32[1,32,128]{2,1,0:T(8,128)S(1)} collective-permute-done((f32[1,32,128]{2,1,0:T(8,128)S(1)}, f32[1,32,128]{2,1,0:T(8,128)S(1)}, u32[]{:S(2)}, u32[]{:S(2)}) %collective-permute-start.15) | collective-permute-done | bytes 16416 | tf_op jit(solution)/shard_map/ppermute | solution.py:329
  80.7 2.0 %factor.1.inv_ref = f32[64,64]{1,0:T(8,128)S(1)} custom-call(f32[1,32,128]{2,1,0:T(8,128)S(1)} %add.19.a_ref, f32[1,32,128]{2,1,0:T(8,128)S(1)} %collective-permute-done.15.b_ref), custom_call_target="tpu_custom_call" | custom-call | flops 1000000000 | bytes 1048576 | tf_op jit(solution)/shard_map/factor/pallas_call | solution.py:382
  82.7 0.0 collective-permute-done.18.refs_1_
  82.7 1.1 image.1
  83.8 14.4 %all_to_all.10 = f32[8,32,128]{2,1,0:T(8,128)S(1)} all-to-all(f32[8,32,128]{2,1,0:T(8,128)S(1)} %get-tuple-element.59), channel_id=1, replica_groups={{0,32,64,96,128,160,192,224},{1,33,65,97,129,161,193,225},{2,34,66,98,1..., dimensions={0} | all-to-all | bytes 262144 | tf_op jit(solution)/shard_map/all_to_all | solution.py:320
  98.2 10.3 %all_to_all.11.gram_ref = f32[8,32,128]{2,1,0:T(8,128)S(1)} all-to-all(f32[8,32,128]{2,1,0:T(8,128)S(1)} %broadcast_in_dim.2), channel_id=1, replica_groups={{0,4,8,12,16,20,24,28},{1,5,9,13,17,21,25,29},{2,6,10,14,18,22,26,30},{..., dimensions={0} | all-to-all | bytes 262144 | tf_op jit(solution)/shard_map/all_to_all | solution.py:320
  108.5 3.3 %last.1 = f32[64,2048]{1,0:T(8,128)} custom-call(f32[8,32,128]{2,1,0:T(8,128)S(1)} %all_to_all.11.gram_ref, f32[64,2048]{1,0:T(8,128)S(1)} %get-tuple-element.60.image_ref), custom_call_target="tpu_custom_call" | custom-call | flops 1000000000 | bytes 1048576 | tf_op jit(solution)/shard_map/last/pallas_call | solution.py:386
  (20 shorter events, 0.1 us)
Async XLA Ops:
  0.0 25.8 %collective-permute-start.3 = (f32[2048,256]{1,0:T(8,128)}, f32[2048,256]{1,0:T(8,128)S(1)}, u32[]{:S(2)}, u32[]{:S(2)}) collective-permute-start(f32[2048,256]{1,0:T(8,128)} %x_ref.3), channel_id=1, source_target_pairs={{0,4},{4,0},{8,12},{12,8},{16,20},{20,16},{24,28},{28,24},{32,36},... | collective-permute-start | bytes 6291464 | tf_op jit(solution)/shard_map/ppermute | solution.py:297
  0.8 1.6 %copy-start = (f32[2048,256]{1,0:T(8,128)S(1)}, f32[2048,256]{1,0:T(8,128)}, u32[]{:S(2)}) copy-start(f32[2048,256]{1,0:T(8,128)} %x_ref.3) | copy-start | bytes 6291460
  2.3 1.0 copy-start.1
  4.1 20.4 %collective-permute-start.4 = (f32[72,2048]{1,0:T(8,128)S(1)}, f32[72,2048]{1,0:T(8,128)S(1)}, u32[]{:S(2)}, u32[]{:S(2)}) collective-permute-start(f32[72,2048]{1,0:T(8,128)S(1)} %get-tuple-element.35), channel_id=1, source_target_pairs={{0,4},{4,0},{8,12},{12,8},{16,20},{20,16},{24,28},{28,24},{32,36},... | collective-permute-start | bytes 1769480 | tf_op jit(solution)/shard_map/ppermute | solution.py:297
  4.7 14.7 %collective-permute-start.2 = (f32[520,256]{1,0:T(8,128)S(1)}, f32[520,256]{1,0:T(8,128)S(1)}, u32[]{:S(2)}, u32[]{:S(2)}) collective-permute-start(f32[520,256]{1,0:T(8,128)S(1)} %get-tuple-element.34), channel_id=1, source_target_pairs={{0,252},{4,8},{8,4},{12,16},{16,12},{20,24},{24,20},{28,32},{32,28... | collective-permute-start | bytes 1597448 | tf_op jit(solution)/shard_map/ppermute | solution.py:293
  12.5 20.9 %collective-permute-start.1 = (f32[64,2048]{1,0:T(8,128)S(1)}, f32[64,2048]{1,0:T(8,128)S(1)}, u32[]{:S(2)}, u32[]{:S(2)}) collective-permute-start(f32[64,2048]{1,0:T(8,128)S(1)} %bitcast.3), channel_id=1, source_target_pairs={{0,252},{4,8},{8,4},{12,16},{16,12},{20,24},{24,20},{28,32},{32,28... | collective-permute-start | bytes 1572872 | tf_op jit(solution)/shard_map/ppermute | solution.py:293
  12.6 24.5 %collective-permute-start = (f32[512,256]{1,0:T(8,128)S(1)}, f32[512,256]{1,0:T(8,128)S(1)}, u32[]{:S(2)}, u32[]{:S(2)}) collective-permute-start(f32[512,256]{1,0:T(8,128)S(1)} %get-tuple-element.33), channel_id=1, source_target_pairs={{0,252},{4,8},{8,4},{12,16},{16,12},{20,24},{24,20},{28,32},{32,28... | collective-permute-start | bytes 1572872 | tf_op jit(solution)/shard_map/ppermute | solution.py:293
  19.4 16.9 %collective-permute-start.5 = (f32[512,256]{1,0:T(8,128)S(1)}, f32[512,256]{1,0:T(8,128)S(1)}, u32[]{:S(2)}, u32[]{:S(2)}) collective-permute-start(f32[512,256]{1,0:T(8,128)S(1)} %get-tuple-element.39), channel_id=1, source_target_pairs={{0,252},{4,8},{8,4},{12,16},{16,12},{20,24},{24,20},{28,32},{32,28... | collective-permute-start | bytes 1572872 | tf_op jit(solution)/shard_map/ppermute | solution.py:293
  24.5 9.7 %collective-permute-start.6 = (f32[520,256]{1,0:T(8,128)S(1)}, f32[520,256]{1,0:T(8,128)S(1)}, u32[]{:S(2)}, u32[]{:S(2)}) collective-permute-start(f32[520,256]{1,0:T(8,128)S(1)} %collective-permute-done.2.x_ref), channel_id=1, source_target_pairs={{0,1},{1,2},{2,3},{3,0},{4,7},{5,4},{6,5},{7,6},{8,9},{9,10},{10,1... | collective-permute-start | bytes 1597448 | tf_op jit(solution)/shard_map/ppermute | solution.py:303
  38.0 5.0 %collective-permute-start.9 = (f32[64,512]{1,0:T(8,128)S(1)}, f32[64,512]{1,0:T(8,128)S(1)}, u32[]{:S(2)}, u32[]{:S(2)}) collective-permute-start(f32[64,512]{1,0:T(8,128)S(1)} %get-tuple-element.44.refs_0_), channel_id=1, source_target_pairs={{0,3},{1,0},{2,1},{3,2},{4,7},{5,4},{6,5},{7,6},{8,11},{9,8},{10,9... | collective-permute-start | bytes 393224 | tf_op jit(solution)/shard_map/ppermute | solution.py:288
  38.5 6.5 %collective-permute-start.8 = (f32[64,512]{1,0:T(8,128)S(1)}, f32[64,512]{1,0:T(8,128)S(1)}, u32[]{:S(2)}, u32[]{:S(2)}) collective-permute-start(f32[64,512]{1,0:T(8,128)S(1)} %get-tuple-element.44.refs_0_), channel_id=1, source_target_pairs={{0,2},{1,3},{2,0},{3,1},{4,6},{5,7},{6,4},{7,5},{8,10},{9,11},{10,... | collective-permute-start | bytes 393224 | tf_op jit(solution)/shard_map/ppermute | solution.py:288
  41.4 5.0 %collective-permute-start.7 = (f32[64,512]{1,0:T(8,128)S(1)}, f32[64,512]{1,0:T(8,128)S(1)}, u32[]{:S(2)}, u32[]{:S(2)}) collective-permute-start(f32[64,512]{1,0:T(8,128)S(1)} %get-tuple-element.44.refs_0_), channel_id=1, source_target_pairs={{0,1},{1,2},{2,3},{3,0},{4,5},{5,6},{6,7},{7,4},{8,9},{9,10},{10,1... | collective-permute-start | bytes 393224 | tf_op jit(solution)/shard_map/ppermute | solution.py:288
  47.0 15.0 %collective-permute-start.17 = (f32[64,2048]{1,0:T(8,128)S(1)}, f32[64,2048]{1,0:T(8,128)S(1)}, u32[]{:S(2)}, u32[]{:S(2)}) collective-permute-start(f32[64,2048]{1,0:T(8,128)S(1)} %get-tuple-element.46.vo_ref), channel_id=1, source_target_pairs={{0,252},{4,8},{8,4},{12,16},{16,12},{20,24},{24,20},{28,32},{32,28... | collective-permute-start | bytes 1572872 | tf_op jit(solution)/shard_map/ppermute | solution.py:293
  51.3 10.7 %collective-permute-start.16 = (f32[64,2048]{1,0:T(8,128)S(1)}, f32[64,2048]{1,0:T(8,128)S(1)}, u32[]{:S(2)}, u32[]{:S(2)}) collective-permute-start(f32[64,2048]{1,0:T(8,128)S(1)} %get-tuple-element.46.vo_ref), channel_id=1, source_target_pairs={{0,4},{4,0},{8,12},{12,8},{16,20},{20,16},{24,28},{28,24},{32,36},... | collective-permute-start | bytes 1572872 | tf_op jit(solution)/shard_map/ppermute | solution.py:297
  51.3 1.9 %collective-permute-start.10 = (f32[1,32,128]{2,1,0:T(8,128)S(1)}, f32[1,32,128]{2,1,0:T(8,128)S(1)}, u32[]{:S(2)}, u32[]{:S(2)}) collective-permute-start(f32[1,32,128]{2,1,0:T(8,128)S(1)} %get-tuple-element.45), channel_id=1, source_target_pairs={{0,4},{4,0},{8,12},{12,8},{16,20},{20,16},{24,28},{28,24},{32,36},... | collective-permute-start | bytes 49160 | tf_op jit(solution)/shard_map/ppermute | solution.py:329
  53.3 3.7 %collective-permute-start.11 = (f32[1,32,128]{2,1,0:T(8,128)S(1)}, f32[1,32,128]{2,1,0:T(8,128)S(1)}, u32[]{:S(2)}, u32[]{:S(2)}) collective-permute-start(f32[1,32,128]{2,1,0:T(8,128)S(1)} %add.15), channel_id=1, source_target_pairs={{0,8},{4,12},{8,0},{12,4},{16,24},{20,28},{24,16},{28,20},{32,40},... | collective-permute-start | bytes 49160 | tf_op jit(solution)/shard_map/ppermute | solution.py:329
  57.0 4.9 %collective-permute-start.12 = (f32[1,32,128]{2,1,0:T(8,128)S(1)}, f32[1,32,128]{2,1,0:T(8,128)S(1)}, u32[]{:S(2)}, u32[]{:S(2)}) collective-permute-start(f32[1,32,128]{2,1,0:T(8,128)S(1)} %add.16), channel_id=1, source_target_pairs={{0,24},{4,28},{8,16},{12,20},{16,8},{20,12},{24,0},{28,4},{32,56},... | collective-permute-start | bytes 49160 | tf_op jit(solution)/shard_map/ppermute | solution.py:329
  62.0 7.9 %collective-permute-start.13 = (f32[1,32,128]{2,1,0:T(8,128)S(1)}, f32[1,32,128]{2,1,0:T(8,128)S(1)}, u32[]{:S(2)}, u32[]{:S(2)}) collective-permute-start(f32[1,32,128]{2,1,0:T(8,128)S(1)} %add.17), channel_id=1, source_target_pairs={{0,32},{4,36},{8,40},{12,44},{16,48},{20,52},{24,56},{28,60},{32,0... | collective-permute-start | bytes 49160 | tf_op jit(solution)/shard_map/ppermute | solution.py:329
  64.2 18.4 %collective-permute-start.20 = (f32[64,512]{1,0:T(8,128)S(1)}, f32[64,512]{1,0:T(8,128)S(1)}, u32[]{:S(2)}, u32[]{:S(2)}) collective-permute-start(f32[64,512]{1,0:T(8,128)S(1)} %second_product.1.refs_0_), channel_id=1, source_target_pairs={{0,3},{1,0},{2,1},{3,2},{4,7},{5,4},{6,5},{7,6},{8,11},{9,8},{10,9... | collective-permute-start | bytes 393224 | tf_op jit(solution)/shard_map/ppermute | solution.py:288
  64.9 17.8 %collective-permute-start.19 = (f32[64,512]{1,0:T(8,128)S(1)}, f32[64,512]{1,0:T(8,128)S(1)}, u32[]{:S(2)}, u32[]{:S(2)}) collective-permute-start(f32[64,512]{1,0:T(8,128)S(1)} %second_product.1.refs_0_), channel_id=1, source_target_pairs={{0,2},{1,3},{2,0},{3,1},{4,6},{5,7},{6,4},{7,5},{8,10},{9,11},{10,... | collective-permute-start | bytes 393224 | tf_op jit(solution)/shard_map/ppermute | solution.py:288
  67.8 14.9 %collective-permute-start.18 = (f32[64,512]{1,0:T(8,128)S(1)}, f32[64,512]{1,0:T(8,128)S(1)}, u32[]{:S(2)}, u32[]{:S(2)}) collective-permute-start(f32[64,512]{1,0:T(8,128)S(1)} %second_product.1.refs_0_), channel_id=1, source_target_pairs={{0,1},{1,2},{2,3},{3,0},{4,5},{5,6},{6,7},{7,4},{8,9},{9,10},{10,1... | collective-permute-start | bytes 393224 | tf_op jit(solution)/shard_map/ppermute | solution.py:288
  69.9 4.9 %collective-permute-start.14 = (f32[1,32,128]{2,1,0:T(8,128)S(1)}, f32[1,32,128]{2,1,0:T(8,128)S(1)}, u32[]{:S(2)}, u32[]{:S(2)}) collective-permute-start(f32[1,32,128]{2,1,0:T(8,128)S(1)} %add.18), channel_id=1, source_target_pairs={{0,64},{4,68},{8,72},{12,76},{16,80},{20,84},{24,88},{28,92},{32,9... | collective-permute-start | bytes 49160 | tf_op jit(solution)/shard_map/ppermute | solution.py:329
  74.8 5.8 %collective-permute-start.15 = (f32[1,32,128]{2,1,0:T(8,128)S(1)}, f32[1,32,128]{2,1,0:T(8,128)S(1)}, u32[]{:S(2)}, u32[]{:S(2)}) collective-permute-start(f32[1,32,128]{2,1,0:T(8,128)S(1)} %add.19.a_ref), channel_id=1, source_target_pairs={{0,192},{4,196},{8,200},{12,204},{16,208},{20,212},{24,216},{28,22... | collective-permute-start | bytes 49160 | tf_op jit(solution)/shard_map/ppermute | solution.py:329

commit v5 on v4

--- a/solution.py
+++ b/solution.py
@@ -37,8 +37,8 @@
 
 def listed(pairs_ref, row_block, col_block):
     hit = jnp.int32(0)
-    for slot in range(pairs_ref.shape[0]):
-        same = (pairs_ref[slot, 0] == row_block) & (pairs_ref[slot, 1] == col_block)
+    for slot in range(pairs_ref.shape[1]):
+        same = (pairs_ref[0, slot] == row_block) & (pairs_ref[1, slot] == col_block)
         hit = hit | same.astype(jnp.int32)
     return hit > 0
 
@@ -55,7 +55,7 @@
     low, high = jnp.minimum(mine, other), jnp.maximum(mine, other)
     hit = listed(pairs_ref, low, high)
     if note_ref is not None:
-        slot = lax.broadcasted_iota(jnp.int32, (1, note_ref.shape[1]), 1) < pairs_ref.shape[0]
+        slot = lax.broadcasted_iota(jnp.int32, (1, note_ref.shape[1]), 1) < pairs_ref.shape[1]
         same = slot & (note_ref[0:1, :] == low.astype(f32)) & (note_ref[1:2, :] == high.astype(f32))
         hit = hit | (jnp.max(same.astype(f32)) > 0.5)
     return hit
@@ -99,22 +99,27 @@
 
 def cut_kernel(members, x_ref, v_ref, pairs_ref, *refs):
     group, member = place()
-    outs, sib_ref = refs[:-1], refs[-1]
+    outs, sib_ref, sems = refs[:-2], refs[-2], refs[-1]
     quarter, width = outs[1].shape
+    k = v_ref.shape[0]
+    copies = [pltpu.make_async_copy(v_ref, sib_ref.at[pl.ds(0, k)], sems.at[len(outs)])]
+    for step, out_ref in enumerate(outs):
+        q = quarter_at(members, -step, group, member)
+        source = x_ref.at[pl.ds(pl.multiple_of(q * quarter, quarter), quarter)]
+        copies.append(pltpu.make_async_copy(source, out_ref.at[pl.ds(0, quarter)], sems.at[step]))
+    for copy in copies:
+        copy.start()
     lane = lax.broadcasted_iota(jnp.int32, (NOTE, width), 1)
     row = lax.broadcasted_iota(jnp.int32, (NOTE, width), 0)
     note = jnp.zeros((NOTE, width), f32)
-    for slot in range(pairs_ref.shape[0]):
+    for slot in range(pairs_ref.shape[1]):
         for c in range(2):
-            note = jnp.where((lane == slot) & (row == c), pairs_ref[slot, c].astype(f32), note)
-    k = v_ref.shape[0]
-    sib_ref[:k, :] = v_ref[...]
+            note = jnp.where((lane == slot) & (row == c), pairs_ref[c, slot].astype(f32), note)
     sib_ref[k:, :width] = note
     sib_ref[k:, width:] = jnp.zeros((NOTE, sib_ref.shape[1] - width), f32)
     outs[0][quarter:, :] = note
-    for step, out_ref in enumerate(outs):
-        q = quarter_at(members, -step, group, member)
-        out_ref[:quarter, :] = x_ref[pl.ds(pl.multiple_of(q * quarter, quarter), quarter), :]
+    for copy in copies:
+        copy.wait()
 
 
 def chip_kernel(members, x_ref, v_ref, sib_x_ref, sib_v_ref, pairs_ref, xah_ref, xal_ref, na_ref, acc_ref, *kept):
@@ -269,13 +274,15 @@
 
 VM = pl.BlockSpec(memory_space=pltpu.VMEM)
 SM = pl.BlockSpec(memory_space=pltpu.SMEM)
-
-
-def call(body, specs, outs, name, limit=16, flops=10**9):
+HB = pl.BlockSpec(memory_space=pltpu.HBM)
+
+
+def call(body, specs, outs, name, limit=16, flops=10**9, scratch=()):
     return pl.pallas_call(
         body,
         in_specs=specs,
         out_specs=[VM] * len(outs),
+        scratch_shapes=scratch,
         out_shape=[jax.ShapeDtypeStruct(s, t) for s, t in outs],
         compiler_params=pltpu.CompilerParams(vmem_limit_bytes=limit * MB),
         cost_estimate=pl.CostEstimate(flops=flops, bytes_accessed=MB, transcendentals=0),
@@ -343,11 +350,14 @@
     quarter = rows // members
     total = rows * groups
     vt = start_vectors.T
+    pairs = pairs.T
     cross_v = crossed(vt)
     piece = ((quarter, width), f32)
     first, second, third, sib_v = call(
-        functools.partial(cut_kernel, members), [VM, VM, SM],
-        [((quarter + NOTE, width), f32), piece, piece, ((k + NOTE, rows), f32)], "cut", flops=10**6)(embeddings, vt, pairs)
+        functools.partial(cut_kernel, members), [HB, HB, SM],
+        [((quarter + NOTE, width), f32), piece, piece, ((k + NOTE, rows), f32)], "cut", flops=10**6,
+        scratch=[pltpu.SemaphoreType.DMA((4,))])(
+        *(pltpu.with_memory_space_constraint(a, pltpu.HBM) for a in (embeddings, vt)), pairs)
     arrived = [crossed(first)]
     sib_e = swapped(embeddings)
     sib_v = swapped(sib_v)

time: 112 us -> 110 us (0.982)
  blocking collectives: 24.7 us -> 21.8 us
  local copies, waits for them, and re-layouts: 3.4 us -> 0.85 us
  waiting for transfers between devices: 23.7 us -> 26 us
  Pallas kernels: 21.1 us -> 22.3 us
    all_to_all x2, blocking collectives: 24.7 us -> 21.8 us  [exchanged(): return lax.all_to_all(x, ('rows', 'sub'), 0, 0, axis_index_groups=sets)]
    unnamed x5 -> x6, local copies, waits for them, and re-layouts: 3.38 us -> 0.84 us
    ppermute x6, waiting for transfers between devices: 15.8 us -> 18 us  [pair_sums(): other = lax.ppermute(gram, 'rows', pairs)]
    ppermute x6, starting transfers between devices: 5.66 us -> 3.39 us  [pair_sums(): other = lax.ppermute(gram, 'rows', pairs)]
    ppermute x5, starting transfers between devices: 22.2 us -> 24.3 us  [crossed(): lax.ppermute(x, 'rows', [(i, (i + 2 * (i % 2) - 1) % n) for i in range(n)])]
    pallas_call x1, Pallas kernels: 0.74 us -> 2.1 us  [on_device(): call(functools.partial(cut_kernel, members), [HB, HB, SM], [((quarter + N...]
  transfers between devices with their start and end apart: 21 -> 21, of which waited for: 10 -> 10; matrix products, arithmetic and copies ran while one was open for 1% -> 0% of each run, Pallas kernels for 14% -> 15%
where the time goes in v5:
time: 110 us
  starting transfers between devices  38.5 us (35%)
  waiting for transfers between devices  26 us (24%)
  Pallas kernels  22.3 us (20%)
  blocking collectives  21.8 us (20%)
    ppermute x5, starting transfers between devices, crossed(): lax.ppermute(x, 'rows', [(i, (i + 2 * (i % 2) - 1) % n) for i in range(n)])  24.3 us
    all_to_all x2, blocking collectives, exchanged(): return lax.all_to_all(x, ('rows', 'sub'), 0, 0, axis_index_groups=sets)  21.8 us
    ppermute x6, waiting for transfers between devices, pair_sums(): other = lax.ppermute(gram, 'rows', pairs)  18 us
    ppermute x6, starting transfers between devices, shifted(): return lax.ppermute(x, axis, [(i, (i + by) % n) for i in range(n)])  9.06 us
    pallas_call x1, Pallas kernels, on_device(): call(functools.partial(chip_kernel, members), [VM, VM, VM, VM, SM], [((qu...  7.61 us
    ppermute x6, waiting for transfers between devices, shifted(): return lax.ppermute(x, axis, [(i, (i + by) % n) for i in range(n)])  4.99 us
    ppermute x6, starting transfers between devices, pair_sums(): other = lax.ppermute(gram, 'rows', pairs)  3.39 us
    pallas_call x1, Pallas kernels, on_device(): out, = call(last_kernel, [VM, VM], [whole], 'last')(gram, image)  3.34 us
  transfers between devices with their start and end apart: 21, of which 10 were waited for; matrix products, arithmetic and copies ran while one was open for 0% of the time, Pallas kernels for 15%

profile of v5, /device:TPU:16, one launch (start us, length us, event | category | flops | bytes accessed | tf_op | source)
XLA Modules:
  0.0 109.7 jit_solution(10629789598504381471)
XLA Ops:
  0.0 0.0 collective-permute-start.3
  0.0 0.8 copy-done.2
  0.9 2.1 %cut.1 = (f32[520,256]{1,0:T(8,128)S(1)}, f32[512,256]{1,0:T(8,128)S(1)}, f32[512,256]{1,0:T(8,128)S(1)}, f32[72,2048]{1,0:T(8,128)S(1)}) custom-call(f32[2048,256]{1,0:T(8,128)} %x_ref.3, f32[64,2048]{1,0:T(8,128)} %bitcast.3, s32[2,8]{1,0:T(2,128)S(1)} %bitcast.6), custom_call_target="tpu_custom_call" | custom-call | flops 1000000 | bytes 1048576 | tf_op jit(solution)/shard_map/cut/pallas_call | solution.py:356
  3.0 0.5 collective-permute-start.4
  3.4 7.8 %collective-permute-start.2 = (f32[520,256]{1,0:T(8,128)S(1)}, f32[520,256]{1,0:T(8,128)S(1)}, u32[]{:S(2)}, u32[]{:S(2)}) collective-permute-start(f32[520,256]{1,0:T(8,128)S(1)} %get-tuple-element.34), channel_id=1, source_target_pairs={{0,252},{4,8},{8,4},{12,16},{16,12},{20,24},{24,20},{28,32},{32,28... | collective-permute-start | bytes 1597448 | tf_op jit(solution)/shard_map/ppermute | solution.py:300
  11.2 0.1 collective-permute-start.1
  11.3 5.0 %collective-permute-start = (f32[512,256]{1,0:T(8,128)S(1)}, f32[512,256]{1,0:T(8,128)S(1)}, u32[]{:S(2)}, u32[]{:S(2)}) collective-permute-start(f32[512,256]{1,0:T(8,128)S(1)} %get-tuple-element.33), channel_id=1, source_target_pairs={{0,252},{4,8},{8,4},{12,16},{16,12},{20,24},{24,20},{28,32},{32,28... | collective-permute-start | bytes 1572872 | tf_op jit(solution)/shard_map/ppermute | solution.py:300
  16.3 1.9 %collective-permute-done.2.x_ref = f32[520,256]{1,0:T(8,128)S(1)} collective-permute-done((f32[520,256]{1,0:T(8,128)S(1)}, f32[520,256]{1,0:T(8,128)S(1)}, u32[]{:S(2)}, u32[]{:S(2)}) %collective-permute-start.2) | collective-permute-done | bytes 532512 | tf_op jit(solution)/shard_map/ppermute | solution.py:300
  18.2 5.1 %collective-permute-start.5 = (f32[512,256]{1,0:T(8,128)S(1)}, f32[512,256]{1,0:T(8,128)S(1)}, u32[]{:S(2)}, u32[]{:S(2)}) collective-permute-start(f32[512,256]{1,0:T(8,128)S(1)} %get-tuple-element.39), channel_id=1, source_target_pairs={{0,252},{4,8},{8,4},{12,16},{16,12},{20,24},{24,20},{28,32},{32,28... | collective-permute-start | bytes 1572872 | tf_op jit(solution)/shard_map/ppermute | solution.py:300
  23.2 1.3 %collective-permute-start.6 = (f32[520,256]{1,0:T(8,128)S(1)}, f32[520,256]{1,0:T(8,128)S(1)}, u32[]{:S(2)}, u32[]{:S(2)}) collective-permute-start(f32[520,256]{1,0:T(8,128)S(1)} %collective-permute-done.2.x_ref), channel_id=1, source_target_pairs={{0,1},{1,2},{2,3},{3,0},{4,7},{5,4},{6,5},{7,6},{8,9},{9,10},{10,1... | collective-permute-start | bytes 1597448 | tf_op jit(solution)/shard_map/ppermute | solution.py:310
  24.5 0.0 collective-permute-done.3.sib_x_ref
  24.5 7.6 %chip_tiles.1 = (bf16[512,256]{1,0:T(8,128)(2,1)S(1)}, bf16[512,256]{1,0:T(8,128)(2,1)S(1)}, f32[8,512]{1,0:T(8,128)S(1)}, f32[64,512]{1,0:T(8,128)S(1)}, bf16[2...) custom-call(f32[2048,256]{1,0:T(8,128)S(1)} %copy-done, ...), custom_call_target="tpu_custom_call" | custom-call | flops 10000000000 | bytes 1048576 | tf_op jit(solution)/shard_map/chip_tiles/pallas_call | solution.py:369
  32.1 0.0 collective-permute-done.1.v_ref
  32.2 0.8 cross_tiles.4
  32.9 0.9 cross_tiles.5
  33.9 1.1 %collective-permute-done.5.x_ref = f32[512,256]{1,0:T(8,128)S(1)} collective-permute-done((f32[512,256]{1,0:T(8,128)S(1)}, f32[512,256]{1,0:T(8,128)S(1)}, u32[]{:S(2)}, u32[]{:S(2)}) %collective-permute-start.5) | collective-permute-done | bytes 524320 | tf_op jit(solution)/shard_map/ppermute | solution.py:300
  35.0 0.8 cross_tiles.6
  35.8 0.8 cross_tiles.7
  36.6 0.5 collective-permute-start.9
  37.1 2.9 %collective-permute-start.8 = (f32[64,512]{1,0:T(8,128)S(1)}, f32[64,512]{1,0:T(8,128)S(1)}, u32[]{:S(2)}, u32[]{:S(2)}) collective-permute-start(f32[64,512]{1,0:T(8,128)S(1)} %get-tuple-element.44.refs_0_), channel_id=1, source_target_pairs={{0,2},{1,3},{2,0},{3,1},{4,6},{5,7},{6,4},{7,5},{8,10},{9,11},{10,... | collective-permute-start | bytes 393224 | tf_op jit(solution)/shard_map/ppermute | solution.py:295
  40.0 0.0 collective-permute-start.7
  40.0 1.6 %collective-permute-done.9.refs_3_ = f32[64,512]{1,0:T(8,128)S(1)} collective-permute-done((f32[64,512]{1,0:T(8,128)S(1)}, f32[64,512]{1,0:T(8,128)S(1)}, u32[]{:S(2)}, u32[]{:S(2)}) %collective-permute-start.9) | collective-permute-done | bytes 131104 | tf_op jit(solution)/shard_map/ppermute | solution.py:295
  41.6 2.0 %collective-permute-done.8.refs_2_ = f32[64,512]{1,0:T(8,128)S(1)} collective-permute-done((f32[64,512]{1,0:T(8,128)S(1)}, f32[64,512]{1,0:T(8,128)S(1)}, u32[]{:S(2)}, u32[]{:S(2)}) %collective-permute-start.8) | collective-permute-done | bytes 131104 | tf_op jit(solution)/shard_map/ppermute | solution.py:295
  43.6 1.4 %collective-permute-done.7.refs_1_ = f32[64,512]{1,0:T(8,128)S(1)} collective-permute-done((f32[64,512]{1,0:T(8,128)S(1)}, f32[64,512]{1,0:T(8,128)S(1)}, u32[]{:S(2)}, u32[]{:S(2)}) %collective-permute-start.7) | collective-permute-done | bytes 131104 | tf_op jit(solution)/shard_map/ppermute | solution.py:295
  45.0 0.7 join.1
  45.6 6.4 %collective-permute-start.17 = (f32[64,2048]{1,0:T(8,128)S(1)}, f32[64,2048]{1,0:T(8,128)S(1)}, u32[]{:S(2)}, u32[]{:S(2)}) collective-permute-start(f32[64,2048]{1,0:T(8,128)S(1)} %get-tuple-element.46.vo_ref), channel_id=1, source_target_pairs={{0,252},{4,8},{8,4},{12,16},{16,12},{20,24},{24,20},{28,32},{32,28... | collective-permute-start | bytes 1572872 | tf_op jit(solution)/shard_map/ppermute | solution.py:300
  52.0 0.5 collective-permute-start.10
  52.5 1.4 %collective-permute-done.10 = f32[1,32,128]{2,1,0:T(8,128)S(1)} collective-permute-done((f32[1,32,128]{2,1,0:T(8,128)S(1)}, f32[1,32,128]{2,1,0:T(8,128)S(1)}, u32[]{:S(2)}, u32[]{:S(2)}) %collective-permute-start.10) | collective-permute-done | bytes 16416 | tf_op jit(solution)/shard_map/ppermute | solution.py:336
  54.0 3.7 %collective-permute-done.11 = f32[1,32,128]{2,1,0:T(8,128)S(1)} collective-permute-done((f32[1,32,128]{2,1,0:T(8,128)S(1)}, f32[1,32,128]{2,1,0:T(8,128)S(1)}, u32[]{:S(2)}, u32[]{:S(2)}) %collective-permute-start.11) | collective-permute-done | bytes 16416 | tf_op jit(solution)/shard_map/ppermute | solution.py:336
  57.7 0.0 collective-permute-start.12
  57.7 4.9 %collective-permute-done.12 = f32[1,32,128]{2,1,0:T(8,128)S(1)} collective-permute-done((f32[1,32,128]{2,1,0:T(8,128)S(1)}, f32[1,32,128]{2,1,0:T(8,128)S(1)}, u32[]{:S(2)}, u32[]{:S(2)}) %collective-permute-start.12) | collective-permute-done | bytes 16416 | tf_op jit(solution)/shard_map/ppermute | solution.py:336
  62.7 0.0 collective-permute-start.13
  62.7 0.0 collective-permute-done.17.vc_ref
  62.7 2.3 %second_product.1.refs_0_ = f32[64,512]{1,0:T(8,128)S(1)} custom-call(f32[64,2048]{1,0:T(8,128)S(1)} %get-tuple-element.46.vo_ref, f32[64,2048]{1,0:T(8,128)S(1)} %collective-permute-done.16.vs_ref, f32[64,2048]{1,0:T(8,128)S(1)} %collective-permute-done.17.vc_ref, bf16[2048,512]{1,0:T(8,128)(2,1)S(1)} %get-tuple-element.47.refs_0_, ...), custom_call_target="tpu_custom_call" | custom-call | flops 1000000000 | bytes 1048576 | tf_op jit(solution)/shard_map/second_product/pallas_call | solution.py:389
  65.0 0.4 collective-permute-start.20
  65.3 2.9 %collective-permute-start.19 = (f32[64,512]{1,0:T(8,128)S(1)}, f32[64,512]{1,0:T(8,128)S(1)}, u32[]{:S(2)}, u32[]{:S(2)}) collective-permute-start(f32[64,512]{1,0:T(8,128)S(1)} %second_product.1.refs_0_), channel_id=1, source_target_pairs={{0,2},{1,3},{2,0},{3,1},{4,6},{5,7},{6,4},{7,5},{8,10},{9,11},{10,... | collective-permute-start | bytes 393224 | tf_op jit(solution)/shard_map/ppermute | solution.py:295
  68.3 2.3 %collective-permute-start.18 = (f32[64,512]{1,0:T(8,128)S(1)}, f32[64,512]{1,0:T(8,128)S(1)}, u32[]{:S(2)}, u32[]{:S(2)}) collective-permute-start(f32[64,512]{1,0:T(8,128)S(1)} %second_product.1.refs_0_), channel_id=1, source_target_pairs={{0,1},{1,2},{2,3},{3,0},{4,5},{5,6},{6,7},{7,4},{8,9},{9,10},{10,1... | collective-permute-start | bytes 393224 | tf_op jit(solution)/shard_map/ppermute | solution.py:295
  70.6 0.0 collective-permute-done.13
  70.6 0.5 collective-permute-start.14
  71.1 4.4 %collective-permute-done.14 = f32[1,32,128]{2,1,0:T(8,128)S(1)} collective-permute-done((f32[1,32,128]{2,1,0:T(8,128)S(1)}, f32[1,32,128]{2,1,0:T(8,128)S(1)}, u32[]{:S(2)}, u32[]{:S(2)}) %collective-permute-start.14) | collective-permute-done | bytes 16416 | tf_op jit(solution)/shard_map/ppermute | solution.py:336
  75.5 2.4 %collective-permute-start.15 = (f32[1,32,128]{2,1,0:T(8,128)S(1)}, f32[1,32,128]{2,1,0:T(8,128)S(1)}, u32[]{:S(2)}, u32[]{:S(2)}) collective-permute-start(f32[1,32,128]{2,1,0:T(8,128)S(1)} %add.19.a_ref), channel_id=1, source_target_pairs={{0,192},{4,196},{8,200},{12,204},{16,208},{20,212},{24,216},{28,22... | collective-permute-start | bytes 49160 | tf_op jit(solution)/shard_map/ppermute | solution.py:336
  77.9 3.5 %collective-permute-done.15.b_ref = f32[1,32,128]{2,1,0:T(8,128)S(1)} collective-permute-done((f32[1,32,128]{2,1,0:T(8,128)S(1)}, f32[1,32,128]{2,1,0:T(8,128)S(1)}, u32[]{:S(2)}, u32[]{:S(2)}) %collective-permute-start.15) | collective-permute-done | bytes 16416 | tf_op jit(solution)/shard_map/ppermute | solution.py:336
  81.4 2.0 %factor.1.inv_ref = f32[64,64]{1,0:T(8,128)S(1)} custom-call(f32[1,32,128]{2,1,0:T(8,128)S(1)} %add.19.a_ref, f32[1,32,128]{2,1,0:T(8,128)S(1)} %collective-permute-done.15.b_ref), custom_call_target="tpu_custom_call" | custom-call | flops 1000000000 | bytes 1048576 | tf_op jit(solution)/shard_map/factor/pallas_call | solution.py:392
  83.4 0.0 collective-permute-done.18.refs_1_
  83.4 1.1 image.1
  84.5 12.5 %all_to_all.10 = f32[8,32,128]{2,1,0:T(8,128)S(1)} all-to-all(f32[8,32,128]{2,1,0:T(8,128)S(1)} %get-tuple-element.59), channel_id=1, replica_groups={{0,32,64,96,128,160,192,224},{1,33,65,97,129,161,193,225},{2,34,66,98,1..., dimensions={0} | all-to-all | bytes 262144 | tf_op jit(solution)/shard_map/all_to_all | solution.py:327
  97.1 9.2 %all_to_all.11.gram_ref = f32[8,32,128]{2,1,0:T(8,128)S(1)} all-to-all(f32[8,32,128]{2,1,0:T(8,128)S(1)} %broadcast_in_dim.2), channel_id=1, replica_groups={{0,4,8,12,16,20,24,28},{1,5,9,13,17,21,25,29},{2,6,10,14,18,22,26,30},{..., dimensions={0} | all-to-all | bytes 262144 | tf_op jit(solution)/shard_map/all_to_all | solution.py:327
  106.3 3.3 %last.1 = f32[64,2048]{1,0:T(8,128)} custom-call(f32[8,32,128]{2,1,0:T(8,128)S(1)} %all_to_all.11.gram_ref, f32[64,2048]{1,0:T(8,128)S(1)} %get-tuple-element.60.image_ref), custom_call_target="tpu_custom_call" | custom-call | flops 1000000000 | bytes 1048576 | tf_op jit(solution)/shard_map/last/pallas_call | solution.py:396
  (21 shorter events, 0.1 us)
Async XLA Ops:
  0.0 24.5 %copy-start = (f32[2048,256]{1,0:T(8,128)S(1)}, f32[2048,256]{1,0:T(8,128)}, u32[]{:S(2)}) copy-start(f32[2048,256]{1,0:T(8,128)} %x_ref.3) | copy-start | bytes 6291460
  0.0 11.2 %copy-start.1 = (f32[2048,64]{0,1:T(8,128)S(1)}, f32[2048,64]{0,1:T(8,128)}, u32[]{:S(2)}) copy-start(f32[2048,64]{0,1:T(8,128)} %param.4) | copy-start | bytes 1572868
  0.0 24.5 %collective-permute-start.3 = (f32[2048,256]{1,0:T(8,128)}, f32[2048,256]{1,0:T(8,128)S(1)}, u32[]{:S(2)}, u32[]{:S(2)}) collective-permute-start(f32[2048,256]{1,0:T(8,128)} %x_ref.3), channel_id=1, source_target_pairs={{0,4},{4,0},{8,12},{12,8},{16,20},{20,16},{24,28},{28,24},{32,36},... | collective-permute-start | bytes 6291464 | tf_op jit(solution)/shard_map/ppermute | solution.py:304
  0.0 0.8 copy-start.2
  3.0 20.3 %collective-permute-start.4 = (f32[72,2048]{1,0:T(8,128)S(1)}, f32[72,2048]{1,0:T(8,128)S(1)}, u32[]{:S(2)}, u32[]{:S(2)}) collective-permute-start(f32[72,2048]{1,0:T(8,128)S(1)} %get-tuple-element.35), channel_id=1, source_target_pairs={{0,4},{4,0},{8,12},{12,8},{16,20},{20,16},{24,28},{28,24},{32,36},... | collective-permute-start | bytes 1769480 | tf_op jit(solution)/shard_map/ppermute | solution.py:304
  3.4 14.7 %collective-permute-start.2 = (f32[520,256]{1,0:T(8,128)S(1)}, f32[520,256]{1,0:T(8,128)S(1)}, u32[]{:S(2)}, u32[]{:S(2)}) collective-permute-start(f32[520,256]{1,0:T(8,128)S(1)} %get-tuple-element.34), channel_id=1, source_target_pairs={{0,252},{4,8},{8,4},{12,16},{16,12},{20,24},{24,20},{28,32},{32,28... | collective-permute-start | bytes 1597448 | tf_op jit(solution)/shard_map/ppermute | solution.py:300
  11.2 20.9 %collective-permute-start.1 = (f32[64,2048]{1,0:T(8,128)S(1)}, f32[64,2048]{1,0:T(8,128)S(1)}, u32[]{:S(2)}, u32[]{:S(2)}) collective-permute-start(f32[64,2048]{1,0:T(8,128)S(1)} %bitcast.4), channel_id=1, source_target_pairs={{0,252},{4,8},{8,4},{12,16},{16,12},{20,24},{24,20},{28,32},{32,28... | collective-permute-start | bytes 1572872 | tf_op jit(solution)/shard_map/ppermute | solution.py:300
  11.3 24.5 %collective-permute-start = (f32[512,256]{1,0:T(8,128)S(1)}, f32[512,256]{1,0:T(8,128)S(1)}, u32[]{:S(2)}, u32[]{:S(2)}) collective-permute-start(f32[512,256]{1,0:T(8,128)S(1)} %get-tuple-element.33), channel_id=1, source_target_pairs={{0,252},{4,8},{8,4},{12,16},{16,12},{20,24},{24,20},{28,32},{32,28... | collective-permute-start | bytes 1572872 | tf_op jit(solution)/shard_map/ppermute | solution.py:300
  18.2 16.9 %collective-permute-start.5 = (f32[512,256]{1,0:T(8,128)S(1)}, f32[512,256]{1,0:T(8,128)S(1)}, u32[]{:S(2)}, u32[]{:S(2)}) collective-permute-start(f32[512,256]{1,0:T(8,128)S(1)} %get-tuple-element.39), channel_id=1, source_target_pairs={{0,252},{4,8},{8,4},{12,16},{16,12},{20,24},{24,20},{28,32},{32,28... | collective-permute-start | bytes 1572872 | tf_op jit(solution)/shard_map/ppermute | solution.py:300
  23.2 9.7 %collective-permute-start.6 = (f32[520,256]{1,0:T(8,128)S(1)}, f32[520,256]{1,0:T(8,128)S(1)}, u32[]{:S(2)}, u32[]{:S(2)}) collective-permute-start(f32[520,256]{1,0:T(8,128)S(1)} %collective-permute-done.2.x_ref), channel_id=1, source_target_pairs={{0,1},{1,2},{2,3},{3,0},{4,7},{5,4},{6,5},{7,6},{8,9},{9,10},{10,1... | collective-permute-start | bytes 1597448 | tf_op jit(solution)/shard_map/ppermute | solution.py:310
  36.6 5.0 %collective-permute-start.9 = (f32[64,512]{1,0:T(8,128)S(1)}, f32[64,512]{1,0:T(8,128)S(1)}, u32[]{:S(2)}, u32[]{:S(2)}) collective-permute-start(f32[64,512]{1,0:T(8,128)S(1)} %get-tuple-element.44.refs_0_), channel_id=1, source_target_pairs={{0,3},{1,0},{2,1},{3,2},{4,7},{5,4},{6,5},{7,6},{8,11},{9,8},{10,9... | collective-permute-start | bytes 393224 | tf_op jit(solution)/shard_map/ppermute | solution.py:295
  37.1 6.5 %collective-permute-start.8 = (f32[64,512]{1,0:T(8,128)S(1)}, f32[64,512]{1,0:T(8,128)S(1)}, u32[]{:S(2)}, u32[]{:S(2)}) collective-permute-start(f32[64,512]{1,0:T(8,128)S(1)} %get-tuple-element.44.refs_0_), channel_id=1, source_target_pairs={{0,2},{1,3},{2,0},{3,1},{4,6},{5,7},{6,4},{7,5},{8,10},{9,11},{10,... | collective-permute-start | bytes 393224 | tf_op jit(solution)/shard_map/ppermute | solution.py:295
  40.0 5.0 %collective-permute-start.7 = (f32[64,512]{1,0:T(8,128)S(1)}, f32[64,512]{1,0:T(8,128)S(1)}, u32[]{:S(2)}, u32[]{:S(2)}) collective-permute-start(f32[64,512]{1,0:T(8,128)S(1)} %get-tuple-element.44.refs_0_), channel_id=1, source_target_pairs={{0,1},{1,2},{2,3},{3,0},{4,5},{5,6},{6,7},{7,4},{8,9},{9,10},{10,1... | collective-permute-start | bytes 393224 | tf_op jit(solution)/shard_map/ppermute | solution.py:295
  45.6 17.1 %collective-permute-start.17 = (f32[64,2048]{1,0:T(8,128)S(1)}, f32[64,2048]{1,0:T(8,128)S(1)}, u32[]{:S(2)}, u32[]{:S(2)}) collective-permute-start(f32[64,2048]{1,0:T(8,128)S(1)} %get-tuple-element.46.vo_ref), channel_id=1, source_target_pairs={{0,252},{4,8},{8,4},{12,16},{16,12},{20,24},{24,20},{28,32},{32,28... | collective-permute-start | bytes 1572872 | tf_op jit(solution)/shard_map/ppermute | solution.py:300
  52.0 10.7 %collective-permute-start.16 = (f32[64,2048]{1,0:T(8,128)S(1)}, f32[64,2048]{1,0:T(8,128)S(1)}, u32[]{:S(2)}, u32[]{:S(2)}) collective-permute-start(f32[64,2048]{1,0:T(8,128)S(1)} %get-tuple-element.46.vo_ref), channel_id=1, source_target_pairs={{0,4},{4,0},{8,12},{12,8},{16,20},{20,16},{24,28},{28,24},{32,36},... | collective-permute-start | bytes 1572872 | tf_op jit(solution)/shard_map/ppermute | solution.py:304
  52.0 1.9 %collective-permute-start.10 = (f32[1,32,128]{2,1,0:T(8,128)S(1)}, f32[1,32,128]{2,1,0:T(8,128)S(1)}, u32[]{:S(2)}, u32[]{:S(2)}) collective-permute-start(f32[1,32,128]{2,1,0:T(8,128)S(1)} %get-tuple-element.45), channel_id=1, source_target_pairs={{0,4},{4,0},{8,12},{12,8},{16,20},{20,16},{24,28},{28,24},{32,36},... | collective-permute-start | bytes 49160 | tf_op jit(solution)/shard_map/ppermute | solution.py:336
  54.0 3.7 %collective-permute-start.11 = (f32[1,32,128]{2,1,0:T(8,128)S(1)}, f32[1,32,128]{2,1,0:T(8,128)S(1)}, u32[]{:S(2)}, u32[]{:S(2)}) collective-permute-start(f32[1,32,128]{2,1,0:T(8,128)S(1)} %add.15), channel_id=1, source_target_pairs={{0,8},{4,12},{8,0},{12,4},{16,24},{20,28},{24,16},{28,20},{32,40},... | collective-permute-start | bytes 49160 | tf_op jit(solution)/shard_map/ppermute | solution.py:336
  57.7 4.9 %collective-permute-start.12 = (f32[1,32,128]{2,1,0:T(8,128)S(1)}, f32[1,32,128]{2,1,0:T(8,128)S(1)}, u32[]{:S(2)}, u32[]{:S(2)}) collective-permute-start(f32[1,32,128]{2,1,0:T(8,128)S(1)} %add.16), channel_id=1, source_target_pairs={{0,24},{4,28},{8,16},{12,20},{16,8},{20,12},{24,0},{28,4},{32,56},... | collective-permute-start | bytes 49160 | tf_op jit(solution)/shard_map/ppermute | solution.py:336
  62.7 7.9 %collective-permute-start.13 = (f32[1,32,128]{2,1,0:T(8,128)S(1)}, f32[1,32,128]{2,1,0:T(8,128)S(1)}, u32[]{:S(2)}, u32[]{:S(2)}) collective-permute-start(f32[1,32,128]{2,1,0:T(8,128)S(1)} %add.17), channel_id=1, source_target_pairs={{0,32},{4,36},{8,40},{12,44},{16,48},{20,52},{24,56},{28,60},{32,0... | collective-permute-start | bytes 49160 | tf_op jit(solution)/shard_map/ppermute | solution.py:336
  65.0 18.4 %collective-permute-start.20 = (f32[64,512]{1,0:T(8,128)S(1)}, f32[64,512]{1,0:T(8,128)S(1)}, u32[]{:S(2)}, u32[]{:S(2)}) collective-permute-start(f32[64,512]{1,0:T(8,128)S(1)} %second_product.1.refs_0_), channel_id=1, source_target_pairs={{0,3},{1,0},{2,1},{3,2},{4,7},{5,4},{6,5},{7,6},{8,11},{9,8},{10,9... | collective-permute-start | bytes 393224 | tf_op jit(solution)/shard_map/ppermute | solution.py:295
  65.3 18.1 %collective-permute-start.19 = (f32[64,512]{1,0:T(8,128)S(1)}, f32[64,512]{1,0:T(8,128)S(1)}, u32[]{:S(2)}, u32[]{:S(2)}) collective-permute-start(f32[64,512]{1,0:T(8,128)S(1)} %second_product.1.refs_0_), channel_id=1, source_target_pairs={{0,2},{1,3},{2,0},{3,1},{4,6},{5,7},{6,4},{7,5},{8,10},{9,11},{10,... | collective-permute-start | bytes 393224 | tf_op jit(solution)/shard_map/ppermute | solution.py:295
  68.3 15.1 %collective-permute-start.18 = (f32[64,512]{1,0:T(8,128)S(1)}, f32[64,512]{1,0:T(8,128)S(1)}, u32[]{:S(2)}, u32[]{:S(2)}) collective-permute-start(f32[64,512]{1,0:T(8,128)S(1)} %second_product.1.refs_0_), channel_id=1, source_target_pairs={{0,1},{1,2},{2,3},{3,0},{4,5},{5,6},{6,7},{7,4},{8,9},{9,10},{10,1... | collective-permute-start | bytes 393224 | tf_op jit(solution)/shard_map/ppermute | solution.py:295
  70.6 4.9 %collective-permute-start.14 = (f32[1,32,128]{2,1,0:T(8,128)S(1)}, f32[1,32,128]{2,1,0:T(8,128)S(1)}, u32[]{:S(2)}, u32[]{:S(2)}) collective-permute-start(f32[1,32,128]{2,1,0:T(8,128)S(1)} %add.18), channel_id=1, source_target_pairs={{0,64},{4,68},{8,72},{12,76},{16,80},{20,84},{24,88},{28,92},{32,9... | collective-permute-start | bytes 49160 | tf_op jit(solution)/shard_map/ppermute | solution.py:336
  75.5 5.8 %collective-permute-start.15 = (f32[1,32,128]{2,1,0:T(8,128)S(1)}, f32[1,32,128]{2,1,0:T(8,128)S(1)}, u32[]{:S(2)}, u32[]{:S(2)}) collective-permute-start(f32[1,32,128]{2,1,0:T(8,128)S(1)} %add.19.a_ref), channel_id=1, source_target_pairs={{0,192},{4,196},{8,200},{12,204},{16,208},{20,212},{24,216},{28,22... | collective-permute-start | bytes 49160 | tf_op jit(solution)/shard_map/ppermute | solution.py:336

commit v6 on v5

--- a/solution.py
+++ b/solution.py
@@ -144,13 +144,17 @@
             tiles_or_zeros(hit, x, xah_ref, xal_ref, na_ref, v, acc_ref, eh_ref, el_ref, j * block, block, j * block)
 
 
-def cross_kernel(members, step, x_ref, v_ref, note_ref, pairs_ref, xah_ref, xal_ref, na_ref, in_ref, acc_ref, eh_ref, el_ref):
+def cross_kernel(members, steps, *refs):
+    n = len(steps)
+    x_refs, (v_ref, note_ref, pairs_ref, xah_ref, xal_ref, na_ref, in_ref, acc_ref), kept = refs[:n], refs[n : n + 8], refs[n + 8 :]
     group, member = place()
-    rows = eh_ref.shape[0]
-    q = quarter_at(members, step, group, member)
+    rows = kept[0].shape[0]
     acc_ref[...] = in_ref[...]
-    hit = want(pairs_ref, note_ref, group, member, members, CROSS, (q * BLK_DEV) // members)
-    tiles_or_zeros(hit, x_ref, xah_ref, xal_ref, na_ref, v_ref, acc_ref, eh_ref, el_ref, 0, rows, pl.multiple_of(q * rows, rows))
+    for i, step in enumerate(steps):
+        eh_ref, el_ref = kept[2 * i : 2 * i + 2]
+        q = quarter_at(members, step, group, member)
+        hit = want(pairs_ref, note_ref, group, member, members, CROSS, (q * BLK_DEV) // members)
+        tiles_or_zeros(hit, x_refs[i], xah_ref, xal_ref, na_ref, v_ref, acc_ref, eh_ref, el_ref, 0, rows, pl.multiple_of(q * rows, rows))
 
 
 def gram_sum(vh, vm, vl):
@@ -177,10 +181,9 @@
         gram_ref[n] = packed
 
 
-def take_gram(gram_ref):
-    packed = gram_ref[0]
-    for n in range(1, gram_ref.shape[0]):
-        packed = packed + gram_ref[n]
+def take_gram(terms):
+    me, opposite, left, right = (ref[...] for ref in terms)
+    packed = (me + opposite) + (left + right)
     k = packed.shape[1] // 2
     return jnp.concatenate([packed[:, :k], packed[:, k:]], 0)
 
@@ -253,8 +256,9 @@
     return jnp.concatenate(a, 0)[:, k:]
 
 
-def factor_kernel(a_ref, b_ref, inv_ref):
-    inv_ref[...] = factor_inverse(take_gram(a_ref) + take_gram(b_ref))
+def factor_kernel(*refs):
+    inv_ref = refs[-1]
+    inv_ref[...] = factor_inverse(take_gram(refs[:-1]))
 
 
 def exact(a, b):
@@ -268,8 +272,9 @@
     put_gram(gram_ref, image_ref[...], total)
 
 
-def last_kernel(gram_ref, image_ref, out_ref):
-    out_ref[...] = exact(factor_inverse(take_gram(gram_ref)), image_ref[...])
+def last_kernel(image_ref, *refs):
+    out_ref = refs[-1]
+    out_ref[...] = exact(factor_inverse(take_gram(refs[:-1])), image_ref[...])
 
 
 VM = pl.BlockSpec(memory_space=pltpu.VMEM)
@@ -318,24 +323,25 @@
     return [[g * members + m for g in range(low, groups, NEAR)] for low in range(NEAR) for m in range(members)]
 
 
-def near_sets():
-    groups, members = lax.axis_size("rows"), lax.axis_size("sub")
-    return [[g * members + m for g in range(base, base + NEAR)] for base in range(0, groups, NEAR) for m in range(members)]
-
-
 def exchanged(x, sets):
     return lax.all_to_all(x, ("rows", "sub"), 0, 0, axis_index_groups=sets)
 
 
-MASKS = (1, 2, 6, 8, 16, 48)
-
-
-def pair_sums(gram):
-    for mask in MASKS:
-        pairs = [(i, i ^ mask) for i in range(lax.axis_size("rows"))]
-        other = lax.ppermute(gram, "rows", pairs)
-        gram = gram + other if mask != MASKS[-1] else (gram, other)
-    return gram
+def sum_kernel(gram_ref, out_ref):
+    packed = gram_ref[0]
+    for n in range(1, gram_ref.shape[0]):
+        packed = packed + gram_ref[n]
+    out_ref[...] = packed
+
+
+RING = (4, 2, 6)
+
+
+def row_sums(gram):
+    (total,) = call(sum_kernel, [VM], [(gram.shape[1:], f32)], "sum_z", flops=10**6)(exchanged(gram, far_sets()))
+    total = total + swapped(total)
+    groups = lax.axis_size("rows")
+    return [total] + [lax.ppermute(total, "rows", [(i, i ^ mask) for i in range(groups)]) for mask in RING]
 
 
 def tie(x, *others):
@@ -371,29 +377,30 @@
         [((quarter, width), bf16)] * 2 + [((8, quarter), f32), part] + tiles(rows) + tiles(rows), "chip_tiles",
         flops=10**10)(embeddings, vt, sib_e, sib_v, pairs)
     arrived.append(passed_on(arrived[0]))
-    for step in (0, 3, 1, 2):
+    far_tiles = {}
+    for steps in ((0,), (3,), (1, 2)):
+        n = len(steps)
         acc, *t = call(
-            functools.partial(cross_kernel, members, step), [VM, VM, VM, SM, VM, VM, VM, VM], [part] + tiles(quarter), "cross_tiles",
-            flops=2 * 10**9)(arrived[step], cross_v, cross_note, pairs, xah, xal, na, acc)
-        arrived[step] = t
-    for t in arrived:
-        kept += t
+            functools.partial(cross_kernel, members, steps), [VM] * (n + 2) + [SM, VM, VM, VM, VM], [part] + tiles(quarter) * n,
+            "cross_tiles", flops=2 * 10**9)(*(arrived[step] for step in steps), cross_v, cross_note, pairs, xah, xal, na, acc)
+        for i, step in enumerate(steps):
+            far_tiles[step] = t[2 * i : 2 * i + 2]
+    for step in range(members):
+        kept += far_tiles[step]
     pieces = [acc] + [shifted(acc, "sub", s) for s in range(1, members)]
     whole = ((k, rows), f32)
-    far, near = far_sets(), near_sets()
-    grams = lambda sets: ((len(sets[0]), k // 2, 2 * k), f32)
-    image, gram = call(functools.partial(join_kernel, members, total), [VM] * members, [whole, ((1, k // 2, 2 * k), f32)], "join")(*pieces)
+    copies = ((groups // NEAR, k // 2, 2 * k), f32)
+    image, gram = call(functools.partial(join_kernel, members, total), [VM] * members, [whole, copies], "join")(*pieces)
     cross_i = crossed(image)
     sib_i = swapped(image)
-    grams_1 = pair_sums(gram)
+    terms = row_sums(gram)
     (acc2,) = call(functools.partial(second_kernel, members), [VM] * (3 + len(kept)), [part], "second_product")(
         image, sib_i, cross_i, *kept)
     pieces = [acc2] + [shifted(acc2, "sub", s) for s in range(1, members)]
-    (inv,) = call(factor_kernel, [VM, VM], [((k, k), f32)], "factor")(*grams_1)
-    image, gram = call(functools.partial(image_kernel, members, total), [VM] * (1 + members), [whole, grams(far)], "image")(inv, *pieces)
-    gram = exchanged(gram, far)
-    gram = exchanged(jnp.broadcast_to(gram.sum(0)[None], grams(near)[0]), near)
-    (out,) = call(last_kernel, [VM, VM], [whole], "last")(gram, image)
+    (inv,) = call(factor_kernel, [VM] * len(terms), [((k, k), f32)], "factor")(*terms)
+    image, gram = call(functools.partial(image_kernel, members, total), [VM] * (1 + members), [whole, copies], "image")(inv, *pieces)
+    terms = row_sums(gram)
+    (out,) = call(last_kernel, [VM] * (1 + len(terms)), [whole], "last")(image, *terms)
     return out.T
 
 

time: 110 us -> 109 us (level)
  waiting for transfers between devices: 26 us -> 19.7 us
  blocking collectives: 21.8 us -> 26.2 us
    ppermute x6, waiting for transfers between devices: 18 us -> 10.6 us  [row_sums(): lax.ppermute(total, 'rows', [(i, i ^ mask) for i in range(groups)])]
    all_to_all x2, blocking collectives: 21.8 us -> 26.2 us  [exchanged(): return lax.all_to_all(x, ('rows', 'sub'), 0, 0, axis_index_groups=sets)]
    ppermute x6, starting transfers between devices: 3.39 us -> 6.28 us  [row_sums(): lax.ppermute(total, 'rows', [(i, i ^ mask) for i in range(groups)])]
    ppermute x5, starting transfers between devices: 24.3 us -> 22.2 us  [crossed(): lax.ppermute(x, 'rows', [(i, (i + 2 * (i % 2) - 1) % n) for i in range(n)])]
    ppermute x3 -> x5, waiting for transfers between devices: 0.01 us -> 1.18 us  [swapped(): lax.ppermute(x, 'rows', [(i, i ^ 1) for i in range(lax.axis_size('rows'))])]
    pallas_call x6 -> x7, Pallas kernels: 8.59 us -> 8.04 us  [the longest x1 3.34 us: on_device(): call(last_kernel, [VM] * (1 + len(terms)), [whole], 'last')(image, *terms)]
  transfers between devices with their start and end apart: 21 -> 23, of which waited for: 10 -> 10; matrix products, arithmetic and copies ran while one was open for 0% -> 0% of each run, Pallas kernels for 15% -> 14%
where the time goes in v6:
time: 109 us; the launch traced here: 108 us
  starting transfers between devices  39.5 us (36%)
  blocking collectives  26.2 us (24%)
  Pallas kernels  21.7 us (20%)
  waiting for transfers between devices  19.7 us (18%)
    all_to_all x2, blocking collectives, exchanged(): return lax.all_to_all(x, ('rows', 'sub'), 0, 0, axis_index_groups=sets)  26.2 us
    ppermute x5, starting transfers between devices, crossed(): lax.ppermute(x, 'rows', [(i, (i + 2 * (i % 2) - 1) % n) for i in range(n)])  22.2 us
    ppermute x6, waiting for transfers between devices, row_sums(): lax.ppermute(total, 'rows', [(i, i ^ mask) for i in range(groups)])  10.6 us
    ppermute x6, starting transfers between devices, shifted(): return lax.ppermute(x, axis, [(i, (i + by) % n) for i in range(n)])  9.05 us
    pallas_call x1, Pallas kernels, on_device(): call(functools.partial(chip_kernel, members), [VM, VM, VM, VM, SM], [((qu...  7.61 us
    ppermute x6, starting transfers between devices, row_sums(): lax.ppermute(total, 'rows', [(i, i ^ mask) for i in range(groups)])  6.28 us
    ppermute x6, waiting for transfers between devices, shifted(): return lax.ppermute(x, axis, [(i, (i + by) % n) for i in range(n)])  4.99 us
    pallas_call x1, Pallas kernels, on_device(): call(last_kernel, [VM] * (1 + len(terms)), [whole], 'last')(image, *terms)  3.34 us
  transfers between devices with their start and end apart: 23, of which 10 were waited for; matrix products, arithmetic and copies ran while one was open for 0% of the time, Pallas kernels for 14%

profile of v6, /device:TPU:16, one launch (start us, length us, event | category | flops | bytes accessed | tf_op | source)
XLA Modules:
  0.0 108.3 jit_solution(6349642931148487882)
XLA Ops:
  0.0 0.0 collective-permute-start.4
  0.0 0.8 copy-done.2
  0.9 2.1 %cut.1 = (f32[520,256]{1,0:T(8,128)S(1)}, f32[512,256]{1,0:T(8,128)S(1)}, f32[512,256]{1,0:T(8,128)S(1)}, f32[72,2048]{1,0:T(8,128)S(1)}) custom-call(f32[2048,256]{1,0:T(8,128)} %x_ref.3, f32[64,2048]{1,0:T(8,128)} %bitcast.3, s32[2,8]{1,0:T(2,128)S(1)} %bitcast.6), custom_call_target="tpu_custom_call" | custom-call | flops 1000000 | bytes 1048576 | tf_op jit(solution)/shard_map/cut/pallas_call | solution.py:362
  3.0 0.5 collective-permute-start.5
  3.4 7.8 %collective-permute-start.3 = (f32[520,256]{1,0:T(8,128)S(1)}, f32[520,256]{1,0:T(8,128)S(1)}, u32[]{:S(2)}, u32[]{:S(2)}) collective-permute-start(f32[520,256]{1,0:T(8,128)S(1)} %get-tuple-element.34), channel_id=1, source_target_pairs={{0,252},{4,8},{8,4},{12,16},{16,12},{20,24},{24,20},{28,32},{32,28... | collective-permute-start | bytes 1597448 | tf_op jit(solution)/shard_map/ppermute | solution.py:305
  11.2 0.1 collective-permute-start.2
  11.3 5.0 %collective-permute-start = (f32[512,256]{1,0:T(8,128)S(1)}, f32[512,256]{1,0:T(8,128)S(1)}, u32[]{:S(2)}, u32[]{:S(2)}) collective-permute-start(f32[512,256]{1,0:T(8,128)S(1)} %get-tuple-element.32), channel_id=1, source_target_pairs={{0,252},{4,8},{8,4},{12,16},{16,12},{20,24},{24,20},{28,32},{32,28... | collective-permute-start | bytes 1572872 | tf_op jit(solution)/shard_map/ppermute | solution.py:305
  16.3 1.9 %collective-permute-done.3.refs_0_ = f32[520,256]{1,0:T(8,128)S(1)} collective-permute-done((f32[520,256]{1,0:T(8,128)S(1)}, f32[520,256]{1,0:T(8,128)S(1)}, u32[]{:S(2)}, u32[]{:S(2)}) %collective-permute-start.3) | collective-permute-done | bytes 532512 | tf_op jit(solution)/shard_map/ppermute | solution.py:305
  18.2 5.1 %collective-permute-start.1 = (f32[512,256]{1,0:T(8,128)S(1)}, f32[512,256]{1,0:T(8,128)S(1)}, u32[]{:S(2)}, u32[]{:S(2)}) collective-permute-start(f32[512,256]{1,0:T(8,128)S(1)} %get-tuple-element.33), channel_id=1, source_target_pairs={{0,252},{4,8},{8,4},{12,16},{16,12},{20,24},{24,20},{28,32},{32,28... | collective-permute-start | bytes 1572872 | tf_op jit(solution)/shard_map/ppermute | solution.py:305
  23.2 0.0 collective-permute-done.5.sib_v_ref
  23.2 1.3 %collective-permute-start.6 = (f32[520,256]{1,0:T(8,128)S(1)}, f32[520,256]{1,0:T(8,128)S(1)}, u32[]{:S(2)}, u32[]{:S(2)}) collective-permute-start(f32[520,256]{1,0:T(8,128)S(1)} %collective-permute-done.3.refs_0_), channel_id=1, source_target_pairs={{0,1},{1,2},{2,3},{3,0},{4,7},{5,4},{6,5},{7,6},{8,9},{9,10},{10,1... | collective-permute-start | bytes 1597448 | tf_op jit(solution)/shard_map/ppermute | solution.py:315
  24.5 0.0 collective-permute-done.4.sib_x_ref
  24.5 7.6 %chip_tiles.1 = (bf16[512,256]{1,0:T(8,128)(2,1)S(1)}, bf16[512,256]{1,0:T(8,128)(2,1)S(1)}, f32[8,512]{1,0:T(8,128)S(1)}, f32[64,512]{1,0:T(8,128)S(1)}, bf16[2...) custom-call(f32[2048,256]{1,0:T(8,128)S(1)} %copy-done, ...), custom_call_target="tpu_custom_call" | custom-call | flops 10000000000 | bytes 1048576 | tf_op jit(solution)/shard_map/chip_tiles/pallas_call | solution.py:375
  32.2 0.8 cross_tiles.3
  32.9 0.0 collective-permute-done.6.refs_0_
  32.9 0.9 cross_tiles.4
  33.9 0.0 collective-permute-done.refs_0_
  33.9 1.1 %collective-permute-done.1.refs_1_ = f32[512,256]{1,0:T(8,128)S(1)} collective-permute-done((f32[512,256]{1,0:T(8,128)S(1)}, f32[512,256]{1,0:T(8,128)S(1)}, u32[]{:S(2)}, u32[]{:S(2)}) %collective-permute-start.1) | collective-permute-done | bytes 524320 | tf_op jit(solution)/shard_map/ppermute | solution.py:305
  35.0 1.0 cross_tiles.5
  36.0 0.5 collective-permute-start.9
  36.5 2.9 %collective-permute-start.8 = (f32[64,512]{1,0:T(8,128)S(1)}, f32[64,512]{1,0:T(8,128)S(1)}, u32[]{:S(2)}, u32[]{:S(2)}) collective-permute-start(f32[64,512]{1,0:T(8,128)S(1)} %get-tuple-element.42.refs_0_), channel_id=1, source_target_pairs={{0,2},{1,3},{2,0},{3,1},{4,6},{5,7},{6,4},{7,5},{8,10},{9,11},{10,... | collective-permute-start | bytes 393224 | tf_op jit(solution)/shard_map/ppermute | solution.py:300
  39.4 1.6 %collective-permute-done.9.refs_3_ = f32[64,512]{1,0:T(8,128)S(1)} collective-permute-done((f32[64,512]{1,0:T(8,128)S(1)}, f32[64,512]{1,0:T(8,128)S(1)}, u32[]{:S(2)}, u32[]{:S(2)}) %collective-permute-start.9) | collective-permute-done | bytes 131104 | tf_op jit(solution)/shard_map/ppermute | solution.py:300
  41.0 2.0 %collective-permute-done.8.refs_2_ = f32[64,512]{1,0:T(8,128)S(1)} collective-permute-done((f32[64,512]{1,0:T(8,128)S(1)}, f32[64,512]{1,0:T(8,128)S(1)}, u32[]{:S(2)}, u32[]{:S(2)}) %collective-permute-start.8) | collective-permute-done | bytes 131104 | tf_op jit(solution)/shard_map/ppermute | solution.py:300
  43.0 1.4 %collective-permute-done.7.refs_1_ = f32[64,512]{1,0:T(8,128)S(1)} collective-permute-done((f32[64,512]{1,0:T(8,128)S(1)}, f32[64,512]{1,0:T(8,128)S(1)}, u32[]{:S(2)}, u32[]{:S(2)}) %collective-permute-start.7) | collective-permute-done | bytes 131104 | tf_op jit(solution)/shard_map/ppermute | solution.py:300
  44.4 0.7 join.1
  45.1 4.3 %collective-permute-start.15 = (f32[64,2048]{1,0:T(8,128)S(1)}, f32[64,2048]{1,0:T(8,128)S(1)}, u32[]{:S(2)}, u32[]{:S(2)}) collective-permute-start(f32[64,2048]{1,0:T(8,128)S(1)} %get-tuple-element.44.vo_ref), channel_id=1, source_target_pairs={{0,252},{4,8},{8,4},{12,16},{16,12},{20,24},{24,20},{28,32},{32,28... | collective-permute-start | bytes 1572872 | tf_op jit(solution)/shard_map/ppermute | solution.py:305
  49.4 14.4 %all_to_all.10.gram_ref = f32[8,32,128]{2,1,0:T(8,128)S(1)} all-to-all(f32[8,32,128]{2,1,0:T(8,128)S(1)} %get-tuple-element.43), channel_id=1, replica_groups={{0,32,64,96,128,160,192,224},{1,33,65,97,129,161,193,225},{2,34,66,98,1..., dimensions={0} | all-to-all | bytes 262144 | tf_op jit(solution)/shard_map/all_to_all | solution.py:327
  63.8 0.1 collective-permute-start.10
  63.9 2.2 %second_product.1.refs_0_ = f32[64,512]{1,0:T(8,128)S(1)} custom-call(f32[64,2048]{1,0:T(8,128)S(1)} %get-tuple-element.44.vo_ref, f32[64,2048]{1,0:T(8,128)S(1)} %collective-permute-done.14.vs_ref, f32[64,2048]{1,0:T(8,128)S(1)} %collective-permute-done.15.vc_ref, bf16[2048,512]{1,0:T(8,128)(2,1)S(1)} %get-tuple-element.45.refs_0_, ...), custom_call_target="tpu_custom_call" | custom-call | flops 1000000000 | bytes 1048576 | tf_op jit(solution)/shard_map/second_product/pallas_call | solution.py:397
  66.1 0.6 collective-permute-start.18
  66.7 3.0 %collective-permute-start.17 = (f32[64,512]{1,0:T(8,128)S(1)}, f32[64,512]{1,0:T(8,128)S(1)}, u32[]{:S(2)}, u32[]{:S(2)}) collective-permute-start(f32[64,512]{1,0:T(8,128)S(1)} %second_product.1.refs_0_), channel_id=1, source_target_pairs={{0,2},{1,3},{2,0},{3,1},{4,6},{5,7},{6,4},{7,5},{8,10},{9,11},{10,... | collective-permute-start | bytes 393224 | tf_op jit(solution)/shard_map/ppermute | solution.py:300
  69.7 2.1 %collective-permute-start.16 = (f32[64,512]{1,0:T(8,128)S(1)}, f32[64,512]{1,0:T(8,128)S(1)}, u32[]{:S(2)}, u32[]{:S(2)}) collective-permute-start(f32[64,512]{1,0:T(8,128)S(1)} %second_product.1.refs_0_), channel_id=1, source_target_pairs={{0,1},{1,2},{2,3},{3,0},{4,5},{5,6},{6,7},{7,4},{8,9},{9,10},{10,1... | collective-permute-start | bytes 393224 | tf_op jit(solution)/shard_map/ppermute | solution.py:300
  71.8 1.0 collective-permute-start.13
  72.8 0.4 collective-permute-start.12
  73.2 3.6 %collective-permute-done.13.refs_3_ = f32[32,128]{1,0:T(8,128)S(1)} collective-permute-done((f32[32,128]{1,0:T(8,128)S(1)}, f32[32,128]{1,0:T(8,128)S(1)}, u32[]{:S(2)}, u32[]{:S(2)}) %collective-permute-start.13) | collective-permute-done | bytes 16416 | tf_op jit(solution)/shard_map/ppermute | solution.py:344
  76.8 0.2 collective-permute-start.11
  77.0 5.1 %collective-permute-done.11.refs_1_ = f32[32,128]{1,0:T(8,128)S(1)} collective-permute-done((f32[32,128]{1,0:T(8,128)S(1)}, f32[32,128]{1,0:T(8,128)S(1)}, u32[]{:S(2)}, u32[]{:S(2)}) %collective-permute-start.11) | collective-permute-done | bytes 16416 | tf_op jit(solution)/shard_map/ppermute | solution.py:344
  82.0 2.0 %factor.1.inv_ref = f32[64,64]{1,0:T(8,128)S(1)} custom-call(f32[32,128]{1,0:T(8,128)S(1)} %add.6.refs_0_, f32[32,128]{1,0:T(8,128)S(1)} %collective-permute-done.11.refs_1_, f32[32,128]{1,0:T(8,128)S(1)} %collective-permute-done.12.refs_2_, f32[32,128]{1,0:T(8,128)S(1)} %collective-permute-done.13.refs_3_), custom_call_target="tpu_custom_call" | custom-call | flops 1000000000 | bytes 1048576 | tf_op jit(solution)/shard_map/factor/pallas_call | solution.py:400
  84.0 0.0 collective-permute-done.16.refs_1_
  84.1 1.1 %image.1 = (f32[64,2048]{1,0:T(8,128)S(1)}, f32[8,32,128]{2,1,0:T(8,128)S(1)}) custom-call(f32[64,64]{1,0:T(8,128)S(1)} %factor.1.inv_ref, f32[64,512]{1,0:T(8,128)S(1)} %second_product.1.refs_0_, f32[64,512]{1,0:T(8,128)S(1)} %collective-permute-done.16.refs_1_, f32[64,512]{1,0:T(8,128)S(1)} %collective-permute-done.17.refs_2_, ...), custom_call_target="tpu_custom_call" | custom-call | flops 1000000000 | bytes 1048576 | tf_op jit(solution)/shard_map/image/pallas_call | solution.py:401
  85.2 11.9 %all_to_all.11.gram_ref = f32[8,32,128]{2,1,0:T(8,128)S(1)} all-to-all(f32[8,32,128]{2,1,0:T(8,128)S(1)} %get-tuple-element.58), channel_id=1, replica_groups={{0,32,64,96,128,160,192,224},{1,33,65,97,129,161,193,225},{2,34,66,98,1..., dimensions={0} | all-to-all | bytes 262144 | tf_op jit(solution)/shard_map/all_to_all | solution.py:327
  97.1 0.1 collective-permute-start.19
  97.2 1.2 %collective-permute-done.19 = f32[32,128]{1,0:T(8,128)S(1)} collective-permute-done((f32[32,128]{1,0:T(8,128)S(1)}, f32[32,128]{1,0:T(8,128)S(1)}, u32[]{:S(2)}, u32[]{:S(2)}) %collective-permute-start.19) | collective-permute-done | bytes 16416 | tf_op jit(solution)/shard_map/ppermute | solution.py:309
  98.3 1.0 collective-permute-start.22
  99.4 3.7 %collective-permute-start.20 = (f32[32,128]{1,0:T(8,128)S(1)}, f32[32,128]{1,0:T(8,128)S(1)}, u32[]{:S(2)}, u32[]{:S(2)}) collective-permute-start(f32[32,128]{1,0:T(8,128)S(1)} %add.7.refs_0_), channel_id=1, source_target_pairs={{0,16},{4,20},{8,24},{12,28},{16,0},{20,4},{24,8},{28,12},{32,48},... | collective-permute-start | bytes 49160 | tf_op jit(solution)/shard_map/ppermute | solution.py:344
  103.0 0.2 collective-permute-done.22.refs_3_
  103.3 1.6 %collective-permute-done.20.refs_1_ = f32[32,128]{1,0:T(8,128)S(1)} collective-permute-done((f32[32,128]{1,0:T(8,128)S(1)}, f32[32,128]{1,0:T(8,128)S(1)}, u32[]{:S(2)}, u32[]{:S(2)}) %collective-permute-start.20) | collective-permute-done | bytes 16416 | tf_op jit(solution)/shard_map/ppermute | solution.py:344
  104.9 3.3 %last.1 = f32[64,2048]{1,0:T(8,128)} custom-call(f32[64,2048]{1,0:T(8,128)S(1)} %get-tuple-element.57.image_ref, f32[32,128]{1,0:T(8,128)S(1)} %add.7.refs_0_, f32[32,128]{1,0:T(8,128)S(1)} %collective-permute-done.20.refs_1_, f32[32,128]{1,0:T(8,128)S(1)} %collective-permute-done.21.refs_2_, f32[32,128]{1,0:T(8,128)S(1)} %collective-permute-done.22.refs_3_), custom_call_target="tpu_custom_call" | custom-call | flops 1000000000 | bytes 1048576 | tf_op jit(solution)/shard_map/last/pallas_call | solution.py:403
  (21 shorter events, 0.1 us)
Async XLA Ops:
  0.0 24.5 %copy-start = (f32[2048,256]{1,0:T(8,128)S(1)}, f32[2048,256]{1,0:T(8,128)}, u32[]{:S(2)}) copy-start(f32[2048,256]{1,0:T(8,128)} %x_ref.3) | copy-start | bytes 6291460
  0.0 11.2 %copy-start.1 = (f32[2048,64]{0,1:T(8,128)S(1)}, f32[2048,64]{0,1:T(8,128)}, u32[]{:S(2)}) copy-start(f32[2048,64]{0,1:T(8,128)} %param.4) | copy-start | bytes 1572868
  0.0 24.5 %collective-permute-start.4 = (f32[2048,256]{1,0:T(8,128)}, f32[2048,256]{1,0:T(8,128)S(1)}, u32[]{:S(2)}, u32[]{:S(2)}) collective-permute-start(f32[2048,256]{1,0:T(8,128)} %x_ref.3), channel_id=1, source_target_pairs={{0,4},{4,0},{8,12},{12,8},{16,20},{20,16},{24,28},{28,24},{32,36},... | collective-permute-start | bytes 6291464 | tf_op jit(solution)/shard_map/ppermute | solution.py:309
  0.0 0.8 copy-start.2
  3.0 20.3 %collective-permute-start.5 = (f32[72,2048]{1,0:T(8,128)S(1)}, f32[72,2048]{1,0:T(8,128)S(1)}, u32[]{:S(2)}, u32[]{:S(2)}) collective-permute-start(f32[72,2048]{1,0:T(8,128)S(1)} %get-tuple-element.35), channel_id=1, source_target_pairs={{0,4},{4,0},{8,12},{12,8},{16,20},{20,16},{24,28},{28,24},{32,36},... | collective-permute-start | bytes 1769480 | tf_op jit(solution)/shard_map/ppermute | solution.py:309
  3.4 14.7 %collective-permute-start.3 = (f32[520,256]{1,0:T(8,128)S(1)}, f32[520,256]{1,0:T(8,128)S(1)}, u32[]{:S(2)}, u32[]{:S(2)}) collective-permute-start(f32[520,256]{1,0:T(8,128)S(1)} %get-tuple-element.34), channel_id=1, source_target_pairs={{0,252},{4,8},{8,4},{12,16},{16,12},{20,24},{24,20},{28,32},{32,28... | collective-permute-start | bytes 1597448 | tf_op jit(solution)/shard_map/ppermute | solution.py:305
  11.2 20.9 %collective-permute-start.2 = (f32[64,2048]{1,0:T(8,128)S(1)}, f32[64,2048]{1,0:T(8,128)S(1)}, u32[]{:S(2)}, u32[]{:S(2)}) collective-permute-start(f32[64,2048]{1,0:T(8,128)S(1)} %bitcast.4), channel_id=1, source_target_pairs={{0,252},{4,8},{8,4},{12,16},{16,12},{20,24},{24,20},{28,32},{32,28... | collective-permute-start | bytes 1572872 | tf_op jit(solution)/shard_map/ppermute | solution.py:305
  11.3 22.6 %collective-permute-start = (f32[512,256]{1,0:T(8,128)S(1)}, f32[512,256]{1,0:T(8,128)S(1)}, u32[]{:S(2)}, u32[]{:S(2)}) collective-permute-start(f32[512,256]{1,0:T(8,128)S(1)} %get-tuple-element.32), channel_id=1, source_target_pairs={{0,252},{4,8},{8,4},{12,16},{16,12},{20,24},{24,20},{28,32},{32,28... | collective-permute-start | bytes 1572872 | tf_op jit(solution)/shard_map/ppermute | solution.py:305
  18.2 16.9 %collective-permute-start.1 = (f32[512,256]{1,0:T(8,128)S(1)}, f32[512,256]{1,0:T(8,128)S(1)}, u32[]{:S(2)}, u32[]{:S(2)}) collective-permute-start(f32[512,256]{1,0:T(8,128)S(1)} %get-tuple-element.33), channel_id=1, source_target_pairs={{0,252},{4,8},{8,4},{12,16},{16,12},{20,24},{24,20},{28,32},{32,28... | collective-permute-start | bytes 1572872 | tf_op jit(solution)/shard_map/ppermute | solution.py:305
  23.2 9.7 %collective-permute-start.6 = (f32[520,256]{1,0:T(8,128)S(1)}, f32[520,256]{1,0:T(8,128)S(1)}, u32[]{:S(2)}, u32[]{:S(2)}) collective-permute-start(f32[520,256]{1,0:T(8,128)S(1)} %collective-permute-done.3.refs_0_), channel_id=1, source_target_pairs={{0,1},{1,2},{2,3},{3,0},{4,7},{5,4},{6,5},{7,6},{8,9},{9,10},{10,1... | collective-permute-start | bytes 1597448 | tf_op jit(solution)/shard_map/ppermute | solution.py:315
  36.0 5.0 %collective-permute-start.9 = (f32[64,512]{1,0:T(8,128)S(1)}, f32[64,512]{1,0:T(8,128)S(1)}, u32[]{:S(2)}, u32[]{:S(2)}) collective-permute-start(f32[64,512]{1,0:T(8,128)S(1)} %get-tuple-element.42.refs_0_), channel_id=1, source_target_pairs={{0,3},{1,0},{2,1},{3,2},{4,7},{5,4},{6,5},{7,6},{8,11},{9,8},{10,9... | collective-permute-start | bytes 393224 | tf_op jit(solution)/shard_map/ppermute | solution.py:300
  36.5 6.5 %collective-permute-start.8 = (f32[64,512]{1,0:T(8,128)S(1)}, f32[64,512]{1,0:T(8,128)S(1)}, u32[]{:S(2)}, u32[]{:S(2)}) collective-permute-start(f32[64,512]{1,0:T(8,128)S(1)} %get-tuple-element.42.refs_0_), channel_id=1, source_target_pairs={{0,2},{1,3},{2,0},{3,1},{4,6},{5,7},{6,4},{7,5},{8,10},{9,11},{10,... | collective-permute-start | bytes 393224 | tf_op jit(solution)/shard_map/ppermute | solution.py:300
  39.4 5.0 %collective-permute-start.7 = (f32[64,512]{1,0:T(8,128)S(1)}, f32[64,512]{1,0:T(8,128)S(1)}, u32[]{:S(2)}, u32[]{:S(2)}) collective-permute-start(f32[64,512]{1,0:T(8,128)S(1)} %get-tuple-element.42.refs_0_), channel_id=1, source_target_pairs={{0,1},{1,2},{2,3},{3,0},{4,5},{5,6},{6,7},{7,4},{8,9},{9,10},{10,1... | collective-permute-start | bytes 393224 | tf_op jit(solution)/shard_map/ppermute | solution.py:300
  45.1 18.8 %collective-permute-start.15 = (f32[64,2048]{1,0:T(8,128)S(1)}, f32[64,2048]{1,0:T(8,128)S(1)}, u32[]{:S(2)}, u32[]{:S(2)}) collective-permute-start(f32[64,2048]{1,0:T(8,128)S(1)} %get-tuple-element.44.vo_ref), channel_id=1, source_target_pairs={{0,252},{4,8},{8,4},{12,16},{16,12},{20,24},{24,20},{28,32},{32,28... | collective-permute-start | bytes 1572872 | tf_op jit(solution)/shard_map/ppermute | solution.py:305
  49.4 14.5 %collective-permute-start.14 = (f32[64,2048]{1,0:T(8,128)S(1)}, f32[64,2048]{1,0:T(8,128)S(1)}, u32[]{:S(2)}, u32[]{:S(2)}) collective-permute-start(f32[64,2048]{1,0:T(8,128)S(1)} %get-tuple-element.44.vo_ref), channel_id=1, source_target_pairs={{0,4},{4,0},{8,12},{12,8},{16,20},{20,16},{24,28},{28,24},{32,36},... | collective-permute-start | bytes 1572872 | tf_op jit(solution)/shard_map/ppermute | solution.py:309
  63.8 8.0 %collective-permute-start.10 = (f32[32,128]{1,0:T(8,128)S(1)}, f32[32,128]{1,0:T(8,128)S(1)}, u32[]{:S(2)}, u32[]{:S(2)}) collective-permute-start(f32[32,128]{1,0:T(8,128)S(1)} %sum_z.2), channel_id=1, source_target_pairs={{0,4},{4,0},{8,12},{12,8},{16,20},{20,16},{24,28},{28,24},{32,36},... | collective-permute-start | bytes 49160 | tf_op jit(solution)/shard_map/ppermute | solution.py:309
  66.1 17.9 %collective-permute-start.18 = (f32[64,512]{1,0:T(8,128)S(1)}, f32[64,512]{1,0:T(8,128)S(1)}, u32[]{:S(2)}, u32[]{:S(2)}) collective-permute-start(f32[64,512]{1,0:T(8,128)S(1)} %second_product.1.refs_0_), channel_id=1, source_target_pairs={{0,3},{1,0},{2,1},{3,2},{4,7},{5,4},{6,5},{7,6},{8,11},{9,8},{10,9... | collective-permute-start | bytes 393224 | tf_op jit(solution)/shard_map/ppermute | solution.py:300
  66.7 17.3 %collective-permute-start.17 = (f32[64,512]{1,0:T(8,128)S(1)}, f32[64,512]{1,0:T(8,128)S(1)}, u32[]{:S(2)}, u32[]{:S(2)}) collective-permute-start(f32[64,512]{1,0:T(8,128)S(1)} %second_product.1.refs_0_), channel_id=1, source_target_pairs={{0,2},{1,3},{2,0},{3,1},{4,6},{5,7},{6,4},{7,5},{8,10},{9,11},{10,... | collective-permute-start | bytes 393224 | tf_op jit(solution)/shard_map/ppermute | solution.py:300
  69.7 14.4 %collective-permute-start.16 = (f32[64,512]{1,0:T(8,128)S(1)}, f32[64,512]{1,0:T(8,128)S(1)}, u32[]{:S(2)}, u32[]{:S(2)}) collective-permute-start(f32[64,512]{1,0:T(8,128)S(1)} %second_product.1.refs_0_), channel_id=1, source_target_pairs={{0,1},{1,2},{2,3},{3,0},{4,5},{5,6},{6,7},{7,4},{8,9},{9,10},{10,1... | collective-permute-start | bytes 393224 | tf_op jit(solution)/shard_map/ppermute | solution.py:300
  71.8 5.0 %collective-permute-start.13 = (f32[32,128]{1,0:T(8,128)S(1)}, f32[32,128]{1,0:T(8,128)S(1)}, u32[]{:S(2)}, u32[]{:S(2)}) collective-permute-start(f32[32,128]{1,0:T(8,128)S(1)} %add.6.refs_0_), channel_id=1, source_target_pairs={{0,24},{4,28},{8,16},{12,20},{16,8},{20,12},{24,0},{28,4},{32,56},... | collective-permute-start | bytes 49160 | tf_op jit(solution)/shard_map/ppermute | solution.py:344
  72.8 4.2 %collective-permute-start.12 = (f32[32,128]{1,0:T(8,128)S(1)}, f32[32,128]{1,0:T(8,128)S(1)}, u32[]{:S(2)}, u32[]{:S(2)}) collective-permute-start(f32[32,128]{1,0:T(8,128)S(1)} %add.6.refs_0_), channel_id=1, source_target_pairs={{0,8},{4,12},{8,0},{12,4},{16,24},{20,28},{24,16},{28,20},{32,40},... | collective-permute-start | bytes 49160 | tf_op jit(solution)/shard_map/ppermute | solution.py:344
  76.8 5.2 %collective-permute-start.11 = (f32[32,128]{1,0:T(8,128)S(1)}, f32[32,128]{1,0:T(8,128)S(1)}, u32[]{:S(2)}, u32[]{:S(2)}) collective-permute-start(f32[32,128]{1,0:T(8,128)S(1)} %add.6.refs_0_), channel_id=1, source_target_pairs={{0,16},{4,20},{8,24},{12,28},{16,0},{20,4},{24,8},{28,12},{32,48},... | collective-permute-start | bytes 49160 | tf_op jit(solution)/shard_map/ppermute | solution.py:344
  97.1 1.3 %collective-permute-start.19 = (f32[32,128]{1,0:T(8,128)S(1)}, f32[32,128]{1,0:T(8,128)S(1)}, u32[]{:S(2)}, u32[]{:S(2)}) collective-permute-start(f32[32,128]{1,0:T(8,128)S(1)} %sum_z.3), channel_id=1, source_target_pairs={{0,4},{4,0},{8,12},{12,8},{16,20},{20,16},{24,28},{28,24},{32,36},... | collective-permute-start | bytes 49160 | tf_op jit(solution)/shard_map/ppermute | solution.py:309
  98.3 4.9 %collective-permute-start.22 = (f32[32,128]{1,0:T(8,128)S(1)}, f32[32,128]{1,0:T(8,128)S(1)}, u32[]{:S(2)}, u32[]{:S(2)}) collective-permute-start(f32[32,128]{1,0:T(8,128)S(1)} %add.7.refs_0_), channel_id=1, source_target_pairs={{0,24},{4,28},{8,16},{12,20},{16,8},{20,12},{24,0},{28,4},{32,56},... | collective-permute-start | bytes 49160 | tf_op jit(solution)/shard_map/ppermute | solution.py:344
  99.4 3.9 %collective-permute-start.21 = (f32[32,128]{1,0:T(8,128)S(1)}, f32[32,128]{1,0:T(8,128)S(1)}, u32[]{:S(2)}, u32[]{:S(2)}) collective-permute-start(f32[32,128]{1,0:T(8,128)S(1)} %add.7.refs_0_), channel_id=1, source_target_pairs={{0,8},{4,12},{8,0},{12,4},{16,24},{20,28},{24,16},{28,20},{32,40},... | collective-permute-start | bytes 49160 | tf_op jit(solution)/shard_map/ppermute | solution.py:344
  99.4 5.6 %collective-permute-start.20 = (f32[32,128]{1,0:T(8,128)S(1)}, f32[32,128]{1,0:T(8,128)S(1)}, u32[]{:S(2)}, u32[]{:S(2)}) collective-permute-start(f32[32,128]{1,0:T(8,128)S(1)} %add.7.refs_0_), channel_id=1, source_target_pairs={{0,16},{4,20},{8,24},{12,28},{16,0},{20,4},{24,8},{28,12},{32,48},... | collective-permute-start | bytes 49160 | tf_op jit(solution)/shard_map/ppermute | solution.py:344

commit v7 on v6

--- a/solution.py
+++ b/solution.py
@@ -73,7 +73,7 @@
     acc_ref[...] += (one[:k] + two[:k]) + (one[k : 2 * k] + two[k:] + one[2 * k :])
 
 
-def tiles_or_zeros(hit, x_ref, xah_ref, xal_ref, na_ref, v_ref, acc_ref, eh_ref, el_ref, start, rows, v_start, chunk=256):
+def tiles_or_zeros(hit, x_ref, xah_ref, xal_ref, na_ref, vectors, acc_ref, eh_ref, el_ref, start, rows, chunk=256):
     @pl.when(hit)
     def _():
         xah, xal, na = xah_ref[...], xal_ref[...], na_ref[0:1, :]
@@ -88,7 +88,7 @@
             eh_ref[here, :] = eh
             el_ref[here, :] = el
         here = pl.ds(start, rows)
-        add_product(acc_ref, v_ref[:, pl.ds(v_start, rows)], eh_ref[here, :], el_ref[here, :])
+        add_product(acc_ref, vectors(), eh_ref[here, :], el_ref[here, :])
 
     @pl.when(jnp.logical_not(hit))
     def _():
@@ -103,6 +103,9 @@
     quarter, width = outs[1].shape
     k = v_ref.shape[0]
     copies = [pltpu.make_async_copy(v_ref, sib_ref.at[pl.ds(0, k)], sems.at[len(outs)])]
+    for h in range(2):
+        source = v_ref.at[:, pl.ds(pl.multiple_of(member * quarter + h * width, width), width)]
+        copies.append(pltpu.make_async_copy(source, outs[0].at[pl.ds(quarter + h * k, k)], sems.at[len(outs) + 1 + h]))
     for step, out_ref in enumerate(outs):
         q = quarter_at(members, -step, group, member)
         source = x_ref.at[pl.ds(pl.multiple_of(q * quarter, quarter), quarter)]
@@ -117,7 +120,7 @@
             note = jnp.where((lane == slot) & (row == c), pairs_ref[c, slot].astype(f32), note)
     sib_ref[k:, :width] = note
     sib_ref[k:, width:] = jnp.zeros((NOTE, sib_ref.shape[1] - width), f32)
-    outs[0][quarter:, :] = note
+    outs[0][quarter + 2 * k :, :] = note
     for copy in copies:
         copy.wait()
 
@@ -141,20 +144,31 @@
     ):
         for j in range(BLK_DEV):
             hit = want(pairs_ref, note, group, member, members, side, j)
-            tiles_or_zeros(hit, x, xah_ref, xal_ref, na_ref, v, acc_ref, eh_ref, el_ref, j * block, block, j * block)
+            vectors = functools.partial(lambda v, j: v[:, pl.ds(j * block, block)], v, j)
+            tiles_or_zeros(hit, x, xah_ref, xal_ref, na_ref, vectors, acc_ref, eh_ref, el_ref, j * block, block)
 
 
 def cross_kernel(members, steps, *refs):
     n = len(steps)
-    x_refs, (v_ref, note_ref, pairs_ref, xah_ref, xal_ref, na_ref, in_ref, acc_ref), kept = refs[:n], refs[n : n + 8], refs[n + 8 :]
+    pairs_ref, xah_ref, xal_ref, na_ref, in_ref, acc_ref = refs[:6]
+    rows = xah_ref.shape[0]
+    kept = refs[6 : 6 + 2 * n]
+    x_refs, tails = refs[6 + 2 * n : 6 + 3 * n], refs[6 + 3 * n :]
     group, member = place()
-    rows = kept[0].shape[0]
+    k = acc_ref.shape[0]
     acc_ref[...] = in_ref[...]
     for i, step in enumerate(steps):
         eh_ref, el_ref = kept[2 * i : 2 * i + 2]
+        tail = tails[i] if tails else x_refs[i].at[rows:]
         q = quarter_at(members, step, group, member)
-        hit = want(pairs_ref, note_ref, group, member, members, CROSS, (q * BLK_DEV) // members)
-        tiles_or_zeros(hit, x_refs[i], xah_ref, xal_ref, na_ref, v_ref, acc_ref, eh_ref, el_ref, 0, rows, pl.multiple_of(q * rows, rows))
+        hit = want(pairs_ref, tail.at[2 * k :], group, member, members, CROSS, (q * BLK_DEV) // members)
+        vectors = functools.partial(lambda tail: jnp.concatenate([tail[:k, :], tail[k : 2 * k, :]], 1), tail)
+        tiles_or_zeros(hit, x_refs[i], xah_ref, xal_ref, na_ref, vectors, acc_ref, eh_ref, el_ref, 0, rows)
+
+
+def cross_first(members, steps, n_in, *refs):
+    far, rest = refs[:n_in], refs[n_in:]
+    cross_kernel(members, steps, *rest, *far)
 
 
 def gram_sum(vh, vm, vl):
@@ -309,10 +323,10 @@
     return lax.ppermute(x, "rows", [(i, i ^ 1) for i in range(lax.axis_size("rows"))])
 
 
-def passed_on(x):
+def passed_on(x, by):
     groups, members = lax.axis_size("rows"), lax.axis_size("sub")
     at = lambda g, m: g * members + m % members
-    return lax.ppermute(x, ("rows", "sub"), [(at(g, m), at(g, m + 1 - 2 * (g % 2))) for g in range(groups) for m in range(members)])
+    return lax.ppermute(x, ("rows", "sub"), [(at(g, m), at(g, m + by * (1 - 2 * (g % 2)))) for g in range(groups) for m in range(members)])
 
 
 NEAR = 8
@@ -357,32 +371,33 @@
     total = rows * groups
     vt = start_vectors.T
     pairs = pairs.T
-    cross_v = crossed(vt)
     piece = ((quarter, width), f32)
     first, second, third, sib_v = call(
         functools.partial(cut_kernel, members), [HB, HB, SM],
-        [((quarter + NOTE, width), f32), piece, piece, ((k + NOTE, rows), f32)], "cut", flops=10**6,
-        scratch=[pltpu.SemaphoreType.DMA((4,))])(
+        [((quarter + 2 * k + NOTE, width), f32), piece, piece, ((k + NOTE, rows), f32)], "cut", flops=10**6,
+        scratch=[pltpu.SemaphoreType.DMA((6,))])(
         *(pltpu.with_memory_space_constraint(a, pltpu.HBM) for a in (embeddings, vt)), pairs)
     arrived = [crossed(first)]
     sib_e = swapped(embeddings)
     sib_v = swapped(sib_v)
     arrived.append(crossed(second))
     arrived.append(crossed(third))
-    cross_note = arrived[0][quarter:]
+    tail = arrived[0][quarter:]
     part = ((k, quarter), f32)
     tiles = lambda n: [((n, quarter), bf16)] * 2
     xah, xal, na, acc, *kept = call(
         functools.partial(chip_kernel, members), [VM, VM, VM, VM, SM],
         [((quarter, width), bf16)] * 2 + [((8, quarter), f32), part] + tiles(rows) + tiles(rows), "chip_tiles",
         flops=10**10)(embeddings, vt, sib_e, sib_v, pairs)
-    arrived.append(passed_on(arrived[0]))
+    arrived.append(passed_on(arrived[0], 1))
+    tails = {1: passed_on(tail, -1), 2: passed_on(tail, 2)}
     far_tiles = {}
     for steps in ((0,), (3,), (1, 2)):
         n = len(steps)
+        far = [arrived[step] for step in steps] + [tails[step] for step in steps if step in tails]
         acc, *t = call(
-            functools.partial(cross_kernel, members, steps), [VM] * (n + 2) + [SM, VM, VM, VM, VM], [part] + tiles(quarter) * n,
-            "cross_tiles", flops=2 * 10**9)(*(arrived[step] for step in steps), cross_v, cross_note, pairs, xah, xal, na, acc)
+            functools.partial(cross_first, members, steps, len(far)), [VM] * len(far) + [SM, VM, VM, VM, VM], [part] + tiles(quarter) * n,
+            "cross_tiles", flops=2 * 10**9)(*far, pairs, xah, xal, na, acc)
         for i, step in enumerate(steps):
             far_tiles[step] = t[2 * i : 2 * i + 2]
     for step in range(members):

time: 109 us -> 109 us (level)
  starting transfers between devices: 39.5 us -> 35.9 us
  blocking collectives: 26.2 us -> 29.1 us
  waiting for transfers between devices: 19.7 us -> 20.9 us
    ppermute x5 -> x4, starting transfers between devices: 22.2 us -> 16.5 us  [crossed(): lax.ppermute(x, 'rows', [(i, (i + 2 * (i % 2) - 1) % n) for i in range(n)])]
    all_to_all x2, blocking collectives: 26.2 us -> 29.1 us  [exchanged(): return lax.all_to_all(x, ('rows', 'sub'), 0, 0, axis_index_groups=sets)]
    ppermute x1 -> x3, waiting for transfers between devices: 0.01 us -> 2.37 us  [passed_on(): lax.ppermute(x, ('rows', 'sub'), [(at(g, m), at(g, m + by * (1 - 2 * (g %...]
    ppermute x1 -> x3, starting transfers between devices: 1.28 us -> 2.83 us  [passed_on(): lax.ppermute(x, ('rows', 'sub'), [(at(g, m), at(g, m + by * (1 - 2 * (g %...]
    ppermute x6, waiting for transfers between devices: 4.99 us -> 3.56 us  [shifted(): return lax.ppermute(x, axis, [(i, (i + by) % n) for i in range(n)])]
    ppermute x5 -> x4, waiting for transfers between devices: 3 us -> 3.3 us  [crossed(): lax.ppermute(x, 'rows', [(i, (i + 2 * (i % 2) - 1) % n) for i in range(n)])]
  transfers between devices with their start and end apart: 23 -> 24, of which waited for: 10 -> 10; matrix products, arithmetic and copies ran while one was open for 0% -> 0% of each run, Pallas kernels for 14% -> 14%
where the time goes in v7:
time: 109 us
  starting transfers between devices  35.9 us (33%)
  blocking collectives  29.1 us (27%)
  Pallas kernels  21.7 us (20%)
  waiting for transfers between devices  20.9 us (19%)
    all_to_all x2, blocking collectives, exchanged(): return lax.all_to_all(x, ('rows', 'sub'), 0, 0, axis_index_groups=sets)  29.1 us
    ppermute x4, starting transfers between devices, crossed(): lax.ppermute(x, 'rows', [(i, (i + 2 * (i % 2) - 1) % n) for i in range(n)])  16.5 us
    ppermute x6, waiting for transfers between devices, row_sums(): lax.ppermute(total, 'rows', [(i, i ^ mask) for i in range(groups)])  10.5 us
    ppermute x6, starting transfers between devices, shifted(): return lax.ppermute(x, axis, [(i, (i + by) % n) for i in range(n)])  9.98 us
    pallas_call x1, Pallas kernels, on_device(): call(functools.partial(chip_kernel, members), [VM, VM, VM, VM, SM], [((qu...  7.57 us
    ppermute x6, starting transfers between devices, row_sums(): lax.ppermute(total, 'rows', [(i, i ^ mask) for i in range(groups)])  6.35 us
    ppermute x6, waiting for transfers between devices, shifted(): return lax.ppermute(x, axis, [(i, (i + by) % n) for i in range(n)])  3.56 us
    pallas_call x1, Pallas kernels, on_device(): call(last_kernel, [VM] * (1 + len(terms)), [whole], 'last')(image, *terms)  3.33 us
  transfers between devices with their start and end apart: 24, of which 10 were waited for; matrix products, arithmetic and copies ran while one was open for 0% of the time, Pallas kernels for 14%

profile of v7, /device:TPU:16, one launch (start us, length us, event | category | flops | bytes accessed | tf_op | source)
XLA Modules:
  0.0 108.7 jit_solution(3778654542980139199)
XLA Ops:
  0.0 0.0 collective-permute-start.5
  0.0 0.8 copy-done.2
  0.8 2.2 %cut.1 = (f32[648,256]{1,0:T(8,128)S(1)}, f32[512,256]{1,0:T(8,128)S(1)}, f32[512,256]{1,0:T(8,128)S(1)}, f32[72,2048]{1,0:T(8,128)S(1)}) custom-call(f32[2048,256]{1,0:T(8,128)} %x_ref.3, f32[64,2048]{1,0:T(8,128)} %bitcast.3, s32[2,8]{1,0:T(2,128)S(1)} %bitcast.5), custom_call_target="tpu_custom_call" | custom-call | flops 1000000 | bytes 1048576 | tf_op jit(solution)/shard_map/cut/pallas_call | solution.py:375
  3.0 8.2 %collective-permute-start.2 = (f32[648,256]{1,0:T(8,128)S(1)}, f32[648,256]{1,0:T(8,128)S(1)}, u32[]{:S(2)}, u32[]{:S(2)}) collective-permute-start(f32[648,256]{1,0:T(8,128)S(1)} %get-tuple-element.34), channel_id=1, source_target_pairs={{0,252},{4,8},{8,4},{12,16},{16,12},{20,24},{24,20},{28,32},{32,28... | collective-permute-start | bytes 1990664 | tf_op jit(solution)/shard_map/ppermute | solution.py:319
  11.2 0.0 collective-permute-start.6
  11.2 0.9 collective-permute-start
  12.2 4.1 %collective-permute-start.1 = (f32[512,256]{1,0:T(8,128)S(1)}, f32[512,256]{1,0:T(8,128)S(1)}, u32[]{:S(2)}, u32[]{:S(2)}) collective-permute-start(f32[512,256]{1,0:T(8,128)S(1)} %get-tuple-element.33), channel_id=1, source_target_pairs={{0,252},{4,8},{8,4},{12,16},{16,12},{20,24},{24,20},{28,32},{32,28... | collective-permute-start | bytes 1572872 | tf_op jit(solution)/shard_map/ppermute | solution.py:319
  16.3 3.3 %collective-permute-done.2.refs_0_ = f32[648,256]{1,0:T(8,128)S(1)} collective-permute-done((f32[648,256]{1,0:T(8,128)S(1)}, f32[648,256]{1,0:T(8,128)S(1)}, u32[]{:S(2)}, u32[]{:S(2)}) %collective-permute-start.2) | collective-permute-done | bytes 663584 | tf_op jit(solution)/shard_map/ppermute | solution.py:319
  19.6 0.4 collective-permute-start.4
  20.0 0.0 collective-permute-done.6.sib_v_ref
  20.0 2.4 %collective-permute-start.3 = (f32[136,256]{1,0:T(8,128)S(1)}, f32[136,256]{1,0:T(8,128)S(1)}, u32[]{:S(2)}, u32[]{:S(2)}) collective-permute-start(f32[136,256]{1,0:T(8,128)S(1)} %slice.4), channel_id=1, source_target_pairs={{0,3},{1,0},{2,1},{3,2},{4,5},{5,6},{6,7},{7,4},{8,11},{9,8},{10,9... | collective-permute-start | bytes 417800 | tf_op jit(solution)/shard_map/ppermute | solution.py:329
  22.4 0.0 collective-permute-done.5.sib_x_ref
  22.4 0.0 collective-permute-start.7
  22.4 7.6 %chip_tiles.1 = (bf16[512,256]{1,0:T(8,128)(2,1)S(1)}, bf16[512,256]{1,0:T(8,128)(2,1)S(1)}, f32[8,512]{1,0:T(8,128)S(1)}, f32[64,512]{1,0:T(8,128)S(1)}, bf16[2...) custom-call(f32[2048,256]{1,0:T(8,128)S(1)} %copy-done, ...), custom_call_target="tpu_custom_call" | custom-call | flops 10000000000 | bytes 1048576 | tf_op jit(solution)/shard_map/chip_tiles/pallas_call | solution.py:388
  30.0 0.9 cross_tiles.3
  31.0 2.4 %collective-permute-done.7.refs_0_ = f32[648,256]{1,0:T(8,128)S(1)} collective-permute-done((f32[648,256]{1,0:T(8,128)S(1)}, f32[648,256]{1,0:T(8,128)S(1)}, u32[]{:S(2)}, u32[]{:S(2)}) %collective-permute-start.7) | collective-permute-done | bytes 663584 | tf_op jit(solution)/shard_map/ppermute | solution.py:329
  33.3 0.8 cross_tiles.4
  34.1 0.0 collective-permute-done.1.refs_1_
  34.2 1.0 cross_tiles.5
  35.1 1.2 %collective-permute-start.10 = (f32[64,512]{1,0:T(8,128)S(1)}, f32[64,512]{1,0:T(8,128)S(1)}, u32[]{:S(2)}, u32[]{:S(2)}) collective-permute-start(f32[64,512]{1,0:T(8,128)S(1)} %get-tuple-element.42.refs_0_), channel_id=1, source_target_pairs={{0,3},{1,0},{2,1},{3,2},{4,7},{5,4},{6,5},{7,6},{8,11},{9,8},{10,9... | collective-permute-start | bytes 393224 | tf_op jit(solution)/shard_map/ppermute | solution.py:314
  36.3 1.8 %collective-permute-start.9 = (f32[64,512]{1,0:T(8,128)S(1)}, f32[64,512]{1,0:T(8,128)S(1)}, u32[]{:S(2)}, u32[]{:S(2)}) collective-permute-start(f32[64,512]{1,0:T(8,128)S(1)} %get-tuple-element.42.refs_0_), channel_id=1, source_target_pairs={{0,2},{1,3},{2,0},{3,1},{4,6},{5,7},{6,4},{7,5},{8,10},{9,11},{10,... | collective-permute-start | bytes 393224 | tf_op jit(solution)/shard_map/ppermute | solution.py:314
  38.1 2.5 %collective-permute-start.8 = (f32[64,512]{1,0:T(8,128)S(1)}, f32[64,512]{1,0:T(8,128)S(1)}, u32[]{:S(2)}, u32[]{:S(2)}) collective-permute-start(f32[64,512]{1,0:T(8,128)S(1)} %get-tuple-element.42.refs_0_), channel_id=1, source_target_pairs={{0,1},{1,2},{2,3},{3,0},{4,5},{5,6},{6,7},{7,4},{8,9},{9,10},{10,1... | collective-permute-start | bytes 393224 | tf_op jit(solution)/shard_map/ppermute | solution.py:314
  40.7 2.2 %collective-permute-done.9.refs_2_ = f32[64,512]{1,0:T(8,128)S(1)} collective-permute-done((f32[64,512]{1,0:T(8,128)S(1)}, f32[64,512]{1,0:T(8,128)S(1)}, u32[]{:S(2)}, u32[]{:S(2)}) %collective-permute-start.9) | collective-permute-done | bytes 131104 | tf_op jit(solution)/shard_map/ppermute | solution.py:314
  42.9 1.3 %collective-permute-done.8.refs_1_ = f32[64,512]{1,0:T(8,128)S(1)} collective-permute-done((f32[64,512]{1,0:T(8,128)S(1)}, f32[64,512]{1,0:T(8,128)S(1)}, u32[]{:S(2)}, u32[]{:S(2)}) %collective-permute-start.8) | collective-permute-done | bytes 131104 | tf_op jit(solution)/shard_map/ppermute | solution.py:314
  44.2 0.6 join.1
  44.9 3.3 %collective-permute-start.16 = (f32[64,2048]{1,0:T(8,128)S(1)}, f32[64,2048]{1,0:T(8,128)S(1)}, u32[]{:S(2)}, u32[]{:S(2)}) collective-permute-start(f32[64,2048]{1,0:T(8,128)S(1)} %get-tuple-element.44.vo_ref), channel_id=1, source_target_pairs={{0,252},{4,8},{8,4},{12,16},{16,12},{20,24},{24,20},{28,32},{32,28... | collective-permute-start | bytes 1572872 | tf_op jit(solution)/shard_map/ppermute | solution.py:319
  48.1 16.6 %all_to_all.10.gram_ref = f32[8,32,128]{2,1,0:T(8,128)S(1)} all-to-all(f32[8,32,128]{2,1,0:T(8,128)S(1)} %get-tuple-element.43), channel_id=1, replica_groups={{0,32,64,96,128,160,192,224},{1,33,65,97,129,161,193,225},{2,34,66,98,1..., dimensions={0} | all-to-all | bytes 262144 | tf_op jit(solution)/shard_map/all_to_all | solution.py:341
  64.7 0.1 collective-permute-start.11
  64.8 2.2 %second_product.1.refs_0_ = f32[64,512]{1,0:T(8,128)S(1)} custom-call(f32[64,2048]{1,0:T(8,128)S(1)} %get-tuple-element.44.vo_ref, f32[64,2048]{1,0:T(8,128)S(1)} %collective-permute-done.15.vs_ref, f32[64,2048]{1,0:T(8,128)S(1)} %collective-permute-done.16.vc_ref, bf16[2048,512]{1,0:T(8,128)(2,1)S(1)} %get-tuple-element.45.refs_0_, ...), custom_call_target="tpu_custom_call" | custom-call | flops 1000000000 | bytes 1048576 | tf_op jit(solution)/shard_map/second_product/pallas_call | solution.py:412
  67.1 1.2 %collective-permute-start.19 = (f32[64,512]{1,0:T(8,128)S(1)}, f32[64,512]{1,0:T(8,128)S(1)}, u32[]{:S(2)}, u32[]{:S(2)}) collective-permute-start(f32[64,512]{1,0:T(8,128)S(1)} %second_product.1.refs_0_), channel_id=1, source_target_pairs={{0,3},{1,0},{2,1},{3,2},{4,7},{5,4},{6,5},{7,6},{8,11},{9,8},{10,9... | collective-permute-start | bytes 393224 | tf_op jit(solution)/shard_map/ppermute | solution.py:314
  68.3 1.3 %collective-permute-start.18 = (f32[64,512]{1,0:T(8,128)S(1)}, f32[64,512]{1,0:T(8,128)S(1)}, u32[]{:S(2)}, u32[]{:S(2)}) collective-permute-start(f32[64,512]{1,0:T(8,128)S(1)} %second_product.1.refs_0_), channel_id=1, source_target_pairs={{0,2},{1,3},{2,0},{3,1},{4,6},{5,7},{6,4},{7,5},{8,10},{9,11},{10,... | collective-permute-start | bytes 393224 | tf_op jit(solution)/shard_map/ppermute | solution.py:314
  69.6 1.9 %collective-permute-start.17 = (f32[64,512]{1,0:T(8,128)S(1)}, f32[64,512]{1,0:T(8,128)S(1)}, u32[]{:S(2)}, u32[]{:S(2)}) collective-permute-start(f32[64,512]{1,0:T(8,128)S(1)} %second_product.1.refs_0_), channel_id=1, source_target_pairs={{0,1},{1,2},{2,3},{3,0},{4,5},{5,6},{6,7},{7,4},{8,9},{9,10},{10,1... | collective-permute-start | bytes 393224 | tf_op jit(solution)/shard_map/ppermute | solution.py:314
  71.6 1.6 %collective-permute-start.14 = (f32[32,128]{1,0:T(8,128)S(1)}, f32[32,128]{1,0:T(8,128)S(1)}, u32[]{:S(2)}, u32[]{:S(2)}) collective-permute-start(f32[32,128]{1,0:T(8,128)S(1)} %add.6.refs_0_), channel_id=1, source_target_pairs={{0,24},{4,28},{8,16},{12,20},{16,8},{20,12},{24,0},{28,4},{32,56},... | collective-permute-start | bytes 49160 | tf_op jit(solution)/shard_map/ppermute | solution.py:358
  73.2 3.4 %collective-permute-done.14.refs_3_ = f32[32,128]{1,0:T(8,128)S(1)} collective-permute-done((f32[32,128]{1,0:T(8,128)S(1)}, f32[32,128]{1,0:T(8,128)S(1)}, u32[]{:S(2)}, u32[]{:S(2)}) %collective-permute-start.14) | collective-permute-done | bytes 16416 | tf_op jit(solution)/shard_map/ppermute | solution.py:358
  76.6 0.0 collective-permute-start.12
  76.6 0.4 collective-permute-done.13.refs_2_
  77.0 4.9 %collective-permute-done.12.refs_1_ = f32[32,128]{1,0:T(8,128)S(1)} collective-permute-done((f32[32,128]{1,0:T(8,128)S(1)}, f32[32,128]{1,0:T(8,128)S(1)}, u32[]{:S(2)}, u32[]{:S(2)}) %collective-permute-start.12) | collective-permute-done | bytes 16416 | tf_op jit(solution)/shard_map/ppermute | solution.py:358
  81.8 2.0 %factor.1.inv_ref = f32[64,64]{1,0:T(8,128)S(1)} custom-call(f32[32,128]{1,0:T(8,128)S(1)} %add.6.refs_0_, f32[32,128]{1,0:T(8,128)S(1)} %collective-permute-done.12.refs_1_, f32[32,128]{1,0:T(8,128)S(1)} %collective-permute-done.13.refs_2_, f32[32,128]{1,0:T(8,128)S(1)} %collective-permute-done.14.refs_3_), custom_call_target="tpu_custom_call" | custom-call | flops 1000000000 | bytes 1048576 | tf_op jit(solution)/shard_map/factor/pallas_call | solution.py:415
  83.8 0.0 collective-permute-done.17.refs_1_
  83.9 1.1 %image.1 = (f32[64,2048]{1,0:T(8,128)S(1)}, f32[8,32,128]{2,1,0:T(8,128)S(1)}) custom-call(f32[64,64]{1,0:T(8,128)S(1)} %factor.1.inv_ref, f32[64,512]{1,0:T(8,128)S(1)} %second_product.1.refs_0_, f32[64,512]{1,0:T(8,128)S(1)} %collective-permute-done.17.refs_1_, f32[64,512]{1,0:T(8,128)S(1)} %collective-permute-done.18.refs_2_, ...), custom_call_target="tpu_custom_call" | custom-call | flops 1000000000 | bytes 1048576 | tf_op jit(solution)/shard_map/image/pallas_call | solution.py:416
  85.0 12.5 %all_to_all.11.gram_ref = f32[8,32,128]{2,1,0:T(8,128)S(1)} all-to-all(f32[8,32,128]{2,1,0:T(8,128)S(1)} %get-tuple-element.58), channel_id=1, replica_groups={{0,32,64,96,128,160,192,224},{1,33,65,97,129,161,193,225},{2,34,66,98,1..., dimensions={0} | all-to-all | bytes 262144 | tf_op jit(solution)/shard_map/all_to_all | solution.py:341
  97.5 0.1 collective-permute-start.20
  97.6 1.2 %collective-permute-done.20 = f32[32,128]{1,0:T(8,128)S(1)} collective-permute-done((f32[32,128]{1,0:T(8,128)S(1)}, f32[32,128]{1,0:T(8,128)S(1)}, u32[]{:S(2)}, u32[]{:S(2)}) %collective-permute-start.20) | collective-permute-done | bytes 16416 | tf_op jit(solution)/shard_map/ppermute | solution.py:323
  98.7 1.1 collective-permute-start.23
  99.8 3.6 %collective-permute-start.21 = (f32[32,128]{1,0:T(8,128)S(1)}, f32[32,128]{1,0:T(8,128)S(1)}, u32[]{:S(2)}, u32[]{:S(2)}) collective-permute-start(f32[32,128]{1,0:T(8,128)S(1)} %add.7.refs_0_), channel_id=1, source_target_pairs={{0,16},{4,20},{8,24},{12,28},{16,0},{20,4},{24,8},{28,12},{32,48},... | collective-permute-start | bytes 49160 | tf_op jit(solution)/shard_map/ppermute | solution.py:358
  103.4 0.2 collective-permute-done.23.refs_3_
  103.7 1.6 %collective-permute-done.21.refs_1_ = f32[32,128]{1,0:T(8,128)S(1)} collective-permute-done((f32[32,128]{1,0:T(8,128)S(1)}, f32[32,128]{1,0:T(8,128)S(1)}, u32[]{:S(2)}, u32[]{:S(2)}) %collective-permute-start.21) | collective-permute-done | bytes 16416 | tf_op jit(solution)/shard_map/ppermute | solution.py:358
  105.3 3.3 %last.1 = f32[64,2048]{1,0:T(8,128)} custom-call(f32[64,2048]{1,0:T(8,128)S(1)} %get-tuple-element.57.image_ref, f32[32,128]{1,0:T(8,128)S(1)} %add.7.refs_0_, f32[32,128]{1,0:T(8,128)S(1)} %collective-permute-done.21.refs_1_, f32[32,128]{1,0:T(8,128)S(1)} %collective-permute-done.22.refs_2_, f32[32,128]{1,0:T(8,128)S(1)} %collective-permute-done.23.refs_3_), custom_call_target="tpu_custom_call" | custom-call | flops 1000000000 | bytes 1048576 | tf_op jit(solution)/shard_map/last/pallas_call | solution.py:418
  (23 shorter events, 0.1 us)
Async XLA Ops:
  0.0 22.4 %copy-start = (f32[2048,256]{1,0:T(8,128)S(1)}, f32[2048,256]{1,0:T(8,128)}, u32[]{:S(2)}) copy-start(f32[2048,256]{1,0:T(8,128)} %x_ref.3) | copy-start | bytes 6291460
  0.0 22.4 %copy-start.1 = (f32[2048,64]{0,1:T(8,128)S(1)}, f32[2048,64]{0,1:T(8,128)}, u32[]{:S(2)}) copy-start(f32[2048,64]{0,1:T(8,128)} %param.4) | copy-start | bytes 1572868
  0.0 22.4 %collective-permute-start.5 = (f32[2048,256]{1,0:T(8,128)}, f32[2048,256]{1,0:T(8,128)S(1)}, u32[]{:S(2)}, u32[]{:S(2)}) collective-permute-start(f32[2048,256]{1,0:T(8,128)} %x_ref.3), channel_id=1, source_target_pairs={{0,4},{4,0},{8,12},{12,8},{16,20},{20,16},{24,28},{28,24},{32,36},... | collective-permute-start | bytes 6291464 | tf_op jit(solution)/shard_map/ppermute | solution.py:323
  0.0 0.8 copy-start.2
  3.0 16.6 %collective-permute-start.2 = (f32[648,256]{1,0:T(8,128)S(1)}, f32[648,256]{1,0:T(8,128)S(1)}, u32[]{:S(2)}, u32[]{:S(2)}) collective-permute-start(f32[648,256]{1,0:T(8,128)S(1)} %get-tuple-element.34), channel_id=1, source_target_pairs={{0,252},{4,8},{8,4},{12,16},{16,12},{20,24},{24,20},{28,32},{32,28... | collective-permute-start | bytes 1990664 | tf_op jit(solution)/shard_map/ppermute | solution.py:319
  11.2 8.8 %collective-permute-start.6 = (f32[72,2048]{1,0:T(8,128)S(1)}, f32[72,2048]{1,0:T(8,128)S(1)}, u32[]{:S(2)}, u32[]{:S(2)}) collective-permute-start(f32[72,2048]{1,0:T(8,128)S(1)} %get-tuple-element.35), channel_id=1, source_target_pairs={{0,4},{4,0},{8,12},{12,8},{16,20},{20,16},{24,28},{28,24},{32,36},... | collective-permute-start | bytes 1769480 | tf_op jit(solution)/shard_map/ppermute | solution.py:323
  11.2 22.9 %collective-permute-start = (f32[512,256]{1,0:T(8,128)S(1)}, f32[512,256]{1,0:T(8,128)S(1)}, u32[]{:S(2)}, u32[]{:S(2)}) collective-permute-start(f32[512,256]{1,0:T(8,128)S(1)} %get-tuple-element.32), channel_id=1, source_target_pairs={{0,252},{4,8},{8,4},{12,16},{16,12},{20,24},{24,20},{28,32},{32,28... | collective-permute-start | bytes 1572872 | tf_op jit(solution)/shard_map/ppermute | solution.py:319
  12.2 22.0 %collective-permute-start.1 = (f32[512,256]{1,0:T(8,128)S(1)}, f32[512,256]{1,0:T(8,128)S(1)}, u32[]{:S(2)}, u32[]{:S(2)}) collective-permute-start(f32[512,256]{1,0:T(8,128)S(1)} %get-tuple-element.33), channel_id=1, source_target_pairs={{0,252},{4,8},{8,4},{12,16},{16,12},{20,24},{24,20},{28,32},{32,28... | collective-permute-start | bytes 1572872 | tf_op jit(solution)/shard_map/ppermute | solution.py:319
  19.6 14.6 %collective-permute-start.4 = (f32[136,256]{1,0:T(8,128)S(1)}, f32[136,256]{1,0:T(8,128)S(1)}, u32[]{:S(2)}, u32[]{:S(2)}) collective-permute-start(f32[136,256]{1,0:T(8,128)S(1)} %slice.4), channel_id=1, source_target_pairs={{0,2},{1,3},{2,0},{3,1},{4,6},{5,7},{6,4},{7,5},{8,10},{9,11},{10,... | collective-permute-start | bytes 417800 | tf_op jit(solution)/shard_map/ppermute | solution.py:329
  20.0 14.1 %collective-permute-start.3 = (f32[136,256]{1,0:T(8,128)S(1)}, f32[136,256]{1,0:T(8,128)S(1)}, u32[]{:S(2)}, u32[]{:S(2)}) collective-permute-start(f32[136,256]{1,0:T(8,128)S(1)} %slice.4), channel_id=1, source_target_pairs={{0,3},{1,0},{2,1},{3,2},{4,5},{5,6},{6,7},{7,4},{8,11},{9,8},{10,9... | collective-permute-start | bytes 417800 | tf_op jit(solution)/shard_map/ppermute | solution.py:329
  22.4 10.9 %collective-permute-start.7 = (f32[648,256]{1,0:T(8,128)S(1)}, f32[648,256]{1,0:T(8,128)S(1)}, u32[]{:S(2)}, u32[]{:S(2)}) collective-permute-start(f32[648,256]{1,0:T(8,128)S(1)} %collective-permute-done.2.refs_0_), channel_id=1, source_target_pairs={{0,1},{1,2},{2,3},{3,0},{4,7},{5,4},{6,5},{7,6},{8,9},{9,10},{10,1... | collective-permute-start | bytes 1990664 | tf_op jit(solution)/shard_map/ppermute | solution.py:329
  35.1 5.5 %collective-permute-start.10 = (f32[64,512]{1,0:T(8,128)S(1)}, f32[64,512]{1,0:T(8,128)S(1)}, u32[]{:S(2)}, u32[]{:S(2)}) collective-permute-start(f32[64,512]{1,0:T(8,128)S(1)} %get-tuple-element.42.refs_0_), channel_id=1, source_target_pairs={{0,3},{1,0},{2,1},{3,2},{4,7},{5,4},{6,5},{7,6},{8,11},{9,8},{10,9... | collective-permute-start | bytes 393224 | tf_op jit(solution)/shard_map/ppermute | solution.py:314
  36.3 6.6 %collective-permute-start.9 = (f32[64,512]{1,0:T(8,128)S(1)}, f32[64,512]{1,0:T(8,128)S(1)}, u32[]{:S(2)}, u32[]{:S(2)}) collective-permute-start(f32[64,512]{1,0:T(8,128)S(1)} %get-tuple-element.42.refs_0_), channel_id=1, source_target_pairs={{0,2},{1,3},{2,0},{3,1},{4,6},{5,7},{6,4},{7,5},{8,10},{9,11},{10,... | collective-permute-start | bytes 393224 | tf_op jit(solution)/shard_map/ppermute | solution.py:314
  38.1 6.1 %collective-permute-start.8 = (f32[64,512]{1,0:T(8,128)S(1)}, f32[64,512]{1,0:T(8,128)S(1)}, u32[]{:S(2)}, u32[]{:S(2)}) collective-permute-start(f32[64,512]{1,0:T(8,128)S(1)} %get-tuple-element.42.refs_0_), channel_id=1, source_target_pairs={{0,1},{1,2},{2,3},{3,0},{4,5},{5,6},{6,7},{7,4},{8,9},{9,10},{10,1... | collective-permute-start | bytes 393224 | tf_op jit(solution)/shard_map/ppermute | solution.py:314
  44.9 20.0 %collective-permute-start.16 = (f32[64,2048]{1,0:T(8,128)S(1)}, f32[64,2048]{1,0:T(8,128)S(1)}, u32[]{:S(2)}, u32[]{:S(2)}) collective-permute-start(f32[64,2048]{1,0:T(8,128)S(1)} %get-tuple-element.44.vo_ref), channel_id=1, source_target_pairs={{0,252},{4,8},{8,4},{12,16},{16,12},{20,24},{24,20},{28,32},{32,28... | collective-permute-start | bytes 1572872 | tf_op jit(solution)/shard_map/ppermute | solution.py:319
  48.1 16.7 %collective-permute-start.15 = (f32[64,2048]{1,0:T(8,128)S(1)}, f32[64,2048]{1,0:T(8,128)S(1)}, u32[]{:S(2)}, u32[]{:S(2)}) collective-permute-start(f32[64,2048]{1,0:T(8,128)S(1)} %get-tuple-element.44.vo_ref), channel_id=1, source_target_pairs={{0,4},{4,0},{8,12},{12,8},{16,20},{20,16},{24,28},{28,24},{32,36},... | collective-permute-start | bytes 1572872 | tf_op jit(solution)/shard_map/ppermute | solution.py:323
  64.7 6.8 %collective-permute-start.11 = (f32[32,128]{1,0:T(8,128)S(1)}, f32[32,128]{1,0:T(8,128)S(1)}, u32[]{:S(2)}, u32[]{:S(2)}) collective-permute-start(f32[32,128]{1,0:T(8,128)S(1)} %sum_z.2), channel_id=1, source_target_pairs={{0,4},{4,0},{8,12},{12,8},{16,20},{20,16},{24,28},{28,24},{32,36},... | collective-permute-start | bytes 49160 | tf_op jit(solution)/shard_map/ppermute | solution.py:323
  67.1 16.7 %collective-permute-start.19 = (f32[64,512]{1,0:T(8,128)S(1)}, f32[64,512]{1,0:T(8,128)S(1)}, u32[]{:S(2)}, u32[]{:S(2)}) collective-permute-start(f32[64,512]{1,0:T(8,128)S(1)} %second_product.1.refs_0_), channel_id=1, source_target_pairs={{0,3},{1,0},{2,1},{3,2},{4,7},{5,4},{6,5},{7,6},{8,11},{9,8},{10,9... | collective-permute-start | bytes 393224 | tf_op jit(solution)/shard_map/ppermute | solution.py:314
  68.3 15.5 %collective-permute-start.18 = (f32[64,512]{1,0:T(8,128)S(1)}, f32[64,512]{1,0:T(8,128)S(1)}, u32[]{:S(2)}, u32[]{:S(2)}) collective-permute-start(f32[64,512]{1,0:T(8,128)S(1)} %second_product.1.refs_0_), channel_id=1, source_target_pairs={{0,2},{1,3},{2,0},{3,1},{4,6},{5,7},{6,4},{7,5},{8,10},{9,11},{10,... | collective-permute-start | bytes 393224 | tf_op jit(solution)/shard_map/ppermute | solution.py:314
  69.6 14.2 %collective-permute-start.17 = (f32[64,512]{1,0:T(8,128)S(1)}, f32[64,512]{1,0:T(8,128)S(1)}, u32[]{:S(2)}, u32[]{:S(2)}) collective-permute-start(f32[64,512]{1,0:T(8,128)S(1)} %second_product.1.refs_0_), channel_id=1, source_target_pairs={{0,1},{1,2},{2,3},{3,0},{4,5},{5,6},{6,7},{7,4},{8,9},{9,10},{10,1... | collective-permute-start | bytes 393224 | tf_op jit(solution)/shard_map/ppermute | solution.py:314
  71.6 5.0 %collective-permute-start.14 = (f32[32,128]{1,0:T(8,128)S(1)}, f32[32,128]{1,0:T(8,128)S(1)}, u32[]{:S(2)}, u32[]{:S(2)}) collective-permute-start(f32[32,128]{1,0:T(8,128)S(1)} %add.6.refs_0_), channel_id=1, source_target_pairs={{0,24},{4,28},{8,16},{12,20},{16,8},{20,12},{24,0},{28,4},{32,56},... | collective-permute-start | bytes 49160 | tf_op jit(solution)/shard_map/ppermute | solution.py:358
  73.2 3.7 %collective-permute-start.13 = (f32[32,128]{1,0:T(8,128)S(1)}, f32[32,128]{1,0:T(8,128)S(1)}, u32[]{:S(2)}, u32[]{:S(2)}) collective-permute-start(f32[32,128]{1,0:T(8,128)S(1)} %add.6.refs_0_), channel_id=1, source_target_pairs={{0,8},{4,12},{8,0},{12,4},{16,24},{20,28},{24,16},{28,20},{32,40},... | collective-permute-start | bytes 49160 | tf_op jit(solution)/shard_map/ppermute | solution.py:358
  76.6 5.2 %collective-permute-start.12 = (f32[32,128]{1,0:T(8,128)S(1)}, f32[32,128]{1,0:T(8,128)S(1)}, u32[]{:S(2)}, u32[]{:S(2)}) collective-permute-start(f32[32,128]{1,0:T(8,128)S(1)} %add.6.refs_0_), channel_id=1, source_target_pairs={{0,16},{4,20},{8,24},{12,28},{16,0},{20,4},{24,8},{28,12},{32,48},... | collective-permute-start | bytes 49160 | tf_op jit(solution)/shard_map/ppermute | solution.py:358
  97.5 1.3 %collective-permute-start.20 = (f32[32,128]{1,0:T(8,128)S(1)}, f32[32,128]{1,0:T(8,128)S(1)}, u32[]{:S(2)}, u32[]{:S(2)}) collective-permute-start(f32[32,128]{1,0:T(8,128)S(1)} %sum_z.3), channel_id=1, source_target_pairs={{0,4},{4,0},{8,12},{12,8},{16,20},{20,16},{24,28},{28,24},{32,36},... | collective-permute-start | bytes 49160 | tf_op jit(solution)/shard_map/ppermute | solution.py:323
  98.7 4.9 %collective-permute-start.23 = (f32[32,128]{1,0:T(8,128)S(1)}, f32[32,128]{1,0:T(8,128)S(1)}, u32[]{:S(2)}, u32[]{:S(2)}) collective-permute-start(f32[32,128]{1,0:T(8,128)S(1)} %add.7.refs_0_), channel_id=1, source_target_pairs={{0,24},{4,28},{8,16},{12,20},{16,8},{20,12},{24,0},{28,4},{32,56},... | collective-permute-start | bytes 49160 | tf_op jit(solution)/shard_map/ppermute | solution.py:358
  99.8 3.9 %collective-permute-start.22 = (f32[32,128]{1,0:T(8,128)S(1)}, f32[32,128]{1,0:T(8,128)S(1)}, u32[]{:S(2)}, u32[]{:S(2)}) collective-permute-start(f32[32,128]{1,0:T(8,128)S(1)} %add.7.refs_0_), channel_id=1, source_target_pairs={{0,8},{4,12},{8,0},{12,4},{16,24},{20,28},{24,16},{28,20},{32,40},... | collective-permute-start | bytes 49160 | tf_op jit(solution)/shard_map/ppermute | solution.py:358
  99.8 5.5 %collective-permute-start.21 = (f32[32,128]{1,0:T(8,128)S(1)}, f32[32,128]{1,0:T(8,128)S(1)}, u32[]{:S(2)}, u32[]{:S(2)}) collective-permute-start(f32[32,128]{1,0:T(8,128)S(1)} %add.7.refs_0_), channel_id=1, source_target_pairs={{0,16},{4,20},{8,24},{12,28},{16,0},{20,4},{24,8},{28,12},{32,48},... | collective-permute-start | bytes 49160 | tf_op jit(solution)/shard_map/ppermute | solution.py:358

commit v8 on v6

--- a/solution.py
+++ b/solution.py
@@ -49,20 +49,14 @@
     return group, member
 
 
-def want(pairs_ref, note_ref, group, member, members, side, j):
-    mine = group * BLK_DEV + (member * BLK_DEV) // members
-    other = (group + side * (1 - 2 * (group & 1))) * BLK_DEV + j
+def want(pairs_ref, note_ref, members, side, j):
+    group, member = place()
+    mine = group * BLK_DEV + j
+    other = (group + side * (1 - 2 * (group & 1))) * BLK_DEV + (member * BLK_DEV) // members
     low, high = jnp.minimum(mine, other), jnp.maximum(mine, other)
-    hit = listed(pairs_ref, low, high)
-    if note_ref is not None:
-        slot = lax.broadcasted_iota(jnp.int32, (1, note_ref.shape[1]), 1) < pairs_ref.shape[1]
-        same = slot & (note_ref[0:1, :] == low.astype(f32)) & (note_ref[1:2, :] == high.astype(f32))
-        hit = hit | (jnp.max(same.astype(f32)) > 0.5)
-    return hit
-
-
-def quarter_at(members, step, group, member):
-    return (member + step * (1 - 2 * (group & 1))) & (members - 1)
+    slot = lax.broadcasted_iota(jnp.int32, (1, note_ref.shape[1]), 1) < pairs_ref.shape[1]
+    same = slot & (note_ref[0:1, :] == low.astype(f32)) & (note_ref[1:2, :] == high.astype(f32))
+    return listed(pairs_ref, low, high) | (jnp.max(same.astype(f32)) > 0.5)
 
 
 def add_product(acc_ref, v, eh, el):
@@ -73,88 +67,51 @@
     acc_ref[...] += (one[:k] + two[:k]) + (one[k : 2 * k] + two[k:] + one[2 * k :])
 
 
-def tiles_or_zeros(hit, x_ref, xah_ref, xal_ref, na_ref, v_ref, acc_ref, eh_ref, el_ref, start, rows, v_start, chunk=256):
-    @pl.when(hit)
-    def _():
-        xah, xal, na = xah_ref[...], xal_ref[...], na_ref[0:1, :]
-        for c in range(rows // chunk):
-            here = pl.ds(start + c * chunk, chunk)
-            x = x_ref[here, :]
-            nb = jnp.sum(x * x, axis=1, keepdims=True) * SCALE
-            xh, xl = split2(x)
-            d = dot(xh, xah, NT) + (dot(xh, xal, NT) + dot(xl, xah, NT))
-            e = jnp.exp2(jnp.minimum(d - nb - na, 0.0))
-            eh, el = split2(e)
-            eh_ref[here, :] = eh
-            el_ref[here, :] = el
-        here = pl.ds(start, rows)
-        add_product(acc_ref, v_ref[:, pl.ds(v_start, rows)], eh_ref[here, :], el_ref[here, :])
-
-    @pl.when(jnp.logical_not(hit))
-    def _():
-        here = pl.ds(start, rows)
-        eh_ref[here, :] = jnp.zeros((rows, eh_ref.shape[1]), bf16)
-        el_ref[here, :] = jnp.zeros((rows, el_ref.shape[1]), bf16)
-
-
-def cut_kernel(members, x_ref, v_ref, pairs_ref, *refs):
-    group, member = place()
-    outs, sib_ref, sems = refs[:-2], refs[-2], refs[-1]
-    quarter, width = outs[1].shape
-    k = v_ref.shape[0]
-    copies = [pltpu.make_async_copy(v_ref, sib_ref.at[pl.ds(0, k)], sems.at[len(outs)])]
-    for step, out_ref in enumerate(outs):
-        q = quarter_at(members, -step, group, member)
-        source = x_ref.at[pl.ds(pl.multiple_of(q * quarter, quarter), quarter)]
-        copies.append(pltpu.make_async_copy(source, out_ref.at[pl.ds(0, quarter)], sems.at[step]))
-    for copy in copies:
-        copy.start()
+def cut_kernel(x_ref, pairs_ref, out_ref, sem):
+    _, member = place()
+    quarter, width = out_ref.shape[0] - NOTE, out_ref.shape[1]
+    source = x_ref.at[pl.ds(pl.multiple_of(member * quarter, quarter), quarter)]
+    copy = pltpu.make_async_copy(source, out_ref.at[pl.ds(0, quarter)], sem)
+    copy.start()
     lane = lax.broadcasted_iota(jnp.int32, (NOTE, width), 1)
     row = lax.broadcasted_iota(jnp.int32, (NOTE, width), 0)
     note = jnp.zeros((NOTE, width), f32)
     for slot in range(pairs_ref.shape[1]):
         for c in range(2):
             note = jnp.where((lane == slot) & (row == c), pairs_ref[c, slot].astype(f32), note)
-    sib_ref[k:, :width] = note
-    sib_ref[k:, width:] = jnp.zeros((NOTE, sib_ref.shape[1] - width), f32)
-    outs[0][quarter:, :] = note
-    for copy in copies:
-        copy.wait()
-
-
-def chip_kernel(members, x_ref, v_ref, sib_x_ref, sib_v_ref, pairs_ref, xah_ref, xal_ref, na_ref, acc_ref, *kept):
-    group, member = place()
-    rows = x_ref.shape[0]
-    quarter = rows // members
-    block = rows // BLK_DEV
-    xa = x_ref[pl.ds(pl.multiple_of(member * quarter, quarter), quarter), :]
+    out_ref[quarter:, :] = note
+    copy.wait()
+
+
+def tiles_kernel(members, side, x_ref, v_ref, message_ref, pairs_ref, acc_ref, eh_ref, el_ref, xah_ref, xal_ref, chunk=256):
+    quarter = message_ref.shape[0] - NOTE
+    block = x_ref.shape[0] // BLK_DEV
+    xa = message_ref[:quarter, :]
     ones = jnp.ones((8, xa.shape[1]), f32)
-    na_ref[...] = lax.dot_general(ones, xa * xa, NT, precision=lax.Precision.HIGHEST, preferred_element_type=f32) * SCALE
-    xah, xal = split2(xa * (2.0 * SCALE))
-    xah_ref[...] = xah
-    xal_ref[...] = xal
+    na = lax.dot_general(ones, xa * xa, NT, precision=lax.Precision.HIGHEST, preferred_element_type=f32)[0:1, :] * SCALE
+    xah_ref[...], xal_ref[...] = split2(xa * (2.0 * SCALE))
     acc_ref[...] = jnp.zeros_like(acc_ref)
-    k = v_ref.shape[0]
-    for x, v, note, side, (eh_ref, el_ref) in (
-        (x_ref, v_ref, None, OWN, kept[:2]),
-        (sib_x_ref, sib_v_ref.at[:k], sib_v_ref.at[k:], SIB, kept[2:]),
-    ):
-        for j in range(BLK_DEV):
-            hit = want(pairs_ref, note, group, member, members, side, j)
-            tiles_or_zeros(hit, x, xah_ref, xal_ref, na_ref, v, acc_ref, eh_ref, el_ref, j * block, block, j * block)
-
-
-def cross_kernel(members, steps, *refs):
-    n = len(steps)
-    x_refs, (v_ref, note_ref, pairs_ref, xah_ref, xal_ref, na_ref, in_ref, acc_ref), kept = refs[:n], refs[n : n + 8], refs[n + 8 :]
-    group, member = place()
-    rows = kept[0].shape[0]
-    acc_ref[...] = in_ref[...]
-    for i, step in enumerate(steps):
-        eh_ref, el_ref = kept[2 * i : 2 * i + 2]
-        q = quarter_at(members, step, group, member)
-        hit = want(pairs_ref, note_ref, group, member, members, CROSS, (q * BLK_DEV) // members)
-        tiles_or_zeros(hit, x_refs[i], xah_ref, xal_ref, na_ref, v_ref, acc_ref, eh_ref, el_ref, 0, rows, pl.multiple_of(q * rows, rows))
+    for j in range(BLK_DEV):
+        hit = want(pairs_ref, message_ref.at[quarter:], members, side, j)
+        all_rows = pl.ds(j * block, block)
+
+        @pl.when(hit)
+        def _():
+            xah, xal = xah_ref[...], xal_ref[...]
+            for c in range(block // chunk):
+                here = pl.ds(j * block + c * chunk, chunk)
+                x = x_ref[here, :]
+                nb = jnp.sum(x * x, axis=1, keepdims=True) * SCALE
+                xh, xl = split2(x)
+                d = dot(xh, xah, NT) + (dot(xh, xal, NT) + dot(xl, xah, NT))
+                e = jnp.exp2(jnp.minimum(d - nb - na, 0.0))
+                eh_ref[here, :], el_ref[here, :] = split2(e)
+            add_product(acc_ref, v_ref[:, all_rows], eh_ref[all_rows, :], el_ref[all_rows, :])
+
+        @pl.when(jnp.logical_not(hit))
+        def _():
+            eh_ref[all_rows, :] = jnp.zeros((block, quarter), bf16)
+            el_ref[all_rows, :] = jnp.zeros((block, quarter), bf16)
 
 
 def gram_sum(vh, vm, vl):
@@ -194,20 +151,15 @@
     put_gram(gram_ref, full_ref[...], total)
 
 
-def second_kernel(members, vo_ref, vs_ref, vc_ref, *refs):
-    group, member = place()
-    kept, out_ref = refs[:-1], refs[-1]
-    out_ref[...] = jnp.zeros_like(out_ref)
-    for v_ref, eh_ref, el_ref in ((vo_ref, kept[0], kept[1]), (vs_ref, kept[2], kept[3])):
-        block = v_ref.shape[1] // BLK_DEV
+def second_kernel(v_ref, *refs):
+    n = len(refs) // 3
+    kept, outs = refs[: 2 * n], refs[2 * n :]
+    block = v_ref.shape[1] // BLK_DEV
+    for i, out_ref in enumerate(outs):
+        out_ref[...] = jnp.zeros_like(out_ref)
         for j in range(BLK_DEV):
             here = pl.ds(j * block, block)
-            add_product(out_ref, v_ref[:, here], eh_ref[here, :], el_ref[here, :])
-    for step in range(members):
-        eh_ref, el_ref = kept[4 + 2 * step : 6 + 2 * step]
-        rows = eh_ref.shape[0]
-        q = quarter_at(members, step, group, member)
-        add_product(out_ref, vc_ref[:, pl.ds(pl.multiple_of(q * rows, rows), rows)], eh_ref[...], el_ref[...])
+            add_product(out_ref, v_ref[:, here], kept[2 * i][here, :], kept[2 * i + 1][here, :])
 
 
 def factor_inverse(gram, w=8):
@@ -309,12 +261,6 @@
     return lax.ppermute(x, "rows", [(i, i ^ 1) for i in range(lax.axis_size("rows"))])
 
 
-def passed_on(x):
-    groups, members = lax.axis_size("rows"), lax.axis_size("sub")
-    at = lambda g, m: g * members + m % members
-    return lax.ppermute(x, ("rows", "sub"), [(at(g, m), at(g, m + 1 - 2 * (g % 2))) for g in range(groups) for m in range(members)])
-
-
 NEAR = 8
 
 
@@ -357,45 +303,32 @@
     total = rows * groups
     vt = start_vectors.T
     pairs = pairs.T
-    cross_v = crossed(vt)
-    piece = ((quarter, width), f32)
-    first, second, third, sib_v = call(
-        functools.partial(cut_kernel, members), [HB, HB, SM],
-        [((quarter + NOTE, width), f32), piece, piece, ((k + NOTE, rows), f32)], "cut", flops=10**6,
-        scratch=[pltpu.SemaphoreType.DMA((4,))])(
-        *(pltpu.with_memory_space_constraint(a, pltpu.HBM) for a in (embeddings, vt)), pairs)
-    arrived = [crossed(first)]
-    sib_e = swapped(embeddings)
-    sib_v = swapped(sib_v)
-    arrived.append(crossed(second))
-    arrived.append(crossed(third))
-    cross_note = arrived[0][quarter:]
     part = ((k, quarter), f32)
-    tiles = lambda n: [((n, quarter), bf16)] * 2
-    xah, xal, na, acc, *kept = call(
-        functools.partial(chip_kernel, members), [VM, VM, VM, VM, SM],
-        [((quarter, width), bf16)] * 2 + [((8, quarter), f32), part] + tiles(rows) + tiles(rows), "chip_tiles",
-        flops=10**10)(embeddings, vt, sib_e, sib_v, pairs)
-    arrived.append(passed_on(arrived[0]))
-    far_tiles = {}
-    for steps in ((0,), (3,), (1, 2)):
-        n = len(steps)
+    kept = [((rows, quarter), bf16)] * 2
+    (mine,) = call(
+        cut_kernel, [HB, SM], [((quarter + NOTE, width), f32)], "cut", flops=10**6, scratch=[pltpu.SemaphoreType.DMA])(
+        pltpu.with_memory_space_constraint(embeddings, pltpu.HBM), pairs)
+    cross = crossed(mine)
+    sib = swapped(mine)
+
+    def make(side, message, name):
         acc, *t = call(
-            functools.partial(cross_kernel, members, steps), [VM] * (n + 2) + [SM, VM, VM, VM, VM], [part] + tiles(quarter) * n,
-            "cross_tiles", flops=2 * 10**9)(*(arrived[step] for step in steps), cross_v, cross_note, pairs, xah, xal, na, acc)
-        for i, step in enumerate(steps):
-            far_tiles[step] = t[2 * i : 2 * i + 2]
-    for step in range(members):
-        kept += far_tiles[step]
+            functools.partial(tiles_kernel, members, side), [VM, VM, VM, SM], [part] + kept, name, flops=5 * 10**9,
+            scratch=[pltpu.VMEM((quarter, width), bf16)] * 2)(embeddings, vt, message, pairs)
+        return acc, t
+
+    acc, own_t = make(OWN, mine, "own_tiles")
+    sib_acc, sib_t = make(SIB, sib, "sib_tiles")
+    cross_acc, cross_t = make(CROSS, tie(cross, sib_acc), "cross_tiles")
+    acc = (acc + swapped(sib_acc)) + crossed(cross_acc)
     pieces = [acc] + [shifted(acc, "sub", s) for s in range(1, members)]
     whole = ((k, rows), f32)
     copies = ((groups // NEAR, k // 2, 2 * k), f32)
     image, gram = call(functools.partial(join_kernel, members, total), [VM] * members, [whole, copies], "join")(*pieces)
-    cross_i = crossed(image)
-    sib_i = swapped(image)
-    terms = row_sums(gram)
-    (acc2,) = call(functools.partial(second_kernel, members), [VM] * (3 + len(kept)), [part], "second_product")(
-        image, sib_i, cross_i, *kept)
+    sib_acc, cross_acc = call(second_kernel, [VM] * 5, [part] * 2, "second_far")(image, *sib_t, *cross_t)
+    (acc2,) = call(second_kernel, [VM] * 3, [part], "second_own")(image, *own_t)
+    terms = row_sums(tie(gram, acc2, sib_acc, cross_acc))
+    acc2 = (acc2 + swapped(sib_acc)) + crossed(cross_acc)
     pieces = [acc2] + [shifted(acc2, "sub", s) for s in range(1, members)]
     (inv,) = call(factor_kernel, [VM] * len(terms), [((k, k), f32)], "factor")(*terms)
     image, gram = call(functools.partial(image_kernel, members, total), [VM] * (1 + members), [whole, copies], "image")(inv, *pieces)

time: 109 us -> 100 us (0.917)
  blocking collectives: 26.2 us -> 14.6 us
  waiting for transfers between devices: 19.7 us -> 26.2 us
  starting transfers between devices: 39.5 us -> 36.2 us
    all_to_all x2 -> x1, blocking collectives: 26.2 us -> 14.6 us  [exchanged(): return lax.all_to_all(x, ('rows', 'sub'), 0, 0, axis_index_groups=sets)]
    all_to_all x0 -> x1, waiting for transfers between devices: none -> 6.19 us  [exchanged(): return lax.all_to_all(x, ('rows', 'sub'), 0, 0, axis_index_groups=sets)]
    ppermute x5 -> x3, starting transfers between devices: 22.2 us -> 16.2 us  [crossed(): lax.ppermute(x, 'rows', [(i, (i + 2 * (i % 2) - 1) % n) for i in range(n)])]
    all_to_all x0 -> x1, starting transfers between devices: none -> 5.01 us  [exchanged(): return lax.all_to_all(x, ('rows', 'sub'), 0, 0, axis_index_groups=sets)]
    ppermute x1 -> x0, starting transfers between devices: 1.28 us -> none  [passed_on(): lax.ppermute(x, ('rows', 'sub'), [(at(g, m), at(g, m + 1 - 2 * (g % 2)))...]
    ppermute x5 -> x3, waiting for transfers between devices: 3 us -> 2.6 us  [crossed(): lax.ppermute(x, 'rows', [(i, (i + 2 * (i % 2) - 1) % n) for i in range(n)])]
  transfers between devices with their start and end apart: 23 -> 21, of which waited for: 10 -> 10; matrix products, arithmetic and copies ran while one was open for 0% -> 0% of each run, Pallas kernels for 14% -> 12%
where the time goes in v8:
time: 100 us
  starting transfers between devices  36.2 us (36%)
  waiting for transfers between devices  26.2 us (26%)
  Pallas kernels  21.9 us (22%)
  blocking collectives  14.6 us (15%)
    ppermute x3, starting transfers between devices, crossed(): lax.ppermute(x, 'rows', [(i, (i + 2 * (i % 2) - 1) % n) for i in range(n)])  16.2 us
    all_to_all x1, blocking collectives, exchanged(): return lax.all_to_all(x, ('rows', 'sub'), 0, 0, axis_index_groups=sets)  14.6 us
    ppermute x6, waiting for transfers between devices, row_sums(): lax.ppermute(total, 'rows', [(i, i ^ mask) for i in range(groups)])  11.3 us
    pallas_call x3, Pallas kernels, make(): call(functools.partial(tiles_kernel, members, side), [VM, VM, VM, SM], [p...  10.2 us
    ppermute x6, starting transfers between devices, shifted(): return lax.ppermute(x, axis, [(i, (i + by) % n) for i in range(n)])  9.04 us
    all_to_all x1, waiting for transfers between devices, exchanged(): return lax.all_to_all(x, ('rows', 'sub'), 0, 0, axis_index_groups=sets)  6.19 us
    ppermute x6, starting transfers between devices, row_sums(): lax.ppermute(total, 'rows', [(i, i ^ mask) for i in range(groups)])  5.59 us
    all_to_all x1, starting transfers between devices, exchanged(): return lax.all_to_all(x, ('rows', 'sub'), 0, 0, axis_index_groups=sets)  5.01 us
  transfers between devices with their start and end apart: 21, of which 10 were waited for; matrix products, arithmetic and copies ran while one was open for 0% of the time, Pallas kernels for 12%

profile of v8, /device:TPU:16, one launch (start us, length us, event | category | flops | bytes accessed | tf_op | source)
XLA Modules:
  0.0 100.0 jit_solution(16598907991770795823)
XLA Ops:
  0.0 0.8 copy-done.1
  0.8 1.6 %cut.1.message_ref = f32[520,256]{1,0:T(8,128)S(1)} custom-call(f32[2048,256]{1,0:T(8,128)} %x_ref.7, s32[2,8]{1,0:T(2,128)S(1)} %bitcast.3), custom_call_target="tpu_custom_call" | custom-call | flops 1000000 | bytes 1048576 | tf_op jit(solution)/shard_map/cut/pallas_call | solution.py:308
  2.4 0.1 collective-permute-start
  2.5 8.2 %collective-permute-start.2 = (f32[520,256]{1,0:T(8,128)S(1)}, f32[520,256]{1,0:T(8,128)S(1)}, u32[]{:S(2)}, u32[]{:S(2)}) collective-permute-start(f32[520,256]{1,0:T(8,128)S(1)} %cut.1.message_ref), channel_id=1, source_target_pairs={{0,252},{4,8},{8,4},{12,16},{16,12},{20,24},{24,20},{28,32},{32,28... | collective-permute-start | bytes 1597448 | tf_op jit(solution)/shard_map/ppermute | solution.py:257
  10.7 4.2 %sib_tiles.1 = (f32[64,512]{1,0:T(8,128)S(1)}, bf16[2048,512]{1,0:T(8,128)(2,1)S(1)}, bf16[2048,512]{1,0:T(8,128)(2,1)S(1)}) custom-call(f32[2048,256]{1,0:T(8,128)S(1)} %copy-done, f32[64,2048]{1,0:T(8,128)S(1)} %bitcast.7, f32[520,256]{1,0:T(8,128)S(1)} %collective-permute-done.message_ref, s32[2,8]{1,0:T(2,128)S(1)} %bitcast.4), custom_call_target="tpu_custom_call" | custom-call | flops 5000000000 | bytes 1048576 | tf_op jit(solution)/shard_map/sib_tiles/pallas_call | solution.py:315
  15.0 0.1 collective-permute-start.1
  15.1 2.6 %collective-permute-done.2.message_ref = f32[520,256]{1,0:T(8,128)S(1)} collective-permute-done((f32[520,256]{1,0:T(8,128)S(1)}, f32[520,256]{1,0:T(8,128)S(1)}, u32[]{:S(2)}, u32[]{:S(2)}) %collective-permute-start.2) | collective-permute-done | bytes 532512 | tf_op jit(solution)/shard_map/ppermute | solution.py:257
  17.7 1.5 %cross_tiles.1 = (f32[64,512]{1,0:T(8,128)S(1)}, bf16[2048,512]{1,0:T(8,128)(2,1)S(1)}, bf16[2048,512]{1,0:T(8,128)(2,1)S(1)}) custom-call(f32[2048,256]{1,0:T(8,128)S(1)} %copy-done, f32[64,2048]{1,0:T(8,128)S(1)} %bitcast.8, f32[520,256]{1,0:T(8,128)S(1)} %collective-permute-done.2.message_ref, s32[2,8]{1,0:T(2,128)S(1)} %bitcast.5), custom_call_target="tpu_custom_call" | custom-call | flops 5000000000 | bytes 1048576 | tf_op jit(solution)/shard_map/cross_tiles/pallas_call | solution.py:315
  19.2 5.1 %collective-permute-start.3 = (f32[64,512]{1,0:T(8,128)S(1)}, f32[64,512]{1,0:T(8,128)S(1)}, u32[]{:S(2)}, u32[]{:S(2)}) collective-permute-start(f32[64,512]{1,0:T(8,128)S(1)} %get-tuple-element.25), channel_id=1, source_target_pairs={{0,252},{4,8},{8,4},{12,16},{16,12},{20,24},{24,20},{28,32},{32,28... | collective-permute-start | bytes 393224 | tf_op jit(solution)/shard_map/ppermute | solution.py:257
  24.4 4.4 %own_tiles.1 = (f32[64,512]{1,0:T(8,128)S(1)}, bf16[2048,512]{1,0:T(8,128)(2,1)S(1)}, bf16[2048,512]{1,0:T(8,128)(2,1)S(1)}) custom-call(f32[2048,256]{1,0:T(8,128)S(1)} %copy-done, f32[64,2048]{1,0:T(8,128)S(1)} %bitcast.9, f32[520,256]{1,0:T(8,128)S(1)} %cut.1.message_ref, s32[2,8]{1,0:T(2,128)S(1)} %bitcast.6), custom_call_target="tpu_custom_call" | custom-call | flops 5000000000 | bytes 1048576 | tf_op jit(solution)/shard_map/own_tiles/pallas_call | solution.py:315
  28.8 0.0 collective-permute-done.1
  28.8 0.5 collective-permute-start.6
  29.4 2.9 %collective-permute-start.5 = (f32[64,512]{1,0:T(8,128)S(1)}, f32[64,512]{1,0:T(8,128)S(1)}, u32[]{:S(2)}, u32[]{:S(2)}) collective-permute-start(f32[64,512]{1,0:T(8,128)S(1)} %add_add_fusion.1.refs_0_), channel_id=1, source_target_pairs={{0,2},{1,3},{2,0},{3,1},{4,6},{5,7},{6,4},{7,5},{8,10},{9,11},{10,... | collective-permute-start | bytes 393224 | tf_op jit(solution)/shard_map/ppermute | solution.py:252
  32.3 1.6 %collective-permute-done.6.refs_3_ = f32[64,512]{1,0:T(8,128)S(1)} collective-permute-done((f32[64,512]{1,0:T(8,128)S(1)}, f32[64,512]{1,0:T(8,128)S(1)}, u32[]{:S(2)}, u32[]{:S(2)}) %collective-permute-start.6) | collective-permute-done | bytes 131104 | tf_op jit(solution)/shard_map/ppermute | solution.py:252
  33.9 2.0 %collective-permute-done.5.refs_2_ = f32[64,512]{1,0:T(8,128)S(1)} collective-permute-done((f32[64,512]{1,0:T(8,128)S(1)}, f32[64,512]{1,0:T(8,128)S(1)}, u32[]{:S(2)}, u32[]{:S(2)}) %collective-permute-start.5) | collective-permute-done | bytes 131104 | tf_op jit(solution)/shard_map/ppermute | solution.py:252
  35.8 1.4 %collective-permute-done.4.refs_1_ = f32[64,512]{1,0:T(8,128)S(1)} collective-permute-done((f32[64,512]{1,0:T(8,128)S(1)}, f32[64,512]{1,0:T(8,128)S(1)}, u32[]{:S(2)}, u32[]{:S(2)}) %collective-permute-start.4) | collective-permute-done | bytes 131104 | tf_op jit(solution)/shard_map/ppermute | solution.py:252
  37.2 1.3 %join.1 = (f32[64,2048]{1,0:T(8,128)S(1)}, f32[8,32,128]{2,1,0:T(8,128)}) custom-call(f32[64,512]{1,0:T(8,128)S(1)} %add_add_fusion.1.refs_0_, f32[64,512]{1,0:T(8,128)S(1)} %collective-permute-done.4.refs_1_, f32[64,512]{1,0:T(8,128)S(1)} %collective-permute-done.5.refs_2_, f32[64,512]{1,0:T(8,128)S(1)} %collective-permute-done.6.refs_3_), custom_call_target="tpu_custom_call" | custom-call | flops 1000000000 | bytes 1048576 | tf_op jit(solution)/shard_map/join/pallas_call | solution.py:327
  38.6 0.8 second_own.1
  39.4 1.5 %second_far.1 = (f32[64,512]{1,0:T(8,128)S(1)}, f32[64,512]{1,0:T(8,128)S(1)}) custom-call(f32[64,2048]{1,0:T(8,128)S(1)} %get-tuple-element.27.v_ref, bf16[2048,512]{1,0:T(8,128)(2,1)S(1)} %get-tuple-element.30.refs_0_, bf16[2048,512]{1,0:T(8,128)(2,1)S(1)} %get-tuple-element.31.refs_1_, bf16[2048,512]{1,0:T(8,128)(2,1)S(1)} %get-tuple-element.32.refs_2_, ...), custom_call_target="tpu_custom_call" | custom-call | flops 1000000000 | bytes 1048576 | tf_op jit(solution)/shard_map/second_far/pallas_call | solution.py:328
  40.9 5.0 %all-to-all-start = ((f32[8,32,128]{2,1,0:T(8,128)}), f32[8,32,128]{2,1,0:T(8,128)S(1)}, u32[]{:S(2)}, u32[]{:S(2)}) async-start(f32[8,32,128]{2,1,0:T(8,128)} %get-tuple-element.36), calls=%async_computation | async-start | bytes 262144 | tf_op jit(solution)/shard_map/all_to_all | solution.py:273
  45.9 0.0 collective-permute-start.11
  46.0 2.9 %collective-permute-start.12 = (f32[64,512]{1,0:T(8,128)S(1)}, f32[64,512]{1,0:T(8,128)S(1)}, u32[]{:S(2)}, u32[]{:S(2)}) collective-permute-start(f32[64,512]{1,0:T(8,128)S(1)} %get-tuple-element.35), channel_id=1, source_target_pairs={{0,252},{4,8},{8,4},{12,16},{16,12},{20,24},{24,20},{28,32},{32,28... | collective-permute-start | bytes 393224 | tf_op jit(solution)/shard_map/ppermute | solution.py:257
  48.8 6.2 %all-to-all-done.gram_ref = f32[8,32,128]{2,1,0:T(8,128)S(1)} async-done(((f32[8,32,128]{2,1,0:T(8,128)}), f32[8,32,128]{2,1,0:T(8,128)S(1)}, u32[]{:S(2)}, u32[]{:S(2)}) %all-to-all-start) | async-done | bytes 131104 | tf_op jit(solution)/shard_map/all_to_all | solution.py:273
  55.0 0.1 collective-permute-start.7
  55.1 0.0 collective-permute-done.12
  55.2 0.3 collective-permute-start.15
  55.5 3.3 %collective-permute-start.14 = (f32[64,512]{1,0:T(8,128)S(1)}, f32[64,512]{1,0:T(8,128)S(1)}, u32[]{:S(2)}, u32[]{:S(2)}) collective-permute-start(f32[64,512]{1,0:T(8,128)S(1)} %add_add_fusion.refs_0_), channel_id=1, source_target_pairs={{0,2},{1,3},{2,0},{3,1},{4,6},{5,7},{6,4},{7,5},{8,10},{9,11},{10,... | collective-permute-start | bytes 393224 | tf_op jit(solution)/shard_map/ppermute | solution.py:252
  58.8 2.0 %collective-permute-start.13 = (f32[64,512]{1,0:T(8,128)S(1)}, f32[64,512]{1,0:T(8,128)S(1)}, u32[]{:S(2)}, u32[]{:S(2)}) collective-permute-start(f32[64,512]{1,0:T(8,128)S(1)} %add_add_fusion.refs_0_), channel_id=1, source_target_pairs={{0,1},{1,2},{2,3},{3,0},{4,5},{5,6},{6,7},{7,4},{8,9},{9,10},{10,1... | collective-permute-start | bytes 393224 | tf_op jit(solution)/shard_map/ppermute | solution.py:252
  60.8 0.0 collective-permute-done.7
  60.8 0.9 collective-permute-start.10
  61.7 0.0 collective-permute-start.9
  61.7 4.1 %collective-permute-done.10.refs_3_ = f32[32,128]{1,0:T(8,128)S(1)} collective-permute-done((f32[32,128]{1,0:T(8,128)S(1)}, f32[32,128]{1,0:T(8,128)S(1)}, u32[]{:S(2)}, u32[]{:S(2)}) %collective-permute-start.10) | collective-permute-done | bytes 16416 | tf_op jit(solution)/shard_map/ppermute | solution.py:290
  65.8 0.0 collective-permute-start.8
  65.8 0.0 collective-permute-done.9.refs_2_
  65.9 5.2 %collective-permute-done.8.refs_1_ = f32[32,128]{1,0:T(8,128)S(1)} collective-permute-done((f32[32,128]{1,0:T(8,128)S(1)}, f32[32,128]{1,0:T(8,128)S(1)}, u32[]{:S(2)}, u32[]{:S(2)}) %collective-permute-start.8) | collective-permute-done | bytes 16416 | tf_op jit(solution)/shard_map/ppermute | solution.py:290
  71.1 2.0 %factor.1.inv_ref = f32[64,64]{1,0:T(8,128)S(1)} custom-call(f32[32,128]{1,0:T(8,128)S(1)} %add.20.refs_0_, f32[32,128]{1,0:T(8,128)S(1)} %collective-permute-done.8.refs_1_, f32[32,128]{1,0:T(8,128)S(1)} %collective-permute-done.9.refs_2_, f32[32,128]{1,0:T(8,128)S(1)} %collective-permute-done.10.refs_3_), custom_call_target="tpu_custom_call" | custom-call | flops 1000000000 | bytes 1048576 | tf_op jit(solution)/shard_map/factor/pallas_call | solution.py:333
  73.1 0.0 collective-permute-done.15.refs_3_
  73.1 0.0 collective-permute-done.13.refs_1_
  73.1 1.1 %image.1 = (f32[64,2048]{1,0:T(8,128)S(1)}, f32[8,32,128]{2,1,0:T(8,128)S(1)}) custom-call(f32[64,64]{1,0:T(8,128)S(1)} %factor.1.inv_ref, f32[64,512]{1,0:T(8,128)S(1)} %add_add_fusion.refs_0_, f32[64,512]{1,0:T(8,128)S(1)} %collective-permute-done.13.refs_1_, f32[64,512]{1,0:T(8,128)S(1)} %collective-permute-done.14.refs_2_, ...), custom_call_target="tpu_custom_call" | custom-call | flops 1000000000 | bytes 1048576 | tf_op jit(solution)/shard_map/image/pallas_call | solution.py:334
  74.2 14.6 %all_to_all.10.gram_ref = f32[8,32,128]{2,1,0:T(8,128)S(1)} all-to-all(f32[8,32,128]{2,1,0:T(8,128)S(1)} %get-tuple-element.38), channel_id=1, replica_groups={{0,32,64,96,128,160,192,224},{1,33,65,97,129,161,193,225},{2,34,66,98,1..., dimensions={0} | all-to-all | bytes 262144 | tf_op jit(solution)/shard_map/all_to_all | solution.py:273
  88.8 0.1 collective-permute-start.16
  88.9 1.2 %collective-permute-done.16 = f32[32,128]{1,0:T(8,128)S(1)} collective-permute-done((f32[32,128]{1,0:T(8,128)S(1)}, f32[32,128]{1,0:T(8,128)S(1)}, u32[]{:S(2)}, u32[]{:S(2)}) %collective-permute-start.16) | collective-permute-done | bytes 16416 | tf_op jit(solution)/shard_map/ppermute | solution.py:261
  90.1 0.0 collective-permute-start.19
  90.1 0.1 collective-permute-start.18
  90.2 4.6 %collective-permute-start.17 = (f32[32,128]{1,0:T(8,128)S(1)}, f32[32,128]{1,0:T(8,128)S(1)}, u32[]{:S(2)}, u32[]{:S(2)}) collective-permute-start(f32[32,128]{1,0:T(8,128)S(1)} %add.23.refs_0_), channel_id=1, source_target_pairs={{0,16},{4,20},{8,24},{12,28},{16,0},{20,4},{24,8},{28,12},{32,48},... | collective-permute-start | bytes 49160 | tf_op jit(solution)/shard_map/ppermute | solution.py:290
  94.8 0.2 collective-permute-done.19.refs_3_
  95.0 1.6 %collective-permute-done.17.refs_1_ = f32[32,128]{1,0:T(8,128)S(1)} collective-permute-done((f32[32,128]{1,0:T(8,128)S(1)}, f32[32,128]{1,0:T(8,128)S(1)}, u32[]{:S(2)}, u32[]{:S(2)}) %collective-permute-start.17) | collective-permute-done | bytes 16416 | tf_op jit(solution)/shard_map/ppermute | solution.py:290
  96.7 3.3 %last.1 = f32[64,2048]{1,0:T(8,128)} custom-call(f32[64,2048]{1,0:T(8,128)S(1)} %get-tuple-element.37.image_ref, f32[32,128]{1,0:T(8,128)S(1)} %add.23.refs_0_, f32[32,128]{1,0:T(8,128)S(1)} %collective-permute-done.17.refs_1_, f32[32,128]{1,0:T(8,128)S(1)} %collective-permute-done.18.refs_2_, f32[32,128]{1,0:T(8,128)S(1)} %collective-permute-done.19.refs_3_), custom_call_target="tpu_custom_call" | custom-call | flops 1000000000 | bytes 1048576 | tf_op jit(solution)/shard_map/last/pallas_call | solution.py:336
  (17 shorter events, 0.1 us)
Async XLA Ops:
  0.0 10.7 %copy-start = (f32[2048,256]{1,0:T(8,128)S(1)}, f32[2048,256]{1,0:T(8,128)}, u32[]{:S(2)}) copy-start(f32[2048,256]{1,0:T(8,128)} %x_ref.7) | copy-start | bytes 6291460
  0.0 0.8 copy-start.1
  0.8 9.9 %copy-start.2 = (f32[2048,64]{0,1:T(8,128)S(1)}, f32[2048,64]{0,1:T(8,128)}, u32[]{:S(2)}) copy-start(f32[2048,64]{0,1:T(8,128)} %param.4) | copy-start | bytes 1572868
  2.4 8.3 %collective-permute-start = (f32[520,256]{1,0:T(8,128)S(1)}, f32[520,256]{1,0:T(8,128)S(1)}, u32[]{:S(2)}, u32[]{:S(2)}) collective-permute-start(f32[520,256]{1,0:T(8,128)S(1)} %cut.1.message_ref), channel_id=1, source_target_pairs={{0,4},{4,0},{8,12},{12,8},{16,20},{20,16},{24,28},{28,24},{32,36},... | collective-permute-start | bytes 1597448 | tf_op jit(solution)/shard_map/ppermute | solution.py:261
  2.5 15.1 %collective-permute-start.2 = (f32[520,256]{1,0:T(8,128)S(1)}, f32[520,256]{1,0:T(8,128)S(1)}, u32[]{:S(2)}, u32[]{:S(2)}) collective-permute-start(f32[520,256]{1,0:T(8,128)S(1)} %cut.1.message_ref), channel_id=1, source_target_pairs={{0,252},{4,8},{8,4},{12,16},{16,12},{20,24},{24,20},{28,32},{32,28... | collective-permute-start | bytes 1597448 | tf_op jit(solution)/shard_map/ppermute | solution.py:257
  15.0 13.8 %collective-permute-start.1 = (f32[64,512]{1,0:T(8,128)S(1)}, f32[64,512]{1,0:T(8,128)S(1)}, u32[]{:S(2)}, u32[]{:S(2)}) collective-permute-start(f32[64,512]{1,0:T(8,128)S(1)} %get-tuple-element.23), channel_id=1, source_target_pairs={{0,4},{4,0},{8,12},{12,8},{16,20},{20,16},{24,28},{28,24},{32,36},... | collective-permute-start | bytes 393224 | tf_op jit(solution)/shard_map/ppermute | solution.py:261
  19.2 9.6 %collective-permute-start.3 = (f32[64,512]{1,0:T(8,128)S(1)}, f32[64,512]{1,0:T(8,128)S(1)}, u32[]{:S(2)}, u32[]{:S(2)}) collective-permute-start(f32[64,512]{1,0:T(8,128)S(1)} %get-tuple-element.25), channel_id=1, source_target_pairs={{0,252},{4,8},{8,4},{12,16},{16,12},{20,24},{24,20},{28,32},{32,28... | collective-permute-start | bytes 393224 | tf_op jit(solution)/shard_map/ppermute | solution.py:257
  28.8 5.0 %collective-permute-start.6 = (f32[64,512]{1,0:T(8,128)S(1)}, f32[64,512]{1,0:T(8,128)S(1)}, u32[]{:S(2)}, u32[]{:S(2)}) collective-permute-start(f32[64,512]{1,0:T(8,128)S(1)} %add_add_fusion.1.refs_0_), channel_id=1, source_target_pairs={{0,3},{1,0},{2,1},{3,2},{4,7},{5,4},{6,5},{7,6},{8,11},{9,8},{10,9... | collective-permute-start | bytes 393224 | tf_op jit(solution)/shard_map/ppermute | solution.py:252
  29.4 6.5 %collective-permute-start.5 = (f32[64,512]{1,0:T(8,128)S(1)}, f32[64,512]{1,0:T(8,128)S(1)}, u32[]{:S(2)}, u32[]{:S(2)}) collective-permute-start(f32[64,512]{1,0:T(8,128)S(1)} %add_add_fusion.1.refs_0_), channel_id=1, source_target_pairs={{0,2},{1,3},{2,0},{3,1},{4,6},{5,7},{6,4},{7,5},{8,10},{9,11},{10,... | collective-permute-start | bytes 393224 | tf_op jit(solution)/shard_map/ppermute | solution.py:252
  32.3 5.0 %collective-permute-start.4 = (f32[64,512]{1,0:T(8,128)S(1)}, f32[64,512]{1,0:T(8,128)S(1)}, u32[]{:S(2)}, u32[]{:S(2)}) collective-permute-start(f32[64,512]{1,0:T(8,128)S(1)} %add_add_fusion.1.refs_0_), channel_id=1, source_target_pairs={{0,1},{1,2},{2,3},{3,0},{4,5},{5,6},{6,7},{7,4},{8,9},{9,10},{10,1... | collective-permute-start | bytes 393224 | tf_op jit(solution)/shard_map/ppermute | solution.py:252
  40.9 14.1 %all-to-all-start = ((f32[8,32,128]{2,1,0:T(8,128)}), f32[8,32,128]{2,1,0:T(8,128)S(1)}, u32[]{:S(2)}, u32[]{:S(2)}) async-start(f32[8,32,128]{2,1,0:T(8,128)} %get-tuple-element.36), calls=%async_computation | async-start | bytes 262144 | tf_op jit(solution)/shard_map/all_to_all | solution.py:273
  45.9 9.2 %collective-permute-start.11 = (f32[64,512]{1,0:T(8,128)S(1)}, f32[64,512]{1,0:T(8,128)S(1)}, u32[]{:S(2)}, u32[]{:S(2)}) collective-permute-start(f32[64,512]{1,0:T(8,128)S(1)} %get-tuple-element.34), channel_id=1, source_target_pairs={{0,4},{4,0},{8,12},{12,8},{16,20},{20,16},{24,28},{28,24},{32,36},... | collective-permute-start | bytes 393224 | tf_op jit(solution)/shard_map/ppermute | solution.py:261
  46.0 9.2 %collective-permute-start.12 = (f32[64,512]{1,0:T(8,128)S(1)}, f32[64,512]{1,0:T(8,128)S(1)}, u32[]{:S(2)}, u32[]{:S(2)}) collective-permute-start(f32[64,512]{1,0:T(8,128)S(1)} %get-tuple-element.35), channel_id=1, source_target_pairs={{0,252},{4,8},{8,4},{12,16},{16,12},{20,24},{24,20},{28,32},{32,28... | collective-permute-start | bytes 393224 | tf_op jit(solution)/shard_map/ppermute | solution.py:257
  55.0 5.8 %collective-permute-start.7 = (f32[32,128]{1,0:T(8,128)S(1)}, f32[32,128]{1,0:T(8,128)S(1)}, u32[]{:S(2)}, u32[]{:S(2)}) collective-permute-start(f32[32,128]{1,0:T(8,128)S(1)} %sum_z.2), channel_id=1, source_target_pairs={{0,4},{4,0},{8,12},{12,8},{16,20},{20,16},{24,28},{28,24},{32,36},... | collective-permute-start | bytes 49160 | tf_op jit(solution)/shard_map/ppermute | solution.py:261
  55.2 17.9 %collective-permute-start.15 = (f32[64,512]{1,0:T(8,128)S(1)}, f32[64,512]{1,0:T(8,128)S(1)}, u32[]{:S(2)}, u32[]{:S(2)}) collective-permute-start(f32[64,512]{1,0:T(8,128)S(1)} %add_add_fusion.refs_0_), channel_id=1, source_target_pairs={{0,3},{1,0},{2,1},{3,2},{4,7},{5,4},{6,5},{7,6},{8,11},{9,8},{10,9... | collective-permute-start | bytes 393224 | tf_op jit(solution)/shard_map/ppermute | solution.py:252
  55.5 17.6 %collective-permute-start.14 = (f32[64,512]{1,0:T(8,128)S(1)}, f32[64,512]{1,0:T(8,128)S(1)}, u32[]{:S(2)}, u32[]{:S(2)}) collective-permute-start(f32[64,512]{1,0:T(8,128)S(1)} %add_add_fusion.refs_0_), channel_id=1, source_target_pairs={{0,2},{1,3},{2,0},{3,1},{4,6},{5,7},{6,4},{7,5},{8,10},{9,11},{10,... | collective-permute-start | bytes 393224 | tf_op jit(solution)/shard_map/ppermute | solution.py:252
  58.8 14.3 %collective-permute-start.13 = (f32[64,512]{1,0:T(8,128)S(1)}, f32[64,512]{1,0:T(8,128)S(1)}, u32[]{:S(2)}, u32[]{:S(2)}) collective-permute-start(f32[64,512]{1,0:T(8,128)S(1)} %add_add_fusion.refs_0_), channel_id=1, source_target_pairs={{0,1},{1,2},{2,3},{3,0},{4,5},{5,6},{6,7},{7,4},{8,9},{9,10},{10,1... | collective-permute-start | bytes 393224 | tf_op jit(solution)/shard_map/ppermute | solution.py:252
  60.8 5.0 %collective-permute-start.10 = (f32[32,128]{1,0:T(8,128)S(1)}, f32[32,128]{1,0:T(8,128)S(1)}, u32[]{:S(2)}, u32[]{:S(2)}) collective-permute-start(f32[32,128]{1,0:T(8,128)S(1)} %add.20.refs_0_), channel_id=1, source_target_pairs={{0,24},{4,28},{8,16},{12,20},{16,8},{20,12},{24,0},{28,4},{32,56},... | collective-permute-start | bytes 49160 | tf_op jit(solution)/shard_map/ppermute | solution.py:290
  61.7 4.1 %collective-permute-start.9 = (f32[32,128]{1,0:T(8,128)S(1)}, f32[32,128]{1,0:T(8,128)S(1)}, u32[]{:S(2)}, u32[]{:S(2)}) collective-permute-start(f32[32,128]{1,0:T(8,128)S(1)} %add.20.refs_0_), channel_id=1, source_target_pairs={{0,8},{4,12},{8,0},{12,4},{16,24},{20,28},{24,16},{28,20},{32,40},... | collective-permute-start | bytes 49160 | tf_op jit(solution)/shard_map/ppermute | solution.py:290
  65.8 5.2 %collective-permute-start.8 = (f32[32,128]{1,0:T(8,128)S(1)}, f32[32,128]{1,0:T(8,128)S(1)}, u32[]{:S(2)}, u32[]{:S(2)}) collective-permute-start(f32[32,128]{1,0:T(8,128)S(1)} %add.20.refs_0_), channel_id=1, source_target_pairs={{0,16},{4,20},{8,24},{12,28},{16,0},{20,4},{24,8},{28,12},{32,48},... | collective-permute-start | bytes 49160 | tf_op jit(solution)/shard_map/ppermute | solution.py:290
  88.8 1.3 %collective-permute-start.16 = (f32[32,128]{1,0:T(8,128)S(1)}, f32[32,128]{1,0:T(8,128)S(1)}, u32[]{:S(2)}, u32[]{:S(2)}) collective-permute-start(f32[32,128]{1,0:T(8,128)S(1)} %sum_z.3), channel_id=1, source_target_pairs={{0,4},{4,0},{8,12},{12,8},{16,20},{20,16},{24,28},{28,24},{32,36},... | collective-permute-start | bytes 49160 | tf_op jit(solution)/shard_map/ppermute | solution.py:261
  90.1 4.9 %collective-permute-start.19 = (f32[32,128]{1,0:T(8,128)S(1)}, f32[32,128]{1,0:T(8,128)S(1)}, u32[]{:S(2)}, u32[]{:S(2)}) collective-permute-start(f32[32,128]{1,0:T(8,128)S(1)} %add.23.refs_0_), channel_id=1, source_target_pairs={{0,24},{4,28},{8,16},{12,20},{16,8},{20,12},{24,0},{28,4},{32,56},... | collective-permute-start | bytes 49160 | tf_op jit(solution)/shard_map/ppermute | solution.py:290
  90.1 4.9 %collective-permute-start.18 = (f32[32,128]{1,0:T(8,128)S(1)}, f32[32,128]{1,0:T(8,128)S(1)}, u32[]{:S(2)}, u32[]{:S(2)}) collective-permute-start(f32[32,128]{1,0:T(8,128)S(1)} %add.23.refs_0_), channel_id=1, source_target_pairs={{0,8},{4,12},{8,0},{12,4},{16,24},{20,28},{24,16},{28,20},{32,40},... | collective-permute-start | bytes 49160 | tf_op jit(solution)/shard_map/ppermute | solution.py:290
  90.2 6.5 %collective-permute-start.17 = (f32[32,128]{1,0:T(8,128)S(1)}, f32[32,128]{1,0:T(8,128)S(1)}, u32[]{:S(2)}, u32[]{:S(2)}) collective-permute-start(f32[32,128]{1,0:T(8,128)S(1)} %add.23.refs_0_), channel_id=1, source_target_pairs={{0,16},{4,20},{8,24},{12,28},{16,0},{20,4},{24,8},{28,12},{32,48},... | collective-permute-start | bytes 49160 | tf_op jit(solution)/shard_map/ppermute | solution.py:290

commit v9 on v8

--- a/solution.py
+++ b/solution.py
@@ -134,13 +134,17 @@
     gram = gram_sum(*split3(image)) / total
     half = gram.shape[0] // 2
     packed = jnp.concatenate([gram[:half], gram[half:]], 1)
+    if len(gram_ref.shape) == 2:
+        gram_ref[...] = packed
+        return
     for n in range(gram_ref.shape[0]):
         gram_ref[n] = packed
 
 
 def take_gram(terms):
-    me, opposite, left, right = (ref[...] for ref in terms)
-    packed = (me + opposite) + (left + right)
+    packed = terms[0][...] + terms[1][...]
+    if len(terms) > 2:
+        packed = packed + (terms[2][...] + terms[3][...])
     k = packed.shape[1] // 2
     return jnp.concatenate([packed[:, :k], packed[:, k:]], 0)
 
@@ -280,6 +284,18 @@
     out_ref[...] = packed
 
 
+MASKS = (1, 2, 6, 8, 16, 48)
+
+
+def pair_sums(total):
+    groups = lax.axis_size("rows")
+    for mask in MASKS:
+        other = lax.ppermute(total, "rows", [(i, i ^ mask) for i in range(groups)])
+        if mask == MASKS[-1]:
+            return [total, other]
+        total = total + other
+
+
 RING = (4, 2, 6)
 
 
@@ -324,10 +340,10 @@
     pieces = [acc] + [shifted(acc, "sub", s) for s in range(1, members)]
     whole = ((k, rows), f32)
     copies = ((groups // NEAR, k // 2, 2 * k), f32)
-    image, gram = call(functools.partial(join_kernel, members, total), [VM] * members, [whole, copies], "join")(*pieces)
+    image, gram = call(functools.partial(join_kernel, members, total), [VM] * members, [whole, (copies[0][1:], f32)], "join")(*pieces)
     sib_acc, cross_acc = call(second_kernel, [VM] * 5, [part] * 2, "second_far")(image, *sib_t, *cross_t)
     (acc2,) = call(second_kernel, [VM] * 3, [part], "second_own")(image, *own_t)
-    terms = row_sums(tie(gram, acc2, sib_acc, cross_acc))
+    terms = pair_sums(gram)
     acc2 = (acc2 + swapped(sib_acc)) + crossed(cross_acc)
     pieces = [acc2] + [shifted(acc2, "sub", s) for s in range(1, members)]
     (inv,) = call(factor_kernel, [VM] * len(terms), [((k, k), f32)], "factor")(*terms)

time: 100 us -> 97.1 us (0.971)
  starting transfers between devices: 36.2 us -> 33.3 us
  waiting for transfers between devices: 26.2 us -> 27.2 us
    ppermute x0 -> x6, waiting for transfers between devices: none -> 15.7 us  [pair_sums(): other = lax.ppermute(total, 'rows', [(i, i ^ mask) for i in range(groups)])]
    ppermute x6 -> x3, waiting for transfers between devices: 11.3 us -> 2.75 us  [row_sums(): lax.ppermute(total, 'rows', [(i, i ^ mask) for i in range(groups)])]
    all_to_all x1 -> x0, waiting for transfers between devices: 6.19 us -> none  [exchanged(): return lax.all_to_all(x, ('rows', 'sub'), 0, 0, axis_index_groups=sets)]
    all_to_all x1 -> x0, starting transfers between devices: 5.01 us -> none  [exchanged(): return lax.all_to_all(x, ('rows', 'sub'), 0, 0, axis_index_groups=sets)]
    ppermute x0 -> x6, starting transfers between devices: none -> 3.92 us  [pair_sums(): other = lax.ppermute(total, 'rows', [(i, i ^ mask) for i in range(groups)])]
    ppermute x6 -> x3, starting transfers between devices: 5.59 us -> 4.7 us  [row_sums(): lax.ppermute(total, 'rows', [(i, i ^ mask) for i in range(groups)])]
  transfers between devices with their start and end apart: 21 -> 22, of which waited for: 10 -> 13; matrix products, arithmetic and copies ran while one was open for 0% -> 0% of each run, Pallas kernels for 12% -> 13%
where the time goes in v9:
time: 97.1 us; the launch traced here: 96.7 us
  starting transfers between devices  33.3 us (34%)
  waiting for transfers between devices  27.2 us (28%)
  Pallas kernels  21.2 us (22%)
  blocking collectives  13.9 us (14%)
    ppermute x6, waiting for transfers between devices, pair_sums(): other = lax.ppermute(total, 'rows', [(i, i ^ mask) for i in range(groups)])  15.7 us
    ppermute x3, starting transfers between devices, crossed(): lax.ppermute(x, 'rows', [(i, (i + 2 * (i % 2) - 1) % n) for i in range(n)])  15.2 us
    all_to_all x1, blocking collectives, exchanged(): return lax.all_to_all(x, ('rows', 'sub'), 0, 0, axis_index_groups=sets)  13.9 us
    pallas_call x3, Pallas kernels, make(): call(functools.partial(tiles_kernel, members, side), [VM, VM, VM, SM], [p...  10.2 us
    ppermute x6, starting transfers between devices, shifted(): return lax.ppermute(x, axis, [(i, (i + by) % n) for i in range(n)])  9.05 us
    ppermute x6, waiting for transfers between devices, shifted(): return lax.ppermute(x, axis, [(i, (i + by) % n) for i in range(n)])  5 us
    ppermute x3, starting transfers between devices, row_sums(): lax.ppermute(total, 'rows', [(i, i ^ mask) for i in range(groups)])  4.7 us
    ppermute x6, starting transfers between devices, pair_sums(): other = lax.ppermute(total, 'rows', [(i, i ^ mask) for i in range(groups)])  3.92 us
  transfers between devices with their start and end apart: 22, of which 13 were waited for; matrix products, arithmetic and copies ran while one was open for 0% of the time, Pallas kernels for 13%

profile of v9, /device:TPU:16, one launch (start us, length us, event | category | flops | bytes accessed | tf_op | source)
XLA Modules:
  0.0 96.7 jit_solution(15858795360202945231)
XLA Ops:
  0.0 0.8 copy-done.1
  0.8 1.6 %cut.1.message_ref = f32[520,256]{1,0:T(8,128)S(1)} custom-call(f32[2048,256]{1,0:T(8,128)} %x_ref.7, s32[2,8]{1,0:T(2,128)S(1)} %bitcast.3), custom_call_target="tpu_custom_call" | custom-call | flops 1000000 | bytes 1048576 | tf_op jit(solution)/shard_map/cut/pallas_call | solution.py:324
  2.4 0.1 collective-permute-start
  2.5 8.2 %collective-permute-start.2 = (f32[520,256]{1,0:T(8,128)S(1)}, f32[520,256]{1,0:T(8,128)S(1)}, u32[]{:S(2)}, u32[]{:S(2)}) collective-permute-start(f32[520,256]{1,0:T(8,128)S(1)} %cut.1.message_ref), channel_id=1, source_target_pairs={{0,252},{4,8},{8,4},{12,16},{16,12},{20,24},{24,20},{28,32},{32,28... | collective-permute-start | bytes 1597448 | tf_op jit(solution)/shard_map/ppermute | solution.py:261
  10.7 4.2 %sib_tiles.1 = (f32[64,512]{1,0:T(8,128)S(1)}, bf16[2048,512]{1,0:T(8,128)(2,1)S(1)}, bf16[2048,512]{1,0:T(8,128)(2,1)S(1)}) custom-call(f32[2048,256]{1,0:T(8,128)S(1)} %copy-done, f32[64,2048]{1,0:T(8,128)S(1)} %bitcast.7, f32[520,256]{1,0:T(8,128)S(1)} %collective-permute-done.message_ref, s32[2,8]{1,0:T(2,128)S(1)} %bitcast.4), custom_call_target="tpu_custom_call" | custom-call | flops 5000000000 | bytes 1048576 | tf_op jit(solution)/shard_map/sib_tiles/pallas_call | solution.py:331
  15.0 0.0 copy-start.2
  15.0 0.1 collective-permute-start.1
  15.1 2.6 %collective-permute-done.2.message_ref = f32[520,256]{1,0:T(8,128)S(1)} collective-permute-done((f32[520,256]{1,0:T(8,128)S(1)}, f32[520,256]{1,0:T(8,128)S(1)}, u32[]{:S(2)}, u32[]{:S(2)}) %collective-permute-start.2) | collective-permute-done | bytes 532512 | tf_op jit(solution)/shard_map/ppermute | solution.py:261
  17.7 1.5 %cross_tiles.1 = (f32[64,512]{1,0:T(8,128)S(1)}, bf16[2048,512]{1,0:T(8,128)(2,1)S(1)}, bf16[2048,512]{1,0:T(8,128)(2,1)S(1)}) custom-call(f32[2048,256]{1,0:T(8,128)S(1)} %copy-done, f32[64,2048]{1,0:T(8,128)S(1)} %bitcast.8, f32[520,256]{1,0:T(8,128)S(1)} %collective-permute-done.2.message_ref, s32[2,8]{1,0:T(2,128)S(1)} %bitcast.5), custom_call_target="tpu_custom_call" | custom-call | flops 5000000000 | bytes 1048576 | tf_op jit(solution)/shard_map/cross_tiles/pallas_call | solution.py:331
  19.2 5.1 %collective-permute-start.3 = (f32[64,512]{1,0:T(8,128)S(1)}, f32[64,512]{1,0:T(8,128)S(1)}, u32[]{:S(2)}, u32[]{:S(2)}) collective-permute-start(f32[64,512]{1,0:T(8,128)S(1)} %get-tuple-element.24), channel_id=1, source_target_pairs={{0,252},{4,8},{8,4},{12,16},{16,12},{20,24},{24,20},{28,32},{32,28... | collective-permute-start | bytes 393224 | tf_op jit(solution)/shard_map/ppermute | solution.py:261
  24.4 4.4 %own_tiles.1 = (f32[64,512]{1,0:T(8,128)S(1)}, bf16[2048,512]{1,0:T(8,128)(2,1)S(1)}, bf16[2048,512]{1,0:T(8,128)(2,1)S(1)}) custom-call(f32[2048,256]{1,0:T(8,128)S(1)} %copy-done, f32[64,2048]{1,0:T(8,128)S(1)} %bitcast.9, f32[520,256]{1,0:T(8,128)S(1)} %cut.1.message_ref, s32[2,8]{1,0:T(2,128)S(1)} %bitcast.6), custom_call_target="tpu_custom_call" | custom-call | flops 5000000000 | bytes 1048576 | tf_op jit(solution)/shard_map/own_tiles/pallas_call | solution.py:331
  28.8 0.0 collective-permute-done.1
  28.8 0.5 collective-permute-start.6
  29.4 2.9 %collective-permute-start.5 = (f32[64,512]{1,0:T(8,128)S(1)}, f32[64,512]{1,0:T(8,128)S(1)}, u32[]{:S(2)}, u32[]{:S(2)}) collective-permute-start(f32[64,512]{1,0:T(8,128)S(1)} %add_add_fusion.1.refs_0_), channel_id=1, source_target_pairs={{0,2},{1,3},{2,0},{3,1},{4,6},{5,7},{6,4},{7,5},{8,10},{9,11},{10,... | collective-permute-start | bytes 393224 | tf_op jit(solution)/shard_map/ppermute | solution.py:256
  32.3 1.6 %collective-permute-done.6.refs_3_ = f32[64,512]{1,0:T(8,128)S(1)} collective-permute-done((f32[64,512]{1,0:T(8,128)S(1)}, f32[64,512]{1,0:T(8,128)S(1)}, u32[]{:S(2)}, u32[]{:S(2)}) %collective-permute-start.6) | collective-permute-done | bytes 131104 | tf_op jit(solution)/shard_map/ppermute | solution.py:256
  33.9 2.0 %collective-permute-done.5.refs_2_ = f32[64,512]{1,0:T(8,128)S(1)} collective-permute-done((f32[64,512]{1,0:T(8,128)S(1)}, f32[64,512]{1,0:T(8,128)S(1)}, u32[]{:S(2)}, u32[]{:S(2)}) %collective-permute-start.5) | collective-permute-done | bytes 131104 | tf_op jit(solution)/shard_map/ppermute | solution.py:256
  35.8 1.4 %collective-permute-done.4.refs_1_ = f32[64,512]{1,0:T(8,128)S(1)} collective-permute-done((f32[64,512]{1,0:T(8,128)S(1)}, f32[64,512]{1,0:T(8,128)S(1)}, u32[]{:S(2)}, u32[]{:S(2)}) %collective-permute-start.4) | collective-permute-done | bytes 131104 | tf_op jit(solution)/shard_map/ppermute | solution.py:256
  37.2 0.6 join.1
  37.9 1.5 %second_far.1 = (f32[64,512]{1,0:T(8,128)S(1)}, f32[64,512]{1,0:T(8,128)S(1)}) custom-call(f32[64,2048]{1,0:T(8,128)S(1)} %get-tuple-element.26.v_ref, bf16[2048,512]{1,0:T(8,128)(2,1)S(1)} %get-tuple-element.29.refs_0_, bf16[2048,512]{1,0:T(8,128)(2,1)S(1)} %get-tuple-element.30.refs_1_, bf16[2048,512]{1,0:T(8,128)(2,1)S(1)} %get-tuple-element.31.refs_2_, ...), custom_call_target="tpu_custom_call" | custom-call | flops 1000000000 | bytes 1048576 | tf_op jit(solution)/shard_map/second_far/pallas_call | solution.py:344
  39.4 0.1 collective-permute-start.13
  39.5 1.9 %collective-permute-start.14 = (f32[64,512]{1,0:T(8,128)S(1)}, f32[64,512]{1,0:T(8,128)S(1)}, u32[]{:S(2)}, u32[]{:S(2)}) collective-permute-start(f32[64,512]{1,0:T(8,128)S(1)} %get-tuple-element.34), channel_id=1, source_target_pairs={{0,252},{4,8},{8,4},{12,16},{16,12},{20,24},{24,20},{28,32},{32,28... | collective-permute-start | bytes 393224 | tf_op jit(solution)/shard_map/ppermute | solution.py:261
  41.4 1.2 %collective-permute-done.7 = f32[32,128]{1,0:T(8,128)S(1)} collective-permute-done((f32[32,128]{1,0:T(8,128)S(1)}, f32[32,128]{1,0:T(8,128)S(1)}, u32[]{:S(2)}, u32[]{:S(2)}) %collective-permute-start.7) | collective-permute-done | bytes 16416 | tf_op jit(solution)/shard_map/ppermute | solution.py:293
  42.6 0.2 collective-permute-start.8
  42.8 3.5 %collective-permute-done.8 = f32[32,128]{1,0:T(8,128)S(1)} collective-permute-done((f32[32,128]{1,0:T(8,128)S(1)}, f32[32,128]{1,0:T(8,128)S(1)}, u32[]{:S(2)}, u32[]{:S(2)}) %collective-permute-start.8) | collective-permute-done | bytes 16416 | tf_op jit(solution)/shard_map/ppermute | solution.py:293
  46.4 0.8 second_own.1
  47.2 4.1 %collective-permute-done.9 = f32[32,128]{1,0:T(8,128)S(1)} collective-permute-done((f32[32,128]{1,0:T(8,128)S(1)}, f32[32,128]{1,0:T(8,128)S(1)}, u32[]{:S(2)}, u32[]{:S(2)}) %collective-permute-start.9) | collective-permute-done | bytes 16416 | tf_op jit(solution)/shard_map/ppermute | solution.py:293
  51.3 0.0 collective-permute-done.13
  51.3 0.0 collective-permute-done.14
  51.4 0.6 collective-permute-start.17
  52.0 2.9 %collective-permute-start.16 = (f32[64,512]{1,0:T(8,128)S(1)}, f32[64,512]{1,0:T(8,128)S(1)}, u32[]{:S(2)}, u32[]{:S(2)}) collective-permute-start(f32[64,512]{1,0:T(8,128)S(1)} %add_add_fusion.refs_0_), channel_id=1, source_target_pairs={{0,2},{1,3},{2,0},{3,1},{4,6},{5,7},{6,4},{7,5},{8,10},{9,11},{10,... | collective-permute-start | bytes 393224 | tf_op jit(solution)/shard_map/ppermute | solution.py:256
  54.9 2.1 %collective-permute-start.15 = (f32[64,512]{1,0:T(8,128)S(1)}, f32[64,512]{1,0:T(8,128)S(1)}, u32[]{:S(2)}, u32[]{:S(2)}) collective-permute-start(f32[64,512]{1,0:T(8,128)S(1)} %add_add_fusion.refs_0_), channel_id=1, source_target_pairs={{0,1},{1,2},{2,3},{3,0},{4,5},{5,6},{6,7},{7,4},{8,9},{9,10},{10,1... | collective-permute-start | bytes 393224 | tf_op jit(solution)/shard_map/ppermute | solution.py:256
  57.0 0.9 collective-permute-start.11
  58.0 3.8 %collective-permute-done.11 = f32[32,128]{1,0:T(8,128)S(1)} collective-permute-done((f32[32,128]{1,0:T(8,128)S(1)}, f32[32,128]{1,0:T(8,128)S(1)}, u32[]{:S(2)}, u32[]{:S(2)}) %collective-permute-start.11) | collective-permute-done | bytes 16416 | tf_op jit(solution)/shard_map/ppermute | solution.py:293
  61.7 2.8 %collective-permute-start.12 = (f32[32,128]{1,0:T(8,128)S(1)}, f32[32,128]{1,0:T(8,128)S(1)}, u32[]{:S(2)}, u32[]{:S(2)}) collective-permute-start(f32[32,128]{1,0:T(8,128)S(1)} %add.36.refs_0_), channel_id=1, source_target_pairs={{0,192},{4,196},{8,200},{12,204},{16,208},{20,212},{24,216},{28,22... | collective-permute-start | bytes 49160 | tf_op jit(solution)/shard_map/ppermute | solution.py:293
  64.5 3.1 %collective-permute-done.12.refs_1_ = f32[32,128]{1,0:T(8,128)S(1)} collective-permute-done((f32[32,128]{1,0:T(8,128)S(1)}, f32[32,128]{1,0:T(8,128)S(1)}, u32[]{:S(2)}, u32[]{:S(2)}) %collective-permute-start.12) | collective-permute-done | bytes 16416 | tf_op jit(solution)/shard_map/ppermute | solution.py:293
  67.6 2.0 %factor.1.inv_ref = f32[64,64]{1,0:T(8,128)S(1)} custom-call(f32[32,128]{1,0:T(8,128)S(1)} %add.36.refs_0_, f32[32,128]{1,0:T(8,128)S(1)} %collective-permute-done.12.refs_1_), custom_call_target="tpu_custom_call" | custom-call | flops 1000000000 | bytes 1048576 | tf_op jit(solution)/shard_map/factor/pallas_call | solution.py:349
  69.6 0.0 collective-permute-done.17.refs_3_
  69.6 0.0 collective-permute-done.15.refs_1_
  69.6 1.1 %image.1 = (f32[64,2048]{1,0:T(8,128)S(1)}, f32[8,32,128]{2,1,0:T(8,128)S(1)}) custom-call(f32[64,64]{1,0:T(8,128)S(1)} %factor.1.inv_ref, f32[64,512]{1,0:T(8,128)S(1)} %add_add_fusion.refs_0_, f32[64,512]{1,0:T(8,128)S(1)} %collective-permute-done.15.refs_1_, f32[64,512]{1,0:T(8,128)S(1)} %collective-permute-done.16.refs_2_, ...), custom_call_target="tpu_custom_call" | custom-call | flops 1000000000 | bytes 1048576 | tf_op jit(solution)/shard_map/image/pallas_call | solution.py:350
  70.7 13.9 %all_to_all.5.gram_ref = f32[8,32,128]{2,1,0:T(8,128)S(1)} all-to-all(f32[8,32,128]{2,1,0:T(8,128)S(1)} %get-tuple-element.36), channel_id=1, replica_groups={{0,32,64,96,128,160,192,224},{1,33,65,97,129,161,193,225},{2,34,66,98,1..., dimensions={0} | all-to-all | bytes 262144 | tf_op jit(solution)/shard_map/all_to_all | solution.py:277
  84.7 0.1 collective-permute-start.18
  84.8 1.2 %collective-permute-done.18 = f32[32,128]{1,0:T(8,128)S(1)} collective-permute-done((f32[32,128]{1,0:T(8,128)S(1)}, f32[32,128]{1,0:T(8,128)S(1)}, u32[]{:S(2)}, u32[]{:S(2)}) %collective-permute-start.18) | collective-permute-done | bytes 16416 | tf_op jit(solution)/shard_map/ppermute | solution.py:265
  85.9 2.2 %collective-permute-start.21 = (f32[32,128]{1,0:T(8,128)S(1)}, f32[32,128]{1,0:T(8,128)S(1)}, u32[]{:S(2)}, u32[]{:S(2)}) collective-permute-start(f32[32,128]{1,0:T(8,128)S(1)} %add.39.refs_0_), channel_id=1, source_target_pairs={{0,24},{4,28},{8,16},{12,20},{16,8},{20,12},{24,0},{28,4},{32,56},... | collective-permute-start | bytes 49160 | tf_op jit(solution)/shard_map/ppermute | solution.py:306
  88.1 2.5 %collective-permute-start.19 = (f32[32,128]{1,0:T(8,128)S(1)}, f32[32,128]{1,0:T(8,128)S(1)}, u32[]{:S(2)}, u32[]{:S(2)}) collective-permute-start(f32[32,128]{1,0:T(8,128)S(1)} %add.39.refs_0_), channel_id=1, source_target_pairs={{0,16},{4,20},{8,24},{12,28},{16,0},{20,4},{24,8},{28,12},{32,48},... | collective-permute-start | bytes 49160 | tf_op jit(solution)/shard_map/ppermute | solution.py:306
  90.6 0.2 collective-permute-done.21.refs_3_
  90.9 1.0 %collective-permute-done.20.refs_2_ = f32[32,128]{1,0:T(8,128)S(1)} collective-permute-done((f32[32,128]{1,0:T(8,128)S(1)}, f32[32,128]{1,0:T(8,128)S(1)}, u32[]{:S(2)}, u32[]{:S(2)}) %collective-permute-start.20) | collective-permute-done | bytes 16416 | tf_op jit(solution)/shard_map/ppermute | solution.py:306
  91.9 1.5 %collective-permute-done.19.refs_1_ = f32[32,128]{1,0:T(8,128)S(1)} collective-permute-done((f32[32,128]{1,0:T(8,128)S(1)}, f32[32,128]{1,0:T(8,128)S(1)}, u32[]{:S(2)}, u32[]{:S(2)}) %collective-permute-start.19) | collective-permute-done | bytes 16416 | tf_op jit(solution)/shard_map/ppermute | solution.py:306
  93.4 3.3 %last.1 = f32[64,2048]{1,0:T(8,128)} custom-call(f32[64,2048]{1,0:T(8,128)S(1)} %get-tuple-element.35.image_ref, f32[32,128]{1,0:T(8,128)S(1)} %add.39.refs_0_, f32[32,128]{1,0:T(8,128)S(1)} %collective-permute-done.19.refs_1_, f32[32,128]{1,0:T(8,128)S(1)} %collective-permute-done.20.refs_2_, f32[32,128]{1,0:T(8,128)S(1)} %collective-permute-done.21.refs_3_), custom_call_target="tpu_custom_call" | custom-call | flops 1000000000 | bytes 1048576 | tf_op jit(solution)/shard_map/last/pallas_call | solution.py:352
  (24 shorter events, 0.1 us)
Async XLA Ops:
  0.0 10.7 %copy-start = (f32[2048,256]{1,0:T(8,128)S(1)}, f32[2048,256]{1,0:T(8,128)}, u32[]{:S(2)}) copy-start(f32[2048,256]{1,0:T(8,128)} %x_ref.7) | copy-start | bytes 6291460
  0.0 0.8 copy-start.1
  0.8 9.9 %copy-start.3 = (f32[2048,64]{0,1:T(8,128)S(1)}, f32[2048,64]{0,1:T(8,128)}, u32[]{:S(2)}) copy-start(f32[2048,64]{0,1:T(8,128)} %param.4) | copy-start | bytes 1572868
  2.4 8.3 %collective-permute-start = (f32[520,256]{1,0:T(8,128)S(1)}, f32[520,256]{1,0:T(8,128)S(1)}, u32[]{:S(2)}, u32[]{:S(2)}) collective-permute-start(f32[520,256]{1,0:T(8,128)S(1)} %cut.1.message_ref), channel_id=1, source_target_pairs={{0,4},{4,0},{8,12},{12,8},{16,20},{20,16},{24,28},{28,24},{32,36},... | collective-permute-start | bytes 1597448 | tf_op jit(solution)/shard_map/ppermute | solution.py:265
  2.5 15.1 %collective-permute-start.2 = (f32[520,256]{1,0:T(8,128)S(1)}, f32[520,256]{1,0:T(8,128)S(1)}, u32[]{:S(2)}, u32[]{:S(2)}) collective-permute-start(f32[520,256]{1,0:T(8,128)S(1)} %cut.1.message_ref), channel_id=1, source_target_pairs={{0,252},{4,8},{8,4},{12,16},{16,12},{20,24},{24,20},{28,32},{32,28... | collective-permute-start | bytes 1597448 | tf_op jit(solution)/shard_map/ppermute | solution.py:261
  15.0 9.4 %copy-start.2 = (s32[8,2]{0,1:T(2,128)S(1)}, s32[8,2]{0,1:T(2,128)}, u32[]{:S(2)}) copy-start(s32[8,2]{0,1:T(2,128)} %param.5) | copy-start | bytes 196
  15.0 13.8 %collective-permute-start.1 = (f32[64,512]{1,0:T(8,128)S(1)}, f32[64,512]{1,0:T(8,128)S(1)}, u32[]{:S(2)}, u32[]{:S(2)}) collective-permute-start(f32[64,512]{1,0:T(8,128)S(1)} %get-tuple-element.22), channel_id=1, source_target_pairs={{0,4},{4,0},{8,12},{12,8},{16,20},{20,16},{24,28},{28,24},{32,36},... | collective-permute-start | bytes 393224 | tf_op jit(solution)/shard_map/ppermute | solution.py:265
  19.2 9.6 %collective-permute-start.3 = (f32[64,512]{1,0:T(8,128)S(1)}, f32[64,512]{1,0:T(8,128)S(1)}, u32[]{:S(2)}, u32[]{:S(2)}) collective-permute-start(f32[64,512]{1,0:T(8,128)S(1)} %get-tuple-element.24), channel_id=1, source_target_pairs={{0,252},{4,8},{8,4},{12,16},{16,12},{20,24},{24,20},{28,32},{32,28... | collective-permute-start | bytes 393224 | tf_op jit(solution)/shard_map/ppermute | solution.py:261
  28.8 5.0 %collective-permute-start.6 = (f32[64,512]{1,0:T(8,128)S(1)}, f32[64,512]{1,0:T(8,128)S(1)}, u32[]{:S(2)}, u32[]{:S(2)}) collective-permute-start(f32[64,512]{1,0:T(8,128)S(1)} %add_add_fusion.1.refs_0_), channel_id=1, source_target_pairs={{0,3},{1,0},{2,1},{3,2},{4,7},{5,4},{6,5},{7,6},{8,11},{9,8},{10,9... | collective-permute-start | bytes 393224 | tf_op jit(solution)/shard_map/ppermute | solution.py:256
  29.4 6.5 %collective-permute-start.5 = (f32[64,512]{1,0:T(8,128)S(1)}, f32[64,512]{1,0:T(8,128)S(1)}, u32[]{:S(2)}, u32[]{:S(2)}) collective-permute-start(f32[64,512]{1,0:T(8,128)S(1)} %add_add_fusion.1.refs_0_), channel_id=1, source_target_pairs={{0,2},{1,3},{2,0},{3,1},{4,6},{5,7},{6,4},{7,5},{8,10},{9,11},{10,... | collective-permute-start | bytes 393224 | tf_op jit(solution)/shard_map/ppermute | solution.py:256
  32.3 5.0 %collective-permute-start.4 = (f32[64,512]{1,0:T(8,128)S(1)}, f32[64,512]{1,0:T(8,128)S(1)}, u32[]{:S(2)}, u32[]{:S(2)}) collective-permute-start(f32[64,512]{1,0:T(8,128)S(1)} %add_add_fusion.1.refs_0_), channel_id=1, source_target_pairs={{0,1},{1,2},{2,3},{3,0},{4,5},{5,6},{6,7},{7,4},{8,9},{9,10},{10,1... | collective-permute-start | bytes 393224 | tf_op jit(solution)/shard_map/ppermute | solution.py:256
  39.4 11.9 %collective-permute-start.13 = (f32[64,512]{1,0:T(8,128)S(1)}, f32[64,512]{1,0:T(8,128)S(1)}, u32[]{:S(2)}, u32[]{:S(2)}) collective-permute-start(f32[64,512]{1,0:T(8,128)S(1)} %get-tuple-element.33), channel_id=1, source_target_pairs={{0,4},{4,0},{8,12},{12,8},{16,20},{20,16},{24,28},{28,24},{32,36},... | collective-permute-start | bytes 393224 | tf_op jit(solution)/shard_map/ppermute | solution.py:265
  39.5 11.8 %collective-permute-start.14 = (f32[64,512]{1,0:T(8,128)S(1)}, f32[64,512]{1,0:T(8,128)S(1)}, u32[]{:S(2)}, u32[]{:S(2)}) collective-permute-start(f32[64,512]{1,0:T(8,128)S(1)} %get-tuple-element.34), channel_id=1, source_target_pairs={{0,252},{4,8},{8,4},{12,16},{16,12},{20,24},{24,20},{28,32},{32,28... | collective-permute-start | bytes 393224 | tf_op jit(solution)/shard_map/ppermute | solution.py:261
  41.4 1.2 %collective-permute-start.7 = (f32[32,128]{1,0:T(8,128)S(1)}, f32[32,128]{1,0:T(8,128)S(1)}, u32[]{:S(2)}, u32[]{:S(2)}) collective-permute-start(f32[32,128]{1,0:T(8,128)S(1)} %get-tuple-element.25), channel_id=1, source_target_pairs={{0,4},{4,0},{8,12},{12,8},{16,20},{20,16},{24,28},{28,24},{32,36},... | collective-permute-start | bytes 49160 | tf_op jit(solution)/shard_map/ppermute | solution.py:293
  42.6 3.7 %collective-permute-start.8 = (f32[32,128]{1,0:T(8,128)S(1)}, f32[32,128]{1,0:T(8,128)S(1)}, u32[]{:S(2)}, u32[]{:S(2)}) collective-permute-start(f32[32,128]{1,0:T(8,128)S(1)} %add.32), channel_id=1, source_target_pairs={{0,8},{4,12},{8,0},{12,4},{16,24},{20,28},{24,16},{28,20},{32,40},... | collective-permute-start | bytes 49160 | tf_op jit(solution)/shard_map/ppermute | solution.py:293
  46.4 4.9 %collective-permute-start.9 = (f32[32,128]{1,0:T(8,128)S(1)}, f32[32,128]{1,0:T(8,128)S(1)}, u32[]{:S(2)}, u32[]{:S(2)}) collective-permute-start(f32[32,128]{1,0:T(8,128)S(1)} %add.33), channel_id=1, source_target_pairs={{0,24},{4,28},{8,16},{12,20},{16,8},{20,12},{24,0},{28,4},{32,56},... | collective-permute-start | bytes 49160 | tf_op jit(solution)/shard_map/ppermute | solution.py:293
  51.3 5.7 %collective-permute-start.10 = (f32[32,128]{1,0:T(8,128)S(1)}, f32[32,128]{1,0:T(8,128)S(1)}, u32[]{:S(2)}, u32[]{:S(2)}) collective-permute-start(f32[32,128]{1,0:T(8,128)S(1)} %add.34), channel_id=1, source_target_pairs={{0,32},{4,36},{8,40},{12,44},{16,48},{20,52},{24,56},{28,60},{32,0... | collective-permute-start | bytes 49160 | tf_op jit(solution)/shard_map/ppermute | solution.py:293
  51.4 18.2 %collective-permute-start.17 = (f32[64,512]{1,0:T(8,128)S(1)}, f32[64,512]{1,0:T(8,128)S(1)}, u32[]{:S(2)}, u32[]{:S(2)}) collective-permute-start(f32[64,512]{1,0:T(8,128)S(1)} %add_add_fusion.refs_0_), channel_id=1, source_target_pairs={{0,3},{1,0},{2,1},{3,2},{4,7},{5,4},{6,5},{7,6},{8,11},{9,8},{10,9... | collective-permute-start | bytes 393224 | tf_op jit(solution)/shard_map/ppermute | solution.py:256
  52.0 17.6 %collective-permute-start.16 = (f32[64,512]{1,0:T(8,128)S(1)}, f32[64,512]{1,0:T(8,128)S(1)}, u32[]{:S(2)}, u32[]{:S(2)}) collective-permute-start(f32[64,512]{1,0:T(8,128)S(1)} %add_add_fusion.refs_0_), channel_id=1, source_target_pairs={{0,2},{1,3},{2,0},{3,1},{4,6},{5,7},{6,4},{7,5},{8,10},{9,11},{10,... | collective-permute-start | bytes 393224 | tf_op jit(solution)/shard_map/ppermute | solution.py:256
  54.9 14.7 %collective-permute-start.15 = (f32[64,512]{1,0:T(8,128)S(1)}, f32[64,512]{1,0:T(8,128)S(1)}, u32[]{:S(2)}, u32[]{:S(2)}) collective-permute-start(f32[64,512]{1,0:T(8,128)S(1)} %add_add_fusion.refs_0_), channel_id=1, source_target_pairs={{0,1},{1,2},{2,3},{3,0},{4,5},{5,6},{6,7},{7,4},{8,9},{9,10},{10,1... | collective-permute-start | bytes 393224 | tf_op jit(solution)/shard_map/ppermute | solution.py:256
  57.0 4.7 %collective-permute-start.11 = (f32[32,128]{1,0:T(8,128)S(1)}, f32[32,128]{1,0:T(8,128)S(1)}, u32[]{:S(2)}, u32[]{:S(2)}) collective-permute-start(f32[32,128]{1,0:T(8,128)S(1)} %add.35), channel_id=1, source_target_pairs={{0,64},{4,68},{8,72},{12,76},{16,80},{20,84},{24,88},{28,92},{32,9... | collective-permute-start | bytes 49160 | tf_op jit(solution)/shard_map/ppermute | solution.py:293
  61.7 5.8 %collective-permute-start.12 = (f32[32,128]{1,0:T(8,128)S(1)}, f32[32,128]{1,0:T(8,128)S(1)}, u32[]{:S(2)}, u32[]{:S(2)}) collective-permute-start(f32[32,128]{1,0:T(8,128)S(1)} %add.36.refs_0_), channel_id=1, source_target_pairs={{0,192},{4,196},{8,200},{12,204},{16,208},{20,212},{24,216},{28,22... | collective-permute-start | bytes 49160 | tf_op jit(solution)/shard_map/ppermute | solution.py:293
  84.7 1.3 %collective-permute-start.18 = (f32[32,128]{1,0:T(8,128)S(1)}, f32[32,128]{1,0:T(8,128)S(1)}, u32[]{:S(2)}, u32[]{:S(2)}) collective-permute-start(f32[32,128]{1,0:T(8,128)S(1)} %sum_z.1), channel_id=1, source_target_pairs={{0,4},{4,0},{8,12},{12,8},{16,20},{20,16},{24,28},{28,24},{32,36},... | collective-permute-start | bytes 49160 | tf_op jit(solution)/shard_map/ppermute | solution.py:265
  85.9 4.9 %collective-permute-start.21 = (f32[32,128]{1,0:T(8,128)S(1)}, f32[32,128]{1,0:T(8,128)S(1)}, u32[]{:S(2)}, u32[]{:S(2)}) collective-permute-start(f32[32,128]{1,0:T(8,128)S(1)} %add.39.refs_0_), channel_id=1, source_target_pairs={{0,24},{4,28},{8,16},{12,20},{16,8},{20,12},{24,0},{28,4},{32,56},... | collective-permute-start | bytes 49160 | tf_op jit(solution)/shard_map/ppermute | solution.py:306
  88.1 3.7 %collective-permute-start.20 = (f32[32,128]{1,0:T(8,128)S(1)}, f32[32,128]{1,0:T(8,128)S(1)}, u32[]{:S(2)}, u32[]{:S(2)}) collective-permute-start(f32[32,128]{1,0:T(8,128)S(1)} %add.39.refs_0_), channel_id=1, source_target_pairs={{0,8},{4,12},{8,0},{12,4},{16,24},{20,28},{24,16},{28,20},{32,40},... | collective-permute-start | bytes 49160 | tf_op jit(solution)/shard_map/ppermute | solution.py:306
  88.1 5.2 %collective-permute-start.19 = (f32[32,128]{1,0:T(8,128)S(1)}, f32[32,128]{1,0:T(8,128)S(1)}, u32[]{:S(2)}, u32[]{:S(2)}) collective-permute-start(f32[32,128]{1,0:T(8,128)S(1)} %add.39.refs_0_), channel_id=1, source_target_pairs={{0,16},{4,20},{8,24},{12,28},{16,0},{20,4},{24,8},{28,12},{32,48},... | collective-permute-start | bytes 49160 | tf_op jit(solution)/shard_map/ppermute | solution.py:306

commit v10 on v9

--- a/solution.py
+++ b/solution.py
@@ -67,20 +67,21 @@
     acc_ref[...] += (one[:k] + two[:k]) + (one[k : 2 * k] + two[k:] + one[2 * k :])
 
 
-def cut_kernel(x_ref, pairs_ref, out_ref, sem):
+def cut_kernel(x_ref, pairs_ref, out_ref, list_ref, sems):
     _, member = place()
-    quarter, width = out_ref.shape[0] - NOTE, out_ref.shape[1]
+    quarter = out_ref.shape[0] - NOTE
     source = x_ref.at[pl.ds(pl.multiple_of(member * quarter, quarter), quarter)]
-    copy = pltpu.make_async_copy(source, out_ref.at[pl.ds(0, quarter)], sem)
-    copy.start()
-    lane = lax.broadcasted_iota(jnp.int32, (NOTE, width), 1)
-    row = lax.broadcasted_iota(jnp.int32, (NOTE, width), 0)
-    note = jnp.zeros((NOTE, width), f32)
-    for slot in range(pairs_ref.shape[1]):
-        for c in range(2):
-            note = jnp.where((lane == slot) & (row == c), pairs_ref[c, slot].astype(f32), note)
-    out_ref[quarter:, :] = note
-    copy.wait()
+    copies = [
+        pltpu.make_async_copy(source, out_ref.at[pl.ds(0, quarter)], sems.at[0]),
+        pltpu.make_async_copy(pairs_ref, list_ref, sems.at[1]),
+    ]
+    for copy in copies:
+        copy.start()
+    copies[1].wait()
+    count, slots = list_ref.shape
+    out_ref[quarter:, :] = jnp.zeros((NOTE, out_ref.shape[1]), f32)
+    out_ref[quarter : quarter + count, :slots] = list_ref[...].astype(f32)
+    copies[0].wait()
 
 
 def tiles_kernel(members, side, x_ref, v_ref, message_ref, pairs_ref, acc_ref, eh_ref, el_ref, xah_ref, xal_ref, chunk=256):
@@ -124,10 +125,11 @@
 
 def gather_into(full_ref, pieces, members):
     _, member = place()
-    quarter = pieces[0].shape[1]
-    for k, piece in enumerate(pieces):
-        q = lax.rem(member - k + members, members)
-        full_ref[:, pl.ds(pl.multiple_of(q * quarter, quarter), quarter)] = piece[...]
+    quarter = full_ref.shape[1] // members
+    for piece, other in zip(pieces, (0, 3)):
+        for near in range(2):
+            q = member ^ (other ^ near)
+            full_ref[:, pl.ds(pl.multiple_of(q * quarter, quarter), quarter)] = piece[:, near * quarter : (near + 1) * quarter]
 
 
 def put_gram(gram_ref, image, total):
@@ -150,7 +152,7 @@
 
 
 def join_kernel(members, total, *refs):
-    pieces, full_ref, gram_ref = refs[:members], refs[members], refs[members + 1]
+    pieces, full_ref, gram_ref = refs[:2], refs[2], refs[3]
     gather_into(full_ref, pieces, members)
     put_gram(gram_ref, full_ref[...], total)
 
@@ -222,7 +224,7 @@
 
 
 def image_kernel(members, total, inv_ref, *refs):
-    pieces, image_ref, gram_ref = refs[:members], refs[members], refs[members + 1]
+    pieces, image_ref, gram_ref = refs[:2], refs[2], refs[3]
     gather_into(image_ref, pieces, members)
     image_ref[...] = exact(inv_ref[...], image_ref[...])
     put_gram(gram_ref, image_ref[...], total)
@@ -251,9 +253,13 @@
     )
 
 
-def shifted(x, axis, by):
-    n = lax.axis_size(axis)
-    return lax.ppermute(x, axis, [(i, (i + by) % n) for i in range(n)])
+def gathered(x, *after):
+    swap = lambda y, mask: lax.ppermute(y, "sub", [(i, i ^ mask) for i in range(lax.axis_size("sub"))])
+    near = swap(x, 1)
+    if after:
+        near = tie(near, *after)
+    both = jnp.concatenate([x, near], 1)
+    return both, swap(both, 3)
 
 
 def crossed(x):
@@ -289,11 +295,11 @@
 
 def pair_sums(total):
     groups = lax.axis_size("rows")
+    sums = [total]
     for mask in MASKS:
-        other = lax.ppermute(total, "rows", [(i, i ^ mask) for i in range(groups)])
-        if mask == MASKS[-1]:
-            return [total, other]
-        total = total + other
+        other = lax.ppermute(sums[-1], "rows", [(i, i ^ mask) for i in range(groups)])
+        sums.append(other if mask == MASKS[-1] else sums[-1] + other)
+    return sums
 
 
 RING = (4, 2, 6)
@@ -322,8 +328,9 @@
     part = ((k, quarter), f32)
     kept = [((rows, quarter), bf16)] * 2
     (mine,) = call(
-        cut_kernel, [HB, SM], [((quarter + NOTE, width), f32)], "cut", flops=10**6, scratch=[pltpu.SemaphoreType.DMA])(
-        pltpu.with_memory_space_constraint(embeddings, pltpu.HBM), pairs)
+        cut_kernel, [HB, HB], [((quarter + NOTE, width), f32)], "cut", flops=10**6,
+        scratch=[pltpu.VMEM(pairs.shape, jnp.int32), pltpu.SemaphoreType.DMA((2,))])(
+        *(pltpu.with_memory_space_constraint(a, pltpu.HBM) for a in (embeddings, pairs)))
     cross = crossed(mine)
     sib = swapped(mine)
 
@@ -337,17 +344,18 @@
     sib_acc, sib_t = make(SIB, sib, "sib_tiles")
     cross_acc, cross_t = make(CROSS, tie(cross, sib_acc), "cross_tiles")
     acc = (acc + swapped(sib_acc)) + crossed(cross_acc)
-    pieces = [acc] + [shifted(acc, "sub", s) for s in range(1, members)]
+    pieces = gathered(acc)
     whole = ((k, rows), f32)
     copies = ((groups // NEAR, k // 2, 2 * k), f32)
-    image, gram = call(functools.partial(join_kernel, members, total), [VM] * members, [whole, (copies[0][1:], f32)], "join")(*pieces)
-    sib_acc, cross_acc = call(second_kernel, [VM] * 5, [part] * 2, "second_far")(image, *sib_t, *cross_t)
-    (acc2,) = call(second_kernel, [VM] * 3, [part], "second_own")(image, *own_t)
-    terms = pair_sums(gram)
+    image, gram = call(functools.partial(join_kernel, members, total), [VM] * 2, [whole, (copies[0][1:], f32)], "join")(*pieces)
+    sums = pair_sums(gram)
+    terms = sums[-2:]
+    sib_acc, cross_acc = call(second_kernel, [VM] * 5, [part] * 2, "second_far")(tie(image, sums[1]), *sib_t, *cross_t)
+    (acc2,) = call(second_kernel, [VM] * 3, [part], "second_own")(tie(image, sums[2]), *own_t)
     acc2 = (acc2 + swapped(sib_acc)) + crossed(cross_acc)
-    pieces = [acc2] + [shifted(acc2, "sub", s) for s in range(1, members)]
+    pieces = gathered(tie(acc2, sums[3]), sums[4])
     (inv,) = call(factor_kernel, [VM] * len(terms), [((k, k), f32)], "factor")(*terms)
-    image, gram = call(functools.partial(image_kernel, members, total), [VM] * (1 + members), [whole, copies], "image")(inv, *pieces)
+    image, gram = call(functools.partial(image_kernel, members, total), [VM] * 3, [whole, copies], "image")(inv, *pieces)
     terms = row_sums(gram)
     (out,) = call(last_kernel, [VM] * (1 + len(terms)), [whole], "last")(image, *terms)
     return out.T

time: 97.1 us -> 103 us (1.061)
  the two profiles are of different devices: /device:TPU:16 before, /device:TPU:4 now
where the time goes in v10:
time: 103 us; the launch traced here: 102 us
  waiting for transfers between devices  35.2 us (34%)
  starting transfers between devices  31.1 us (30%)
  Pallas kernels  20.9 us (20%)
  blocking collectives  15 us (15%)
    all_to_all x1, blocking collectives, exchanged(): return lax.all_to_all(x, ('rows', 'sub'), 0, 0, axis_index_groups=sets)  15 us
    ppermute x6, waiting for transfers between devices, pair_sums(): lax.ppermute(sums[-1], 'rows', [(i, i ^ mask) for i in range(groups)])  13.8 us
    ppermute x6, starting transfers between devices, pair_sums(): lax.ppermute(sums[-1], 'rows', [(i, i ^ mask) for i in range(groups)])  11.6 us
    pallas_call x3, Pallas kernels, make(): call(functools.partial(tiles_kernel, members, side), [VM, VM, VM, SM], [p...  10.2 us
    ppermute x4, waiting for transfers between devices, gathered(): lax.ppermute(y, 'sub', [(i, i ^ mask) for i in range(lax.axis_size('sub'))])  9.32 us
    ppermute x4, starting transfers between devices, gathered(): lax.ppermute(y, 'sub', [(i, i ^ mask) for i in range(lax.axis_size('sub'))])  8.31 us
    ppermute x3, starting transfers between devices, crossed(): lax.ppermute(x, 'rows', [(i, (i + 2 * (i % 2) - 1) % n) for i in range(n)])  5.45 us
    ppermute x3, starting transfers between devices, row_sums(): lax.ppermute(total, 'rows', [(i, i ^ mask) for i in range(groups)])  5.25 us
  transfers between devices with their start and end apart: 20, of which 15 were waited for; matrix products, arithmetic and copies ran while one was open for 0% of the time, Pallas kernels for 13%

profile of v10, /device:TPU:4, one launch (start us, length us, event | category | flops | bytes accessed | tf_op | source)
XLA Modules:
  0.0 102.4 jit_solution(7004475132303080565)
XLA Ops:
  0.0 1.2 %cut.1.message_ref = f32[520,256]{1,0:T(8,128)S(1)} custom-call(f32[2048,256]{1,0:T(8,128)} %x_ref.7, s32[2,8]{1,0:T(2,128)} %bitcast.3), custom_call_target="tpu_custom_call" | custom-call | flops 1000000 | bytes 1048576 | tf_op jit(solution)/shard_map/cut/pallas_call | solution.py:330
  1.2 0.1 collective-permute-start
  1.3 0.6 collective-permute-start.2
  2.0 1.3 %collective-permute-done.message_ref = f32[520,256]{1,0:T(8,128)S(1)} collective-permute-done((f32[520,256]{1,0:T(8,128)S(1)}, f32[520,256]{1,0:T(8,128)S(1)}, u32[]{:S(2)}, u32[]{:S(2)}) %collective-permute-start) | collective-permute-done | bytes 532512 | tf_op jit(solution)/shard_map/ppermute | solution.py:271
  3.3 2.9 %sib_tiles.1 = (f32[64,512]{1,0:T(8,128)S(1)}, bf16[2048,512]{1,0:T(8,128)(2,1)S(1)}, bf16[2048,512]{1,0:T(8,128)(2,1)S(1)}) custom-call(f32[2048,256]{1,0:T(8,128)S(1)} %copy-done, f32[64,2048]{1,0:T(8,128)S(1)} %bitcast.7, f32[520,256]{1,0:T(8,128)S(1)} %collective-permute-done.message_ref, s32[2,8]{1,0:T(2,128)S(1)} %bitcast.4), custom_call_target="tpu_custom_call" | custom-call | flops 5000000000 | bytes 1048576 | tf_op jit(solution)/shard_map/sib_tiles/pallas_call | solution.py:338
  6.2 0.1 collective-permute-start.1
  6.3 3.9 %collective-permute-done.2.message_ref = f32[520,256]{1,0:T(8,128)S(1)} collective-permute-done((f32[520,256]{1,0:T(8,128)S(1)}, f32[520,256]{1,0:T(8,128)S(1)}, u32[]{:S(2)}, u32[]{:S(2)}) %collective-permute-start.2) | collective-permute-done | bytes 532512 | tf_op jit(solution)/shard_map/ppermute | solution.py:267
  10.1 4.2 %cross_tiles.1 = (f32[64,512]{1,0:T(8,128)S(1)}, bf16[2048,512]{1,0:T(8,128)(2,1)S(1)}, bf16[2048,512]{1,0:T(8,128)(2,1)S(1)}) custom-call(f32[2048,256]{1,0:T(8,128)S(1)} %copy-done, f32[64,2048]{1,0:T(8,128)S(1)} %bitcast.8, f32[520,256]{1,0:T(8,128)S(1)} %collective-permute-done.2.message_ref, s32[2,8]{1,0:T(2,128)S(1)} %bitcast.5), custom_call_target="tpu_custom_call" | custom-call | flops 5000000000 | bytes 1048576 | tf_op jit(solution)/shard_map/cross_tiles/pallas_call | solution.py:338
  14.4 0.9 collective-permute-start.3
  15.2 3.1 %own_tiles.1 = (f32[64,512]{1,0:T(8,128)S(1)}, bf16[2048,512]{1,0:T(8,128)(2,1)S(1)}, bf16[2048,512]{1,0:T(8,128)(2,1)S(1)}) custom-call(f32[2048,256]{1,0:T(8,128)S(1)} %copy-done, f32[64,2048]{1,0:T(8,128)S(1)} %bitcast.9, f32[520,256]{1,0:T(8,128)S(1)} %cut.1.message_ref, s32[2,8]{1,0:T(2,128)S(1)} %bitcast.6), custom_call_target="tpu_custom_call" | custom-call | flops 5000000000 | bytes 1048576 | tf_op jit(solution)/shard_map/own_tiles/pallas_call | solution.py:338
  18.3 0.0 collective-permute-done.1
  18.3 0.5 collective-permute-done.3
  18.9 1.7 %collective-permute-start.4 = (f32[64,512]{1,0:T(8,128)S(1)}, f32[64,512]{1,0:T(8,128)S(1)}, u32[]{:S(2)}, u32[]{:S(2)}) collective-permute-start(f32[64,512]{1,0:T(8,128)S(1)} %add_add_fusion.1), channel_id=1, source_target_pairs={{0,1},{1,0},{2,3},{3,2},{4,5},{5,4},{6,7},{7,6},{8,9},{9,8},{10,11... | collective-permute-start | bytes 393224 | tf_op jit(solution)/shard_map/ppermute | solution.py:257
  20.5 3.4 %collective-permute-done.4 = f32[64,512]{1,0:T(8,128)S(1)} collective-permute-done((f32[64,512]{1,0:T(8,128)S(1)}, f32[64,512]{1,0:T(8,128)S(1)}, u32[]{:S(2)}, u32[]{:S(2)}) %collective-permute-start.4) | collective-permute-done | bytes 131104 | tf_op jit(solution)/shard_map/ppermute | solution.py:257
  23.9 3.1 %collective-permute-start.5 = (f32[64,1024]{1,0:T(8,128)S(1)}, f32[64,1024]{1,0:T(8,128)S(1)}, u32[]{:S(2)}, u32[]{:S(2)}) collective-permute-start(f32[64,1024]{1,0:T(8,128)S(1)} %pad_maximum_fusion.refs_0_), channel_id=1, source_target_pairs={{0,3},{1,2},{2,1},{3,0},{4,7},{5,6},{6,5},{7,4},{8,11},{9,10},{10,... | collective-permute-start | bytes 786440 | tf_op jit(solution)/shard_map/ppermute | solution.py:257
  27.1 4.6 %collective-permute-done.5.refs_1_ = f32[64,1024]{1,0:T(8,128)S(1)} collective-permute-done((f32[64,1024]{1,0:T(8,128)S(1)}, f32[64,1024]{1,0:T(8,128)S(1)}, u32[]{:S(2)}, u32[]{:S(2)}) %collective-permute-start.5) | collective-permute-done | bytes 262176 | tf_op jit(solution)/shard_map/ppermute | solution.py:257
  31.6 0.6 join.1
  32.3 0.0 collective-permute-start.6
  32.3 1.2 %collective-permute-done.6 = f32[32,128]{1,0:T(8,128)S(1)} collective-permute-done((f32[32,128]{1,0:T(8,128)S(1)}, f32[32,128]{1,0:T(8,128)S(1)}, u32[]{:S(2)}, u32[]{:S(2)}) %collective-permute-start.6) | collective-permute-done | bytes 16416 | tf_op jit(solution)/shard_map/ppermute | solution.py:300
  33.5 1.5 %second_far.1 = (f32[64,512]{1,0:T(8,128)S(1)}, f32[64,512]{1,0:T(8,128)S(1)}) custom-call(f32[64,2048]{1,0:T(8,128)S(1)} %get-tuple-element.31.v_ref, bf16[2048,512]{1,0:T(8,128)(2,1)S(1)} %get-tuple-element.35.refs_0_, bf16[2048,512]{1,0:T(8,128)(2,1)S(1)} %get-tuple-element.36.refs_1_, bf16[2048,512]{1,0:T(8,128)(2,1)S(1)} %get-tuple-element.37.refs_2_, ...), custom_call_target="tpu_custom_call" | custom-call | flops 1000000000 | bytes 1048576 | tf_op jit(solution)/shard_map/second_far/pallas_call | solution.py:353
  35.0 0.3 collective-permute-start.12
  35.3 3.9 %collective-permute-start.13 = (f32[64,512]{1,0:T(8,128)S(1)}, f32[64,512]{1,0:T(8,128)S(1)}, u32[]{:S(2)}, u32[]{:S(2)}) collective-permute-start(f32[64,512]{1,0:T(8,128)S(1)} %get-tuple-element.40), channel_id=1, source_target_pairs={{0,252},{4,8},{8,4},{12,16},{16,12},{20,24},{24,20},{28,32},{32,28... | collective-permute-start | bytes 393224 | tf_op jit(solution)/shard_map/ppermute | solution.py:267
  39.2 0.0 collective-permute-start.7
  39.2 3.7 %collective-permute-done.7 = f32[32,128]{1,0:T(8,128)S(1)} collective-permute-done((f32[32,128]{1,0:T(8,128)S(1)}, f32[32,128]{1,0:T(8,128)S(1)}, u32[]{:S(2)}, u32[]{:S(2)}) %collective-permute-start.7) | collective-permute-done | bytes 16416 | tf_op jit(solution)/shard_map/ppermute | solution.py:300
  43.0 5.8 %collective-permute-start.8 = (f32[32,128]{1,0:T(8,128)S(1)}, f32[32,128]{1,0:T(8,128)S(1)}, u32[]{:S(2)}, u32[]{:S(2)}) collective-permute-start(f32[32,128]{1,0:T(8,128)S(1)} %add.33), channel_id=1, source_target_pairs={{0,24},{4,28},{8,16},{12,20},{16,8},{20,12},{24,0},{28,4},{32,56},... | collective-permute-start | bytes 49160 | tf_op jit(solution)/shard_map/ppermute | solution.py:300
  48.8 0.8 second_own.1
  49.6 0.9 collective-permute-done.8
  50.5 0.0 collective-permute-done.12
  50.5 0.0 collective-permute-done.13
  50.6 0.5 collective-permute-start.14
  51.0 3.2 %collective-permute-done.9 = f32[32,128]{1,0:T(8,128)S(1)} collective-permute-done((f32[32,128]{1,0:T(8,128)S(1)}, f32[32,128]{1,0:T(8,128)S(1)}, u32[]{:S(2)}, u32[]{:S(2)}) %collective-permute-start.9) | collective-permute-done | bytes 16416 | tf_op jit(solution)/shard_map/ppermute | solution.py:300
  54.3 1.4 %collective-permute-done.14 = f32[64,512]{1,0:T(8,128)S(1)} collective-permute-done((f32[64,512]{1,0:T(8,128)S(1)}, f32[64,512]{1,0:T(8,128)S(1)}, u32[]{:S(2)}, u32[]{:S(2)}) %collective-permute-start.14) | collective-permute-done | bytes 131104 | tf_op jit(solution)/shard_map/ppermute | solution.py:257
  55.6 3.1 %collective-permute-start.15 = (f32[64,1024]{1,0:T(8,128)S(1)}, f32[64,1024]{1,0:T(8,128)S(1)}, u32[]{:S(2)}, u32[]{:S(2)}) collective-permute-start(f32[64,1024]{1,0:T(8,128)S(1)} %constant_dynamic-update-slice_fusion.refs_0_), channel_id=1, source_target_pairs={{0,3},{1,2},{2,1},{3,0},{4,7},{5,6},{6,5},{7,4},{8,11},{9,10},{10,... | collective-permute-start | bytes 786440 | tf_op jit(solution)/shard_map/ppermute | solution.py:257
  58.7 2.7 %collective-permute-start.10 = (f32[32,128]{1,0:T(8,128)S(1)}, f32[32,128]{1,0:T(8,128)S(1)}, u32[]{:S(2)}, u32[]{:S(2)}) collective-permute-start(f32[32,128]{1,0:T(8,128)S(1)} %add.35), channel_id=1, source_target_pairs={{0,64},{4,68},{8,72},{12,76},{16,80},{20,84},{24,88},{28,92},{32,9... | collective-permute-start | bytes 49160 | tf_op jit(solution)/shard_map/ppermute | solution.py:300
  61.4 2.0 %collective-permute-done.10 = f32[32,128]{1,0:T(8,128)S(1)} collective-permute-done((f32[32,128]{1,0:T(8,128)S(1)}, f32[32,128]{1,0:T(8,128)S(1)}, u32[]{:S(2)}, u32[]{:S(2)}) %collective-permute-start.10) | collective-permute-done | bytes 16416 | tf_op jit(solution)/shard_map/ppermute | solution.py:300
  63.4 3.0 %collective-permute-start.11 = (f32[32,128]{1,0:T(8,128)S(1)}, f32[32,128]{1,0:T(8,128)S(1)}, u32[]{:S(2)}, u32[]{:S(2)}) collective-permute-start(f32[32,128]{1,0:T(8,128)S(1)} %add.36.refs_0_), channel_id=1, source_target_pairs={{0,192},{4,196},{8,200},{12,204},{16,208},{20,212},{24,216},{28,22... | collective-permute-start | bytes 49160 | tf_op jit(solution)/shard_map/ppermute | solution.py:300
  66.4 2.8 %collective-permute-done.11.refs_1_ = f32[32,128]{1,0:T(8,128)S(1)} collective-permute-done((f32[32,128]{1,0:T(8,128)S(1)}, f32[32,128]{1,0:T(8,128)S(1)}, u32[]{:S(2)}, u32[]{:S(2)}) %collective-permute-start.11) | collective-permute-done | bytes 16416 | tf_op jit(solution)/shard_map/ppermute | solution.py:300
  69.2 2.0 %factor.1.inv_ref = f32[64,64]{1,0:T(8,128)S(1)} custom-call(f32[32,128]{1,0:T(8,128)S(1)} %add.36.refs_0_, f32[32,128]{1,0:T(8,128)S(1)} %collective-permute-done.11.refs_1_), custom_call_target="tpu_custom_call" | custom-call | flops 1000000000 | bytes 1048576 | tf_op jit(solution)/shard_map/factor/pallas_call | solution.py:357
  71.2 0.0 collective-permute-done.15.refs_1_
  71.2 1.1 %image.1 = (f32[64,2048]{1,0:T(8,128)S(1)}, f32[8,32,128]{2,1,0:T(8,128)S(1)}) custom-call(f32[64,64]{1,0:T(8,128)S(1)} %factor.1.inv_ref, f32[64,1024]{1,0:T(8,128)S(1)} %constant_dynamic-update-slice_fusion.refs_0_, f32[64,1024]{1,0:T(8,128)S(1)} %collective-permute-done.15.refs_1_), custom_call_target="tpu_custom_call" | custom-call | flops 1000000000 | bytes 1048576 | tf_op jit(solution)/shard_map/image/pallas_call | solution.py:358
  72.3 15.0 %all_to_all.5.gram_ref = f32[8,32,128]{2,1,0:T(8,128)S(1)} all-to-all(f32[8,32,128]{2,1,0:T(8,128)S(1)} %get-tuple-element.44), channel_id=1, replica_groups={{0,32,64,96,128,160,192,224},{1,33,65,97,129,161,193,225},{2,34,66,98,1..., dimensions={0} | all-to-all | bytes 262144 | tf_op jit(solution)/shard_map/all_to_all | solution.py:283
  87.3 0.1 collective-permute-start.16
  87.4 1.2 %collective-permute-done.16 = f32[32,128]{1,0:T(8,128)S(1)} collective-permute-done((f32[32,128]{1,0:T(8,128)S(1)}, f32[32,128]{1,0:T(8,128)S(1)}, u32[]{:S(2)}, u32[]{:S(2)}) %collective-permute-start.16) | collective-permute-done | bytes 16416 | tf_op jit(solution)/shard_map/ppermute | solution.py:271
  88.6 2.1 %collective-permute-start.19 = (f32[32,128]{1,0:T(8,128)S(1)}, f32[32,128]{1,0:T(8,128)S(1)}, u32[]{:S(2)}, u32[]{:S(2)}) collective-permute-start(f32[32,128]{1,0:T(8,128)S(1)} %add.39.refs_0_), channel_id=1, source_target_pairs={{0,24},{4,28},{8,16},{12,20},{16,8},{20,12},{24,0},{28,4},{32,56},... | collective-permute-start | bytes 49160 | tf_op jit(solution)/shard_map/ppermute | solution.py:312
  90.7 3.2 %collective-permute-start.18 = (f32[32,128]{1,0:T(8,128)S(1)}, f32[32,128]{1,0:T(8,128)S(1)}, u32[]{:S(2)}, u32[]{:S(2)}) collective-permute-start(f32[32,128]{1,0:T(8,128)S(1)} %add.39.refs_0_), channel_id=1, source_target_pairs={{0,8},{4,12},{8,0},{12,4},{16,24},{20,28},{24,16},{28,20},{32,40},... | collective-permute-start | bytes 49160 | tf_op jit(solution)/shard_map/ppermute | solution.py:312
  93.8 1.7 %collective-permute-done.18.refs_2_ = f32[32,128]{1,0:T(8,128)S(1)} collective-permute-done((f32[32,128]{1,0:T(8,128)S(1)}, f32[32,128]{1,0:T(8,128)S(1)}, u32[]{:S(2)}, u32[]{:S(2)}) %collective-permute-start.18) | collective-permute-done | bytes 16416 | tf_op jit(solution)/shard_map/ppermute | solution.py:312
  95.5 3.5 %collective-permute-done.17.refs_1_ = f32[32,128]{1,0:T(8,128)S(1)} collective-permute-done((f32[32,128]{1,0:T(8,128)S(1)}, f32[32,128]{1,0:T(8,128)S(1)}, u32[]{:S(2)}, u32[]{:S(2)}) %collective-permute-start.17) | collective-permute-done | bytes 16416 | tf_op jit(solution)/shard_map/ppermute | solution.py:312
  99.1 3.3 %last.1 = f32[64,2048]{1,0:T(8,128)} custom-call(f32[64,2048]{1,0:T(8,128)S(1)} %get-tuple-element.43.image_ref, f32[32,128]{1,0:T(8,128)S(1)} %add.39.refs_0_, f32[32,128]{1,0:T(8,128)S(1)} %collective-permute-done.17.refs_1_, f32[32,128]{1,0:T(8,128)S(1)} %collective-permute-done.18.refs_2_, f32[32,128]{1,0:T(8,128)S(1)} %collective-permute-done.19.refs_3_), custom_call_target="tpu_custom_call" | custom-call | flops 1000000000 | bytes 1048576 | tf_op jit(solution)/shard_map/last/pallas_call | solution.py:360
  (21 shorter events, 0.2 us)
Async XLA Ops:
  0.0 3.2 %copy-start = (f32[2048,256]{1,0:T(8,128)S(1)}, f32[2048,256]{1,0:T(8,128)}, u32[]{:S(2)}) copy-start(f32[2048,256]{1,0:T(8,128)} %x_ref.7) | copy-start | bytes 6291460
  0.0 3.2 %copy-start.1 = (s32[8,2]{0,1:T(2,128)S(1)}, s32[8,2]{0,1:T(2,128)}, u32[]{:S(2)}) copy-start(s32[8,2]{0,1:T(2,128)} %param.5) | copy-start | bytes 196
  0.0 3.2 %copy-start.2 = (f32[2048,64]{0,1:T(8,128)S(1)}, f32[2048,64]{0,1:T(8,128)}, u32[]{:S(2)}) copy-start(f32[2048,64]{0,1:T(8,128)} %param.4) | copy-start | bytes 1572868
  1.2 2.0 %collective-permute-start = (f32[520,256]{1,0:T(8,128)S(1)}, f32[520,256]{1,0:T(8,128)S(1)}, u32[]{:S(2)}, u32[]{:S(2)}) collective-permute-start(f32[520,256]{1,0:T(8,128)S(1)} %cut.1.message_ref), channel_id=1, source_target_pairs={{0,4},{4,0},{8,12},{12,8},{16,20},{20,16},{24,28},{28,24},{32,36},... | collective-permute-start | bytes 1597448 | tf_op jit(solution)/shard_map/ppermute | solution.py:271
  1.3 8.8 %collective-permute-start.2 = (f32[520,256]{1,0:T(8,128)S(1)}, f32[520,256]{1,0:T(8,128)S(1)}, u32[]{:S(2)}, u32[]{:S(2)}) collective-permute-start(f32[520,256]{1,0:T(8,128)S(1)} %cut.1.message_ref), channel_id=1, source_target_pairs={{0,252},{4,8},{8,4},{12,16},{16,12},{20,24},{24,20},{28,32},{32,28... | collective-permute-start | bytes 1597448 | tf_op jit(solution)/shard_map/ppermute | solution.py:267
  6.2 12.2 %collective-permute-start.1 = (f32[64,512]{1,0:T(8,128)S(1)}, f32[64,512]{1,0:T(8,128)S(1)}, u32[]{:S(2)}, u32[]{:S(2)}) collective-permute-start(f32[64,512]{1,0:T(8,128)S(1)} %get-tuple-element.26), channel_id=1, source_target_pairs={{0,4},{4,0},{8,12},{12,8},{16,20},{20,16},{24,28},{28,24},{32,36},... | collective-permute-start | bytes 393224 | tf_op jit(solution)/shard_map/ppermute | solution.py:271
  14.4 4.5 %collective-permute-start.3 = (f32[64,512]{1,0:T(8,128)S(1)}, f32[64,512]{1,0:T(8,128)S(1)}, u32[]{:S(2)}, u32[]{:S(2)}) collective-permute-start(f32[64,512]{1,0:T(8,128)S(1)} %get-tuple-element.28), channel_id=1, source_target_pairs={{0,252},{4,8},{8,4},{12,16},{16,12},{20,24},{24,20},{28,32},{32,28... | collective-permute-start | bytes 393224 | tf_op jit(solution)/shard_map/ppermute | solution.py:267
  18.9 5.1 %collective-permute-start.4 = (f32[64,512]{1,0:T(8,128)S(1)}, f32[64,512]{1,0:T(8,128)S(1)}, u32[]{:S(2)}, u32[]{:S(2)}) collective-permute-start(f32[64,512]{1,0:T(8,128)S(1)} %add_add_fusion.1), channel_id=1, source_target_pairs={{0,1},{1,0},{2,3},{3,2},{4,5},{5,4},{6,7},{7,6},{8,9},{9,8},{10,11... | collective-permute-start | bytes 393224 | tf_op jit(solution)/shard_map/ppermute | solution.py:257
  23.9 7.7 %collective-permute-start.5 = (f32[64,1024]{1,0:T(8,128)S(1)}, f32[64,1024]{1,0:T(8,128)S(1)}, u32[]{:S(2)}, u32[]{:S(2)}) collective-permute-start(f32[64,1024]{1,0:T(8,128)S(1)} %pad_maximum_fusion.refs_0_), channel_id=1, source_target_pairs={{0,3},{1,2},{2,1},{3,0},{4,7},{5,6},{6,5},{7,4},{8,11},{9,10},{10,... | collective-permute-start | bytes 786440 | tf_op jit(solution)/shard_map/ppermute | solution.py:257
  32.3 1.2 %collective-permute-start.6 = (f32[32,128]{1,0:T(8,128)S(1)}, f32[32,128]{1,0:T(8,128)S(1)}, u32[]{:S(2)}, u32[]{:S(2)}) collective-permute-start(f32[32,128]{1,0:T(8,128)S(1)} %get-tuple-element.29), channel_id=1, source_target_pairs={{0,4},{4,0},{8,12},{12,8},{16,20},{20,16},{24,28},{28,24},{32,36},... | collective-permute-start | bytes 49160 | tf_op jit(solution)/shard_map/ppermute | solution.py:300
  35.0 15.5 %collective-permute-start.12 = (f32[64,512]{1,0:T(8,128)S(1)}, f32[64,512]{1,0:T(8,128)S(1)}, u32[]{:S(2)}, u32[]{:S(2)}) collective-permute-start(f32[64,512]{1,0:T(8,128)S(1)} %get-tuple-element.39), channel_id=1, source_target_pairs={{0,4},{4,0},{8,12},{12,8},{16,20},{20,16},{24,28},{28,24},{32,36},... | collective-permute-start | bytes 393224 | tf_op jit(solution)/shard_map/ppermute | solution.py:271
  35.3 15.3 %collective-permute-start.13 = (f32[64,512]{1,0:T(8,128)S(1)}, f32[64,512]{1,0:T(8,128)S(1)}, u32[]{:S(2)}, u32[]{:S(2)}) collective-permute-start(f32[64,512]{1,0:T(8,128)S(1)} %get-tuple-element.40), channel_id=1, source_target_pairs={{0,252},{4,8},{8,4},{12,16},{16,12},{20,24},{24,20},{28,32},{32,28... | collective-permute-start | bytes 393224 | tf_op jit(solution)/shard_map/ppermute | solution.py:267
  39.2 3.7 %collective-permute-start.7 = (f32[32,128]{1,0:T(8,128)S(1)}, f32[32,128]{1,0:T(8,128)S(1)}, u32[]{:S(2)}, u32[]{:S(2)}) collective-permute-start(f32[32,128]{1,0:T(8,128)S(1)} %add.32), channel_id=1, source_target_pairs={{0,8},{4,12},{8,0},{12,4},{16,24},{20,28},{24,16},{28,20},{32,40},... | collective-permute-start | bytes 49160 | tf_op jit(solution)/shard_map/ppermute | solution.py:300
  43.0 7.5 %collective-permute-start.8 = (f32[32,128]{1,0:T(8,128)S(1)}, f32[32,128]{1,0:T(8,128)S(1)}, u32[]{:S(2)}, u32[]{:S(2)}) collective-permute-start(f32[32,128]{1,0:T(8,128)S(1)} %add.33), channel_id=1, source_target_pairs={{0,24},{4,28},{8,16},{12,20},{16,8},{20,12},{24,0},{28,4},{32,56},... | collective-permute-start | bytes 49160 | tf_op jit(solution)/shard_map/ppermute | solution.py:300
  50.5 3.7 %collective-permute-start.9 = (f32[32,128]{1,0:T(8,128)S(1)}, f32[32,128]{1,0:T(8,128)S(1)}, u32[]{:S(2)}, u32[]{:S(2)}) collective-permute-start(f32[32,128]{1,0:T(8,128)S(1)} %add.34), channel_id=1, source_target_pairs={{0,32},{4,36},{8,40},{12,44},{16,48},{20,52},{24,56},{28,60},{32,0... | collective-permute-start | bytes 49160 | tf_op jit(solution)/shard_map/ppermute | solution.py:300
  50.6 5.1 %collective-permute-start.14 = (f32[64,512]{1,0:T(8,128)S(1)}, f32[64,512]{1,0:T(8,128)S(1)}, u32[]{:S(2)}, u32[]{:S(2)}) collective-permute-start(f32[64,512]{1,0:T(8,128)S(1)} %add_add_fusion), channel_id=1, source_target_pairs={{0,1},{1,0},{2,3},{3,2},{4,5},{5,4},{6,7},{7,6},{8,9},{9,8},{10,11... | collective-permute-start | bytes 393224 | tf_op jit(solution)/shard_map/ppermute | solution.py:257
  55.6 15.6 %collective-permute-start.15 = (f32[64,1024]{1,0:T(8,128)S(1)}, f32[64,1024]{1,0:T(8,128)S(1)}, u32[]{:S(2)}, u32[]{:S(2)}) collective-permute-start(f32[64,1024]{1,0:T(8,128)S(1)} %constant_dynamic-update-slice_fusion.refs_0_), channel_id=1, source_target_pairs={{0,3},{1,2},{2,1},{3,0},{4,7},{5,6},{6,5},{7,4},{8,11},{9,10},{10,... | collective-permute-start | bytes 786440 | tf_op jit(solution)/shard_map/ppermute | solution.py:257
  58.7 4.6 %collective-permute-start.10 = (f32[32,128]{1,0:T(8,128)S(1)}, f32[32,128]{1,0:T(8,128)S(1)}, u32[]{:S(2)}, u32[]{:S(2)}) collective-permute-start(f32[32,128]{1,0:T(8,128)S(1)} %add.35), channel_id=1, source_target_pairs={{0,64},{4,68},{8,72},{12,76},{16,80},{20,84},{24,88},{28,92},{32,9... | collective-permute-start | bytes 49160 | tf_op jit(solution)/shard_map/ppermute | solution.py:300
  63.4 5.8 %collective-permute-start.11 = (f32[32,128]{1,0:T(8,128)S(1)}, f32[32,128]{1,0:T(8,128)S(1)}, u32[]{:S(2)}, u32[]{:S(2)}) collective-permute-start(f32[32,128]{1,0:T(8,128)S(1)} %add.36.refs_0_), channel_id=1, source_target_pairs={{0,192},{4,196},{8,200},{12,204},{16,208},{20,212},{24,216},{28,22... | collective-permute-start | bytes 49160 | tf_op jit(solution)/shard_map/ppermute | solution.py:300
  87.3 1.3 %collective-permute-start.16 = (f32[32,128]{1,0:T(8,128)S(1)}, f32[32,128]{1,0:T(8,128)S(1)}, u32[]{:S(2)}, u32[]{:S(2)}) collective-permute-start(f32[32,128]{1,0:T(8,128)S(1)} %sum_z.1), channel_id=1, source_target_pairs={{0,4},{4,0},{8,12},{12,8},{16,20},{20,16},{24,28},{28,24},{32,36},... | collective-permute-start | bytes 49160 | tf_op jit(solution)/shard_map/ppermute | solution.py:271
  88.6 5.2 %collective-permute-start.19 = (f32[32,128]{1,0:T(8,128)S(1)}, f32[32,128]{1,0:T(8,128)S(1)}, u32[]{:S(2)}, u32[]{:S(2)}) collective-permute-start(f32[32,128]{1,0:T(8,128)S(1)} %add.39.refs_0_), channel_id=1, source_target_pairs={{0,24},{4,28},{8,16},{12,20},{16,8},{20,12},{24,0},{28,4},{32,56},... | collective-permute-start | bytes 49160 | tf_op jit(solution)/shard_map/ppermute | solution.py:312
  90.7 4.9 %collective-permute-start.18 = (f32[32,128]{1,0:T(8,128)S(1)}, f32[32,128]{1,0:T(8,128)S(1)}, u32[]{:S(2)}, u32[]{:S(2)}) collective-permute-start(f32[32,128]{1,0:T(8,128)S(1)} %add.39.refs_0_), channel_id=1, source_target_pairs={{0,8},{4,12},{8,0},{12,4},{16,24},{20,28},{24,16},{28,20},{32,40},... | collective-permute-start | bytes 49160 | tf_op jit(solution)/shard_map/ppermute | solution.py:312
  93.8 5.2 %collective-permute-start.17 = (f32[32,128]{1,0:T(8,128)S(1)}, f32[32,128]{1,0:T(8,128)S(1)}, u32[]{:S(2)}, u32[]{:S(2)}) collective-permute-start(f32[32,128]{1,0:T(8,128)S(1)} %add.39.refs_0_), channel_id=1, source_target_pairs={{0,16},{4,20},{8,24},{12,28},{16,0},{20,4},{24,8},{28,12},{32,48},... | collective-permute-start | bytes 49160 | tf_op jit(solution)/shard_map/ppermute | solution.py:312

commit v11 on v9

--- a/solution.py
+++ b/solution.py
@@ -67,20 +67,21 @@
     acc_ref[...] += (one[:k] + two[:k]) + (one[k : 2 * k] + two[k:] + one[2 * k :])
 
 
-def cut_kernel(x_ref, pairs_ref, out_ref, sem):
+def cut_kernel(x_ref, pairs_ref, out_ref, list_ref, sems):
     _, member = place()
-    quarter, width = out_ref.shape[0] - NOTE, out_ref.shape[1]
+    quarter = out_ref.shape[0] - NOTE
     source = x_ref.at[pl.ds(pl.multiple_of(member * quarter, quarter), quarter)]
-    copy = pltpu.make_async_copy(source, out_ref.at[pl.ds(0, quarter)], sem)
-    copy.start()
-    lane = lax.broadcasted_iota(jnp.int32, (NOTE, width), 1)
-    row = lax.broadcasted_iota(jnp.int32, (NOTE, width), 0)
-    note = jnp.zeros((NOTE, width), f32)
-    for slot in range(pairs_ref.shape[1]):
-        for c in range(2):
-            note = jnp.where((lane == slot) & (row == c), pairs_ref[c, slot].astype(f32), note)
-    out_ref[quarter:, :] = note
-    copy.wait()
+    copies = [
+        pltpu.make_async_copy(source, out_ref.at[pl.ds(0, quarter)], sems.at[0]),
+        pltpu.make_async_copy(pairs_ref, list_ref, sems.at[1]),
+    ]
+    for copy in copies:
+        copy.start()
+    copies[1].wait()
+    count, slots = list_ref.shape
+    out_ref[quarter:, :] = jnp.zeros((NOTE, out_ref.shape[1]), f32)
+    out_ref[quarter : quarter + count, :slots] = list_ref[...].astype(f32)
+    copies[0].wait()
 
 
 def tiles_kernel(members, side, x_ref, v_ref, message_ref, pairs_ref, acc_ref, eh_ref, el_ref, xah_ref, xal_ref, chunk=256):
@@ -322,8 +323,9 @@
     part = ((k, quarter), f32)
     kept = [((rows, quarter), bf16)] * 2
     (mine,) = call(
-        cut_kernel, [HB, SM], [((quarter + NOTE, width), f32)], "cut", flops=10**6, scratch=[pltpu.SemaphoreType.DMA])(
-        pltpu.with_memory_space_constraint(embeddings, pltpu.HBM), pairs)
+        cut_kernel, [HB, HB], [((quarter + NOTE, width), f32)], "cut", flops=10**6,
+        scratch=[pltpu.VMEM(pairs.shape, jnp.int32), pltpu.SemaphoreType.DMA((2,))])(
+        *(pltpu.with_memory_space_constraint(a, pltpu.HBM) for a in (embeddings, pairs)))
     cross = crossed(mine)
     sib = swapped(mine)
 

time: 97.1 us -> 96 us (0.989)
  waiting for transfers between devices: 27.2 us -> 24.8 us
  starting transfers between devices: 33.3 us -> 34.8 us
    ppermute x6, waiting for transfers between devices: 15.7 us -> 14.1 us  [pair_sums(): other = lax.ppermute(total, 'rows', [(i, i ^ mask) for i in range(groups)])]
    ppermute x6, starting transfers between devices: 3.92 us -> 5.5 us  [pair_sums(): other = lax.ppermute(total, 'rows', [(i, i ^ mask) for i in range(groups)])]
  transfers between devices with their start and end apart: 22 -> 22, of which waited for: 13 -> 13; matrix products, arithmetic and copies ran while one was open for 0% -> 0% of each run, Pallas kernels for 13% -> 14%
where the time goes in v11:
time: 96 us; the launch traced here: 95.3 us
  starting transfers between devices  34.8 us (36%)
  waiting for transfers between devices  24.8 us (26%)
  Pallas kernels  20.8 us (22%)
  blocking collectives  14.6 us (15%)
    ppermute x3, starting transfers between devices, crossed(): lax.ppermute(x, 'rows', [(i, (i + 2 * (i % 2) - 1) % n) for i in range(n)])  15.2 us
    all_to_all x1, blocking collectives, exchanged(): return lax.all_to_all(x, ('rows', 'sub'), 0, 0, axis_index_groups=sets)  14.6 us
    ppermute x6, waiting for transfers between devices, pair_sums(): other = lax.ppermute(total, 'rows', [(i, i ^ mask) for i in range(groups)])  14.1 us
    pallas_call x3, Pallas kernels, make(): call(functools.partial(tiles_kernel, members, side), [VM, VM, VM, SM], [p...  10.2 us
    ppermute x6, starting transfers between devices, shifted(): return lax.ppermute(x, axis, [(i, (i + by) % n) for i in range(n)])  9.04 us
    ppermute x6, starting transfers between devices, pair_sums(): other = lax.ppermute(total, 'rows', [(i, i ^ mask) for i in range(groups)])  5.5 us
    ppermute x6, waiting for transfers between devices, shifted(): return lax.ppermute(x, axis, [(i, (i + by) % n) for i in range(n)])  4.99 us
    ppermute x3, starting transfers between devices, row_sums(): lax.ppermute(total, 'rows', [(i, i ^ mask) for i in range(groups)])  4.7 us
  transfers between devices with their start and end apart: 22, of which 13 were waited for; matrix products, arithmetic and copies ran while one was open for 0% of the time, Pallas kernels for 14%

profile of v11, /device:TPU:16, one launch (start us, length us, event | category | flops | bytes accessed | tf_op | source)
XLA Modules:
  0.0 95.3 jit_solution(10728212661728427214)
XLA Ops:
  0.0 1.2 %cut.1.message_ref = f32[520,256]{1,0:T(8,128)S(1)} custom-call(f32[2048,256]{1,0:T(8,128)} %x_ref.7, s32[2,8]{1,0:T(2,128)} %bitcast.3), custom_call_target="tpu_custom_call" | custom-call | flops 1000000 | bytes 1048576 | tf_op jit(solution)/shard_map/cut/pallas_call | solution.py:325
  1.2 0.1 collective-permute-start
  1.3 8.2 %collective-permute-start.2 = (f32[520,256]{1,0:T(8,128)S(1)}, f32[520,256]{1,0:T(8,128)S(1)}, u32[]{:S(2)}, u32[]{:S(2)}) collective-permute-start(f32[520,256]{1,0:T(8,128)S(1)} %cut.1.message_ref), channel_id=1, source_target_pairs={{0,252},{4,8},{8,4},{12,16},{16,12},{20,24},{24,20},{28,32},{32,28... | collective-permute-start | bytes 1597448 | tf_op jit(solution)/shard_map/ppermute | solution.py:262
  9.5 0.0 collective-permute-done.message_ref
  9.5 4.2 %sib_tiles.1 = (f32[64,512]{1,0:T(8,128)S(1)}, bf16[2048,512]{1,0:T(8,128)(2,1)S(1)}, bf16[2048,512]{1,0:T(8,128)(2,1)S(1)}) custom-call(f32[2048,256]{1,0:T(8,128)S(1)} %copy-done, f32[64,2048]{1,0:T(8,128)S(1)} %bitcast.7, f32[520,256]{1,0:T(8,128)S(1)} %collective-permute-done.message_ref, s32[2,8]{1,0:T(2,128)S(1)} %bitcast.4), custom_call_target="tpu_custom_call" | custom-call | flops 5000000000 | bytes 1048576 | tf_op jit(solution)/shard_map/sib_tiles/pallas_call | solution.py:333
  13.7 0.1 collective-permute-start.1
  13.8 2.6 %collective-permute-done.2.message_ref = f32[520,256]{1,0:T(8,128)S(1)} collective-permute-done((f32[520,256]{1,0:T(8,128)S(1)}, f32[520,256]{1,0:T(8,128)S(1)}, u32[]{:S(2)}, u32[]{:S(2)}) %collective-permute-start.2) | collective-permute-done | bytes 532512 | tf_op jit(solution)/shard_map/ppermute | solution.py:262
  16.4 1.5 %cross_tiles.1 = (f32[64,512]{1,0:T(8,128)S(1)}, bf16[2048,512]{1,0:T(8,128)(2,1)S(1)}, bf16[2048,512]{1,0:T(8,128)(2,1)S(1)}) custom-call(f32[2048,256]{1,0:T(8,128)S(1)} %copy-done, f32[64,2048]{1,0:T(8,128)S(1)} %bitcast.8, f32[520,256]{1,0:T(8,128)S(1)} %collective-permute-done.2.message_ref, s32[2,8]{1,0:T(2,128)S(1)} %bitcast.5), custom_call_target="tpu_custom_call" | custom-call | flops 5000000000 | bytes 1048576 | tf_op jit(solution)/shard_map/cross_tiles/pallas_call | solution.py:333
  18.0 5.1 %collective-permute-start.3 = (f32[64,512]{1,0:T(8,128)S(1)}, f32[64,512]{1,0:T(8,128)S(1)}, u32[]{:S(2)}, u32[]{:S(2)}) collective-permute-start(f32[64,512]{1,0:T(8,128)S(1)} %get-tuple-element.24), channel_id=1, source_target_pairs={{0,252},{4,8},{8,4},{12,16},{16,12},{20,24},{24,20},{28,32},{32,28... | collective-permute-start | bytes 393224 | tf_op jit(solution)/shard_map/ppermute | solution.py:262
  23.1 4.4 %own_tiles.1 = (f32[64,512]{1,0:T(8,128)S(1)}, bf16[2048,512]{1,0:T(8,128)(2,1)S(1)}, bf16[2048,512]{1,0:T(8,128)(2,1)S(1)}) custom-call(f32[2048,256]{1,0:T(8,128)S(1)} %copy-done, f32[64,2048]{1,0:T(8,128)S(1)} %bitcast.9, f32[520,256]{1,0:T(8,128)S(1)} %cut.1.message_ref, s32[2,8]{1,0:T(2,128)S(1)} %bitcast.6), custom_call_target="tpu_custom_call" | custom-call | flops 5000000000 | bytes 1048576 | tf_op jit(solution)/shard_map/own_tiles/pallas_call | solution.py:333
  27.6 0.5 collective-permute-start.6
  28.1 2.9 %collective-permute-start.5 = (f32[64,512]{1,0:T(8,128)S(1)}, f32[64,512]{1,0:T(8,128)S(1)}, u32[]{:S(2)}, u32[]{:S(2)}) collective-permute-start(f32[64,512]{1,0:T(8,128)S(1)} %add_add_fusion.1.refs_0_), channel_id=1, source_target_pairs={{0,2},{1,3},{2,0},{3,1},{4,6},{5,7},{6,4},{7,5},{8,10},{9,11},{10,... | collective-permute-start | bytes 393224 | tf_op jit(solution)/shard_map/ppermute | solution.py:257
  31.0 0.0 collective-permute-start.4
  31.0 1.6 %collective-permute-done.6.refs_3_ = f32[64,512]{1,0:T(8,128)S(1)} collective-permute-done((f32[64,512]{1,0:T(8,128)S(1)}, f32[64,512]{1,0:T(8,128)S(1)}, u32[]{:S(2)}, u32[]{:S(2)}) %collective-permute-start.6) | collective-permute-done | bytes 131104 | tf_op jit(solution)/shard_map/ppermute | solution.py:257
  32.7 2.0 %collective-permute-done.5.refs_2_ = f32[64,512]{1,0:T(8,128)S(1)} collective-permute-done((f32[64,512]{1,0:T(8,128)S(1)}, f32[64,512]{1,0:T(8,128)S(1)}, u32[]{:S(2)}, u32[]{:S(2)}) %collective-permute-start.5) | collective-permute-done | bytes 131104 | tf_op jit(solution)/shard_map/ppermute | solution.py:257
  34.6 1.4 %collective-permute-done.4.refs_1_ = f32[64,512]{1,0:T(8,128)S(1)} collective-permute-done((f32[64,512]{1,0:T(8,128)S(1)}, f32[64,512]{1,0:T(8,128)S(1)}, u32[]{:S(2)}, u32[]{:S(2)}) %collective-permute-start.4) | collective-permute-done | bytes 131104 | tf_op jit(solution)/shard_map/ppermute | solution.py:257
  36.0 0.6 join.1
  36.7 1.5 %second_far.1 = (f32[64,512]{1,0:T(8,128)S(1)}, f32[64,512]{1,0:T(8,128)S(1)}) custom-call(f32[64,2048]{1,0:T(8,128)S(1)} %get-tuple-element.26.v_ref, bf16[2048,512]{1,0:T(8,128)(2,1)S(1)} %get-tuple-element.29.refs_0_, bf16[2048,512]{1,0:T(8,128)(2,1)S(1)} %get-tuple-element.30.refs_1_, bf16[2048,512]{1,0:T(8,128)(2,1)S(1)} %get-tuple-element.31.refs_2_, ...), custom_call_target="tpu_custom_call" | custom-call | flops 1000000000 | bytes 1048576 | tf_op jit(solution)/shard_map/second_far/pallas_call | solution.py:346
  38.2 0.1 collective-permute-start.13
  38.3 1.9 %collective-permute-start.14 = (f32[64,512]{1,0:T(8,128)S(1)}, f32[64,512]{1,0:T(8,128)S(1)}, u32[]{:S(2)}, u32[]{:S(2)}) collective-permute-start(f32[64,512]{1,0:T(8,128)S(1)} %get-tuple-element.34), channel_id=1, source_target_pairs={{0,252},{4,8},{8,4},{12,16},{16,12},{20,24},{24,20},{28,32},{32,28... | collective-permute-start | bytes 393224 | tf_op jit(solution)/shard_map/ppermute | solution.py:262
  40.2 1.2 %collective-permute-done.7 = f32[32,128]{1,0:T(8,128)S(1)} collective-permute-done((f32[32,128]{1,0:T(8,128)S(1)}, f32[32,128]{1,0:T(8,128)S(1)}, u32[]{:S(2)}, u32[]{:S(2)}) %collective-permute-start.7) | collective-permute-done | bytes 16416 | tf_op jit(solution)/shard_map/ppermute | solution.py:294
  41.4 0.2 collective-permute-start.8
  41.6 3.5 %collective-permute-done.8 = f32[32,128]{1,0:T(8,128)S(1)} collective-permute-done((f32[32,128]{1,0:T(8,128)S(1)}, f32[32,128]{1,0:T(8,128)S(1)}, u32[]{:S(2)}, u32[]{:S(2)}) %collective-permute-start.8) | collective-permute-done | bytes 16416 | tf_op jit(solution)/shard_map/ppermute | solution.py:294
  45.2 0.8 second_own.1
  46.0 4.1 %collective-permute-done.9 = f32[32,128]{1,0:T(8,128)S(1)} collective-permute-done((f32[32,128]{1,0:T(8,128)S(1)}, f32[32,128]{1,0:T(8,128)S(1)}, u32[]{:S(2)}, u32[]{:S(2)}) %collective-permute-start.9) | collective-permute-done | bytes 16416 | tf_op jit(solution)/shard_map/ppermute | solution.py:294
  50.1 0.0 collective-permute-done.13
  50.2 0.6 collective-permute-start.17
  50.8 2.9 %collective-permute-start.16 = (f32[64,512]{1,0:T(8,128)S(1)}, f32[64,512]{1,0:T(8,128)S(1)}, u32[]{:S(2)}, u32[]{:S(2)}) collective-permute-start(f32[64,512]{1,0:T(8,128)S(1)} %add_add_fusion.refs_0_), channel_id=1, source_target_pairs={{0,2},{1,3},{2,0},{3,1},{4,6},{5,7},{6,4},{7,5},{8,10},{9,11},{10,... | collective-permute-start | bytes 393224 | tf_op jit(solution)/shard_map/ppermute | solution.py:257
  53.7 2.1 %collective-permute-start.15 = (f32[64,512]{1,0:T(8,128)S(1)}, f32[64,512]{1,0:T(8,128)S(1)}, u32[]{:S(2)}, u32[]{:S(2)}) collective-permute-start(f32[64,512]{1,0:T(8,128)S(1)} %add_add_fusion.refs_0_), channel_id=1, source_target_pairs={{0,1},{1,2},{2,3},{3,0},{4,5},{5,6},{6,7},{7,4},{8,9},{9,10},{10,1... | collective-permute-start | bytes 393224 | tf_op jit(solution)/shard_map/ppermute | solution.py:257
  55.8 2.6 %collective-permute-start.11 = (f32[32,128]{1,0:T(8,128)S(1)}, f32[32,128]{1,0:T(8,128)S(1)}, u32[]{:S(2)}, u32[]{:S(2)}) collective-permute-start(f32[32,128]{1,0:T(8,128)S(1)} %add.35), channel_id=1, source_target_pairs={{0,64},{4,68},{8,72},{12,76},{16,80},{20,84},{24,88},{28,92},{32,9... | collective-permute-start | bytes 49160 | tf_op jit(solution)/shard_map/ppermute | solution.py:294
  58.4 2.1 %collective-permute-done.11 = f32[32,128]{1,0:T(8,128)S(1)} collective-permute-done((f32[32,128]{1,0:T(8,128)S(1)}, f32[32,128]{1,0:T(8,128)S(1)}, u32[]{:S(2)}, u32[]{:S(2)}) %collective-permute-start.11) | collective-permute-done | bytes 16416 | tf_op jit(solution)/shard_map/ppermute | solution.py:294
  60.5 2.7 %collective-permute-start.12 = (f32[32,128]{1,0:T(8,128)S(1)}, f32[32,128]{1,0:T(8,128)S(1)}, u32[]{:S(2)}, u32[]{:S(2)}) collective-permute-start(f32[32,128]{1,0:T(8,128)S(1)} %add.36.refs_0_), channel_id=1, source_target_pairs={{0,192},{4,196},{8,200},{12,204},{16,208},{20,212},{24,216},{28,22... | collective-permute-start | bytes 49160 | tf_op jit(solution)/shard_map/ppermute | solution.py:294
  63.2 3.1 %collective-permute-done.12.refs_1_ = f32[32,128]{1,0:T(8,128)S(1)} collective-permute-done((f32[32,128]{1,0:T(8,128)S(1)}, f32[32,128]{1,0:T(8,128)S(1)}, u32[]{:S(2)}, u32[]{:S(2)}) %collective-permute-start.12) | collective-permute-done | bytes 16416 | tf_op jit(solution)/shard_map/ppermute | solution.py:294
  66.4 2.0 %factor.1.inv_ref = f32[64,64]{1,0:T(8,128)S(1)} custom-call(f32[32,128]{1,0:T(8,128)S(1)} %add.36.refs_0_, f32[32,128]{1,0:T(8,128)S(1)} %collective-permute-done.12.refs_1_), custom_call_target="tpu_custom_call" | custom-call | flops 1000000000 | bytes 1048576 | tf_op jit(solution)/shard_map/factor/pallas_call | solution.py:351
  68.4 0.0 collective-permute-done.17.refs_3_
  68.4 0.0 collective-permute-done.16.refs_2_
  68.4 0.0 collective-permute-done.15.refs_1_
  68.4 1.1 %image.1 = (f32[64,2048]{1,0:T(8,128)S(1)}, f32[8,32,128]{2,1,0:T(8,128)S(1)}) custom-call(f32[64,64]{1,0:T(8,128)S(1)} %factor.1.inv_ref, f32[64,512]{1,0:T(8,128)S(1)} %add_add_fusion.refs_0_, f32[64,512]{1,0:T(8,128)S(1)} %collective-permute-done.15.refs_1_, f32[64,512]{1,0:T(8,128)S(1)} %collective-permute-done.16.refs_2_, ...), custom_call_target="tpu_custom_call" | custom-call | flops 1000000000 | bytes 1048576 | tf_op jit(solution)/shard_map/image/pallas_call | solution.py:352
  69.5 14.6 %all_to_all.5.gram_ref = f32[8,32,128]{2,1,0:T(8,128)S(1)} all-to-all(f32[8,32,128]{2,1,0:T(8,128)S(1)} %get-tuple-element.36), channel_id=1, replica_groups={{0,32,64,96,128,160,192,224},{1,33,65,97,129,161,193,225},{2,34,66,98,1..., dimensions={0} | all-to-all | bytes 262144 | tf_op jit(solution)/shard_map/all_to_all | solution.py:278
  84.1 0.1 collective-permute-start.18
  84.2 1.2 %collective-permute-done.18 = f32[32,128]{1,0:T(8,128)S(1)} collective-permute-done((f32[32,128]{1,0:T(8,128)S(1)}, f32[32,128]{1,0:T(8,128)S(1)}, u32[]{:S(2)}, u32[]{:S(2)}) %collective-permute-start.18) | collective-permute-done | bytes 16416 | tf_op jit(solution)/shard_map/ppermute | solution.py:266
  85.3 1.3 %collective-permute-start.21 = (f32[32,128]{1,0:T(8,128)S(1)}, f32[32,128]{1,0:T(8,128)S(1)}, u32[]{:S(2)}, u32[]{:S(2)}) collective-permute-start(f32[32,128]{1,0:T(8,128)S(1)} %add.39.refs_0_), channel_id=1, source_target_pairs={{0,24},{4,28},{8,16},{12,20},{16,8},{20,12},{24,0},{28,4},{32,56},... | collective-permute-start | bytes 49160 | tf_op jit(solution)/shard_map/ppermute | solution.py:307
  86.7 0.0 collective-permute-start.20
  86.7 3.4 %collective-permute-start.19 = (f32[32,128]{1,0:T(8,128)S(1)}, f32[32,128]{1,0:T(8,128)S(1)}, u32[]{:S(2)}, u32[]{:S(2)}) collective-permute-start(f32[32,128]{1,0:T(8,128)S(1)} %add.39.refs_0_), channel_id=1, source_target_pairs={{0,16},{4,20},{8,24},{12,28},{16,0},{20,4},{24,8},{28,12},{32,48},... | collective-permute-start | bytes 49160 | tf_op jit(solution)/shard_map/ppermute | solution.py:307
  90.0 0.2 collective-permute-done.21.refs_3_
  90.3 0.1 collective-permute-done.20.refs_2_
  90.4 1.5 %collective-permute-done.19.refs_1_ = f32[32,128]{1,0:T(8,128)S(1)} collective-permute-done((f32[32,128]{1,0:T(8,128)S(1)}, f32[32,128]{1,0:T(8,128)S(1)}, u32[]{:S(2)}, u32[]{:S(2)}) %collective-permute-start.19) | collective-permute-done | bytes 16416 | tf_op jit(solution)/shard_map/ppermute | solution.py:307
  91.9 3.3 %last.1 = f32[64,2048]{1,0:T(8,128)} custom-call(f32[64,2048]{1,0:T(8,128)S(1)} %get-tuple-element.35.image_ref, f32[32,128]{1,0:T(8,128)S(1)} %add.39.refs_0_, f32[32,128]{1,0:T(8,128)S(1)} %collective-permute-done.19.refs_1_, f32[32,128]{1,0:T(8,128)S(1)} %collective-permute-done.20.refs_2_, f32[32,128]{1,0:T(8,128)S(1)} %collective-permute-done.21.refs_3_), custom_call_target="tpu_custom_call" | custom-call | flops 1000000000 | bytes 1048576 | tf_op jit(solution)/shard_map/last/pallas_call | solution.py:354
  (22 shorter events, 0.1 us)
Async XLA Ops:
  0.0 9.5 %copy-start = (f32[2048,256]{1,0:T(8,128)S(1)}, f32[2048,256]{1,0:T(8,128)}, u32[]{:S(2)}) copy-start(f32[2048,256]{1,0:T(8,128)} %x_ref.7) | copy-start | bytes 6291460
  0.0 9.5 %copy-start.1 = (s32[8,2]{0,1:T(2,128)S(1)}, s32[8,2]{0,1:T(2,128)}, u32[]{:S(2)}) copy-start(s32[8,2]{0,1:T(2,128)} %param.5) | copy-start | bytes 196
  0.0 9.5 %copy-start.2 = (f32[2048,64]{0,1:T(8,128)S(1)}, f32[2048,64]{0,1:T(8,128)}, u32[]{:S(2)}) copy-start(f32[2048,64]{0,1:T(8,128)} %param.4) | copy-start | bytes 1572868
  1.2 8.3 %collective-permute-start = (f32[520,256]{1,0:T(8,128)S(1)}, f32[520,256]{1,0:T(8,128)S(1)}, u32[]{:S(2)}, u32[]{:S(2)}) collective-permute-start(f32[520,256]{1,0:T(8,128)S(1)} %cut.1.message_ref), channel_id=1, source_target_pairs={{0,4},{4,0},{8,12},{12,8},{16,20},{20,16},{24,28},{28,24},{32,36},... | collective-permute-start | bytes 1597448 | tf_op jit(solution)/shard_map/ppermute | solution.py:266
  1.3 15.1 %collective-permute-start.2 = (f32[520,256]{1,0:T(8,128)S(1)}, f32[520,256]{1,0:T(8,128)S(1)}, u32[]{:S(2)}, u32[]{:S(2)}) collective-permute-start(f32[520,256]{1,0:T(8,128)S(1)} %cut.1.message_ref), channel_id=1, source_target_pairs={{0,252},{4,8},{8,4},{12,16},{16,12},{20,24},{24,20},{28,32},{32,28... | collective-permute-start | bytes 1597448 | tf_op jit(solution)/shard_map/ppermute | solution.py:262
  13.7 13.8 %collective-permute-start.1 = (f32[64,512]{1,0:T(8,128)S(1)}, f32[64,512]{1,0:T(8,128)S(1)}, u32[]{:S(2)}, u32[]{:S(2)}) collective-permute-start(f32[64,512]{1,0:T(8,128)S(1)} %get-tuple-element.22), channel_id=1, source_target_pairs={{0,4},{4,0},{8,12},{12,8},{16,20},{20,16},{24,28},{28,24},{32,36},... | collective-permute-start | bytes 393224 | tf_op jit(solution)/shard_map/ppermute | solution.py:266
  18.0 9.6 %collective-permute-start.3 = (f32[64,512]{1,0:T(8,128)S(1)}, f32[64,512]{1,0:T(8,128)S(1)}, u32[]{:S(2)}, u32[]{:S(2)}) collective-permute-start(f32[64,512]{1,0:T(8,128)S(1)} %get-tuple-element.24), channel_id=1, source_target_pairs={{0,252},{4,8},{8,4},{12,16},{16,12},{20,24},{24,20},{28,32},{32,28... | collective-permute-start | bytes 393224 | tf_op jit(solution)/shard_map/ppermute | solution.py:262
  27.6 5.0 %collective-permute-start.6 = (f32[64,512]{1,0:T(8,128)S(1)}, f32[64,512]{1,0:T(8,128)S(1)}, u32[]{:S(2)}, u32[]{:S(2)}) collective-permute-start(f32[64,512]{1,0:T(8,128)S(1)} %add_add_fusion.1.refs_0_), channel_id=1, source_target_pairs={{0,3},{1,0},{2,1},{3,2},{4,7},{5,4},{6,5},{7,6},{8,11},{9,8},{10,9... | collective-permute-start | bytes 393224 | tf_op jit(solution)/shard_map/ppermute | solution.py:257
  28.1 6.5 %collective-permute-start.5 = (f32[64,512]{1,0:T(8,128)S(1)}, f32[64,512]{1,0:T(8,128)S(1)}, u32[]{:S(2)}, u32[]{:S(2)}) collective-permute-start(f32[64,512]{1,0:T(8,128)S(1)} %add_add_fusion.1.refs_0_), channel_id=1, source_target_pairs={{0,2},{1,3},{2,0},{3,1},{4,6},{5,7},{6,4},{7,5},{8,10},{9,11},{10,... | collective-permute-start | bytes 393224 | tf_op jit(solution)/shard_map/ppermute | solution.py:257
  31.0 5.0 %collective-permute-start.4 = (f32[64,512]{1,0:T(8,128)S(1)}, f32[64,512]{1,0:T(8,128)S(1)}, u32[]{:S(2)}, u32[]{:S(2)}) collective-permute-start(f32[64,512]{1,0:T(8,128)S(1)} %add_add_fusion.1.refs_0_), channel_id=1, source_target_pairs={{0,1},{1,2},{2,3},{3,0},{4,5},{5,6},{6,7},{7,4},{8,9},{9,10},{10,1... | collective-permute-start | bytes 393224 | tf_op jit(solution)/shard_map/ppermute | solution.py:257
  38.2 11.9 %collective-permute-start.13 = (f32[64,512]{1,0:T(8,128)S(1)}, f32[64,512]{1,0:T(8,128)S(1)}, u32[]{:S(2)}, u32[]{:S(2)}) collective-permute-start(f32[64,512]{1,0:T(8,128)S(1)} %get-tuple-element.33), channel_id=1, source_target_pairs={{0,4},{4,0},{8,12},{12,8},{16,20},{20,16},{24,28},{28,24},{32,36},... | collective-permute-start | bytes 393224 | tf_op jit(solution)/shard_map/ppermute | solution.py:266
  38.3 11.8 %collective-permute-start.14 = (f32[64,512]{1,0:T(8,128)S(1)}, f32[64,512]{1,0:T(8,128)S(1)}, u32[]{:S(2)}, u32[]{:S(2)}) collective-permute-start(f32[64,512]{1,0:T(8,128)S(1)} %get-tuple-element.34), channel_id=1, source_target_pairs={{0,252},{4,8},{8,4},{12,16},{16,12},{20,24},{24,20},{28,32},{32,28... | collective-permute-start | bytes 393224 | tf_op jit(solution)/shard_map/ppermute | solution.py:262
  40.2 1.2 %collective-permute-start.7 = (f32[32,128]{1,0:T(8,128)S(1)}, f32[32,128]{1,0:T(8,128)S(1)}, u32[]{:S(2)}, u32[]{:S(2)}) collective-permute-start(f32[32,128]{1,0:T(8,128)S(1)} %get-tuple-element.25), channel_id=1, source_target_pairs={{0,4},{4,0},{8,12},{12,8},{16,20},{20,16},{24,28},{28,24},{32,36},... | collective-permute-start | bytes 49160 | tf_op jit(solution)/shard_map/ppermute | solution.py:294
  41.4 3.7 %collective-permute-start.8 = (f32[32,128]{1,0:T(8,128)S(1)}, f32[32,128]{1,0:T(8,128)S(1)}, u32[]{:S(2)}, u32[]{:S(2)}) collective-permute-start(f32[32,128]{1,0:T(8,128)S(1)} %add.32), channel_id=1, source_target_pairs={{0,8},{4,12},{8,0},{12,4},{16,24},{20,28},{24,16},{28,20},{32,40},... | collective-permute-start | bytes 49160 | tf_op jit(solution)/shard_map/ppermute | solution.py:294
  45.2 4.9 %collective-permute-start.9 = (f32[32,128]{1,0:T(8,128)S(1)}, f32[32,128]{1,0:T(8,128)S(1)}, u32[]{:S(2)}, u32[]{:S(2)}) collective-permute-start(f32[32,128]{1,0:T(8,128)S(1)} %add.33), channel_id=1, source_target_pairs={{0,24},{4,28},{8,16},{12,20},{16,8},{20,12},{24,0},{28,4},{32,56},... | collective-permute-start | bytes 49160 | tf_op jit(solution)/shard_map/ppermute | solution.py:294
  50.1 5.7 %collective-permute-start.10 = (f32[32,128]{1,0:T(8,128)S(1)}, f32[32,128]{1,0:T(8,128)S(1)}, u32[]{:S(2)}, u32[]{:S(2)}) collective-permute-start(f32[32,128]{1,0:T(8,128)S(1)} %add.34), channel_id=1, source_target_pairs={{0,32},{4,36},{8,40},{12,44},{16,48},{20,52},{24,56},{28,60},{32,0... | collective-permute-start | bytes 49160 | tf_op jit(solution)/shard_map/ppermute | solution.py:294
  50.2 18.2 %collective-permute-start.17 = (f32[64,512]{1,0:T(8,128)S(1)}, f32[64,512]{1,0:T(8,128)S(1)}, u32[]{:S(2)}, u32[]{:S(2)}) collective-permute-start(f32[64,512]{1,0:T(8,128)S(1)} %add_add_fusion.refs_0_), channel_id=1, source_target_pairs={{0,3},{1,0},{2,1},{3,2},{4,7},{5,4},{6,5},{7,6},{8,11},{9,8},{10,9... | collective-permute-start | bytes 393224 | tf_op jit(solution)/shard_map/ppermute | solution.py:257
  50.8 17.5 %collective-permute-start.16 = (f32[64,512]{1,0:T(8,128)S(1)}, f32[64,512]{1,0:T(8,128)S(1)}, u32[]{:S(2)}, u32[]{:S(2)}) collective-permute-start(f32[64,512]{1,0:T(8,128)S(1)} %add_add_fusion.refs_0_), channel_id=1, source_target_pairs={{0,2},{1,3},{2,0},{3,1},{4,6},{5,7},{6,4},{7,5},{8,10},{9,11},{10,... | collective-permute-start | bytes 393224 | tf_op jit(solution)/shard_map/ppermute | solution.py:257
  53.7 14.7 %collective-permute-start.15 = (f32[64,512]{1,0:T(8,128)S(1)}, f32[64,512]{1,0:T(8,128)S(1)}, u32[]{:S(2)}, u32[]{:S(2)}) collective-permute-start(f32[64,512]{1,0:T(8,128)S(1)} %add_add_fusion.refs_0_), channel_id=1, source_target_pairs={{0,1},{1,2},{2,3},{3,0},{4,5},{5,6},{6,7},{7,4},{8,9},{9,10},{10,1... | collective-permute-start | bytes 393224 | tf_op jit(solution)/shard_map/ppermute | solution.py:257
  55.8 4.7 %collective-permute-start.11 = (f32[32,128]{1,0:T(8,128)S(1)}, f32[32,128]{1,0:T(8,128)S(1)}, u32[]{:S(2)}, u32[]{:S(2)}) collective-permute-start(f32[32,128]{1,0:T(8,128)S(1)} %add.35), channel_id=1, source_target_pairs={{0,64},{4,68},{8,72},{12,76},{16,80},{20,84},{24,88},{28,92},{32,9... | collective-permute-start | bytes 49160 | tf_op jit(solution)/shard_map/ppermute | solution.py:294
  60.5 5.8 %collective-permute-start.12 = (f32[32,128]{1,0:T(8,128)S(1)}, f32[32,128]{1,0:T(8,128)S(1)}, u32[]{:S(2)}, u32[]{:S(2)}) collective-permute-start(f32[32,128]{1,0:T(8,128)S(1)} %add.36.refs_0_), channel_id=1, source_target_pairs={{0,192},{4,196},{8,200},{12,204},{16,208},{20,212},{24,216},{28,22... | collective-permute-start | bytes 49160 | tf_op jit(solution)/shard_map/ppermute | solution.py:294
  84.1 1.3 %collective-permute-start.18 = (f32[32,128]{1,0:T(8,128)S(1)}, f32[32,128]{1,0:T(8,128)S(1)}, u32[]{:S(2)}, u32[]{:S(2)}) collective-permute-start(f32[32,128]{1,0:T(8,128)S(1)} %sum_z.1), channel_id=1, source_target_pairs={{0,4},{4,0},{8,12},{12,8},{16,20},{20,16},{24,28},{28,24},{32,36},... | collective-permute-start | bytes 49160 | tf_op jit(solution)/shard_map/ppermute | solution.py:266
  85.3 4.9 %collective-permute-start.21 = (f32[32,128]{1,0:T(8,128)S(1)}, f32[32,128]{1,0:T(8,128)S(1)}, u32[]{:S(2)}, u32[]{:S(2)}) collective-permute-start(f32[32,128]{1,0:T(8,128)S(1)} %add.39.refs_0_), channel_id=1, source_target_pairs={{0,24},{4,28},{8,16},{12,20},{16,8},{20,12},{24,0},{28,4},{32,56},... | collective-permute-start | bytes 49160 | tf_op jit(solution)/shard_map/ppermute | solution.py:307
  86.7 3.7 %collective-permute-start.20 = (f32[32,128]{1,0:T(8,128)S(1)}, f32[32,128]{1,0:T(8,128)S(1)}, u32[]{:S(2)}, u32[]{:S(2)}) collective-permute-start(f32[32,128]{1,0:T(8,128)S(1)} %add.39.refs_0_), channel_id=1, source_target_pairs={{0,8},{4,12},{8,0},{12,4},{16,24},{20,28},{24,16},{28,20},{32,40},... | collective-permute-start | bytes 49160 | tf_op jit(solution)/shard_map/ppermute | solution.py:307
  86.7 5.3 %collective-permute-start.19 = (f32[32,128]{1,0:T(8,128)S(1)}, f32[32,128]{1,0:T(8,128)S(1)}, u32[]{:S(2)}, u32[]{:S(2)}) collective-permute-start(f32[32,128]{1,0:T(8,128)S(1)} %add.39.refs_0_), channel_id=1, source_target_pairs={{0,16},{4,20},{8,24},{12,28},{16,0},{20,4},{24,8},{28,12},{32,48},... | collective-permute-start | bytes 49160 | tf_op jit(solution)/shard_map/ppermute | solution.py:307

commit v12 on v11

--- a/solution.py
+++ b/solution.py
@@ -290,11 +290,11 @@
 
 def pair_sums(total):
     groups = lax.axis_size("rows")
+    sums = [total]
     for mask in MASKS:
-        other = lax.ppermute(total, "rows", [(i, i ^ mask) for i in range(groups)])
-        if mask == MASKS[-1]:
-            return [total, other]
-        total = total + other
+        other = lax.ppermute(sums[-1], "rows", [(i, i ^ mask) for i in range(groups)])
+        sums.append(other if mask == MASKS[-1] else sums[-1] + other)
+    return sums
 
 
 RING = (4, 2, 6)
@@ -343,10 +343,11 @@
     whole = ((k, rows), f32)
     copies = ((groups // NEAR, k // 2, 2 * k), f32)
     image, gram = call(functools.partial(join_kernel, members, total), [VM] * members, [whole, (copies[0][1:], f32)], "join")(*pieces)
-    sib_acc, cross_acc = call(second_kernel, [VM] * 5, [part] * 2, "second_far")(image, *sib_t, *cross_t)
-    (acc2,) = call(second_kernel, [VM] * 3, [part], "second_own")(image, *own_t)
-    terms = pair_sums(gram)
-    acc2 = (acc2 + swapped(sib_acc)) + crossed(cross_acc)
+    sums = pair_sums(gram)
+    terms = sums[-2:]
+    sib_acc, cross_acc = call(second_kernel, [VM] * 5, [part] * 2, "second_far")(tie(image, sums[1]), *sib_t, *cross_t)
+    (acc2,) = call(second_kernel, [VM] * 3, [part], "second_own")(tie(image, sums[2]), *own_t)
+    acc2 = (acc2 + swapped(tie(sib_acc, sums[2]))) + crossed(tie(cross_acc, sums[2]))
     pieces = [acc2] + [shifted(acc2, "sub", s) for s in range(1, members)]
     (inv,) = call(factor_kernel, [VM] * len(terms), [((k, k), f32)], "factor")(*terms)
     image, gram = call(functools.partial(image_kernel, members, total), [VM] * (1 + members), [whole, copies], "image")(inv, *pieces)

time: 96 us -> 93.9 us (0.978); the launches traced: 95.3 us -> 94.2 us
  starting transfers between devices: 34.8 us -> 31.2 us
  waiting for transfers between devices: 24.8 us -> 27.9 us
    ppermute x6, starting transfers between devices: 5.5 us -> 1.87 us  [pair_sums(): lax.ppermute(sums[-1], 'rows', [(i, i ^ mask) for i in range(groups)])]
    ppermute x6, waiting for transfers between devices: 14.1 us -> 17.2 us  [pair_sums(): lax.ppermute(sums[-1], 'rows', [(i, i ^ mask) for i in range(groups)])]
  transfers between devices with their start and end apart: 22 -> 22, of which waited for: 13 -> 12; matrix products, arithmetic and copies ran while one was open for 0% -> 0% of each run, Pallas kernels for 14% -> 15%
where the time goes in v12:
time: 93.9 us; the launch traced here: 94.2 us
  starting transfers between devices  31.2 us (33%)
  waiting for transfers between devices  27.9 us (30%)
  Pallas kernels  20.8 us (22%)
  blocking collectives  14 us (15%)
    ppermute x6, waiting for transfers between devices, pair_sums(): lax.ppermute(sums[-1], 'rows', [(i, i ^ mask) for i in range(groups)])  17.2 us
    ppermute x3, starting transfers between devices, crossed(): lax.ppermute(x, 'rows', [(i, (i + 2 * (i % 2) - 1) % n) for i in range(n)])  15.3 us
    all_to_all x1, blocking collectives, exchanged(): return lax.all_to_all(x, ('rows', 'sub'), 0, 0, axis_index_groups=sets)  14 us
    pallas_call x3, Pallas kernels, make(): call(functools.partial(tiles_kernel, members, side), [VM, VM, VM, SM], [p...  10.2 us
    ppermute x6, starting transfers between devices, shifted(): return lax.ppermute(x, axis, [(i, (i + by) % n) for i in range(n)])  9.04 us
    ppermute x6, waiting for transfers between devices, shifted(): return lax.ppermute(x, axis, [(i, (i + by) % n) for i in range(n)])  4.99 us
    ppermute x3, starting transfers between devices, row_sums(): lax.ppermute(total, 'rows', [(i, i ^ mask) for i in range(groups)])  4.69 us
    pallas_call x1, Pallas kernels, on_device(): call(last_kernel, [VM] * (1 + len(terms)), [whole], 'last')(image, *terms)  3.33 us
  transfers between devices with their start and end apart: 22, of which 12 were waited for; matrix products, arithmetic and copies ran while one was open for 0% of the time, Pallas kernels for 15%

profile of v12, /device:TPU:16, one launch (start us, length us, event | category | flops | bytes accessed | tf_op | source)
XLA Modules:
  0.0 94.2 jit_solution(1477031761010581493)
XLA Ops:
  0.0 1.2 %cut.1.message_ref = f32[520,256]{1,0:T(8,128)S(1)} custom-call(f32[2048,256]{1,0:T(8,128)} %x_ref.7, s32[2,8]{1,0:T(2,128)} %bitcast.3), custom_call_target="tpu_custom_call" | custom-call | flops 1000000 | bytes 1048576 | tf_op jit(solution)/shard_map/cut/pallas_call | solution.py:325
  1.2 0.1 collective-permute-start
  1.3 8.2 %collective-permute-start.2 = (f32[520,256]{1,0:T(8,128)S(1)}, f32[520,256]{1,0:T(8,128)S(1)}, u32[]{:S(2)}, u32[]{:S(2)}) collective-permute-start(f32[520,256]{1,0:T(8,128)S(1)} %cut.1.message_ref), channel_id=1, source_target_pairs={{0,252},{4,8},{8,4},{12,16},{16,12},{20,24},{24,20},{28,32},{32,28... | collective-permute-start | bytes 1597448 | tf_op jit(solution)/shard_map/ppermute | solution.py:262
  9.5 0.0 collective-permute-done.message_ref
  9.5 4.2 %sib_tiles.1 = (f32[64,512]{1,0:T(8,128)S(1)}, bf16[2048,512]{1,0:T(8,128)(2,1)S(1)}, bf16[2048,512]{1,0:T(8,128)(2,1)S(1)}) custom-call(f32[2048,256]{1,0:T(8,128)S(1)} %copy-done, f32[64,2048]{1,0:T(8,128)S(1)} %bitcast.7, f32[520,256]{1,0:T(8,128)S(1)} %collective-permute-done.message_ref, s32[2,8]{1,0:T(2,128)S(1)} %bitcast.4), custom_call_target="tpu_custom_call" | custom-call | flops 5000000000 | bytes 1048576 | tf_op jit(solution)/shard_map/sib_tiles/pallas_call | solution.py:333
  13.7 0.1 collective-permute-start.1
  13.8 2.6 %collective-permute-done.2.message_ref = f32[520,256]{1,0:T(8,128)S(1)} collective-permute-done((f32[520,256]{1,0:T(8,128)S(1)}, f32[520,256]{1,0:T(8,128)S(1)}, u32[]{:S(2)}, u32[]{:S(2)}) %collective-permute-start.2) | collective-permute-done | bytes 532512 | tf_op jit(solution)/shard_map/ppermute | solution.py:262
  16.4 1.5 %cross_tiles.1 = (f32[64,512]{1,0:T(8,128)S(1)}, bf16[2048,512]{1,0:T(8,128)(2,1)S(1)}, bf16[2048,512]{1,0:T(8,128)(2,1)S(1)}) custom-call(f32[2048,256]{1,0:T(8,128)S(1)} %copy-done, f32[64,2048]{1,0:T(8,128)S(1)} %bitcast.8, f32[520,256]{1,0:T(8,128)S(1)} %collective-permute-done.2.message_ref, s32[2,8]{1,0:T(2,128)S(1)} %bitcast.5), custom_call_target="tpu_custom_call" | custom-call | flops 5000000000 | bytes 1048576 | tf_op jit(solution)/shard_map/cross_tiles/pallas_call | solution.py:333
  18.0 5.1 %collective-permute-start.3 = (f32[64,512]{1,0:T(8,128)S(1)}, f32[64,512]{1,0:T(8,128)S(1)}, u32[]{:S(2)}, u32[]{:S(2)}) collective-permute-start(f32[64,512]{1,0:T(8,128)S(1)} %get-tuple-element.28), channel_id=1, source_target_pairs={{0,252},{4,8},{8,4},{12,16},{16,12},{20,24},{24,20},{28,32},{32,28... | collective-permute-start | bytes 393224 | tf_op jit(solution)/shard_map/ppermute | solution.py:262
  23.1 4.4 %own_tiles.1 = (f32[64,512]{1,0:T(8,128)S(1)}, bf16[2048,512]{1,0:T(8,128)(2,1)S(1)}, bf16[2048,512]{1,0:T(8,128)(2,1)S(1)}) custom-call(f32[2048,256]{1,0:T(8,128)S(1)} %copy-done, f32[64,2048]{1,0:T(8,128)S(1)} %bitcast.9, f32[520,256]{1,0:T(8,128)S(1)} %cut.1.message_ref, s32[2,8]{1,0:T(2,128)S(1)} %bitcast.6), custom_call_target="tpu_custom_call" | custom-call | flops 5000000000 | bytes 1048576 | tf_op jit(solution)/shard_map/own_tiles/pallas_call | solution.py:333
  27.6 0.0 collective-permute-done.1
  27.6 0.5 collective-permute-start.6
  28.1 2.9 %collective-permute-start.5 = (f32[64,512]{1,0:T(8,128)S(1)}, f32[64,512]{1,0:T(8,128)S(1)}, u32[]{:S(2)}, u32[]{:S(2)}) collective-permute-start(f32[64,512]{1,0:T(8,128)S(1)} %add_add_fusion.1.refs_0_), channel_id=1, source_target_pairs={{0,2},{1,3},{2,0},{3,1},{4,6},{5,7},{6,4},{7,5},{8,10},{9,11},{10,... | collective-permute-start | bytes 393224 | tf_op jit(solution)/shard_map/ppermute | solution.py:257
  31.0 1.6 %collective-permute-done.6.refs_3_ = f32[64,512]{1,0:T(8,128)S(1)} collective-permute-done((f32[64,512]{1,0:T(8,128)S(1)}, f32[64,512]{1,0:T(8,128)S(1)}, u32[]{:S(2)}, u32[]{:S(2)}) %collective-permute-start.6) | collective-permute-done | bytes 131104 | tf_op jit(solution)/shard_map/ppermute | solution.py:257
  32.7 2.0 %collective-permute-done.5.refs_2_ = f32[64,512]{1,0:T(8,128)S(1)} collective-permute-done((f32[64,512]{1,0:T(8,128)S(1)}, f32[64,512]{1,0:T(8,128)S(1)}, u32[]{:S(2)}, u32[]{:S(2)}) %collective-permute-start.5) | collective-permute-done | bytes 131104 | tf_op jit(solution)/shard_map/ppermute | solution.py:257
  34.6 1.4 %collective-permute-done.4.refs_1_ = f32[64,512]{1,0:T(8,128)S(1)} collective-permute-done((f32[64,512]{1,0:T(8,128)S(1)}, f32[64,512]{1,0:T(8,128)S(1)}, u32[]{:S(2)}, u32[]{:S(2)}) %collective-permute-start.4) | collective-permute-done | bytes 131104 | tf_op jit(solution)/shard_map/ppermute | solution.py:257
  36.0 0.6 join.1
  36.7 0.0 collective-permute-start.7
  36.7 1.2 %collective-permute-done.7 = f32[32,128]{1,0:T(8,128)S(1)} collective-permute-done((f32[32,128]{1,0:T(8,128)S(1)}, f32[32,128]{1,0:T(8,128)S(1)}, u32[]{:S(2)}, u32[]{:S(2)}) %collective-permute-start.7) | collective-permute-done | bytes 16416 | tf_op jit(solution)/shard_map/ppermute | solution.py:295
  37.9 1.5 %second_far.1 = (f32[64,512]{1,0:T(8,128)S(1)}, f32[64,512]{1,0:T(8,128)S(1)}) custom-call(f32[64,2048]{1,0:T(8,128)S(1)} %get-tuple-element.31.v_ref, bf16[2048,512]{1,0:T(8,128)(2,1)S(1)} %get-tuple-element.35.refs_0_, bf16[2048,512]{1,0:T(8,128)(2,1)S(1)} %get-tuple-element.36.refs_1_, bf16[2048,512]{1,0:T(8,128)(2,1)S(1)} %get-tuple-element.37.refs_2_, ...), custom_call_target="tpu_custom_call" | custom-call | flops 1000000000 | bytes 1048576 | tf_op jit(solution)/shard_map/second_far/pallas_call | solution.py:348
  39.4 2.2 %collective-permute-done.8 = f32[32,128]{1,0:T(8,128)S(1)} collective-permute-done((f32[32,128]{1,0:T(8,128)S(1)}, f32[32,128]{1,0:T(8,128)S(1)}, u32[]{:S(2)}, u32[]{:S(2)}) %collective-permute-start.8) | collective-permute-done | bytes 16416 | tf_op jit(solution)/shard_map/ppermute | solution.py:295
  41.6 0.0 collective-permute-start.13
  41.6 2.0 %collective-permute-start.14 = (f32[64,512]{1,0:T(8,128)S(1)}, f32[64,512]{1,0:T(8,128)S(1)}, u32[]{:S(2)}, u32[]{:S(2)}) collective-permute-start(f32[64,512]{1,0:T(8,128)S(1)} %get-tuple-element.42), channel_id=1, source_target_pairs={{0,252},{4,8},{8,4},{12,16},{16,12},{20,24},{24,20},{28,32},{32,28... | collective-permute-start | bytes 393224 | tf_op jit(solution)/shard_map/ppermute | solution.py:262
  43.7 0.8 second_own.1
  44.5 5.1 %collective-permute-done.9 = f32[32,128]{1,0:T(8,128)S(1)} collective-permute-done((f32[32,128]{1,0:T(8,128)S(1)}, f32[32,128]{1,0:T(8,128)S(1)}, u32[]{:S(2)}, u32[]{:S(2)}) %collective-permute-start.9) | collective-permute-done | bytes 16416 | tf_op jit(solution)/shard_map/ppermute | solution.py:295
  49.6 0.0 collective-permute-start.10
  49.6 0.0 collective-permute-done.13
  49.7 0.6 collective-permute-start.17
  50.3 2.9 %collective-permute-start.16 = (f32[64,512]{1,0:T(8,128)S(1)}, f32[64,512]{1,0:T(8,128)S(1)}, u32[]{:S(2)}, u32[]{:S(2)}) collective-permute-start(f32[64,512]{1,0:T(8,128)S(1)} %add_add_fusion.refs_0_), channel_id=1, source_target_pairs={{0,2},{1,3},{2,0},{3,1},{4,6},{5,7},{6,4},{7,5},{8,10},{9,11},{10,... | collective-permute-start | bytes 393224 | tf_op jit(solution)/shard_map/ppermute | solution.py:257
  53.2 2.1 %collective-permute-start.15 = (f32[64,512]{1,0:T(8,128)S(1)}, f32[64,512]{1,0:T(8,128)S(1)}, u32[]{:S(2)}, u32[]{:S(2)}) collective-permute-start(f32[64,512]{1,0:T(8,128)S(1)} %add_add_fusion.refs_0_), channel_id=1, source_target_pairs={{0,1},{1,2},{2,3},{3,0},{4,5},{5,6},{6,7},{7,4},{8,9},{9,10},{10,1... | collective-permute-start | bytes 393224 | tf_op jit(solution)/shard_map/ppermute | solution.py:257
  55.3 0.0 collective-permute-done.10
  55.3 0.1 collective-permute-start.11
  55.4 4.6 %collective-permute-done.11 = f32[32,128]{1,0:T(8,128)S(1)} collective-permute-done((f32[32,128]{1,0:T(8,128)S(1)}, f32[32,128]{1,0:T(8,128)S(1)}, u32[]{:S(2)}, u32[]{:S(2)}) %collective-permute-start.11) | collective-permute-done | bytes 16416 | tf_op jit(solution)/shard_map/ppermute | solution.py:295
  60.0 1.7 %collective-permute-start.12 = (f32[32,128]{1,0:T(8,128)S(1)}, f32[32,128]{1,0:T(8,128)S(1)}, u32[]{:S(2)}, u32[]{:S(2)}) collective-permute-start(f32[32,128]{1,0:T(8,128)S(1)} %add.36.refs_0_), channel_id=1, source_target_pairs={{0,192},{4,196},{8,200},{12,204},{16,208},{20,212},{24,216},{28,22... | collective-permute-start | bytes 49160 | tf_op jit(solution)/shard_map/ppermute | solution.py:295
  61.8 4.1 %collective-permute-done.12.refs_1_ = f32[32,128]{1,0:T(8,128)S(1)} collective-permute-done((f32[32,128]{1,0:T(8,128)S(1)}, f32[32,128]{1,0:T(8,128)S(1)}, u32[]{:S(2)}, u32[]{:S(2)}) %collective-permute-start.12) | collective-permute-done | bytes 16416 | tf_op jit(solution)/shard_map/ppermute | solution.py:295
  65.9 2.0 %factor.1.inv_ref = f32[64,64]{1,0:T(8,128)S(1)} custom-call(f32[32,128]{1,0:T(8,128)S(1)} %add.36.refs_0_, f32[32,128]{1,0:T(8,128)S(1)} %collective-permute-done.12.refs_1_), custom_call_target="tpu_custom_call" | custom-call | flops 1000000000 | bytes 1048576 | tf_op jit(solution)/shard_map/factor/pallas_call | solution.py:352
  67.9 0.0 collective-permute-done.16.refs_2_
  67.9 0.0 collective-permute-done.15.refs_1_
  67.9 1.1 %image.1 = (f32[64,2048]{1,0:T(8,128)S(1)}, f32[8,32,128]{2,1,0:T(8,128)S(1)}) custom-call(f32[64,64]{1,0:T(8,128)S(1)} %factor.1.inv_ref, f32[64,512]{1,0:T(8,128)S(1)} %add_add_fusion.refs_0_, f32[64,512]{1,0:T(8,128)S(1)} %collective-permute-done.15.refs_1_, f32[64,512]{1,0:T(8,128)S(1)} %collective-permute-done.16.refs_2_, ...), custom_call_target="tpu_custom_call" | custom-call | flops 1000000000 | bytes 1048576 | tf_op jit(solution)/shard_map/image/pallas_call | solution.py:353
  69.0 14.0 %all_to_all.5.gram_ref = f32[8,32,128]{2,1,0:T(8,128)S(1)} all-to-all(f32[8,32,128]{2,1,0:T(8,128)S(1)} %get-tuple-element.44), channel_id=1, replica_groups={{0,32,64,96,128,160,192,224},{1,33,65,97,129,161,193,225},{2,34,66,98,1..., dimensions={0} | all-to-all | bytes 262144 | tf_op jit(solution)/shard_map/all_to_all | solution.py:278
  83.0 0.1 collective-permute-start.18
  83.1 1.2 %collective-permute-done.18 = f32[32,128]{1,0:T(8,128)S(1)} collective-permute-done((f32[32,128]{1,0:T(8,128)S(1)}, f32[32,128]{1,0:T(8,128)S(1)}, u32[]{:S(2)}, u32[]{:S(2)}) %collective-permute-start.18) | collective-permute-done | bytes 16416 | tf_op jit(solution)/shard_map/ppermute | solution.py:266
  84.3 0.0 collective-permute-start.21
  84.3 0.1 collective-permute-start.20
  84.4 4.6 %collective-permute-start.19 = (f32[32,128]{1,0:T(8,128)S(1)}, f32[32,128]{1,0:T(8,128)S(1)}, u32[]{:S(2)}, u32[]{:S(2)}) collective-permute-start(f32[32,128]{1,0:T(8,128)S(1)} %add.39.refs_0_), channel_id=1, source_target_pairs={{0,16},{4,20},{8,24},{12,28},{16,0},{20,4},{24,8},{28,12},{32,48},... | collective-permute-start | bytes 49160 | tf_op jit(solution)/shard_map/ppermute | solution.py:307
  89.0 0.2 collective-permute-done.21.refs_3_
  89.2 1.6 %collective-permute-done.19.refs_1_ = f32[32,128]{1,0:T(8,128)S(1)} collective-permute-done((f32[32,128]{1,0:T(8,128)S(1)}, f32[32,128]{1,0:T(8,128)S(1)}, u32[]{:S(2)}, u32[]{:S(2)}) %collective-permute-start.19) | collective-permute-done | bytes 16416 | tf_op jit(solution)/shard_map/ppermute | solution.py:307
  90.8 3.3 %last.1 = f32[64,2048]{1,0:T(8,128)} custom-call(f32[64,2048]{1,0:T(8,128)S(1)} %get-tuple-element.43.image_ref, f32[32,128]{1,0:T(8,128)S(1)} %add.39.refs_0_, f32[32,128]{1,0:T(8,128)S(1)} %collective-permute-done.19.refs_1_, f32[32,128]{1,0:T(8,128)S(1)} %collective-permute-done.20.refs_2_, f32[32,128]{1,0:T(8,128)S(1)} %collective-permute-done.21.refs_3_), custom_call_target="tpu_custom_call" | custom-call | flops 1000000000 | bytes 1048576 | tf_op jit(solution)/shard_map/last/pallas_call | solution.py:355
  (22 shorter events, 0.1 us)
Async XLA Ops:
  0.0 9.5 %copy-start = (f32[2048,256]{1,0:T(8,128)S(1)}, f32[2048,256]{1,0:T(8,128)}, u32[]{:S(2)}) copy-start(f32[2048,256]{1,0:T(8,128)} %x_ref.7) | copy-start | bytes 6291460
  0.0 9.5 %copy-start.1 = (s32[8,2]{0,1:T(2,128)S(1)}, s32[8,2]{0,1:T(2,128)}, u32[]{:S(2)}) copy-start(s32[8,2]{0,1:T(2,128)} %param.5) | copy-start | bytes 196
  0.0 9.5 %copy-start.2 = (f32[2048,64]{0,1:T(8,128)S(1)}, f32[2048,64]{0,1:T(8,128)}, u32[]{:S(2)}) copy-start(f32[2048,64]{0,1:T(8,128)} %param.4) | copy-start | bytes 1572868
  1.2 8.3 %collective-permute-start = (f32[520,256]{1,0:T(8,128)S(1)}, f32[520,256]{1,0:T(8,128)S(1)}, u32[]{:S(2)}, u32[]{:S(2)}) collective-permute-start(f32[520,256]{1,0:T(8,128)S(1)} %cut.1.message_ref), channel_id=1, source_target_pairs={{0,4},{4,0},{8,12},{12,8},{16,20},{20,16},{24,28},{28,24},{32,36},... | collective-permute-start | bytes 1597448 | tf_op jit(solution)/shard_map/ppermute | solution.py:266
  1.3 15.1 %collective-permute-start.2 = (f32[520,256]{1,0:T(8,128)S(1)}, f32[520,256]{1,0:T(8,128)S(1)}, u32[]{:S(2)}, u32[]{:S(2)}) collective-permute-start(f32[520,256]{1,0:T(8,128)S(1)} %cut.1.message_ref), channel_id=1, source_target_pairs={{0,252},{4,8},{8,4},{12,16},{16,12},{20,24},{24,20},{28,32},{32,28... | collective-permute-start | bytes 1597448 | tf_op jit(solution)/shard_map/ppermute | solution.py:262
  13.7 13.8 %collective-permute-start.1 = (f32[64,512]{1,0:T(8,128)S(1)}, f32[64,512]{1,0:T(8,128)S(1)}, u32[]{:S(2)}, u32[]{:S(2)}) collective-permute-start(f32[64,512]{1,0:T(8,128)S(1)} %get-tuple-element.26), channel_id=1, source_target_pairs={{0,4},{4,0},{8,12},{12,8},{16,20},{20,16},{24,28},{28,24},{32,36},... | collective-permute-start | bytes 393224 | tf_op jit(solution)/shard_map/ppermute | solution.py:266
  18.0 9.6 %collective-permute-start.3 = (f32[64,512]{1,0:T(8,128)S(1)}, f32[64,512]{1,0:T(8,128)S(1)}, u32[]{:S(2)}, u32[]{:S(2)}) collective-permute-start(f32[64,512]{1,0:T(8,128)S(1)} %get-tuple-element.28), channel_id=1, source_target_pairs={{0,252},{4,8},{8,4},{12,16},{16,12},{20,24},{24,20},{28,32},{32,28... | collective-permute-start | bytes 393224 | tf_op jit(solution)/shard_map/ppermute | solution.py:262
  27.6 5.0 %collective-permute-start.6 = (f32[64,512]{1,0:T(8,128)S(1)}, f32[64,512]{1,0:T(8,128)S(1)}, u32[]{:S(2)}, u32[]{:S(2)}) collective-permute-start(f32[64,512]{1,0:T(8,128)S(1)} %add_add_fusion.1.refs_0_), channel_id=1, source_target_pairs={{0,3},{1,0},{2,1},{3,2},{4,7},{5,4},{6,5},{7,6},{8,11},{9,8},{10,9... | collective-permute-start | bytes 393224 | tf_op jit(solution)/shard_map/ppermute | solution.py:257
  28.1 6.5 %collective-permute-start.5 = (f32[64,512]{1,0:T(8,128)S(1)}, f32[64,512]{1,0:T(8,128)S(1)}, u32[]{:S(2)}, u32[]{:S(2)}) collective-permute-start(f32[64,512]{1,0:T(8,128)S(1)} %add_add_fusion.1.refs_0_), channel_id=1, source_target_pairs={{0,2},{1,3},{2,0},{3,1},{4,6},{5,7},{6,4},{7,5},{8,10},{9,11},{10,... | collective-permute-start | bytes 393224 | tf_op jit(solution)/shard_map/ppermute | solution.py:257
  31.0 5.0 %collective-permute-start.4 = (f32[64,512]{1,0:T(8,128)S(1)}, f32[64,512]{1,0:T(8,128)S(1)}, u32[]{:S(2)}, u32[]{:S(2)}) collective-permute-start(f32[64,512]{1,0:T(8,128)S(1)} %add_add_fusion.1.refs_0_), channel_id=1, source_target_pairs={{0,1},{1,2},{2,3},{3,0},{4,5},{5,6},{6,7},{7,4},{8,9},{9,10},{10,1... | collective-permute-start | bytes 393224 | tf_op jit(solution)/shard_map/ppermute | solution.py:257
  36.7 1.2 %collective-permute-start.7 = (f32[32,128]{1,0:T(8,128)S(1)}, f32[32,128]{1,0:T(8,128)S(1)}, u32[]{:S(2)}, u32[]{:S(2)}) collective-permute-start(f32[32,128]{1,0:T(8,128)S(1)} %get-tuple-element.29), channel_id=1, source_target_pairs={{0,4},{4,0},{8,12},{12,8},{16,20},{20,16},{24,28},{28,24},{32,36},... | collective-permute-start | bytes 49160 | tf_op jit(solution)/shard_map/ppermute | solution.py:295
  37.9 3.7 %collective-permute-start.8 = (f32[32,128]{1,0:T(8,128)S(1)}, f32[32,128]{1,0:T(8,128)S(1)}, u32[]{:S(2)}, u32[]{:S(2)}) collective-permute-start(f32[32,128]{1,0:T(8,128)S(1)} %add.32), channel_id=1, source_target_pairs={{0,8},{4,12},{8,0},{12,4},{16,24},{20,28},{24,16},{28,20},{32,40},... | collective-permute-start | bytes 49160 | tf_op jit(solution)/shard_map/ppermute | solution.py:295
  41.6 8.0 %collective-permute-start.13 = (f32[64,512]{1,0:T(8,128)S(1)}, f32[64,512]{1,0:T(8,128)S(1)}, u32[]{:S(2)}, u32[]{:S(2)}) collective-permute-start(f32[64,512]{1,0:T(8,128)S(1)} %get-tuple-element.40), channel_id=1, source_target_pairs={{0,4},{4,0},{8,12},{12,8},{16,20},{20,16},{24,28},{28,24},{32,36},... | collective-permute-start | bytes 393224 | tf_op jit(solution)/shard_map/ppermute | solution.py:266
  41.6 8.0 %collective-permute-start.14 = (f32[64,512]{1,0:T(8,128)S(1)}, f32[64,512]{1,0:T(8,128)S(1)}, u32[]{:S(2)}, u32[]{:S(2)}) collective-permute-start(f32[64,512]{1,0:T(8,128)S(1)} %get-tuple-element.42), channel_id=1, source_target_pairs={{0,252},{4,8},{8,4},{12,16},{16,12},{20,24},{24,20},{28,32},{32,28... | collective-permute-start | bytes 393224 | tf_op jit(solution)/shard_map/ppermute | solution.py:262
  43.6 6.0 %collective-permute-start.9 = (f32[32,128]{1,0:T(8,128)S(1)}, f32[32,128]{1,0:T(8,128)S(1)}, u32[]{:S(2)}, u32[]{:S(2)}) collective-permute-start(f32[32,128]{1,0:T(8,128)S(1)} %add.33), channel_id=1, source_target_pairs={{0,24},{4,28},{8,16},{12,20},{16,8},{20,12},{24,0},{28,4},{32,56},... | collective-permute-start | bytes 49160 | tf_op jit(solution)/shard_map/ppermute | solution.py:295
  49.6 5.7 %collective-permute-start.10 = (f32[32,128]{1,0:T(8,128)S(1)}, f32[32,128]{1,0:T(8,128)S(1)}, u32[]{:S(2)}, u32[]{:S(2)}) collective-permute-start(f32[32,128]{1,0:T(8,128)S(1)} %add.34), channel_id=1, source_target_pairs={{0,32},{4,36},{8,40},{12,44},{16,48},{20,52},{24,56},{28,60},{32,0... | collective-permute-start | bytes 49160 | tf_op jit(solution)/shard_map/ppermute | solution.py:295
  49.7 18.2 %collective-permute-start.17 = (f32[64,512]{1,0:T(8,128)S(1)}, f32[64,512]{1,0:T(8,128)S(1)}, u32[]{:S(2)}, u32[]{:S(2)}) collective-permute-start(f32[64,512]{1,0:T(8,128)S(1)} %add_add_fusion.refs_0_), channel_id=1, source_target_pairs={{0,3},{1,0},{2,1},{3,2},{4,7},{5,4},{6,5},{7,6},{8,11},{9,8},{10,9... | collective-permute-start | bytes 393224 | tf_op jit(solution)/shard_map/ppermute | solution.py:257
  50.3 17.5 %collective-permute-start.16 = (f32[64,512]{1,0:T(8,128)S(1)}, f32[64,512]{1,0:T(8,128)S(1)}, u32[]{:S(2)}, u32[]{:S(2)}) collective-permute-start(f32[64,512]{1,0:T(8,128)S(1)} %add_add_fusion.refs_0_), channel_id=1, source_target_pairs={{0,2},{1,3},{2,0},{3,1},{4,6},{5,7},{6,4},{7,5},{8,10},{9,11},{10,... | collective-permute-start | bytes 393224 | tf_op jit(solution)/shard_map/ppermute | solution.py:257
  53.2 14.7 %collective-permute-start.15 = (f32[64,512]{1,0:T(8,128)S(1)}, f32[64,512]{1,0:T(8,128)S(1)}, u32[]{:S(2)}, u32[]{:S(2)}) collective-permute-start(f32[64,512]{1,0:T(8,128)S(1)} %add_add_fusion.refs_0_), channel_id=1, source_target_pairs={{0,1},{1,2},{2,3},{3,0},{4,5},{5,6},{6,7},{7,4},{8,9},{9,10},{10,1... | collective-permute-start | bytes 393224 | tf_op jit(solution)/shard_map/ppermute | solution.py:257
  55.3 4.7 %collective-permute-start.11 = (f32[32,128]{1,0:T(8,128)S(1)}, f32[32,128]{1,0:T(8,128)S(1)}, u32[]{:S(2)}, u32[]{:S(2)}) collective-permute-start(f32[32,128]{1,0:T(8,128)S(1)} %add.35), channel_id=1, source_target_pairs={{0,64},{4,68},{8,72},{12,76},{16,80},{20,84},{24,88},{28,92},{32,9... | collective-permute-start | bytes 49160 | tf_op jit(solution)/shard_map/ppermute | solution.py:295
  60.0 5.8 %collective-permute-start.12 = (f32[32,128]{1,0:T(8,128)S(1)}, f32[32,128]{1,0:T(8,128)S(1)}, u32[]{:S(2)}, u32[]{:S(2)}) collective-permute-start(f32[32,128]{1,0:T(8,128)S(1)} %add.36.refs_0_), channel_id=1, source_target_pairs={{0,192},{4,196},{8,200},{12,204},{16,208},{20,212},{24,216},{28,22... | collective-permute-start | bytes 49160 | tf_op jit(solution)/shard_map/ppermute | solution.py:295
  83.0 1.3 %collective-permute-start.18 = (f32[32,128]{1,0:T(8,128)S(1)}, f32[32,128]{1,0:T(8,128)S(1)}, u32[]{:S(2)}, u32[]{:S(2)}) collective-permute-start(f32[32,128]{1,0:T(8,128)S(1)} %sum_z.1), channel_id=1, source_target_pairs={{0,4},{4,0},{8,12},{12,8},{16,20},{20,16},{24,28},{28,24},{32,36},... | collective-permute-start | bytes 49160 | tf_op jit(solution)/shard_map/ppermute | solution.py:266
  84.3 4.9 %collective-permute-start.21 = (f32[32,128]{1,0:T(8,128)S(1)}, f32[32,128]{1,0:T(8,128)S(1)}, u32[]{:S(2)}, u32[]{:S(2)}) collective-permute-start(f32[32,128]{1,0:T(8,128)S(1)} %add.39.refs_0_), channel_id=1, source_target_pairs={{0,24},{4,28},{8,16},{12,20},{16,8},{20,12},{24,0},{28,4},{32,56},... | collective-permute-start | bytes 49160 | tf_op jit(solution)/shard_map/ppermute | solution.py:307
  84.3 4.9 %collective-permute-start.20 = (f32[32,128]{1,0:T(8,128)S(1)}, f32[32,128]{1,0:T(8,128)S(1)}, u32[]{:S(2)}, u32[]{:S(2)}) collective-permute-start(f32[32,128]{1,0:T(8,128)S(1)} %add.39.refs_0_), channel_id=1, source_target_pairs={{0,8},{4,12},{8,0},{12,4},{16,24},{20,28},{24,16},{28,20},{32,40},... | collective-permute-start | bytes 49160 | tf_op jit(solution)/shard_map/ppermute | solution.py:307
  84.4 6.5 %collective-permute-start.19 = (f32[32,128]{1,0:T(8,128)S(1)}, f32[32,128]{1,0:T(8,128)S(1)}, u32[]{:S(2)}, u32[]{:S(2)}) collective-permute-start(f32[32,128]{1,0:T(8,128)S(1)} %add.39.refs_0_), channel_id=1, source_target_pairs={{0,16},{4,20},{8,24},{12,28},{16,0},{20,4},{24,8},{28,12},{32,48},... | collective-permute-start | bytes 49160 | tf_op jit(solution)/shard_map/ppermute | solution.py:307

commit v13 on v12

--- a/solution.py
+++ b/solution.py
@@ -134,18 +134,13 @@
 def put_gram(gram_ref, image, total):
     gram = gram_sum(*split3(image)) / total
     half = gram.shape[0] // 2
-    packed = jnp.concatenate([gram[:half], gram[half:]], 1)
-    if len(gram_ref.shape) == 2:
-        gram_ref[...] = packed
-        return
-    for n in range(gram_ref.shape[0]):
-        gram_ref[n] = packed
+    gram_ref[...] = jnp.concatenate([gram[:half], gram[half:]], 1)
 
 
 def take_gram(terms):
-    packed = terms[0][...] + terms[1][...]
-    if len(terms) > 2:
-        packed = packed + (terms[2][...] + terms[3][...])
+    packed = terms[0]
+    for term in terms[1:]:
+        packed = packed + term
     k = packed.shape[1] // 2
     return jnp.concatenate([packed[:, :k], packed[:, k:]], 0)
 
@@ -215,7 +210,7 @@
 
 def factor_kernel(*refs):
     inv_ref = refs[-1]
-    inv_ref[...] = factor_inverse(take_gram(refs[:-1]))
+    inv_ref[...] = factor_inverse(take_gram([ref[...] for ref in refs[:-1]]))
 
 
 def exact(a, b):
@@ -229,9 +224,9 @@
     put_gram(gram_ref, image_ref[...], total)
 
 
-def last_kernel(image_ref, *refs):
-    out_ref = refs[-1]
-    out_ref[...] = exact(factor_inverse(take_gram(refs[:-1])), image_ref[...])
+def last_kernel(image_ref, gram_ref, out_ref):
+    gram = take_gram([gram_ref[n] for n in range(gram_ref.shape[0])])
+    out_ref[...] = exact(factor_inverse(gram), image_ref[...])
 
 
 VM = pl.BlockSpec(memory_space=pltpu.VMEM)
@@ -278,11 +273,10 @@
     return lax.all_to_all(x, ("rows", "sub"), 0, 0, axis_index_groups=sets)
 
 
-def sum_kernel(gram_ref, out_ref):
-    packed = gram_ref[0]
-    for n in range(1, gram_ref.shape[0]):
-        packed = packed + gram_ref[n]
-    out_ref[...] = packed
+def spread_kernel(me_ref, opposite_ref, left_ref, right_ref, out_ref):
+    packed = (me_ref[...] + opposite_ref[...]) + (left_ref[...] + right_ref[...])
+    for n in range(out_ref.shape[0]):
+        out_ref[n] = packed
 
 
 MASKS = (1, 2, 6, 8, 16, 48)
@@ -301,10 +295,11 @@
 
 
 def row_sums(gram):
-    (total,) = call(sum_kernel, [VM], [(gram.shape[1:], f32)], "sum_z", flops=10**6)(exchanged(gram, far_sets()))
-    total = total + swapped(total)
     groups = lax.axis_size("rows")
-    return [total] + [lax.ppermute(total, "rows", [(i, i ^ mask) for i in range(groups)]) for mask in RING]
+    total = gram + swapped(gram)
+    terms = [total] + [lax.ppermute(total, "rows", [(i, i ^ mask) for i in range(groups)]) for mask in RING]
+    (spread,) = call(spread_kernel, [VM] * len(terms), [((groups // NEAR, *gram.shape), f32)], "sum_x", flops=10**6)(*terms)
+    return exchanged(spread, far_sets())
 
 
 def tie(x, *others):
@@ -341,8 +336,8 @@
     acc = (acc + swapped(sib_acc)) + crossed(cross_acc)
     pieces = [acc] + [shifted(acc, "sub", s) for s in range(1, members)]
     whole = ((k, rows), f32)
-    copies = ((groups // NEAR, k // 2, 2 * k), f32)
-    image, gram = call(functools.partial(join_kernel, members, total), [VM] * members, [whole, (copies[0][1:], f32)], "join")(*pieces)
+    packed = ((k // 2, 2 * k), f32)
+    image, gram = call(functools.partial(join_kernel, members, total), [VM] * members, [whole, packed], "join")(*pieces)
     sums = pair_sums(gram)
     terms = sums[-2:]
     sib_acc, cross_acc = call(second_kernel, [VM] * 5, [part] * 2, "second_far")(tie(image, sums[1]), *sib_t, *cross_t)
@@ -350,9 +345,8 @@
     acc2 = (acc2 + swapped(tie(sib_acc, sums[2]))) + crossed(tie(cross_acc, sums[2]))
     pieces = [acc2] + [shifted(acc2, "sub", s) for s in range(1, members)]
     (inv,) = call(factor_kernel, [VM] * len(terms), [((k, k), f32)], "factor")(*terms)
-    image, gram = call(functools.partial(image_kernel, members, total), [VM] * (1 + members), [whole, copies], "image")(inv, *pieces)
-    terms = row_sums(gram)
-    (out,) = call(last_kernel, [VM] * (1 + len(terms)), [whole], "last")(image, *terms)
+    image, gram = call(functools.partial(image_kernel, members, total), [VM] * (1 + members), [whole, packed], "image")(inv, *pieces)
+    (out,) = call(last_kernel, [VM, VM], [whole], "last")(image, row_sums(gram))
     return out.T
 
 

time: 93.9 us -> 95 us (1.012)
  blocking collectives: 14 us -> 15 us
    all_to_all x1, blocking collectives: 14 us -> 15 us  [exchanged(): return lax.all_to_all(x, ('rows', 'sub'), 0, 0, axis_index_groups=sets)]
where the time goes in v13:
time: 95 us; the launch traced here: 95.2 us
  starting transfers between devices  31.9 us (34%)
  waiting for transfers between devices  27.1 us (29%)
  Pallas kernels  20.8 us (22%)
  blocking collectives  15 us (16%)
    ppermute x6, waiting for transfers between devices, pair_sums(): lax.ppermute(sums[-1], 'rows', [(i, i ^ mask) for i in range(groups)])  16.5 us
    ppermute x3, starting transfers between devices, crossed(): lax.ppermute(x, 'rows', [(i, (i + 2 * (i % 2) - 1) % n) for i in range(n)])  15.3 us
    all_to_all x1, blocking collectives, exchanged(): return lax.all_to_all(x, ('rows', 'sub'), 0, 0, axis_index_groups=sets)  15 us
    pallas_call x3, Pallas kernels, make(): call(functools.partial(tiles_kernel, members, side), [VM, VM, VM, SM], [p...  10.2 us
    ppermute x6, starting transfers between devices, shifted(): return lax.ppermute(x, axis, [(i, (i + by) % n) for i in range(n)])  9.04 us
    ppermute x6, waiting for transfers between devices, shifted(): return lax.ppermute(x, axis, [(i, (i + by) % n) for i in range(n)])  4.99 us
    ppermute x3, starting transfers between devices, row_sums(): lax.ppermute(total, 'rows', [(i, i ^ mask) for i in range(groups)])  4.69 us
    pallas_call x1, Pallas kernels, on_device(): out, = call(last_kernel, [VM, VM], [whole], 'last')(image, row_sums(gram))  3.34 us
  transfers between devices with their start and end apart: 22, of which 12 were waited for; matrix products, arithmetic and copies ran while one was open for 0% of the time, Pallas kernels for 15%

profile of v13, /device:TPU:16, one launch (start us, length us, event | category | flops | bytes accessed | tf_op | source)
XLA Modules:
  0.0 95.2 jit_solution(17840448247744532775)
XLA Ops:
  0.0 1.2 %cut.1.message_ref = f32[520,256]{1,0:T(8,128)S(1)} custom-call(f32[2048,256]{1,0:T(8,128)} %x_ref.7, s32[2,8]{1,0:T(2,128)} %bitcast.3), custom_call_target="tpu_custom_call" | custom-call | flops 1000000 | bytes 1048576 | tf_op jit(solution)/shard_map/cut/pallas_call | solution.py:320
  1.2 0.1 collective-permute-start
  1.3 8.2 %collective-permute-start.2 = (f32[520,256]{1,0:T(8,128)S(1)}, f32[520,256]{1,0:T(8,128)S(1)}, u32[]{:S(2)}, u32[]{:S(2)}) collective-permute-start(f32[520,256]{1,0:T(8,128)S(1)} %cut.1.message_ref), channel_id=1, source_target_pairs={{0,252},{4,8},{8,4},{12,16},{16,12},{20,24},{24,20},{28,32},{32,28... | collective-permute-start | bytes 1597448 | tf_op jit(solution)/shard_map/ppermute | solution.py:257
  9.5 0.0 collective-permute-done.message_ref
  9.5 4.2 %sib_tiles.1 = (f32[64,512]{1,0:T(8,128)S(1)}, bf16[2048,512]{1,0:T(8,128)(2,1)S(1)}, bf16[2048,512]{1,0:T(8,128)(2,1)S(1)}) custom-call(f32[2048,256]{1,0:T(8,128)S(1)} %copy-done, f32[64,2048]{1,0:T(8,128)S(1)} %bitcast.7, f32[520,256]{1,0:T(8,128)S(1)} %collective-permute-done.message_ref, s32[2,8]{1,0:T(2,128)S(1)} %bitcast.4), custom_call_target="tpu_custom_call" | custom-call | flops 5000000000 | bytes 1048576 | tf_op jit(solution)/shard_map/sib_tiles/pallas_call | solution.py:328
  13.7 0.1 collective-permute-start.1
  13.8 2.6 %collective-permute-done.2.message_ref = f32[520,256]{1,0:T(8,128)S(1)} collective-permute-done((f32[520,256]{1,0:T(8,128)S(1)}, f32[520,256]{1,0:T(8,128)S(1)}, u32[]{:S(2)}, u32[]{:S(2)}) %collective-permute-start.2) | collective-permute-done | bytes 532512 | tf_op jit(solution)/shard_map/ppermute | solution.py:257
  16.4 1.5 %cross_tiles.1 = (f32[64,512]{1,0:T(8,128)S(1)}, bf16[2048,512]{1,0:T(8,128)(2,1)S(1)}, bf16[2048,512]{1,0:T(8,128)(2,1)S(1)}) custom-call(f32[2048,256]{1,0:T(8,128)S(1)} %copy-done, f32[64,2048]{1,0:T(8,128)S(1)} %bitcast.8, f32[520,256]{1,0:T(8,128)S(1)} %collective-permute-done.2.message_ref, s32[2,8]{1,0:T(2,128)S(1)} %bitcast.5), custom_call_target="tpu_custom_call" | custom-call | flops 5000000000 | bytes 1048576 | tf_op jit(solution)/shard_map/cross_tiles/pallas_call | solution.py:328
  18.0 5.1 %collective-permute-start.3 = (f32[64,512]{1,0:T(8,128)S(1)}, f32[64,512]{1,0:T(8,128)S(1)}, u32[]{:S(2)}, u32[]{:S(2)}) collective-permute-start(f32[64,512]{1,0:T(8,128)S(1)} %get-tuple-element.28), channel_id=1, source_target_pairs={{0,252},{4,8},{8,4},{12,16},{16,12},{20,24},{24,20},{28,32},{32,28... | collective-permute-start | bytes 393224 | tf_op jit(solution)/shard_map/ppermute | solution.py:257
  23.1 4.4 %own_tiles.1 = (f32[64,512]{1,0:T(8,128)S(1)}, bf16[2048,512]{1,0:T(8,128)(2,1)S(1)}, bf16[2048,512]{1,0:T(8,128)(2,1)S(1)}) custom-call(f32[2048,256]{1,0:T(8,128)S(1)} %copy-done, f32[64,2048]{1,0:T(8,128)S(1)} %bitcast.9, f32[520,256]{1,0:T(8,128)S(1)} %cut.1.message_ref, s32[2,8]{1,0:T(2,128)S(1)} %bitcast.6), custom_call_target="tpu_custom_call" | custom-call | flops 5000000000 | bytes 1048576 | tf_op jit(solution)/shard_map/own_tiles/pallas_call | solution.py:328
  27.6 0.0 collective-permute-done.1
  27.6 0.0 collective-permute-done.3
  27.6 0.5 collective-permute-start.6
  28.1 2.9 %collective-permute-start.5 = (f32[64,512]{1,0:T(8,128)S(1)}, f32[64,512]{1,0:T(8,128)S(1)}, u32[]{:S(2)}, u32[]{:S(2)}) collective-permute-start(f32[64,512]{1,0:T(8,128)S(1)} %add_add_fusion.1.refs_0_), channel_id=1, source_target_pairs={{0,2},{1,3},{2,0},{3,1},{4,6},{5,7},{6,4},{7,5},{8,10},{9,11},{10,... | collective-permute-start | bytes 393224 | tf_op jit(solution)/shard_map/ppermute | solution.py:252
  31.0 0.0 collective-permute-start.4
  31.0 1.6 %collective-permute-done.6.refs_3_ = f32[64,512]{1,0:T(8,128)S(1)} collective-permute-done((f32[64,512]{1,0:T(8,128)S(1)}, f32[64,512]{1,0:T(8,128)S(1)}, u32[]{:S(2)}, u32[]{:S(2)}) %collective-permute-start.6) | collective-permute-done | bytes 131104 | tf_op jit(solution)/shard_map/ppermute | solution.py:252
  32.7 2.0 %collective-permute-done.5.refs_2_ = f32[64,512]{1,0:T(8,128)S(1)} collective-permute-done((f32[64,512]{1,0:T(8,128)S(1)}, f32[64,512]{1,0:T(8,128)S(1)}, u32[]{:S(2)}, u32[]{:S(2)}) %collective-permute-start.5) | collective-permute-done | bytes 131104 | tf_op jit(solution)/shard_map/ppermute | solution.py:252
  34.6 1.4 %collective-permute-done.4.refs_1_ = f32[64,512]{1,0:T(8,128)S(1)} collective-permute-done((f32[64,512]{1,0:T(8,128)S(1)}, f32[64,512]{1,0:T(8,128)S(1)}, u32[]{:S(2)}, u32[]{:S(2)}) %collective-permute-start.4) | collective-permute-done | bytes 131104 | tf_op jit(solution)/shard_map/ppermute | solution.py:252
  36.0 0.6 join.1
  36.7 0.0 collective-permute-start.7
  36.7 1.2 %collective-permute-done.7 = f32[32,128]{1,0:T(8,128)S(1)} collective-permute-done((f32[32,128]{1,0:T(8,128)S(1)}, f32[32,128]{1,0:T(8,128)S(1)}, u32[]{:S(2)}, u32[]{:S(2)}) %collective-permute-start.7) | collective-permute-done | bytes 16416 | tf_op jit(solution)/shard_map/ppermute | solution.py:289
  37.9 0.0 collective-permute-start.8
  37.9 1.5 %second_far.1 = (f32[64,512]{1,0:T(8,128)S(1)}, f32[64,512]{1,0:T(8,128)S(1)}) custom-call(f32[64,2048]{1,0:T(8,128)S(1)} %get-tuple-element.31.v_ref, bf16[2048,512]{1,0:T(8,128)(2,1)S(1)} %get-tuple-element.35.refs_0_, bf16[2048,512]{1,0:T(8,128)(2,1)S(1)} %get-tuple-element.36.refs_1_, bf16[2048,512]{1,0:T(8,128)(2,1)S(1)} %get-tuple-element.37.refs_2_, ...), custom_call_target="tpu_custom_call" | custom-call | flops 1000000000 | bytes 1048576 | tf_op jit(solution)/shard_map/second_far/pallas_call | solution.py:343
  39.4 2.2 %collective-permute-done.8 = f32[32,128]{1,0:T(8,128)S(1)} collective-permute-done((f32[32,128]{1,0:T(8,128)S(1)}, f32[32,128]{1,0:T(8,128)S(1)}, u32[]{:S(2)}, u32[]{:S(2)}) %collective-permute-start.8) | collective-permute-done | bytes 16416 | tf_op jit(solution)/shard_map/ppermute | solution.py:289
  41.6 2.0 %collective-permute-start.14 = (f32[64,512]{1,0:T(8,128)S(1)}, f32[64,512]{1,0:T(8,128)S(1)}, u32[]{:S(2)}, u32[]{:S(2)}) collective-permute-start(f32[64,512]{1,0:T(8,128)S(1)} %get-tuple-element.42), channel_id=1, source_target_pairs={{0,252},{4,8},{8,4},{12,16},{16,12},{20,24},{24,20},{28,32},{32,28... | collective-permute-start | bytes 393224 | tf_op jit(solution)/shard_map/ppermute | solution.py:257
  43.6 0.0 collective-permute-start.9
  43.7 0.8 second_own.1
  44.5 5.1 %collective-permute-done.9 = f32[32,128]{1,0:T(8,128)S(1)} collective-permute-done((f32[32,128]{1,0:T(8,128)S(1)}, f32[32,128]{1,0:T(8,128)S(1)}, u32[]{:S(2)}, u32[]{:S(2)}) %collective-permute-start.9) | collective-permute-done | bytes 16416 | tf_op jit(solution)/shard_map/ppermute | solution.py:289
  49.6 0.0 collective-permute-done.13
  49.6 0.0 collective-permute-done.14
  49.7 0.6 collective-permute-start.17
  50.3 2.9 %collective-permute-start.16 = (f32[64,512]{1,0:T(8,128)S(1)}, f32[64,512]{1,0:T(8,128)S(1)}, u32[]{:S(2)}, u32[]{:S(2)}) collective-permute-start(f32[64,512]{1,0:T(8,128)S(1)} %add_add_fusion.refs_0_), channel_id=1, source_target_pairs={{0,2},{1,3},{2,0},{3,1},{4,6},{5,7},{6,4},{7,5},{8,10},{9,11},{10,... | collective-permute-start | bytes 393224 | tf_op jit(solution)/shard_map/ppermute | solution.py:252
  53.2 2.1 %collective-permute-start.15 = (f32[64,512]{1,0:T(8,128)S(1)}, f32[64,512]{1,0:T(8,128)S(1)}, u32[]{:S(2)}, u32[]{:S(2)}) collective-permute-start(f32[64,512]{1,0:T(8,128)S(1)} %add_add_fusion.refs_0_), channel_id=1, source_target_pairs={{0,1},{1,2},{2,3},{3,0},{4,5},{5,6},{6,7},{7,4},{8,9},{9,10},{10,1... | collective-permute-start | bytes 393224 | tf_op jit(solution)/shard_map/ppermute | solution.py:252
  55.3 0.1 collective-permute-start.11
  55.4 4.6 %collective-permute-done.11 = f32[32,128]{1,0:T(8,128)S(1)} collective-permute-done((f32[32,128]{1,0:T(8,128)S(1)}, f32[32,128]{1,0:T(8,128)S(1)}, u32[]{:S(2)}, u32[]{:S(2)}) %collective-permute-start.11) | collective-permute-done | bytes 16416 | tf_op jit(solution)/shard_map/ppermute | solution.py:289
  60.0 2.5 %collective-permute-start.12 = (f32[32,128]{1,0:T(8,128)S(1)}, f32[32,128]{1,0:T(8,128)S(1)}, u32[]{:S(2)}, u32[]{:S(2)}) collective-permute-start(f32[32,128]{1,0:T(8,128)S(1)} %add.36.refs_0_), channel_id=1, source_target_pairs={{0,192},{4,196},{8,200},{12,204},{16,208},{20,212},{24,216},{28,22... | collective-permute-start | bytes 49160 | tf_op jit(solution)/shard_map/ppermute | solution.py:289
  62.5 3.3 %collective-permute-done.12.refs_1_ = f32[32,128]{1,0:T(8,128)S(1)} collective-permute-done((f32[32,128]{1,0:T(8,128)S(1)}, f32[32,128]{1,0:T(8,128)S(1)}, u32[]{:S(2)}, u32[]{:S(2)}) %collective-permute-start.12) | collective-permute-done | bytes 16416 | tf_op jit(solution)/shard_map/ppermute | solution.py:289
  65.9 2.0 %factor.1.inv_ref = f32[64,64]{1,0:T(8,128)S(1)} custom-call(f32[32,128]{1,0:T(8,128)S(1)} %add.36.refs_0_, f32[32,128]{1,0:T(8,128)S(1)} %collective-permute-done.12.refs_1_), custom_call_target="tpu_custom_call" | custom-call | flops 1000000000 | bytes 1048576 | tf_op jit(solution)/shard_map/factor/pallas_call | solution.py:347
  67.9 0.0 collective-permute-done.15.refs_1_
  67.9 1.1 %image.1 = (f32[64,2048]{1,0:T(8,128)S(1)}, f32[32,128]{1,0:T(8,128)S(1)}) custom-call(f32[64,64]{1,0:T(8,128)S(1)} %factor.1.inv_ref, f32[64,512]{1,0:T(8,128)S(1)} %add_add_fusion.refs_0_, f32[64,512]{1,0:T(8,128)S(1)} %collective-permute-done.15.refs_1_, f32[64,512]{1,0:T(8,128)S(1)} %collective-permute-done.16.refs_2_, ...), custom_call_target="tpu_custom_call" | custom-call | flops 1000000000 | bytes 1048576 | tf_op jit(solution)/shard_map/image/pallas_call | solution.py:348
  69.0 0.1 collective-permute-start.18
  69.0 1.2 %collective-permute-done.18 = f32[32,128]{1,0:T(8,128)S(1)} collective-permute-done((f32[32,128]{1,0:T(8,128)S(1)}, f32[32,128]{1,0:T(8,128)S(1)}, u32[]{:S(2)}, u32[]{:S(2)}) %collective-permute-start.18) | collective-permute-done | bytes 16416 | tf_op jit(solution)/shard_map/ppermute | solution.py:261
  70.2 0.1 collective-permute-start.20
  70.3 4.6 %collective-permute-start.19 = (f32[32,128]{1,0:T(8,128)S(1)}, f32[32,128]{1,0:T(8,128)S(1)}, u32[]{:S(2)}, u32[]{:S(2)}) collective-permute-start(f32[32,128]{1,0:T(8,128)S(1)} %add.39.me_ref), channel_id=1, source_target_pairs={{0,16},{4,20},{8,24},{12,28},{16,0},{20,4},{24,8},{28,12},{32,48},... | collective-permute-start | bytes 49160 | tf_op jit(solution)/shard_map/ppermute | solution.py:300
  74.9 0.2 collective-permute-done.21.right_ref
  75.2 1.6 %collective-permute-done.19.opposite_ref = f32[32,128]{1,0:T(8,128)S(1)} collective-permute-done((f32[32,128]{1,0:T(8,128)S(1)}, f32[32,128]{1,0:T(8,128)S(1)}, u32[]{:S(2)}, u32[]{:S(2)}) %collective-permute-start.19) | collective-permute-done | bytes 16416 | tf_op jit(solution)/shard_map/ppermute | solution.py:300
  76.8 15.0 %all_to_all.5.gram_ref = f32[8,32,128]{2,1,0:T(8,128)S(1)} all-to-all(f32[8,32,128]{2,1,0:T(8,128)S(1)} %sum_x.1), channel_id=1, replica_groups={{0,32,64,96,128,160,192,224},{1,33,65,97,129,161,193,225},{2,34,66,98,1..., dimensions={0} | all-to-all | bytes 262144 | tf_op jit(solution)/shard_map/all_to_all | solution.py:273
  91.9 3.3 %last.1 = f32[64,2048]{1,0:T(8,128)} custom-call(f32[64,2048]{1,0:T(8,128)S(1)} %get-tuple-element.43.image_ref, f32[8,32,128]{2,1,0:T(8,128)S(1)} %all_to_all.5.gram_ref), custom_call_target="tpu_custom_call" | custom-call | flops 1000000000 | bytes 1048576 | tf_op jit(solution)/shard_map/last/pallas_call | solution.py:349
  (22 shorter events, 0.1 us)
Async XLA Ops:
  0.0 9.5 %copy-start = (f32[2048,256]{1,0:T(8,128)S(1)}, f32[2048,256]{1,0:T(8,128)}, u32[]{:S(2)}) copy-start(f32[2048,256]{1,0:T(8,128)} %x_ref.7) | copy-start | bytes 6291460
  0.0 9.5 %copy-start.1 = (s32[8,2]{0,1:T(2,128)S(1)}, s32[8,2]{0,1:T(2,128)}, u32[]{:S(2)}) copy-start(s32[8,2]{0,1:T(2,128)} %param.5) | copy-start | bytes 196
  0.0 9.5 %copy-start.2 = (f32[2048,64]{0,1:T(8,128)S(1)}, f32[2048,64]{0,1:T(8,128)}, u32[]{:S(2)}) copy-start(f32[2048,64]{0,1:T(8,128)} %param.4) | copy-start | bytes 1572868
  1.2 8.3 %collective-permute-start = (f32[520,256]{1,0:T(8,128)S(1)}, f32[520,256]{1,0:T(8,128)S(1)}, u32[]{:S(2)}, u32[]{:S(2)}) collective-permute-start(f32[520,256]{1,0:T(8,128)S(1)} %cut.1.message_ref), channel_id=1, source_target_pairs={{0,4},{4,0},{8,12},{12,8},{16,20},{20,16},{24,28},{28,24},{32,36},... | collective-permute-start | bytes 1597448 | tf_op jit(solution)/shard_map/ppermute | solution.py:261
  1.3 15.1 %collective-permute-start.2 = (f32[520,256]{1,0:T(8,128)S(1)}, f32[520,256]{1,0:T(8,128)S(1)}, u32[]{:S(2)}, u32[]{:S(2)}) collective-permute-start(f32[520,256]{1,0:T(8,128)S(1)} %cut.1.message_ref), channel_id=1, source_target_pairs={{0,252},{4,8},{8,4},{12,16},{16,12},{20,24},{24,20},{28,32},{32,28... | collective-permute-start | bytes 1597448 | tf_op jit(solution)/shard_map/ppermute | solution.py:257
  13.7 13.8 %collective-permute-start.1 = (f32[64,512]{1,0:T(8,128)S(1)}, f32[64,512]{1,0:T(8,128)S(1)}, u32[]{:S(2)}, u32[]{:S(2)}) collective-permute-start(f32[64,512]{1,0:T(8,128)S(1)} %get-tuple-element.26), channel_id=1, source_target_pairs={{0,4},{4,0},{8,12},{12,8},{16,20},{20,16},{24,28},{28,24},{32,36},... | collective-permute-start | bytes 393224 | tf_op jit(solution)/shard_map/ppermute | solution.py:261
  18.0 9.6 %collective-permute-start.3 = (f32[64,512]{1,0:T(8,128)S(1)}, f32[64,512]{1,0:T(8,128)S(1)}, u32[]{:S(2)}, u32[]{:S(2)}) collective-permute-start(f32[64,512]{1,0:T(8,128)S(1)} %get-tuple-element.28), channel_id=1, source_target_pairs={{0,252},{4,8},{8,4},{12,16},{16,12},{20,24},{24,20},{28,32},{32,28... | collective-permute-start | bytes 393224 | tf_op jit(solution)/shard_map/ppermute | solution.py:257
  27.6 5.0 %collective-permute-start.6 = (f32[64,512]{1,0:T(8,128)S(1)}, f32[64,512]{1,0:T(8,128)S(1)}, u32[]{:S(2)}, u32[]{:S(2)}) collective-permute-start(f32[64,512]{1,0:T(8,128)S(1)} %add_add_fusion.1.refs_0_), channel_id=1, source_target_pairs={{0,3},{1,0},{2,1},{3,2},{4,7},{5,4},{6,5},{7,6},{8,11},{9,8},{10,9... | collective-permute-start | bytes 393224 | tf_op jit(solution)/shard_map/ppermute | solution.py:252
  28.1 6.5 %collective-permute-start.5 = (f32[64,512]{1,0:T(8,128)S(1)}, f32[64,512]{1,0:T(8,128)S(1)}, u32[]{:S(2)}, u32[]{:S(2)}) collective-permute-start(f32[64,512]{1,0:T(8,128)S(1)} %add_add_fusion.1.refs_0_), channel_id=1, source_target_pairs={{0,2},{1,3},{2,0},{3,1},{4,6},{5,7},{6,4},{7,5},{8,10},{9,11},{10,... | collective-permute-start | bytes 393224 | tf_op jit(solution)/shard_map/ppermute | solution.py:252
  31.0 5.0 %collective-permute-start.4 = (f32[64,512]{1,0:T(8,128)S(1)}, f32[64,512]{1,0:T(8,128)S(1)}, u32[]{:S(2)}, u32[]{:S(2)}) collective-permute-start(f32[64,512]{1,0:T(8,128)S(1)} %add_add_fusion.1.refs_0_), channel_id=1, source_target_pairs={{0,1},{1,2},{2,3},{3,0},{4,5},{5,6},{6,7},{7,4},{8,9},{9,10},{10,1... | collective-permute-start | bytes 393224 | tf_op jit(solution)/shard_map/ppermute | solution.py:252
  36.7 1.2 %collective-permute-start.7 = (f32[32,128]{1,0:T(8,128)S(1)}, f32[32,128]{1,0:T(8,128)S(1)}, u32[]{:S(2)}, u32[]{:S(2)}) collective-permute-start(f32[32,128]{1,0:T(8,128)S(1)} %get-tuple-element.29), channel_id=1, source_target_pairs={{0,4},{4,0},{8,12},{12,8},{16,20},{20,16},{24,28},{28,24},{32,36},... | collective-permute-start | bytes 49160 | tf_op jit(solution)/shard_map/ppermute | solution.py:289
  37.9 3.7 %collective-permute-start.8 = (f32[32,128]{1,0:T(8,128)S(1)}, f32[32,128]{1,0:T(8,128)S(1)}, u32[]{:S(2)}, u32[]{:S(2)}) collective-permute-start(f32[32,128]{1,0:T(8,128)S(1)} %add.32), channel_id=1, source_target_pairs={{0,8},{4,12},{8,0},{12,4},{16,24},{20,28},{24,16},{28,20},{32,40},... | collective-permute-start | bytes 49160 | tf_op jit(solution)/shard_map/ppermute | solution.py:289
  41.6 8.0 %collective-permute-start.13 = (f32[64,512]{1,0:T(8,128)S(1)}, f32[64,512]{1,0:T(8,128)S(1)}, u32[]{:S(2)}, u32[]{:S(2)}) collective-permute-start(f32[64,512]{1,0:T(8,128)S(1)} %get-tuple-element.40), channel_id=1, source_target_pairs={{0,4},{4,0},{8,12},{12,8},{16,20},{20,16},{24,28},{28,24},{32,36},... | collective-permute-start | bytes 393224 | tf_op jit(solution)/shard_map/ppermute | solution.py:261
  41.6 8.0 %collective-permute-start.14 = (f32[64,512]{1,0:T(8,128)S(1)}, f32[64,512]{1,0:T(8,128)S(1)}, u32[]{:S(2)}, u32[]{:S(2)}) collective-permute-start(f32[64,512]{1,0:T(8,128)S(1)} %get-tuple-element.42), channel_id=1, source_target_pairs={{0,252},{4,8},{8,4},{12,16},{16,12},{20,24},{24,20},{28,32},{32,28... | collective-permute-start | bytes 393224 | tf_op jit(solution)/shard_map/ppermute | solution.py:257
  43.6 6.0 %collective-permute-start.9 = (f32[32,128]{1,0:T(8,128)S(1)}, f32[32,128]{1,0:T(8,128)S(1)}, u32[]{:S(2)}, u32[]{:S(2)}) collective-permute-start(f32[32,128]{1,0:T(8,128)S(1)} %add.33), channel_id=1, source_target_pairs={{0,24},{4,28},{8,16},{12,20},{16,8},{20,12},{24,0},{28,4},{32,56},... | collective-permute-start | bytes 49160 | tf_op jit(solution)/shard_map/ppermute | solution.py:289
  49.6 5.7 %collective-permute-start.10 = (f32[32,128]{1,0:T(8,128)S(1)}, f32[32,128]{1,0:T(8,128)S(1)}, u32[]{:S(2)}, u32[]{:S(2)}) collective-permute-start(f32[32,128]{1,0:T(8,128)S(1)} %add.34), channel_id=1, source_target_pairs={{0,32},{4,36},{8,40},{12,44},{16,48},{20,52},{24,56},{28,60},{32,0... | collective-permute-start | bytes 49160 | tf_op jit(solution)/shard_map/ppermute | solution.py:289
  49.7 18.2 %collective-permute-start.17 = (f32[64,512]{1,0:T(8,128)S(1)}, f32[64,512]{1,0:T(8,128)S(1)}, u32[]{:S(2)}, u32[]{:S(2)}) collective-permute-start(f32[64,512]{1,0:T(8,128)S(1)} %add_add_fusion.refs_0_), channel_id=1, source_target_pairs={{0,3},{1,0},{2,1},{3,2},{4,7},{5,4},{6,5},{7,6},{8,11},{9,8},{10,9... | collective-permute-start | bytes 393224 | tf_op jit(solution)/shard_map/ppermute | solution.py:252
  50.3 17.5 %collective-permute-start.16 = (f32[64,512]{1,0:T(8,128)S(1)}, f32[64,512]{1,0:T(8,128)S(1)}, u32[]{:S(2)}, u32[]{:S(2)}) collective-permute-start(f32[64,512]{1,0:T(8,128)S(1)} %add_add_fusion.refs_0_), channel_id=1, source_target_pairs={{0,2},{1,3},{2,0},{3,1},{4,6},{5,7},{6,4},{7,5},{8,10},{9,11},{10,... | collective-permute-start | bytes 393224 | tf_op jit(solution)/shard_map/ppermute | solution.py:252
  53.2 14.7 %collective-permute-start.15 = (f32[64,512]{1,0:T(8,128)S(1)}, f32[64,512]{1,0:T(8,128)S(1)}, u32[]{:S(2)}, u32[]{:S(2)}) collective-permute-start(f32[64,512]{1,0:T(8,128)S(1)} %add_add_fusion.refs_0_), channel_id=1, source_target_pairs={{0,1},{1,2},{2,3},{3,0},{4,5},{5,6},{6,7},{7,4},{8,9},{9,10},{10,1... | collective-permute-start | bytes 393224 | tf_op jit(solution)/shard_map/ppermute | solution.py:252
  55.3 4.7 %collective-permute-start.11 = (f32[32,128]{1,0:T(8,128)S(1)}, f32[32,128]{1,0:T(8,128)S(1)}, u32[]{:S(2)}, u32[]{:S(2)}) collective-permute-start(f32[32,128]{1,0:T(8,128)S(1)} %add.35), channel_id=1, source_target_pairs={{0,64},{4,68},{8,72},{12,76},{16,80},{20,84},{24,88},{28,92},{32,9... | collective-permute-start | bytes 49160 | tf_op jit(solution)/shard_map/ppermute | solution.py:289
  60.0 5.8 %collective-permute-start.12 = (f32[32,128]{1,0:T(8,128)S(1)}, f32[32,128]{1,0:T(8,128)S(1)}, u32[]{:S(2)}, u32[]{:S(2)}) collective-permute-start(f32[32,128]{1,0:T(8,128)S(1)} %add.36.refs_0_), channel_id=1, source_target_pairs={{0,192},{4,196},{8,200},{12,204},{16,208},{20,212},{24,216},{28,22... | collective-permute-start | bytes 49160 | tf_op jit(solution)/shard_map/ppermute | solution.py:289
  69.0 1.2 %collective-permute-start.18 = (f32[32,128]{1,0:T(8,128)S(1)}, f32[32,128]{1,0:T(8,128)S(1)}, u32[]{:S(2)}, u32[]{:S(2)}) collective-permute-start(f32[32,128]{1,0:T(8,128)S(1)} %get-tuple-element.44), channel_id=1, source_target_pairs={{0,4},{4,0},{8,12},{12,8},{16,20},{20,16},{24,28},{28,24},{32,36},... | collective-permute-start | bytes 49160 | tf_op jit(solution)/shard_map/ppermute | solution.py:261
  70.2 4.9 %collective-permute-start.21 = (f32[32,128]{1,0:T(8,128)S(1)}, f32[32,128]{1,0:T(8,128)S(1)}, u32[]{:S(2)}, u32[]{:S(2)}) collective-permute-start(f32[32,128]{1,0:T(8,128)S(1)} %add.39.me_ref), channel_id=1, source_target_pairs={{0,24},{4,28},{8,16},{12,20},{16,8},{20,12},{24,0},{28,4},{32,56},... | collective-permute-start | bytes 49160 | tf_op jit(solution)/shard_map/ppermute | solution.py:300
  70.2 4.9 %collective-permute-start.20 = (f32[32,128]{1,0:T(8,128)S(1)}, f32[32,128]{1,0:T(8,128)S(1)}, u32[]{:S(2)}, u32[]{:S(2)}) collective-permute-start(f32[32,128]{1,0:T(8,128)S(1)} %add.39.me_ref), channel_id=1, source_target_pairs={{0,8},{4,12},{8,0},{12,4},{16,24},{20,28},{24,16},{28,20},{32,40},... | collective-permute-start | bytes 49160 | tf_op jit(solution)/shard_map/ppermute | solution.py:300
  70.3 6.5 %collective-permute-start.19 = (f32[32,128]{1,0:T(8,128)S(1)}, f32[32,128]{1,0:T(8,128)S(1)}, u32[]{:S(2)}, u32[]{:S(2)}) collective-permute-start(f32[32,128]{1,0:T(8,128)S(1)} %add.39.me_ref), channel_id=1, source_target_pairs={{0,16},{4,20},{8,24},{12,28},{16,0},{20,4},{24,8},{28,12},{32,48},... | collective-permute-start | bytes 49160 | tf_op jit(solution)/shard_map/ppermute | solution.py:300

commit v14 on v13

--- a/solution.py
+++ b/solution.py
@@ -84,7 +84,7 @@
     copies[0].wait()
 
 
-def tiles_kernel(members, side, x_ref, v_ref, message_ref, pairs_ref, acc_ref, eh_ref, el_ref, xah_ref, xal_ref, chunk=256):
+def tiles_kernel(members, side, blocks, x_ref, v_ref, message_ref, pairs_ref, acc_ref, eh_ref, el_ref, xah_ref, xal_ref, chunk=256):
     quarter = message_ref.shape[0] - NOTE
     block = x_ref.shape[0] // BLK_DEV
     xa = message_ref[:quarter, :]
@@ -92,22 +92,23 @@
     na = lax.dot_general(ones, xa * xa, NT, precision=lax.Precision.HIGHEST, preferred_element_type=f32)[0:1, :] * SCALE
     xah_ref[...], xal_ref[...] = split2(xa * (2.0 * SCALE))
     acc_ref[...] = jnp.zeros_like(acc_ref)
-    for j in range(BLK_DEV):
+    for i, j in enumerate(blocks):
         hit = want(pairs_ref, message_ref.at[quarter:], members, side, j)
-        all_rows = pl.ds(j * block, block)
+        all_rows = pl.ds(i * block, block)
+        v_rows = pl.ds(j * block, block)
 
         @pl.when(hit)
         def _():
             xah, xal = xah_ref[...], xal_ref[...]
             for c in range(block // chunk):
-                here = pl.ds(j * block + c * chunk, chunk)
-                x = x_ref[here, :]
+                here = pl.ds(i * block + c * chunk, chunk)
+                x = x_ref[pl.ds(j * block + c * chunk, chunk), :]
                 nb = jnp.sum(x * x, axis=1, keepdims=True) * SCALE
                 xh, xl = split2(x)
                 d = dot(xh, xah, NT) + (dot(xh, xal, NT) + dot(xl, xah, NT))
                 e = jnp.exp2(jnp.minimum(d - nb - na, 0.0))
                 eh_ref[here, :], el_ref[here, :] = split2(e)
-            add_product(acc_ref, v_ref[:, all_rows], eh_ref[all_rows, :], el_ref[all_rows, :])
+            add_product(acc_ref, v_ref[:, v_rows], eh_ref[all_rows, :], el_ref[all_rows, :])
 
         @pl.when(jnp.logical_not(hit))
         def _():
@@ -160,6 +161,14 @@
         for j in range(BLK_DEV):
             here = pl.ds(j * block, block)
             add_product(out_ref, v_ref[:, here], kept[2 * i][here, :], kept[2 * i + 1][here, :])
+
+
+def second_own_kernel(v_ref, *refs):
+    kept, out_ref = refs[:-1], refs[-1]
+    out_ref[...] = jnp.zeros_like(out_ref)
+    block = kept[0].shape[0]
+    for j in range(len(kept) // 2):
+        add_product(out_ref, v_ref[:, pl.ds(j * block, block)], kept[2 * j][...], kept[2 * j + 1][...])
 
 
 def factor_inverse(gram, w=8):
@@ -316,7 +325,6 @@
     vt = start_vectors.T
     pairs = pairs.T
     part = ((k, quarter), f32)
-    kept = [((rows, quarter), bf16)] * 2
     (mine,) = call(
         cut_kernel, [HB, HB], [((quarter + NOTE, width), f32)], "cut", flops=10**6,
         scratch=[pltpu.VMEM(pairs.shape, jnp.int32), pltpu.SemaphoreType.DMA((2,))])(
@@ -324,15 +332,21 @@
     cross = crossed(mine)
     sib = swapped(mine)
 
-    def make(side, message, name):
+    every = tuple(range(BLK_DEV))
+
+    def make(side, message, name, blocks=every):
+        kept = [((rows * len(blocks) // BLK_DEV, quarter), bf16)] * 2
         acc, *t = call(
-            functools.partial(tiles_kernel, members, side), [VM, VM, VM, SM], [part] + kept, name, flops=5 * 10**9,
+            functools.partial(tiles_kernel, members, side, blocks), [VM, VM, VM, SM], [part] + kept, name, flops=5 * 10**9,
             scratch=[pltpu.VMEM((quarter, width), bf16)] * 2)(embeddings, vt, message, pairs)
         return acc, t
 
-    acc, own_t = make(OWN, mine, "own_tiles")
     sib_acc, sib_t = make(SIB, sib, "sib_tiles")
-    cross_acc, cross_t = make(CROSS, tie(cross, sib_acc), "cross_tiles")
+    acc, own_t = make(OWN, tie(mine, sib_acc), "own_tiles", every[:1])
+    cross_acc, cross_t = make(CROSS, tie(cross, acc), "cross_tiles")
+    more, t = make(OWN, mine, "own_tiles", every[1:])
+    acc = acc + more
+    own_t += t
     acc = (acc + swapped(sib_acc)) + crossed(cross_acc)
     pieces = [acc] + [shifted(acc, "sub", s) for s in range(1, members)]
     whole = ((k, rows), f32)
@@ -341,7 +355,7 @@
     sums = pair_sums(gram)
     terms = sums[-2:]
     sib_acc, cross_acc = call(second_kernel, [VM] * 5, [part] * 2, "second_far")(tie(image, sums[1]), *sib_t, *cross_t)
-    (acc2,) = call(second_kernel, [VM] * 3, [part], "second_own")(tie(image, sums[2]), *own_t)
+    (acc2,) = call(second_own_kernel, [VM] * 5, [part], "second_own")(tie(image, sums[2]), *own_t)
     acc2 = (acc2 + swapped(tie(sib_acc, sums[2]))) + crossed(tie(cross_acc, sums[2]))
     pieces = [acc2] + [shifted(acc2, "sub", s) for s in range(1, members)]
     (inv,) = call(factor_kernel, [VM] * len(terms), [((k, k), f32)], "factor")(*terms)

time: 95 us -> 95.7 us (level)
  waiting for transfers between devices: 27.1 us -> 22.8 us
  starting transfers between devices: 31.9 us -> 34.3 us
  blocking collectives: 15 us -> 16.1 us
  Pallas kernels: 20.8 us -> 21.8 us
    ppermute x3, waiting for transfers between devices: 2.6 us -> 0.01 us  [crossed(): lax.ppermute(x, 'rows', [(i, (i + 2 * (i % 2) - 1) % n) for i in range(n)])]
    ppermute x6, waiting for transfers between devices: 16.5 us -> 14 us  [pair_sums(): lax.ppermute(sums[-1], 'rows', [(i, i ^ mask) for i in range(groups)])]
    ppermute x6, starting transfers between devices: 2.66 us -> 4.13 us  [pair_sums(): lax.ppermute(sums[-1], 'rows', [(i, i ^ mask) for i in range(groups)])]
    all_to_all x1, blocking collectives: 15 us -> 16.1 us  [exchanged(): return lax.all_to_all(x, ('rows', 'sub'), 0, 0, axis_index_groups=sets)]
    pallas_call x4 -> x5, Pallas kernels: 11 us -> 12 us  [the longest x4 11.2 us: make(): call(functools.partial(tiles_kernel, members, side, blocks), [VM, VM, VM,...]
  transfers between devices with their start and end apart: 22 -> 22, of which waited for: 12 -> 11; matrix products, arithmetic and copies ran while one was open for 0% -> 0% of each run, Pallas kernels for 15% -> 16%
where the time goes in v14:
time: 95.7 us; the launch traced here: 95.2 us
  starting transfers between devices  34.3 us (36%)
  waiting for transfers between devices  22.8 us (24%)
  Pallas kernels  21.8 us (23%)
  blocking collectives  16.1 us (17%)
    ppermute x3, starting transfers between devices, crossed(): lax.ppermute(x, 'rows', [(i, (i + 2 * (i % 2) - 1) % n) for i in range(n)])  16.2 us
    all_to_all x1, blocking collectives, exchanged(): return lax.all_to_all(x, ('rows', 'sub'), 0, 0, axis_index_groups=sets)  16.1 us
    ppermute x6, waiting for transfers between devices, pair_sums(): lax.ppermute(sums[-1], 'rows', [(i, i ^ mask) for i in range(groups)])  14 us
    pallas_call x4, Pallas kernels, make(): call(functools.partial(tiles_kernel, members, side, blocks), [VM, VM, VM,...  11.2 us
    ppermute x6, starting transfers between devices, shifted(): return lax.ppermute(x, axis, [(i, (i + by) % n) for i in range(n)])  8.98 us
    ppermute x6, waiting for transfers between devices, shifted(): return lax.ppermute(x, axis, [(i, (i + by) % n) for i in range(n)])  5.69 us
    ppermute x3, starting transfers between devices, row_sums(): lax.ppermute(total, 'rows', [(i, i ^ mask) for i in range(groups)])  4.7 us
    ppermute x6, starting transfers between devices, pair_sums(): lax.ppermute(sums[-1], 'rows', [(i, i ^ mask) for i in range(groups)])  4.13 us
  transfers between devices with their start and end apart: 22, of which 11 were waited for; matrix products, arithmetic and copies ran while one was open for 0% of the time, Pallas kernels for 16%

profile of v14, /device:TPU:16, one launch (start us, length us, event | category | flops | bytes accessed | tf_op | source)
XLA Modules:
  0.0 95.2 jit_solution(1194381512889616472)
XLA Ops:
  0.0 1.2 %cut.1.message_ref = f32[520,256]{1,0:T(8,128)S(1)} custom-call(f32[2048,256]{1,0:T(8,128)} %x_ref.9, s32[2,8]{1,0:T(2,128)} %bitcast.3), custom_call_target="tpu_custom_call" | custom-call | flops 1000000 | bytes 1048576 | tf_op jit(solution)/shard_map/cut/pallas_call | solution.py:328
  1.2 0.1 collective-permute-start
  1.3 8.2 %collective-permute-start.2 = (f32[520,256]{1,0:T(8,128)S(1)}, f32[520,256]{1,0:T(8,128)S(1)}, u32[]{:S(2)}, u32[]{:S(2)}) collective-permute-start(f32[520,256]{1,0:T(8,128)S(1)} %cut.1.message_ref), channel_id=1, source_target_pairs={{0,252},{4,8},{8,4},{12,16},{16,12},{20,24},{24,20},{28,32},{32,28... | collective-permute-start | bytes 1597448 | tf_op jit(solution)/shard_map/ppermute | solution.py:266
  9.5 0.0 collective-permute-done.message_ref
  9.5 4.2 %sib_tiles.1 = (f32[64,512]{1,0:T(8,128)S(1)}, bf16[2048,512]{1,0:T(8,128)(2,1)S(1)}, bf16[2048,512]{1,0:T(8,128)(2,1)S(1)}) custom-call(f32[2048,256]{1,0:T(8,128)S(1)} %copy-done, f32[64,2048]{1,0:T(8,128)S(1)} %bitcast.8, f32[520,256]{1,0:T(8,128)S(1)} %collective-permute-done.message_ref, s32[2,8]{1,0:T(2,128)S(1)} %bitcast.4), custom_call_target="tpu_custom_call" | custom-call | flops 5000000000 | bytes 1048576 | tf_op jit(solution)/shard_map/sib_tiles/pallas_call | solution.py:339
  13.7 0.1 collective-permute-start.1
  13.8 2.6 %own_tiles.2 = (f32[64,512]{1,0:T(8,128)S(1)}, bf16[1024,512]{1,0:T(8,128)(2,1)S(1)}, bf16[1024,512]{1,0:T(8,128)(2,1)S(1)}) custom-call(f32[2048,256]{1,0:T(8,128)S(1)} %copy-done, f32[64,2048]{1,0:T(8,128)S(1)} %bitcast.9, f32[520,256]{1,0:T(8,128)S(1)} %cut.1.message_ref, s32[2,8]{1,0:T(2,128)S(1)} %bitcast.5), custom_call_target="tpu_custom_call" | custom-call | flops 5000000000 | bytes 1048576 | tf_op jit(solution)/shard_map/own_tiles/pallas_call | solution.py:339
  16.5 0.0 collective-permute-done.2.message_ref
  16.5 1.5 %cross_tiles.1 = (f32[64,512]{1,0:T(8,128)S(1)}, bf16[2048,512]{1,0:T(8,128)(2,1)S(1)}, bf16[2048,512]{1,0:T(8,128)(2,1)S(1)}) custom-call(f32[2048,256]{1,0:T(8,128)S(1)} %copy-done, f32[64,2048]{1,0:T(8,128)S(1)} %bitcast.10, f32[520,256]{1,0:T(8,128)S(1)} %collective-permute-done.2.message_ref, s32[2,8]{1,0:T(2,128)S(1)} %bitcast.6), custom_call_target="tpu_custom_call" | custom-call | flops 5000000000 | bytes 1048576 | tf_op jit(solution)/shard_map/cross_tiles/pallas_call | solution.py:339
  18.1 5.1 %collective-permute-start.3 = (f32[64,512]{1,0:T(8,128)S(1)}, f32[64,512]{1,0:T(8,128)S(1)}, u32[]{:S(2)}, u32[]{:S(2)}) collective-permute-start(f32[64,512]{1,0:T(8,128)S(1)} %get-tuple-element.34), channel_id=1, source_target_pairs={{0,252},{4,8},{8,4},{12,16},{16,12},{20,24},{24,20},{28,32},{32,28... | collective-permute-start | bytes 393224 | tf_op jit(solution)/shard_map/ppermute | solution.py:266
  23.1 2.7 %own_tiles.3 = (f32[64,512]{1,0:T(8,128)S(1)}, bf16[1024,512]{1,0:T(8,128)(2,1)S(1)}, bf16[1024,512]{1,0:T(8,128)(2,1)S(1)}) custom-call(f32[2048,256]{1,0:T(8,128)S(1)} %copy-done, f32[64,2048]{1,0:T(8,128)S(1)} %bitcast.11, f32[520,256]{1,0:T(8,128)S(1)} %cut.1.message_ref, s32[2,8]{1,0:T(2,128)S(1)} %bitcast.7), custom_call_target="tpu_custom_call" | custom-call | flops 5000000000 | bytes 1048576 | tf_op jit(solution)/shard_map/own_tiles/pallas_call | solution.py:339
  25.9 0.0 collective-permute-done.1
  25.9 0.0 collective-permute-done.3
  26.0 0.5 collective-permute-start.6
  26.5 2.9 %collective-permute-start.5 = (f32[64,512]{1,0:T(8,128)S(1)}, f32[64,512]{1,0:T(8,128)S(1)}, u32[]{:S(2)}, u32[]{:S(2)}) collective-permute-start(f32[64,512]{1,0:T(8,128)S(1)} %add_add_fusion.1.refs_0_), channel_id=1, source_target_pairs={{0,2},{1,3},{2,0},{3,1},{4,6},{5,7},{6,4},{7,5},{8,10},{9,11},{10,... | collective-permute-start | bytes 393224 | tf_op jit(solution)/shard_map/ppermute | solution.py:261
  29.4 2.8 %collective-permute-done.6.refs_3_ = f32[64,512]{1,0:T(8,128)S(1)} collective-permute-done((f32[64,512]{1,0:T(8,128)S(1)}, f32[64,512]{1,0:T(8,128)S(1)}, u32[]{:S(2)}, u32[]{:S(2)}) %collective-permute-start.6) | collective-permute-done | bytes 131104 | tf_op jit(solution)/shard_map/ppermute | solution.py:261
  32.2 2.2 %collective-permute-done.5.refs_2_ = f32[64,512]{1,0:T(8,128)S(1)} collective-permute-done((f32[64,512]{1,0:T(8,128)S(1)}, f32[64,512]{1,0:T(8,128)S(1)}, u32[]{:S(2)}, u32[]{:S(2)}) %collective-permute-start.5) | collective-permute-done | bytes 131104 | tf_op jit(solution)/shard_map/ppermute | solution.py:261
  34.4 0.7 collective-permute-done.4.refs_1_
  35.1 0.6 join.1
  35.7 0.0 collective-permute-start.7
  35.8 1.2 %collective-permute-done.7 = f32[32,128]{1,0:T(8,128)S(1)} collective-permute-done((f32[32,128]{1,0:T(8,128)S(1)}, f32[32,128]{1,0:T(8,128)S(1)}, u32[]{:S(2)}, u32[]{:S(2)}) %collective-permute-start.7) | collective-permute-done | bytes 16416 | tf_op jit(solution)/shard_map/ppermute | solution.py:298
  36.9 0.0 collective-permute-start.8
  36.9 1.5 %second_far.1 = (f32[64,512]{1,0:T(8,128)S(1)}, f32[64,512]{1,0:T(8,128)S(1)}) custom-call(f32[64,2048]{1,0:T(8,128)S(1)} %get-tuple-element.37.v_ref, bf16[2048,512]{1,0:T(8,128)(2,1)S(1)} %get-tuple-element.43.refs_0_, bf16[2048,512]{1,0:T(8,128)(2,1)S(1)} %get-tuple-element.44.refs_1_, bf16[2048,512]{1,0:T(8,128)(2,1)S(1)} %get-tuple-element.45.refs_2_, ...), custom_call_target="tpu_custom_call" | custom-call | flops 1000000000 | bytes 1048576 | tf_op jit(solution)/shard_map/second_far/pallas_call | solution.py:357
  38.5 2.2 %collective-permute-done.8 = f32[32,128]{1,0:T(8,128)S(1)} collective-permute-done((f32[32,128]{1,0:T(8,128)S(1)}, f32[32,128]{1,0:T(8,128)S(1)}, u32[]{:S(2)}, u32[]{:S(2)}) %collective-permute-start.8) | collective-permute-done | bytes 16416 | tf_op jit(solution)/shard_map/ppermute | solution.py:298
  40.7 3.0 %collective-permute-start.14 = (f32[64,512]{1,0:T(8,128)S(1)}, f32[64,512]{1,0:T(8,128)S(1)}, u32[]{:S(2)}, u32[]{:S(2)}) collective-permute-start(f32[64,512]{1,0:T(8,128)S(1)} %get-tuple-element.50), channel_id=1, source_target_pairs={{0,252},{4,8},{8,4},{12,16},{16,12},{20,24},{24,20},{28,32},{32,28... | collective-permute-start | bytes 393224 | tf_op jit(solution)/shard_map/ppermute | solution.py:266
  43.7 0.0 collective-permute-start.9
  43.7 0.9 second_own.1
  44.5 4.1 %collective-permute-done.9 = f32[32,128]{1,0:T(8,128)S(1)} collective-permute-done((f32[32,128]{1,0:T(8,128)S(1)}, f32[32,128]{1,0:T(8,128)S(1)}, u32[]{:S(2)}, u32[]{:S(2)}) %collective-permute-start.9) | collective-permute-done | bytes 16416 | tf_op jit(solution)/shard_map/ppermute | solution.py:298
  48.7 0.0 collective-permute-start.10
  48.7 0.0 collective-permute-done.14
  48.7 1.6 %collective-permute-start.17 = (f32[64,512]{1,0:T(8,128)S(1)}, f32[64,512]{1,0:T(8,128)S(1)}, u32[]{:S(2)}, u32[]{:S(2)}) collective-permute-start(f32[64,512]{1,0:T(8,128)S(1)} %add_add_fusion.refs_0_), channel_id=1, source_target_pairs={{0,3},{1,0},{2,1},{3,2},{4,7},{5,4},{6,5},{7,6},{8,11},{9,8},{10,9... | collective-permute-start | bytes 393224 | tf_op jit(solution)/shard_map/ppermute | solution.py:261
  50.3 1.9 %collective-permute-start.16 = (f32[64,512]{1,0:T(8,128)S(1)}, f32[64,512]{1,0:T(8,128)S(1)}, u32[]{:S(2)}, u32[]{:S(2)}) collective-permute-start(f32[64,512]{1,0:T(8,128)S(1)} %add_add_fusion.refs_0_), channel_id=1, source_target_pairs={{0,2},{1,3},{2,0},{3,1},{4,6},{5,7},{6,4},{7,5},{8,10},{9,11},{10,... | collective-permute-start | bytes 393224 | tf_op jit(solution)/shard_map/ppermute | solution.py:261
  52.2 2.1 %collective-permute-start.15 = (f32[64,512]{1,0:T(8,128)S(1)}, f32[64,512]{1,0:T(8,128)S(1)}, u32[]{:S(2)}, u32[]{:S(2)}) collective-permute-start(f32[64,512]{1,0:T(8,128)S(1)} %add_add_fusion.refs_0_), channel_id=1, source_target_pairs={{0,1},{1,2},{2,3},{3,0},{4,5},{5,6},{6,7},{7,4},{8,9},{9,10},{10,1... | collective-permute-start | bytes 393224 | tf_op jit(solution)/shard_map/ppermute | solution.py:261
  54.3 0.5 collective-permute-start.11
  54.8 4.2 %collective-permute-done.11 = f32[32,128]{1,0:T(8,128)S(1)} collective-permute-done((f32[32,128]{1,0:T(8,128)S(1)}, f32[32,128]{1,0:T(8,128)S(1)}, u32[]{:S(2)}, u32[]{:S(2)}) %collective-permute-start.11) | collective-permute-done | bytes 16416 | tf_op jit(solution)/shard_map/ppermute | solution.py:298
  59.0 3.5 %collective-permute-start.12 = (f32[32,128]{1,0:T(8,128)S(1)}, f32[32,128]{1,0:T(8,128)S(1)}, u32[]{:S(2)}, u32[]{:S(2)}) collective-permute-start(f32[32,128]{1,0:T(8,128)S(1)} %add.40.refs_0_), channel_id=1, source_target_pairs={{0,192},{4,196},{8,200},{12,204},{16,208},{20,212},{24,216},{28,22... | collective-permute-start | bytes 49160 | tf_op jit(solution)/shard_map/ppermute | solution.py:298
  62.6 2.3 %collective-permute-done.12.refs_1_ = f32[32,128]{1,0:T(8,128)S(1)} collective-permute-done((f32[32,128]{1,0:T(8,128)S(1)}, f32[32,128]{1,0:T(8,128)S(1)}, u32[]{:S(2)}, u32[]{:S(2)}) %collective-permute-start.12) | collective-permute-done | bytes 16416 | tf_op jit(solution)/shard_map/ppermute | solution.py:298
  64.9 2.0 %factor.1.inv_ref = f32[64,64]{1,0:T(8,128)S(1)} custom-call(f32[32,128]{1,0:T(8,128)S(1)} %add.40.refs_0_, f32[32,128]{1,0:T(8,128)S(1)} %collective-permute-done.12.refs_1_), custom_call_target="tpu_custom_call" | custom-call | flops 1000000000 | bytes 1048576 | tf_op jit(solution)/shard_map/factor/pallas_call | solution.py:361
  66.9 0.0 collective-permute-done.15.refs_1_
  66.9 1.1 %image.1 = (f32[64,2048]{1,0:T(8,128)S(1)}, f32[32,128]{1,0:T(8,128)S(1)}) custom-call(f32[64,64]{1,0:T(8,128)S(1)} %factor.1.inv_ref, f32[64,512]{1,0:T(8,128)S(1)} %add_add_fusion.refs_0_, f32[64,512]{1,0:T(8,128)S(1)} %collective-permute-done.15.refs_1_, f32[64,512]{1,0:T(8,128)S(1)} %collective-permute-done.16.refs_2_, ...), custom_call_target="tpu_custom_call" | custom-call | flops 1000000000 | bytes 1048576 | tf_op jit(solution)/shard_map/image/pallas_call | solution.py:362
  68.0 0.1 collective-permute-start.18
  68.0 1.2 %collective-permute-done.18 = f32[32,128]{1,0:T(8,128)S(1)} collective-permute-done((f32[32,128]{1,0:T(8,128)S(1)}, f32[32,128]{1,0:T(8,128)S(1)}, u32[]{:S(2)}, u32[]{:S(2)}) %collective-permute-start.18) | collective-permute-done | bytes 16416 | tf_op jit(solution)/shard_map/ppermute | solution.py:270
  69.2 0.1 collective-permute-start.21
  69.4 4.6 %collective-permute-start.19 = (f32[32,128]{1,0:T(8,128)S(1)}, f32[32,128]{1,0:T(8,128)S(1)}, u32[]{:S(2)}, u32[]{:S(2)}) collective-permute-start(f32[32,128]{1,0:T(8,128)S(1)} %add.43.me_ref), channel_id=1, source_target_pairs={{0,16},{4,20},{8,24},{12,28},{16,0},{20,4},{24,8},{28,12},{32,48},... | collective-permute-start | bytes 49160 | tf_op jit(solution)/shard_map/ppermute | solution.py:309
  73.9 0.2 collective-permute-done.21.right_ref
  74.2 1.6 %collective-permute-done.19.opposite_ref = f32[32,128]{1,0:T(8,128)S(1)} collective-permute-done((f32[32,128]{1,0:T(8,128)S(1)}, f32[32,128]{1,0:T(8,128)S(1)}, u32[]{:S(2)}, u32[]{:S(2)}) %collective-permute-start.19) | collective-permute-done | bytes 16416 | tf_op jit(solution)/shard_map/ppermute | solution.py:309
  75.8 16.1 %all_to_all.5.gram_ref = f32[8,32,128]{2,1,0:T(8,128)S(1)} all-to-all(f32[8,32,128]{2,1,0:T(8,128)S(1)} %sum_x.1), channel_id=1, replica_groups={{0,32,64,96,128,160,192,224},{1,33,65,97,129,161,193,225},{2,34,66,98,1..., dimensions={0} | all-to-all | bytes 262144 | tf_op jit(solution)/shard_map/all_to_all | solution.py:282
  91.9 3.3 %last.1 = f32[64,2048]{1,0:T(8,128)} custom-call(f32[64,2048]{1,0:T(8,128)S(1)} %get-tuple-element.51.image_ref, f32[8,32,128]{2,1,0:T(8,128)S(1)} %all_to_all.5.gram_ref), custom_call_target="tpu_custom_call" | custom-call | flops 1000000000 | bytes 1048576 | tf_op jit(solution)/shard_map/last/pallas_call | solution.py:363
  (23 shorter events, 0.1 us)
Async XLA Ops:
  0.0 9.5 %copy-start = (f32[2048,256]{1,0:T(8,128)S(1)}, f32[2048,256]{1,0:T(8,128)}, u32[]{:S(2)}) copy-start(f32[2048,256]{1,0:T(8,128)} %x_ref.9) | copy-start | bytes 6291460
  0.0 9.5 %copy-start.1 = (s32[8,2]{0,1:T(2,128)S(1)}, s32[8,2]{0,1:T(2,128)}, u32[]{:S(2)}) copy-start(s32[8,2]{0,1:T(2,128)} %param.5) | copy-start | bytes 196
  0.0 9.5 %copy-start.2 = (f32[2048,64]{0,1:T(8,128)S(1)}, f32[2048,64]{0,1:T(8,128)}, u32[]{:S(2)}) copy-start(f32[2048,64]{0,1:T(8,128)} %param.4) | copy-start | bytes 1572868
  1.2 8.3 %collective-permute-start = (f32[520,256]{1,0:T(8,128)S(1)}, f32[520,256]{1,0:T(8,128)S(1)}, u32[]{:S(2)}, u32[]{:S(2)}) collective-permute-start(f32[520,256]{1,0:T(8,128)S(1)} %cut.1.message_ref), channel_id=1, source_target_pairs={{0,4},{4,0},{8,12},{12,8},{16,20},{20,16},{24,28},{28,24},{32,36},... | collective-permute-start | bytes 1597448 | tf_op jit(solution)/shard_map/ppermute | solution.py:270
  1.3 15.2 %collective-permute-start.2 = (f32[520,256]{1,0:T(8,128)S(1)}, f32[520,256]{1,0:T(8,128)S(1)}, u32[]{:S(2)}, u32[]{:S(2)}) collective-permute-start(f32[520,256]{1,0:T(8,128)S(1)} %cut.1.message_ref), channel_id=1, source_target_pairs={{0,252},{4,8},{8,4},{12,16},{16,12},{20,24},{24,20},{28,32},{32,28... | collective-permute-start | bytes 1597448 | tf_op jit(solution)/shard_map/ppermute | solution.py:266
  13.7 12.1 %collective-permute-start.1 = (f32[64,512]{1,0:T(8,128)S(1)}, f32[64,512]{1,0:T(8,128)S(1)}, u32[]{:S(2)}, u32[]{:S(2)}) collective-permute-start(f32[64,512]{1,0:T(8,128)S(1)} %get-tuple-element.29), channel_id=1, source_target_pairs={{0,4},{4,0},{8,12},{12,8},{16,20},{20,16},{24,28},{28,24},{32,36},... | collective-permute-start | bytes 393224 | tf_op jit(solution)/shard_map/ppermute | solution.py:270
  18.1 7.8 %collective-permute-start.3 = (f32[64,512]{1,0:T(8,128)S(1)}, f32[64,512]{1,0:T(8,128)S(1)}, u32[]{:S(2)}, u32[]{:S(2)}) collective-permute-start(f32[64,512]{1,0:T(8,128)S(1)} %get-tuple-element.34), channel_id=1, source_target_pairs={{0,252},{4,8},{8,4},{12,16},{16,12},{20,24},{24,20},{28,32},{32,28... | collective-permute-start | bytes 393224 | tf_op jit(solution)/shard_map/ppermute | solution.py:266
  26.0 6.2 %collective-permute-start.6 = (f32[64,512]{1,0:T(8,128)S(1)}, f32[64,512]{1,0:T(8,128)S(1)}, u32[]{:S(2)}, u32[]{:S(2)}) collective-permute-start(f32[64,512]{1,0:T(8,128)S(1)} %add_add_fusion.1.refs_0_), channel_id=1, source_target_pairs={{0,3},{1,0},{2,1},{3,2},{4,7},{5,4},{6,5},{7,6},{8,11},{9,8},{10,9... | collective-permute-start | bytes 393224 | tf_op jit(solution)/shard_map/ppermute | solution.py:261
  26.5 7.9 %collective-permute-start.5 = (f32[64,512]{1,0:T(8,128)S(1)}, f32[64,512]{1,0:T(8,128)S(1)}, u32[]{:S(2)}, u32[]{:S(2)}) collective-permute-start(f32[64,512]{1,0:T(8,128)S(1)} %add_add_fusion.1.refs_0_), channel_id=1, source_target_pairs={{0,2},{1,3},{2,0},{3,1},{4,6},{5,7},{6,4},{7,5},{8,10},{9,11},{10,... | collective-permute-start | bytes 393224 | tf_op jit(solution)/shard_map/ppermute | solution.py:261
  29.4 5.7 %collective-permute-start.4 = (f32[64,512]{1,0:T(8,128)S(1)}, f32[64,512]{1,0:T(8,128)S(1)}, u32[]{:S(2)}, u32[]{:S(2)}) collective-permute-start(f32[64,512]{1,0:T(8,128)S(1)} %add_add_fusion.1.refs_0_), channel_id=1, source_target_pairs={{0,1},{1,2},{2,3},{3,0},{4,5},{5,6},{6,7},{7,4},{8,9},{9,10},{10,1... | collective-permute-start | bytes 393224 | tf_op jit(solution)/shard_map/ppermute | solution.py:261
  35.7 1.2 %collective-permute-start.7 = (f32[32,128]{1,0:T(8,128)S(1)}, f32[32,128]{1,0:T(8,128)S(1)}, u32[]{:S(2)}, u32[]{:S(2)}) collective-permute-start(f32[32,128]{1,0:T(8,128)S(1)} %get-tuple-element.35), channel_id=1, source_target_pairs={{0,4},{4,0},{8,12},{12,8},{16,20},{20,16},{24,28},{28,24},{32,36},... | collective-permute-start | bytes 49160 | tf_op jit(solution)/shard_map/ppermute | solution.py:298
  36.9 3.7 %collective-permute-start.8 = (f32[32,128]{1,0:T(8,128)S(1)}, f32[32,128]{1,0:T(8,128)S(1)}, u32[]{:S(2)}, u32[]{:S(2)}) collective-permute-start(f32[32,128]{1,0:T(8,128)S(1)} %add.36), channel_id=1, source_target_pairs={{0,8},{4,12},{8,0},{12,4},{16,24},{20,28},{24,16},{28,20},{32,40},... | collective-permute-start | bytes 49160 | tf_op jit(solution)/shard_map/ppermute | solution.py:298
  40.7 8.0 %collective-permute-start.13 = (f32[64,512]{1,0:T(8,128)S(1)}, f32[64,512]{1,0:T(8,128)S(1)}, u32[]{:S(2)}, u32[]{:S(2)}) collective-permute-start(f32[64,512]{1,0:T(8,128)S(1)} %get-tuple-element.48), channel_id=1, source_target_pairs={{0,4},{4,0},{8,12},{12,8},{16,20},{20,16},{24,28},{28,24},{32,36},... | collective-permute-start | bytes 393224 | tf_op jit(solution)/shard_map/ppermute | solution.py:270
  40.7 8.0 %collective-permute-start.14 = (f32[64,512]{1,0:T(8,128)S(1)}, f32[64,512]{1,0:T(8,128)S(1)}, u32[]{:S(2)}, u32[]{:S(2)}) collective-permute-start(f32[64,512]{1,0:T(8,128)S(1)} %get-tuple-element.50), channel_id=1, source_target_pairs={{0,252},{4,8},{8,4},{12,16},{16,12},{20,24},{24,20},{28,32},{32,28... | collective-permute-start | bytes 393224 | tf_op jit(solution)/shard_map/ppermute | solution.py:266
  43.7 5.0 %collective-permute-start.9 = (f32[32,128]{1,0:T(8,128)S(1)}, f32[32,128]{1,0:T(8,128)S(1)}, u32[]{:S(2)}, u32[]{:S(2)}) collective-permute-start(f32[32,128]{1,0:T(8,128)S(1)} %add.37), channel_id=1, source_target_pairs={{0,24},{4,28},{8,16},{12,20},{16,8},{20,12},{24,0},{28,4},{32,56},... | collective-permute-start | bytes 49160 | tf_op jit(solution)/shard_map/ppermute | solution.py:298
  48.7 5.6 %collective-permute-start.10 = (f32[32,128]{1,0:T(8,128)S(1)}, f32[32,128]{1,0:T(8,128)S(1)}, u32[]{:S(2)}, u32[]{:S(2)}) collective-permute-start(f32[32,128]{1,0:T(8,128)S(1)} %add.38), channel_id=1, source_target_pairs={{0,32},{4,36},{8,40},{12,44},{16,48},{20,52},{24,56},{28,60},{32,0... | collective-permute-start | bytes 49160 | tf_op jit(solution)/shard_map/ppermute | solution.py:298
  48.7 18.1 %collective-permute-start.17 = (f32[64,512]{1,0:T(8,128)S(1)}, f32[64,512]{1,0:T(8,128)S(1)}, u32[]{:S(2)}, u32[]{:S(2)}) collective-permute-start(f32[64,512]{1,0:T(8,128)S(1)} %add_add_fusion.refs_0_), channel_id=1, source_target_pairs={{0,3},{1,0},{2,1},{3,2},{4,7},{5,4},{6,5},{7,6},{8,11},{9,8},{10,9... | collective-permute-start | bytes 393224 | tf_op jit(solution)/shard_map/ppermute | solution.py:261
  50.3 16.6 %collective-permute-start.16 = (f32[64,512]{1,0:T(8,128)S(1)}, f32[64,512]{1,0:T(8,128)S(1)}, u32[]{:S(2)}, u32[]{:S(2)}) collective-permute-start(f32[64,512]{1,0:T(8,128)S(1)} %add_add_fusion.refs_0_), channel_id=1, source_target_pairs={{0,2},{1,3},{2,0},{3,1},{4,6},{5,7},{6,4},{7,5},{8,10},{9,11},{10,... | collective-permute-start | bytes 393224 | tf_op jit(solution)/shard_map/ppermute | solution.py:261
  52.2 14.7 %collective-permute-start.15 = (f32[64,512]{1,0:T(8,128)S(1)}, f32[64,512]{1,0:T(8,128)S(1)}, u32[]{:S(2)}, u32[]{:S(2)}) collective-permute-start(f32[64,512]{1,0:T(8,128)S(1)} %add_add_fusion.refs_0_), channel_id=1, source_target_pairs={{0,1},{1,2},{2,3},{3,0},{4,5},{5,6},{6,7},{7,4},{8,9},{9,10},{10,1... | collective-permute-start | bytes 393224 | tf_op jit(solution)/shard_map/ppermute | solution.py:261
  54.3 4.7 %collective-permute-start.11 = (f32[32,128]{1,0:T(8,128)S(1)}, f32[32,128]{1,0:T(8,128)S(1)}, u32[]{:S(2)}, u32[]{:S(2)}) collective-permute-start(f32[32,128]{1,0:T(8,128)S(1)} %add.39), channel_id=1, source_target_pairs={{0,64},{4,68},{8,72},{12,76},{16,80},{20,84},{24,88},{28,92},{32,9... | collective-permute-start | bytes 49160 | tf_op jit(solution)/shard_map/ppermute | solution.py:298
  59.0 5.8 %collective-permute-start.12 = (f32[32,128]{1,0:T(8,128)S(1)}, f32[32,128]{1,0:T(8,128)S(1)}, u32[]{:S(2)}, u32[]{:S(2)}) collective-permute-start(f32[32,128]{1,0:T(8,128)S(1)} %add.40.refs_0_), channel_id=1, source_target_pairs={{0,192},{4,196},{8,200},{12,204},{16,208},{20,212},{24,216},{28,22... | collective-permute-start | bytes 49160 | tf_op jit(solution)/shard_map/ppermute | solution.py:298
  68.0 1.2 %collective-permute-start.18 = (f32[32,128]{1,0:T(8,128)S(1)}, f32[32,128]{1,0:T(8,128)S(1)}, u32[]{:S(2)}, u32[]{:S(2)}) collective-permute-start(f32[32,128]{1,0:T(8,128)S(1)} %get-tuple-element.52), channel_id=1, source_target_pairs={{0,4},{4,0},{8,12},{12,8},{16,20},{20,16},{24,28},{28,24},{32,36},... | collective-permute-start | bytes 49160 | tf_op jit(solution)/shard_map/ppermute | solution.py:270
  69.2 4.9 %collective-permute-start.21 = (f32[32,128]{1,0:T(8,128)S(1)}, f32[32,128]{1,0:T(8,128)S(1)}, u32[]{:S(2)}, u32[]{:S(2)}) collective-permute-start(f32[32,128]{1,0:T(8,128)S(1)} %add.43.me_ref), channel_id=1, source_target_pairs={{0,24},{4,28},{8,16},{12,20},{16,8},{20,12},{24,0},{28,4},{32,56},... | collective-permute-start | bytes 49160 | tf_op jit(solution)/shard_map/ppermute | solution.py:309
  69.4 4.8 %collective-permute-start.20 = (f32[32,128]{1,0:T(8,128)S(1)}, f32[32,128]{1,0:T(8,128)S(1)}, u32[]{:S(2)}, u32[]{:S(2)}) collective-permute-start(f32[32,128]{1,0:T(8,128)S(1)} %add.43.me_ref), channel_id=1, source_target_pairs={{0,8},{4,12},{8,0},{12,4},{16,24},{20,28},{24,16},{28,20},{32,40},... | collective-permute-start | bytes 49160 | tf_op jit(solution)/shard_map/ppermute | solution.py:309
  69.4 6.4 %collective-permute-start.19 = (f32[32,128]{1,0:T(8,128)S(1)}, f32[32,128]{1,0:T(8,128)S(1)}, u32[]{:S(2)}, u32[]{:S(2)}) collective-permute-start(f32[32,128]{1,0:T(8,128)S(1)} %add.43.me_ref), channel_id=1, source_target_pairs={{0,16},{4,20},{8,24},{12,28},{16,0},{20,4},{24,8},{28,12},{32,48},... | collective-permute-start | bytes 49160 | tf_op jit(solution)/shard_map/ppermute | solution.py:309
